TPU v7x, 1024 devices: a whole 8x8x8 slice. The times are simulated.
1024 devices in a mesh: dp: 64 (over z, y_lo, core), tensor: 16 (over y_hi, x).
Axes of the slice: x: 8, y: 8 (y_hi: 2, y_lo: 4; y = y_hi * 4 + y_lo), z: 8, core: 2. Of those that a mesh axis runs over, the one named last changes fastest.
Arguments:
- policy: bfloat16 [64, 128, 16384], P('dp', 'tensor'), may hold values from -4 to 4
- ref_weight: bfloat16 [8192, 16384], P('tensor', 'dp'), may hold values from -4 to 4
- tokens: bfloat16 [2, 3072, 8192], P(None, 'dp', 'tensor'), may hold values from -400 to 400
- gain: float32 [8192], P('tensor'), may hold values from 0.5 to 2
Outputs:
- blended: bfloat16 [8192, 16384], P('tensor', 'dp')
- activated: bfloat16 [2, 3072, 16384], P(None, 'tensor', 'dp')
All inputs are finite; a program needn't handle non-finite values.
Results may differ from a plain program's by a relative error of at most 0.022.
Values may be sent and summed in bfloat16 or wider, within the bound.
No kernel may reach another device: no remote copies, remote signals or barrier semaphores. Data moves between devices by JAX's collectives and lax.ppermute only.
A program may use at most 64 MiB of HBM per device.

v0:
```python
import math

import jax
import jax.numpy as jnp
from jax import lax
from jax.sharding import PartitionSpec as P

D = 8192


ema_rate = 0.5
norm_eps = 1e-06


def body(policy, ref_weight, tokens, gain):
    arrived = lax.all_to_all(policy, "dp", split_axis=2, concat_axis=0, tiled=True)
    piece_count, piece_rows, piece_cols = arrived.shape
    policy_slice = arrived.reshape(piece_count * piece_rows, piece_cols)
    ref_f = ref_weight.astype(jnp.float32)
    blended = (ref_f + ema_rate * (policy_slice.astype(jnp.float32) - ref_f)).astype(jnp.bfloat16)
    out_scale = 1.0 / math.sqrt(D)
    tensor_count = lax.axis_size("tensor")

    def partial_maker(all_rows):
        micro_count, gath_rows, local_width = all_rows.shape
        per_device = gath_rows // tensor_count
        blocked = all_rows.reshape(micro_count, tensor_count, per_device, local_width)
        span_rows = micro_count * per_device

        def partial_term(first_row, row_count):
            block_count = row_count // span_rows
            flat_rows = jnp.transpose(blocked, (1, 0, 2, 3)).reshape(
                block_count * span_rows, local_width
            )
            return jnp.dot(flat_rows, blended, preferred_element_type=jnp.float32) * out_scale

        return (partial_term, span_rows, per_device)

    pieces = []
    for micro in range(tokens.shape[0]):
        normed_tok_block = tokens[micro : micro + 1]
        tok_f = normed_tok_block.astype(jnp.float32)
        normed_row_total = lax.psum(jnp.sum(tok_f * tok_f, axis=2), "tensor")
        scaled = (
            normed_tok_block.astype(jnp.float32)
            * lax.rsqrt(normed_row_total / D + norm_eps)[..., None]
        )
        all_rows = lax.all_gather((scaled * gain).astype(jnp.bfloat16), "dp", axis=1, tiled=True)
        partial_term, dev_rows, per_device = partial_maker(all_rows)
        summed = lax.psum_scatter(
            partial_term(jnp.int32(0), dev_rows * lax.axis_size("tensor")).astype(jnp.bfloat16),
            "tensor",
            scatter_dimension=0,
            tiled=True,
        ).astype(jnp.float32)
        pieces.append(summed.reshape(1, per_device, summed.shape[1]))
    gate = jnp.concatenate(pieces, axis=0)
    return (blended, jax.nn.silu(gate).astype(jnp.bfloat16))


def solution(mesh):
    return jax.shard_map(
        body,
        mesh=mesh,
        in_specs=(P("dp", "tensor", None), P("tensor", "dp"), P(None, "dp", "tensor"), P("tensor")),
        out_specs=(P("tensor", "dp"), P(None, "tensor", "dp")),
        check_vma=False,
    )
```

profile of v0, /device:TPU:1, one launch (start us, length us, event | category | flops | bytes accessed | tf_op | source)
XLA Modules:
  0.0 791.5 jit_solution(10090110709815239890)
XLA Ops:
  7.2 0.0 all-gather.5.cloned.1.call-start
  7.2 0.9 fusion.10
  8.2 48.4 %all-reduce = (f32[1,48]{1,0:T(1,128)S(1)}, f32[1,48]{1,0:T(1,128)S(1)}) all-reduce(f32[1,48]{1,0:T(1,128)S(1)} %bitcast.29, f32[1,48]{1,0:T(1,128)S(1)} %bitcast.28), channel_id=1, replica_groups=mesh['dp'=64,'tensor'=16] {'tensor'}, use_global_device_ids=true, to_apply=%region_4.0 | all-reduce | flops 96 | bytes 768 | tf_op jit(solution)/shard_map/psum | solution.py:43
  56.6 1.6 fusion.12
  58.2 0.0 all-gather.5.cloned.1.call-update
  58.2 0.0 all-gather.3.cloned.1.call-start
  58.2 0.7 all-gather.3.cloned.1.call-update
  58.9 0.0 reduce-scatter.5.cloned.1.call-start
  59.0 15.3 %copy.6 = bf16[1,8,16384]{1,0,2:T(2,128)(2,1)} copy(bf16[1,8,16384]{2,1,0:T(8,128)(2,1)} %param.4) | data formatting | bytes 524288 | tf_op args[0]
  74.3 0.5 broadcast.26
  74.8 90.8 %reduce.2 = bf16[16384,8]{1,0:T(8,128)(2,1)} reduce(bf16[16384,1,8]{2,1,0:T(2,128)(2,1)} %bitcast.24, bf16[]{:T(256)} %broadcast.26), dimensions={1}, to_apply=%bitcast.19.reduce_sub_computation | reduce | bytes 524290
  165.6 6.2 reshape.33
  171.8 39.2 %all_to_all.4 = bf16[64,2,1024]{2,1,0:T(2,128)(2,1)S(1)} all-to-all(bf16[64,2,1024]{2,1,0:T(2,128)(2,1)S(1)} %reshape.33), channel_id=1, replica_groups=mesh['dp'=64,'tensor'=16] {'dp'}, dimensions={0} | all-to-all | bytes 524288 | tf_op jit(solution)/shard_map/all_to_all | solution.py:16
  211.0 17.1 %reshape.34 = bf16[16384,1,8]{2,1,0:T(2,128)(2,1)} reshape(bf16[64,2,1024]{2,1,0:T(2,128)(2,1)S(1)} %all_to_all.4) | data formatting | bytes 524288
  228.2 10.8 %bitcast_convert_fusion = f32[1,8,16384]{1,0,2:T(1,128)} fusion(bf16[16384,1,8]{2,1,0:T(2,128)(2,1)} %reshape.34), kind=kLoop, calls=%fused_computation.28 | loop fusion | flops 131072 | bytes 786432 | tf_op jit(solution)/shard_map/convert_element_type | solution.py:20
  239.0 0.0 copy-start
  239.0 5.3 copy.7
  244.3 0.0 copy-done
  244.3 0.1 fusion.5
  244.4 0.0 copy-start.1
  244.4 0.0 all-gather.5.cloned.1.call-done
  244.4 4.1 fusion.1
  248.6 0.0 reduce-scatter.5.cloned.1.call-update
  248.6 0.0 reduce-scatter.3.cloned.1.call-start
  248.6 67.1 %all-gather.3.cloned.1.call-done = bf16[1,3072,512]{2,1,0:T(8,128)(2,1)} async-done(((bf16[1,48,512]{2,1,0:T(8,128)(2,1)}), bf16[1,3072,512]{2,1,0:T(8,128)(2,1)}) %all-gather.3.cloned.1.call-update) | async-done | bytes 3145744 | tf_op jit(solution)/shard_map/all_gather | solution.py:48
  315.7 0.0 copy-done.1
  315.7 4.0 fusion
  319.7 0.0 reduce-scatter.3.cloned.1.call-update
  319.7 228.2 %reduce-scatter.5.cloned.1.call-done = bf16[192,256]{1,0:T(8,128)(2,1)} async-done(((bf16[3072,256]{1,0:T(8,128)(2,1)}), bf16[192,256]{1,0:T(8,128)(2,1)}) %reduce-scatter.5.cloned.1.call-update) | async-done | bytes 98320 | tf_op jit(solution)/shard_map/reduce_scatter | solution.py:50
  548.0 235.2 %reduce-scatter.3.cloned.1.call-done = bf16[192,256]{1,0:T(8,128)(2,1)} async-done(((bf16[3072,256]{1,0:T(8,128)(2,1)}), bf16[192,256]{1,0:T(8,128)(2,1)}) %reduce-scatter.3.cloned.1.call-update) | async-done | bytes 98320 | tf_op jit(solution)/shard_map/reduce_scatter | solution.py:50
  783.2 1.7 fusion.9
  (1 shorter events, 0.0 us)
Async XLA Ops:
  7.2 237.3 %all-gather.5.cloned.1.call-start = ((), (), s32[]{:S(2)}) async-start(), calls=%async_computation.5 | async-start | bytes 3194880 | tf_op jit(solution)/shard_map/all_gather | solution.py:48
  58.2 257.5 %all-gather.3.cloned.1.call-start = ((), (), s32[]{:S(2)}) async-start(), calls=%async_computation.3 | async-start | bytes 3194880 | tf_op jit(solution)/shard_map/all_gather | solution.py:48
  58.9 489.1 %reduce-scatter.5.cloned.1.call-start = ((), (), s32[]{:S(2)}) async-start(), calls=%async_computation.6 | async-start | bytes 1671168 | tf_op jit(solution)/shard_map/reduce_scatter | solution.py:50
  239.0 5.3 copy-start
  244.4 71.3 %copy-start.1 = (bf16[512,256]{1,0:T(8,128)(2,1)}, bf16[512,256]{1,0:T(8,128)(2,1)S(1)}, u32[]{:S(2)}) copy-start(bf16[512,256]{1,0:T(8,128)(2,1)S(1)} %fusion.5) | copy-start | bytes 786436
  248.6 534.6 %reduce-scatter.3.cloned.1.call-start = ((), (), s32[]{:S(2)}) async-start(), calls=%async_computation.4 | async-start | bytes 1671168 | tf_op jit(solution)/shard_map/reduce_scatter | solution.py:50
Sparse Core Ops, SparseCore 0:
  58.3 131.0 all-gather.4
  192.7 122.9 all-gather.2
  321.4 226.5 reduce-scatter.4
  553.5 229.6 reduce-scatter.2
where the time goes:
time: 797 us; the launch traced here: 791 us
  waiting for transfers between devices  531 us (67%)
  other arithmetic  106 us (13%)
  blocking collectives  87.6 us (11%)
  local copies, waits for them, and re-layouts  44.5 us (6%)
  between operations  13.8 us (2%)
  matrix products  8.14 us (1%)
    reduce_scatter x2, waiting for transfers between devices, body(): lax.psum_scatter(partial_term(jnp.int32(0), dev_rows * lax.axis_size('ten...  463 us
    unnamed x1, other arithmetic  90.8 us
    all_gather x2, waiting for transfers between devices, body(): lax.all_gather((scaled * gain).astype(jnp.bfloat16), 'dp', axis=1, tiled=...  67.1 us
    psum x1, blocking collectives, body(): normed_row_total = lax.psum(jnp.sum(tok_f * tok_f, axis=2), 'tensor')  48.4 us
    all_to_all x1, blocking collectives, body(): lax.all_to_all(policy, 'dp', split_axis=2, concat_axis=0, tiled=True)  39.2 us
    unnamed x8, local copies, waits for them, and re-layouts  39.2 us
  transfers between devices with their start and end apart: 4, of which 3 were waited for; matrix products, arithmetic and copies ran while one was open for 19% of the time, Pallas kernels for 0%

commit v1 on v0

v1 whole, which is shorter than its diff:
```python
import math

import jax
import jax.numpy as jnp
from jax import lax
from jax.experimental import pallas as pl
from jax.experimental.pallas import tpu as pltpu
from jax.sharding import Mesh
from jax.sharding import PartitionSpec as P

D = 8192
AXES = ("z", "yl", "c", "yh", "x")
NZ, NYL, NC, NYH, NX = SIZES = (8, 4, 2, 2, 8)

ema_rate = 0.5
norm_eps = 1e-06


def flat(z, yl, c, yh, x):
    return (((z * NYL + yl) * NC + c) * NYH + yh) * NX + x


def token_moves(e):
    moves = []
    for j in range(NZ * NYL * NC):
        i, a = divmod(j, 4)
        yh2, x = divmod(i, NX)
        z, rest = divmod(j, NYL * NC)
        yl, c = divmod(rest, NC)
        for yh in range(NYH):
            for x2 in range(NX):
                to = flat(x2, (2 * yh2 + a // 2) ^ e, a % 2, yh, x)
                moves.append((flat(z, yl, c, yh, x2), to))
    return moves


def shift(count, by):
    return [(i, (i + by) % count) for i in range(count)]


def core_shift():
    moves = []
    for z in range(NZ):
        for c in range(NC):
            to = (z + (1 if c == 0 else -1)) % NZ
            moves.append((z * NC + c, to * NC + c))
    return moves


def gate_kernel(place, rows_of, *refs):
    blocks, weights = refs[:NX], refs[NX : 2 * NX]
    kept, sent, a_buf, b_buf, acc, a_sem, b_sem = refs[2 * NX :]
    b_copies = [
        pltpu.make_async_copy(w, b_buf.at[place[d]], b_sem.at[d]) for d, w in enumerate(weights)
    ]
    a_copies = [
        pltpu.make_async_copy(b, a_buf.at[s], a_sem.at[s]) for s, b in enumerate(blocks)
    ]
    for copy in b_copies + a_copies:
        copy.start()
    for copy in b_copies:
        copy.wait()
    for s, copy in enumerate(a_copies):
        copy.wait()
        part = jnp.dot(a_buf[s], b_buf[s], preferred_element_type=jnp.float32)
        acc[...] = part if s == 0 else acc[...] + part
    size = kept.shape[0] // 4
    for b in range(2):
        for core in range(NC):
            to = pl.ds((b * NC + core) * size, size)
            mine = pl.multiple_of((core * NYL + rows_of[b]) * size, size)
            theirs = pl.multiple_of((core * NYL + rows_of[2 + b]) * size, size)
            kept[to, :] = acc[pl.ds(mine, size), :]
            sent[to, :] = acc[pl.ds(theirs, size), :].astype(sent.dtype)


def gate_parts(place, rows_of, blocks, weights):
    rows, depth = blocks[0].shape
    cols = weights[0].shape[1]
    smem = pl.BlockSpec(memory_space=pltpu.SMEM)
    hbm = pl.BlockSpec(memory_space=pl.ANY)
    vmem = pl.BlockSpec(memory_space=pltpu.VMEM)
    half = rows // 2
    return pl.pallas_call(
        gate_kernel,
        out_shape=(
            jax.ShapeDtypeStruct((half, cols), jnp.float32),
            jax.ShapeDtypeStruct((half, cols), jnp.bfloat16),
        ),
        in_specs=[smem, smem] + [hbm] * (2 * NX),
        out_specs=(vmem, vmem),
        scratch_shapes=[
            pltpu.VMEM((NX, rows, depth), jnp.bfloat16),
            pltpu.VMEM((NX, depth, cols), jnp.bfloat16),
            pltpu.VMEM((rows, cols), jnp.float32),
            pltpu.SemaphoreType.DMA((NX,)),
            pltpu.SemaphoreType.DMA((NX,)),
        ],
        compiler_params=pltpu.CompilerParams(vmem_limit_bytes=48 * 2**20),
        cost_estimate=pl.CostEstimate(
            flops=2 * NX * rows * depth * cols,
            bytes_accessed=2 * NX * depth * (rows + cols),
            transcendentals=0,
        ),
    )(place, rows_of, *blocks, *weights)


def body(policy, ref_weight, tokens, gain):
    z, yl, c, yh, x = (lax.axis_index(a) for a in AXES)
    micro, toks, width = tokens.shape
    pieces = policy.reshape(8, NZ * NYL * NC, 256).transpose(1, 0, 2)
    arrived = lax.all_to_all(pieces, ("z", "yl", "c"), 0, 0, tiled=True)
    four = jnp.stack([lax.ppermute(tokens, AXES, token_moves(e)) for e in range(NYL)])
    four = four.reshape(NYL * micro * toks, width)
    four, arrived = lax.optimization_barrier((four, arrived))
    other = lax.ppermute(four, "c", shift(NC, 1))
    first = c == 0
    own = jnp.concatenate([jnp.where(first, four, other), jnp.where(first, other, four)])
    policy_slice = arrived.reshape(ref_weight.shape)
    ref_f = ref_weight.astype(jnp.float32)
    blended = (ref_f + ema_rate * (policy_slice.astype(jnp.float32) - ref_f)).astype(jnp.bfloat16)
    scaled = (blended.astype(jnp.float32) * gain[:, None]).astype(jnp.bfloat16)
    sign = 1 - 2 * c
    blocks, weights = [own] + [None] * (NX - 1), [scaled] + [None] * (NX - 1)
    travelling, up, down = own, scaled, scaled
    half = NX // 2
    for step in range(1, half + 1):
        if step > 1:
            travelling, up, down = lax.optimization_barrier((travelling, up, down))
        arriving = lax.ppermute(travelling, ("z", "c"), core_shift())
        up = lax.ppermute(up, "x", shift(NX, 1))
        if step < half:
            down = lax.ppermute(down, "x", shift(NX, -1))
        if step > 1:
            blocks[step - 1] = lax.ppermute(travelling, "c", shift(NC, 1))
        travelling = arriving
        blocks[NX - step], weights[NX - step] = travelling, up
        if step < half:
            weights[step] = down
    squares = 0.0
    for block in blocks:
        block_f = block.astype(jnp.float32)
        squares = squares + jnp.sum(block_f * block_f, axis=1)
    squares = squares.reshape(NC, NYL, 1, micro * toks)

    def rows_of(group):
        return [yl ^ (2 * group + b) for b in range(2)]

    def part(v, group):
        return jnp.stack(
            [lax.dynamic_index_in_dim(v, q, 1, keepdims=False) for q in rows_of(group)]
        ).reshape(1, -1)

    swap = shift(NYH, 1)
    squares = part(squares, yh) + lax.ppermute(part(squares, 1 - yh), "yh", swap)
    place = jnp.stack([(sign * (x + d - z)) % NX for d in range(NX)])
    kept, sent = gate_parts(
        place, jnp.stack(rows_of(yh) + rows_of(1 - yh)), blocks, weights
    )
    other = lax.ppermute(sent, "yh", swap)
    factor = lax.rsqrt(squares.reshape(-1, 1) / D + norm_eps) * (1.0 / math.sqrt(D))
    gate = (kept + other.astype(jnp.float32)) * factor
    activated = jax.nn.silu(gate).astype(jnp.bfloat16)
    activated = activated.reshape(4, micro, toks, -1).transpose(1, 0, 2, 3)
    return blended, activated.reshape(micro, 4 * toks, -1)


def solution(mesh):
    fine = Mesh(mesh.devices.reshape(SIZES), AXES)
    dp, tensor = ("z", "yl", "c"), ("yh", "x")
    return jax.shard_map(
        body,
        mesh=fine,
        in_specs=(P(dp, tensor, None), P(tensor, dp), P(None, dp, tensor), P(tensor)),
        out_specs=(P(tensor, dp), P(None, tensor, dp)),
        check_vma=False,
    )
```

time: 797 us -> 216 us (0.27)
  the two profiles are of different devices: /device:TPU:1 before, /device:TPU:33 now
where the time goes in v1:
time: 216 us; the launch traced here: 215 us
  starting transfers between devices  103 us (48%)
  waiting for transfers between devices  86.5 us (40%)
  local copies, waits for them, and re-layouts  9.86 us (5%)
  other arithmetic  8.57 us (4%)
  Pallas kernels  6.26 us (3%)
    ppermute x4, waiting for transfers between devices, body(): lax.ppermute(tokens, AXES, token_moves(e))  63.9 us
    ppermute x3, starting transfers between devices, body(): down = lax.ppermute(down, 'x', shift(NX, -1))  21.6 us
    all_to_all x1, starting transfers between devices, body(): arrived = lax.all_to_all(pieces, ('z', 'yl', 'c'), 0, 0, tiled=True)  21.1 us
    ppermute x4, starting transfers between devices, body(): lax.ppermute(tokens, AXES, token_moves(e))  15.2 us
    ppermute x4, starting transfers between devices, body(): arriving = lax.ppermute(travelling, ('z', 'c'), core_shift())  11.8 us
    ppermute x1, waiting for transfers between devices, body(): other = lax.ppermute(sent, 'yh', swap)  11.1 us
    ppermute x3, starting transfers between devices, body(): blocks[step - 1] = lax.ppermute(travelling, 'c', shift(NC, 1))  11 us
    ppermute x4, starting transfers between devices, body(): up = lax.ppermute(up, 'x', shift(NX, 1))  9.11 us
  transfers between devices with their start and end apart: 22, of which 11 were waited for; matrix products, arithmetic and copies ran while one was open for 4% of the time, Pallas kernels for 3%

profile of v1, /device:TPU:33, one launch (start us, length us, event | category | flops | bytes accessed | tf_op | source)
XLA Modules:
  0.0 215.0 jit_solution(2582505682193119158)
XLA Ops:
  0.6 21.1 %all-to-all-start = ((bf16[64,8,256]{2,1,0:T(8,128)(2,1)}), bf16[64,8,256]{2,1,0:T(8,128)(2,1)S(1)}, u32[]{:S(2)}, u32[]{:S(2)}) async-start(bf16[64,8,256]{2,1,0:T(8,128)(2,1)} %bitcast.39), calls=%async_computation | async-start | bytes 524288 | tf_op jit(solution)/shard_map/all_to_all | solution.py:112
  21.7 2.9 %collective-permute-start = (bf16[2,48,512]{2,1,0:T(8,128)(2,1)}, bf16[2,48,512]{2,1,0:T(8,128)(2,1)S(1)}, u32[]{:S(2)}, u32[]{:S(2)}) collective-permute-start(bf16[2,48,512]{2,1,0:T(8,128)(2,1)} %param.6), channel_id=1, source_target_pairs={{0,0},{1,128},{2,256},{3,384},{4,512},{5,640},{6,768},{7,896},{8,8... | collective-permute-start | bytes 294920 | tf_op jit(solution)/shard_map/ppermute | solution.py:113
  24.6 3.3 %collective-permute-start.1 = (bf16[2,48,512]{2,1,0:T(8,128)(2,1)}, bf16[2,48,512]{2,1,0:T(8,128)(2,1)S(1)}, u32[]{:S(2)}, u32[]{:S(2)}) collective-permute-start(bf16[2,48,512]{2,1,0:T(8,128)(2,1)} %param.6), channel_id=1, source_target_pairs={{0,32},{1,160},{2,288},{3,416},{4,544},{5,672},{6,800},{7,928},{8,... | collective-permute-start | bytes 294920 | tf_op jit(solution)/shard_map/ppermute | solution.py:113
  27.9 3.2 %collective-permute-start.2 = (bf16[2,48,512]{2,1,0:T(8,128)(2,1)}, bf16[2,48,512]{2,1,0:T(8,128)(2,1)S(1)}, u32[]{:S(2)}, u32[]{:S(2)}) collective-permute-start(bf16[2,48,512]{2,1,0:T(8,128)(2,1)} %param.6), channel_id=1, source_target_pairs={{0,64},{1,192},{2,320},{3,448},{4,576},{5,704},{6,832},{7,960},{8,... | collective-permute-start | bytes 294920 | tf_op jit(solution)/shard_map/ppermute | solution.py:113
  31.1 5.8 %collective-permute-start.3 = (bf16[2,48,512]{2,1,0:T(8,128)(2,1)}, bf16[2,48,512]{2,1,0:T(8,128)(2,1)S(1)}, u32[]{:S(2)}, u32[]{:S(2)}) collective-permute-start(bf16[2,48,512]{2,1,0:T(8,128)(2,1)} %param.6), channel_id=1, source_target_pairs={{0,96},{1,224},{2,352},{3,480},{4,608},{5,736},{6,864},{7,992},{8,... | collective-permute-start | bytes 294920 | tf_op jit(solution)/shard_map/ppermute | solution.py:113
  36.9 59.8 %collective-permute-done = bf16[2,48,512]{2,1,0:T(8,128)(2,1)S(1)} collective-permute-done((bf16[2,48,512]{2,1,0:T(8,128)(2,1)}, bf16[2,48,512]{2,1,0:T(8,128)(2,1)S(1)}, u32[]{:S(2)}, u32[]{:S(2)}) %collective-permute-start) | collective-permute-done | bytes 98336 | tf_op jit(solution)/shard_map/ppermute | solution.py:113
  96.7 4.1 %collective-permute-done.1 = bf16[2,48,512]{2,1,0:T(8,128)(2,1)S(1)} collective-permute-done((bf16[2,48,512]{2,1,0:T(8,128)(2,1)}, bf16[2,48,512]{2,1,0:T(8,128)(2,1)S(1)}, u32[]{:S(2)}, u32[]{:S(2)}) %collective-permute-start.1) | collective-permute-done | bytes 98336 | tf_op jit(solution)/shard_map/ppermute | solution.py:113
  100.9 2.5 %collective-permute-start.4 = (bf16[384,512]{1,0:T(8,128)(2,1)S(1)}, bf16[384,512]{1,0:T(8,128)(2,1)S(1)}, u32[]{:S(2)}, u32[]{:S(2)}) collective-permute-start(bf16[384,512]{1,0:T(8,128)(2,1)S(1)} %bitcast.36), channel_id=1, source_target_pairs={{0,16},{16,0},{1,17},{17,1},{2,18},{18,2},{3,19},{19,3},{4,20},{20... | collective-permute-start | bytes 1179656 | tf_op jit(solution)/shard_map/ppermute | solution.py:116
  105.7 1.9 collective-permute-start.5
  108.4 1.9 collective-permute-start.6
  110.3 7.7 %collective-permute-start.7 = (bf16[512,256]{1,0:T(8,128)(2,1)S(1)}, bf16[512,256]{1,0:T(8,128)(2,1)S(1)}, u32[]{:S(2)}, u32[]{:S(2)}) collective-permute-start(bf16[512,256]{1,0:T(8,128)(2,1)S(1)} %get-tuple-element.26.refs_8_), channel_id=1, source_target_pairs={{0,7},{1,0},{2,1},{3,2},{4,3},{5,4},{6,5},{7,6},{8,15},{9,8},{10,9... | collective-permute-start | bytes 786440 | tf_op jit(solution)/shard_map/ppermute | solution.py:133
  118.0 2.8 %collective-permute-done.6.refs_15_ = bf16[512,256]{1,0:T(8,128)(2,1)S(1)} collective-permute-done((bf16[512,256]{1,0:T(8,128)(2,1)S(1)}, bf16[512,256]{1,0:T(8,128)(2,1)S(1)}, u32[]{:S(2)}, u32[]{:S(2)}) %collective-permute-start.6) | collective-permute-done | bytes 262176 | tf_op jit(solution)/shard_map/ppermute | solution.py:131
  120.8 1.4 collective-permute-done.7.refs_9_
  122.1 3.0 %collective-permute-start.9 = (bf16[768,512]{1,0:T(8,128)(2,1)}, bf16[768,512]{1,0:T(8,128)(2,1)}, u32[]{:S(2)}, u32[]{:S(2)}) collective-permute-start(bf16[768,512]{1,0:T(8,128)(2,1)} %collective-permute-done.5.refs_7_), channel_id=1, source_target_pairs={{0,128},{16,912},{128,256},{144,16},{256,384},{272,144},{384,512},... | collective-permute-start | bytes 2359304 | tf_op jit(solution)/shard_map/ppermute | solution.py:130
  125.1 1.9 collective-permute-start.10
  127.8 9.3 %collective-permute-start.11 = (bf16[512,256]{1,0:T(8,128)(2,1)S(1)}, bf16[512,256]{1,0:T(8,128)(2,1)S(1)}, u32[]{:S(2)}, u32[]{:S(2)}) collective-permute-start(bf16[512,256]{1,0:T(8,128)(2,1)S(1)} %collective-permute-done.7.refs_9_), channel_id=1, source_target_pairs={{0,7},{1,0},{2,1},{3,2},{4,3},{5,4},{6,5},{7,6},{8,15},{9,8},{10,9... | collective-permute-start | bytes 786440 | tf_op jit(solution)/shard_map/ppermute | solution.py:133
  137.8 3.1 %collective-permute-done.10.refs_14_ = bf16[512,256]{1,0:T(8,128)(2,1)S(1)} collective-permute-done((bf16[512,256]{1,0:T(8,128)(2,1)S(1)}, bf16[512,256]{1,0:T(8,128)(2,1)S(1)}, u32[]{:S(2)}, u32[]{:S(2)}) %collective-permute-start.10) | collective-permute-done | bytes 262176 | tf_op jit(solution)/shard_map/ppermute | solution.py:131
  140.9 1.6 collective-permute-done.11.refs_10_
  142.5 1.9 collective-permute-start.13
  144.4 3.9 %collective-permute-start.8 = (bf16[768,512]{1,0:T(8,128)(2,1)}, bf16[768,512]{1,0:T(8,128)(2,1)S(1)}, u32[]{:S(2)}, u32[]{:S(2)}) collective-permute-start(bf16[768,512]{1,0:T(8,128)(2,1)} %collective-permute-done.5.refs_7_), channel_id=1, source_target_pairs={{0,16},{16,0},{1,17},{17,1},{2,18},{18,2},{3,19},{19,3},{4,20},{20... | collective-permute-start | bytes 2359304 | tf_op jit(solution)/shard_map/ppermute | solution.py:135
  148.3 1.9 collective-permute-start.14
  150.2 4.6 %collective-permute-start.15 = (bf16[512,256]{1,0:T(8,128)(2,1)S(1)}, bf16[512,256]{1,0:T(8,128)(2,1)S(1)}, u32[]{:S(2)}, u32[]{:S(2)}) collective-permute-start(bf16[512,256]{1,0:T(8,128)(2,1)S(1)} %collective-permute-done.11.refs_10_), channel_id=1, source_target_pairs={{0,7},{1,0},{2,1},{3,2},{4,3},{5,4},{6,5},{7,6},{8,15},{9,8},{10,9... | collective-permute-start | bytes 786440 | tf_op jit(solution)/shard_map/ppermute | solution.py:133
  155.1 2.5 %collective-permute-start.12 = (bf16[768,512]{1,0:T(8,128)(2,1)}, bf16[768,512]{1,0:T(8,128)(2,1)S(1)}, u32[]{:S(2)}, u32[]{:S(2)}) collective-permute-start(bf16[768,512]{1,0:T(8,128)(2,1)} %collective-permute-done.9.refs_6_), channel_id=1, source_target_pairs={{0,16},{16,0},{1,17},{17,1},{2,18},{18,2},{3,19},{19,3},{4,20},{20... | collective-permute-start | bytes 2359304 | tf_op jit(solution)/shard_map/ppermute | solution.py:135
  160.9 5.0 %collective-permute-start.17 = (bf16[768,512]{1,0:T(8,128)(2,1)}, bf16[768,512]{1,0:T(8,128)(2,1)S(1)}, u32[]{:S(2)}, u32[]{:S(2)}) collective-permute-start(bf16[768,512]{1,0:T(8,128)(2,1)} %collective-permute-done.13.refs_5_), channel_id=1, source_target_pairs={{0,128},{16,912},{128,256},{144,16},{256,384},{272,144},{384,512},... | collective-permute-start | bytes 2359304 | tf_op jit(solution)/shard_map/ppermute | solution.py:130
  165.9 1.4 multiply_reduce_fusion
  167.3 4.6 %collective-permute-start.16 = (bf16[768,512]{1,0:T(8,128)(2,1)}, bf16[768,512]{1,0:T(8,128)(2,1)S(1)}, u32[]{:S(2)}, u32[]{:S(2)}) collective-permute-start(bf16[768,512]{1,0:T(8,128)(2,1)} %collective-permute-done.13.refs_5_), channel_id=1, source_target_pairs={{0,16},{16,0},{1,17},{17,1},{2,18},{18,2},{3,19},{19,3},{4,20},{20... | collective-permute-start | bytes 2359304 | tf_op jit(solution)/shard_map/ppermute | solution.py:135
  171.9 1.4 multiply_reduce_fusion.1
  173.5 3.4 %collective-permute-start.18 = (bf16[512,256]{1,0:T(8,128)(2,1)}, bf16[512,256]{1,0:T(8,128)(2,1)}, u32[]{:S(2)}, u32[]{:S(2)}) collective-permute-start(bf16[512,256]{1,0:T(8,128)(2,1)} %collective-permute-done.14.refs_13_), channel_id=1, source_target_pairs={{0,1},{1,2},{2,3},{3,4},{4,5},{5,6},{6,7},{7,0},{8,9},{9,10},{10,1... | collective-permute-start | bytes 786440 | tf_op jit(solution)/shard_map/ppermute | solution.py:131
  179.6 5.2 %collective-permute-start.20 = (f32[1,384]{1,0:T(1,128)S(1)}, f32[1,384]{1,0:T(1,128)S(1)}, u32[]{:S(2)}, u32[]{:S(2)}) collective-permute-start(f32[1,384]{1,0:T(1,128)S(1)} %reshape.136), channel_id=1, source_target_pairs={{0,8},{8,0},{1,9},{9,1},{2,10},{10,2},{3,11},{11,3},{4,12},{12,4},... | collective-permute-start | bytes 4616 | tf_op jit(solution)/shard_map/ppermute | solution.py:155
  189.6 6.3 %shard_map.59 = (f32[384,256]{1,0:T(8,128)S(1)}, bf16[384,256]{1,0:T(8,128)(2,1)}) custom-call(s32[8]{0:T(128)S(1)} %stack.88.place, s32[4]{0:T(128)S(1)} %pad_add_fusion.rows_of, bf16[768,512]{1,0:T(8,128)(2,1)S(1)} %pad_maximum_fusion.refs_0_, bf16[768,512]{1,0:T(8,128)(2,1)S(1)} %collective-permute-done.8.refs_1_, ...), custom_call_target="tpu_custom_call" | custom-call | flops 1610612736 | bytes 8388608 | tf_op jit(solution)/shard_map/pallas_call | solution.py:84
  196.6 5.2 %collective-permute-start.19 = (bf16[384,256]{1,0:T(8,128)(2,1)}, bf16[384,256]{1,0:T(8,128)(2,1)S(1)}, u32[]{:S(2)}, u32[]{:S(2)}) collective-permute-start(bf16[384,256]{1,0:T(8,128)(2,1)} %get-tuple-element.25), channel_id=1, source_target_pairs={{0,8},{8,0},{1,9},{9,1},{2,10},{10,2},{3,11},{11,3},{4,12},{12,4},... | collective-permute-start | bytes 589832 | tf_op jit(solution)/shard_map/ppermute | solution.py:160
  202.0 11.1 %collective-permute-done.19 = bf16[384,256]{1,0:T(8,128)(2,1)S(1)} collective-permute-done((bf16[384,256]{1,0:T(8,128)(2,1)}, bf16[384,256]{1,0:T(8,128)(2,1)S(1)}, u32[]{:S(2)}, u32[]{:S(2)}) %collective-permute-start.19) | collective-permute-done | bytes 196640 | tf_op jit(solution)/shard_map/ppermute | solution.py:160
  (69 shorter events, 18.4 us)
Async XLA Ops:
  0.6 100.2 %all-to-all-start = ((bf16[64,8,256]{2,1,0:T(8,128)(2,1)}), bf16[64,8,256]{2,1,0:T(8,128)(2,1)S(1)}, u32[]{:S(2)}, u32[]{:S(2)}) async-start(bf16[64,8,256]{2,1,0:T(8,128)(2,1)} %bitcast.39), calls=%async_computation | async-start | bytes 524288 | tf_op jit(solution)/shard_map/all_to_all | solution.py:112
  21.7 75.0 %collective-permute-start = (bf16[2,48,512]{2,1,0:T(8,128)(2,1)}, bf16[2,48,512]{2,1,0:T(8,128)(2,1)S(1)}, u32[]{:S(2)}, u32[]{:S(2)}) collective-permute-start(bf16[2,48,512]{2,1,0:T(8,128)(2,1)} %param.6), channel_id=1, source_target_pairs={{0,0},{1,128},{2,256},{3,384},{4,512},{5,640},{6,768},{7,896},{8,8... | collective-permute-start | bytes 294920 | tf_op jit(solution)/shard_map/ppermute | solution.py:113
  24.6 76.2 %collective-permute-start.1 = (bf16[2,48,512]{2,1,0:T(8,128)(2,1)}, bf16[2,48,512]{2,1,0:T(8,128)(2,1)S(1)}, u32[]{:S(2)}, u32[]{:S(2)}) collective-permute-start(bf16[2,48,512]{2,1,0:T(8,128)(2,1)} %param.6), channel_id=1, source_target_pairs={{0,32},{1,160},{2,288},{3,416},{4,544},{5,672},{6,800},{7,928},{8,... | collective-permute-start | bytes 294920 | tf_op jit(solution)/shard_map/ppermute | solution.py:113
  27.9 72.9 %collective-permute-start.2 = (bf16[2,48,512]{2,1,0:T(8,128)(2,1)}, bf16[2,48,512]{2,1,0:T(8,128)(2,1)S(1)}, u32[]{:S(2)}, u32[]{:S(2)}) collective-permute-start(bf16[2,48,512]{2,1,0:T(8,128)(2,1)} %param.6), channel_id=1, source_target_pairs={{0,64},{1,192},{2,320},{3,448},{4,576},{5,704},{6,832},{7,960},{8,... | collective-permute-start | bytes 294920 | tf_op jit(solution)/shard_map/ppermute | solution.py:113
  31.1 69.8 %collective-permute-start.3 = (bf16[2,48,512]{2,1,0:T(8,128)(2,1)}, bf16[2,48,512]{2,1,0:T(8,128)(2,1)S(1)}, u32[]{:S(2)}, u32[]{:S(2)}) collective-permute-start(bf16[2,48,512]{2,1,0:T(8,128)(2,1)} %param.6), channel_id=1, source_target_pairs={{0,96},{1,224},{2,352},{3,480},{4,608},{5,736},{6,864},{7,992},{8,... | collective-permute-start | bytes 294920 | tf_op jit(solution)/shard_map/ppermute | solution.py:113
  100.9 3.8 %collective-permute-start.4 = (bf16[384,512]{1,0:T(8,128)(2,1)S(1)}, bf16[384,512]{1,0:T(8,128)(2,1)S(1)}, u32[]{:S(2)}, u32[]{:S(2)}) collective-permute-start(bf16[384,512]{1,0:T(8,128)(2,1)S(1)} %bitcast.36), channel_id=1, source_target_pairs={{0,16},{16,0},{1,17},{17,1},{2,18},{18,2},{3,19},{19,3},{4,20},{20... | collective-permute-start | bytes 1179656 | tf_op jit(solution)/shard_map/ppermute | solution.py:116
  104.8 2.8 %copy-start.14 = (bf16[512,256]{1,0:T(8,128)(2,1)S(1)}, bf16[512,256]{1,0:T(8,128)(2,1)}, u32[]{:S(2)}) copy-start(bf16[512,256]{1,0:T(8,128)(2,1)} %param.5) | copy-start | bytes 786436
  104.8 2.8 %copy-start.15 = (f32[512]{0:T(512)S(1)}, f32[512]{0:T(512)}, u32[]{:S(2)}) copy-start(f32[512]{0:T(512)} %param.7) | copy-start | bytes 6148
  105.7 16.5 %collective-permute-start.5 = (bf16[768,512]{1,0:T(8,128)(2,1)S(1)}, bf16[768,512]{1,0:T(8,128)(2,1)}, u32[]{:S(2)}, u32[]{:S(2)}) collective-permute-start(bf16[768,512]{1,0:T(8,128)(2,1)S(1)} %pad_maximum_fusion.refs_0_), channel_id=1, source_target_pairs={{0,128},{16,912},{128,256},{144,16},{256,384},{272,144},{384,512},... | collective-permute-start | bytes 2359304 | tf_op jit(solution)/shard_map/ppermute | solution.py:130
  108.4 12.4 %collective-permute-start.6 = (bf16[512,256]{1,0:T(8,128)(2,1)S(1)}, bf16[512,256]{1,0:T(8,128)(2,1)S(1)}, u32[]{:S(2)}, u32[]{:S(2)}) collective-permute-start(bf16[512,256]{1,0:T(8,128)(2,1)S(1)} %get-tuple-element.26.refs_8_), channel_id=1, source_target_pairs={{0,1},{1,2},{2,3},{3,4},{4,5},{5,6},{6,7},{7,0},{8,9},{9,10},{10,1... | collective-permute-start | bytes 786440 | tf_op jit(solution)/shard_map/ppermute | solution.py:131
  110.3 11.8 %collective-permute-start.7 = (bf16[512,256]{1,0:T(8,128)(2,1)S(1)}, bf16[512,256]{1,0:T(8,128)(2,1)S(1)}, u32[]{:S(2)}, u32[]{:S(2)}) collective-permute-start(bf16[512,256]{1,0:T(8,128)(2,1)S(1)} %get-tuple-element.26.refs_8_), channel_id=1, source_target_pairs={{0,7},{1,0},{2,1},{3,2},{4,3},{5,4},{6,5},{7,6},{8,15},{9,8},{10,9... | collective-permute-start | bytes 786440 | tf_op jit(solution)/shard_map/ppermute | solution.py:133
  122.1 20.3 %collective-permute-start.9 = (bf16[768,512]{1,0:T(8,128)(2,1)}, bf16[768,512]{1,0:T(8,128)(2,1)}, u32[]{:S(2)}, u32[]{:S(2)}) collective-permute-start(bf16[768,512]{1,0:T(8,128)(2,1)} %collective-permute-done.5.refs_7_), channel_id=1, source_target_pairs={{0,128},{16,912},{128,256},{144,16},{256,384},{272,144},{384,512},... | collective-permute-start | bytes 2359304 | tf_op jit(solution)/shard_map/ppermute | solution.py:130
  125.1 15.8 %collective-permute-start.10 = (bf16[512,256]{1,0:T(8,128)(2,1)S(1)}, bf16[512,256]{1,0:T(8,128)(2,1)S(1)}, u32[]{:S(2)}, u32[]{:S(2)}) collective-permute-start(bf16[512,256]{1,0:T(8,128)(2,1)S(1)} %collective-permute-done.6.refs_15_), channel_id=1, source_target_pairs={{0,1},{1,2},{2,3},{3,4},{4,5},{5,6},{6,7},{7,0},{8,9},{9,10},{10,1... | collective-permute-start | bytes 786440 | tf_op jit(solution)/shard_map/ppermute | solution.py:131
  127.8 14.7 %collective-permute-start.11 = (bf16[512,256]{1,0:T(8,128)(2,1)S(1)}, bf16[512,256]{1,0:T(8,128)(2,1)S(1)}, u32[]{:S(2)}, u32[]{:S(2)}) collective-permute-start(bf16[512,256]{1,0:T(8,128)(2,1)S(1)} %collective-permute-done.7.refs_9_), channel_id=1, source_target_pairs={{0,7},{1,0},{2,1},{3,2},{4,3},{5,4},{6,5},{7,6},{8,15},{9,8},{10,9... | collective-permute-start | bytes 786440 | tf_op jit(solution)/shard_map/ppermute | solution.py:133
  140.9 25.0 %copy-start.5 = (bf16[512,256]{1,0:T(8,128)(2,1)}, bf16[512,256]{1,0:T(8,128)(2,1)S(1)}, u32[]{:S(2)}) copy-start(bf16[512,256]{1,0:T(8,128)(2,1)S(1)} %collective-permute-done.10.refs_14_) | copy-start | bytes 786436
  142.5 23.5 %copy-start.7 = (bf16[512,256]{1,0:T(8,128)(2,1)}, bf16[512,256]{1,0:T(8,128)(2,1)S(1)}, u32[]{:S(2)}) copy-start(bf16[512,256]{1,0:T(8,128)(2,1)S(1)} %collective-permute-done.11.refs_10_) | copy-start | bytes 786436
  142.5 18.5 %collective-permute-start.13 = (bf16[768,512]{1,0:T(8,128)(2,1)}, bf16[768,512]{1,0:T(8,128)(2,1)}, u32[]{:S(2)}, u32[]{:S(2)}) collective-permute-start(bf16[768,512]{1,0:T(8,128)(2,1)} %collective-permute-done.9.refs_6_), channel_id=1, source_target_pairs={{0,128},{16,912},{128,256},{144,16},{256,384},{272,144},{384,512},... | collective-permute-start | bytes 2359304 | tf_op jit(solution)/shard_map/ppermute | solution.py:130
  144.4 28.9 %collective-permute-start.8 = (bf16[768,512]{1,0:T(8,128)(2,1)}, bf16[768,512]{1,0:T(8,128)(2,1)S(1)}, u32[]{:S(2)}, u32[]{:S(2)}) collective-permute-start(bf16[768,512]{1,0:T(8,128)(2,1)} %collective-permute-done.5.refs_7_), channel_id=1, source_target_pairs={{0,16},{16,0},{1,17},{17,1},{2,18},{18,2},{3,19},{19,3},{4,20},{20... | collective-permute-start | bytes 2359304 | tf_op jit(solution)/shard_map/ppermute | solution.py:135
  148.3 11.1 %collective-permute-start.14 = (bf16[512,256]{1,0:T(8,128)(2,1)S(1)}, bf16[512,256]{1,0:T(8,128)(2,1)}, u32[]{:S(2)}, u32[]{:S(2)}) collective-permute-start(bf16[512,256]{1,0:T(8,128)(2,1)S(1)} %collective-permute-done.10.refs_14_), channel_id=1, source_target_pairs={{0,1},{1,2},{2,3},{3,4},{4,5},{5,6},{6,7},{7,0},{8,9},{9,10},{10,1... | collective-permute-start | bytes 786440 | tf_op jit(solution)/shard_map/ppermute | solution.py:131
  150.2 10.0 %collective-permute-start.15 = (bf16[512,256]{1,0:T(8,128)(2,1)S(1)}, bf16[512,256]{1,0:T(8,128)(2,1)S(1)}, u32[]{:S(2)}, u32[]{:S(2)}) collective-permute-start(bf16[512,256]{1,0:T(8,128)(2,1)S(1)} %collective-permute-done.11.refs_10_), channel_id=1, source_target_pairs={{0,7},{1,0},{2,1},{3,2},{4,3},{5,4},{6,5},{7,6},{8,15},{9,8},{10,9... | collective-permute-start | bytes 786440 | tf_op jit(solution)/shard_map/ppermute | solution.py:133
  155.1 23.2 %collective-permute-start.12 = (bf16[768,512]{1,0:T(8,128)(2,1)}, bf16[768,512]{1,0:T(8,128)(2,1)S(1)}, u32[]{:S(2)}, u32[]{:S(2)}) collective-permute-start(bf16[768,512]{1,0:T(8,128)(2,1)} %collective-permute-done.9.refs_6_), channel_id=1, source_target_pairs={{0,16},{16,0},{1,17},{17,1},{2,18},{18,2},{3,19},{19,3},{4,20},{20... | collective-permute-start | bytes 2359304 | tf_op jit(solution)/shard_map/ppermute | solution.py:135
  160.9 17.6 %collective-permute-start.17 = (bf16[768,512]{1,0:T(8,128)(2,1)}, bf16[768,512]{1,0:T(8,128)(2,1)S(1)}, u32[]{:S(2)}, u32[]{:S(2)}) collective-permute-start(bf16[768,512]{1,0:T(8,128)(2,1)} %collective-permute-done.13.refs_5_), channel_id=1, source_target_pairs={{0,128},{16,912},{128,256},{144,16},{256,384},{272,144},{384,512},... | collective-permute-start | bytes 2359304 | tf_op jit(solution)/shard_map/ppermute | solution.py:130
  167.3 11.4 %collective-permute-start.16 = (bf16[768,512]{1,0:T(8,128)(2,1)}, bf16[768,512]{1,0:T(8,128)(2,1)S(1)}, u32[]{:S(2)}, u32[]{:S(2)}) collective-permute-start(bf16[768,512]{1,0:T(8,128)(2,1)} %collective-permute-done.13.refs_5_), channel_id=1, source_target_pairs={{0,16},{16,0},{1,17},{17,1},{2,18},{18,2},{3,19},{19,3},{4,20},{20... | collective-permute-start | bytes 2359304 | tf_op jit(solution)/shard_map/ppermute | solution.py:135
  173.5 11.3 %collective-permute-start.18 = (bf16[512,256]{1,0:T(8,128)(2,1)}, bf16[512,256]{1,0:T(8,128)(2,1)}, u32[]{:S(2)}, u32[]{:S(2)}) collective-permute-start(bf16[512,256]{1,0:T(8,128)(2,1)} %collective-permute-done.14.refs_13_), channel_id=1, source_target_pairs={{0,1},{1,2},{2,3},{3,4},{4,5},{5,6},{6,7},{7,0},{8,9},{9,10},{10,1... | collective-permute-start | bytes 786440 | tf_op jit(solution)/shard_map/ppermute | solution.py:131
  178.5 0.9 copy-start.13
  179.6 22.4 %collective-permute-start.20 = (f32[1,384]{1,0:T(1,128)S(1)}, f32[1,384]{1,0:T(1,128)S(1)}, u32[]{:S(2)}, u32[]{:S(2)}) collective-permute-start(f32[1,384]{1,0:T(1,128)S(1)} %reshape.136), channel_id=1, source_target_pairs={{0,8},{8,0},{1,9},{9,1},{2,10},{10,2},{3,11},{11,3},{4,12},{12,4},... | collective-permute-start | bytes 4616 | tf_op jit(solution)/shard_map/ppermute | solution.py:155
  184.9 1.0 copy-start.2
  185.8 0.9 copy-start.4
  186.8 0.9 copy-start.6
  187.7 0.9 copy-start.8
  188.7 0.9 copy-start.10
  196.6 16.5 %collective-permute-start.19 = (bf16[384,256]{1,0:T(8,128)(2,1)}, bf16[384,256]{1,0:T(8,128)(2,1)S(1)}, u32[]{:S(2)}, u32[]{:S(2)}) collective-permute-start(bf16[384,256]{1,0:T(8,128)(2,1)} %get-tuple-element.25), channel_id=1, source_target_pairs={{0,8},{8,0},{1,9},{9,1},{2,10},{10,2},{3,11},{11,3},{4,12},{12,4},... | collective-permute-start | bytes 589832 | tf_op jit(solution)/shard_map/ppermute | solution.py:160
  (6 other events, 4.5 us)

commit v2 on v1

--- a/solution.py
+++ b/solution.py
@@ -20,7 +20,7 @@
     return (((z * NYL + yl) * NC + c) * NYH + yh) * NX + x
 
 
-def token_moves(e):
+def token_moves():
     moves = []
     for j in range(NZ * NYL * NC):
         i, a = divmod(j, 4)
@@ -29,7 +29,7 @@
         yl, c = divmod(rest, NC)
         for yh in range(NYH):
             for x2 in range(NX):
-                to = flat(x2, (2 * yh2 + a // 2) ^ e, a % 2, yh, x)
+                to = flat(x2, 2 * yh2 + a // 2, a % 2, yh, x)
                 moves.append((flat(z, yl, c, yh, x2), to))
     return moves
 
@@ -48,10 +48,10 @@
 
 
 def gate_kernel(place, rows_of, *refs):
-    blocks, weights = refs[:NX], refs[NX : 2 * NX]
-    kept, sent, a_buf, b_buf, acc, a_sem, b_sem = refs[2 * NX :]
+    blocks, weights = refs[:NX], refs[NX]
+    kept, sent, a_buf, b_buf, acc, a_sem, b_sem = refs[NX + 1 :]
     b_copies = [
-        pltpu.make_async_copy(w, b_buf.at[place[d]], b_sem.at[d]) for d, w in enumerate(weights)
+        pltpu.make_async_copy(weights.at[d], b_buf.at[place[d]], b_sem.at[d]) for d in range(NX)
     ]
     a_copies = [
         pltpu.make_async_copy(b, a_buf.at[s], a_sem.at[s]) for s, b in enumerate(blocks)
@@ -76,7 +76,7 @@
 
 def gate_parts(place, rows_of, blocks, weights):
     rows, depth = blocks[0].shape
-    cols = weights[0].shape[1]
+    cols = weights.shape[2]
     smem = pl.BlockSpec(memory_space=pltpu.SMEM)
     hbm = pl.BlockSpec(memory_space=pl.ANY)
     vmem = pl.BlockSpec(memory_space=pltpu.VMEM)
@@ -87,7 +87,7 @@
             jax.ShapeDtypeStruct((half, cols), jnp.float32),
             jax.ShapeDtypeStruct((half, cols), jnp.bfloat16),
         ),
-        in_specs=[smem, smem] + [hbm] * (2 * NX),
+        in_specs=[smem, smem] + [hbm] * (NX + 1),
         out_specs=(vmem, vmem),
         scratch_shapes=[
             pltpu.VMEM((NX, rows, depth), jnp.bfloat16),
@@ -102,7 +102,7 @@
             bytes_accessed=2 * NX * depth * (rows + cols),
             transcendentals=0,
         ),
-    )(place, rows_of, *blocks, *weights)
+    )(place, rows_of, *blocks, weights)
 
 
 def body(policy, ref_weight, tokens, gain):
@@ -110,7 +110,10 @@
     micro, toks, width = tokens.shape
     pieces = policy.reshape(8, NZ * NYL * NC, 256).transpose(1, 0, 2)
     arrived = lax.all_to_all(pieces, ("z", "yl", "c"), 0, 0, tiled=True)
-    four = jnp.stack([lax.ppermute(tokens, AXES, token_moves(e)) for e in range(NYL)])
+    moved = lax.ppermute(tokens, AXES, token_moves())
+    four = jnp.stack(
+        [moved] + [lax.ppermute(moved, "yl", [(i, i ^ e) for i in range(NYL)]) for e in range(1, NYL)]
+    )
     four = four.reshape(NYL * micro * toks, width)
     four, arrived = lax.optimization_barrier((four, arrived))
     other = lax.ppermute(four, "c", shift(NC, 1))
@@ -120,23 +123,17 @@
     ref_f = ref_weight.astype(jnp.float32)
     blended = (ref_f + ema_rate * (policy_slice.astype(jnp.float32) - ref_f)).astype(jnp.bfloat16)
     scaled = (blended.astype(jnp.float32) * gain[:, None]).astype(jnp.bfloat16)
+    weights = lax.all_to_all(
+        jnp.broadcast_to(scaled[None], (NX,) + scaled.shape), "x", 0, 0, tiled=True
+    )
     sign = 1 - 2 * c
-    blocks, weights = [own] + [None] * (NX - 1), [scaled] + [None] * (NX - 1)
-    travelling, up, down = own, scaled, scaled
+    blocks, travelling = [own] + [None] * (NX - 1), own
     half = NX // 2
     for step in range(1, half + 1):
-        if step > 1:
-            travelling, up, down = lax.optimization_barrier((travelling, up, down))
-        arriving = lax.ppermute(travelling, ("z", "c"), core_shift())
-        up = lax.ppermute(up, "x", shift(NX, 1))
+        travelling = lax.ppermute(travelling, ("z", "c"), core_shift())
+        blocks[NX - step] = travelling
         if step < half:
-            down = lax.ppermute(down, "x", shift(NX, -1))
-        if step > 1:
-            blocks[step - 1] = lax.ppermute(travelling, "c", shift(NC, 1))
-        travelling = arriving
-        blocks[NX - step], weights[NX - step] = travelling, up
-        if step < half:
-            weights[step] = down
+            blocks[step] = lax.ppermute(travelling, "c", shift(NC, 1))
     squares = 0.0
     for block in blocks:
         block_f = block.astype(jnp.float32)
@@ -153,7 +150,7 @@
 
     swap = shift(NYH, 1)
     squares = part(squares, yh) + lax.ppermute(part(squares, 1 - yh), "yh", swap)
-    place = jnp.stack([(sign * (x + d - z)) % NX for d in range(NX)])
+    place = jnp.stack([(sign * (d - z)) % NX for d in range(NX)])
     kept, sent = gate_parts(
         place, jnp.stack(rows_of(yh) + rows_of(1 - yh)), blocks, weights
     )

time: 216 us -> 180 us (0.83)
  the two profiles are of different devices: /device:TPU:33 before, /device:TPU:32 now
where the time goes in v2:
time: 180 us
  waiting for transfers between devices  90.5 us (50%)
  starting transfers between devices  68.3 us (38%)
  local copies, waits for them, and re-layouts  7.14 us (4%)
  Pallas kernels  6.66 us (4%)
  other arithmetic  5.84 us (3%)
    ppermute x1, waiting for transfers between devices, body(): moved = lax.ppermute(tokens, AXES, token_moves())  39.6 us
    ppermute x4, waiting for transfers between devices, body(): travelling = lax.ppermute(travelling, ('z', 'c'), core_shift())  35.9 us
    all_to_all x1, starting transfers between devices, body(): arrived = lax.all_to_all(pieces, ('z', 'yl', 'c'), 0, 0, tiled=True)  20.7 us
    ppermute x3, starting transfers between devices, body(): lax.ppermute(moved, 'yl', [(i, i ^ e) for i in range(NYL)])  14.3 us
    ppermute x1, waiting for transfers between devices, body(): other = lax.ppermute(sent, 'yh', swap)  8.74 us
    ppermute x4, starting transfers between devices, body(): travelling = lax.ppermute(travelling, ('z', 'c'), core_shift())  7.65 us
    pallas_call x1, Pallas kernels, gate_parts(): pl.pallas_call(gate_kernel, out_shape=(jax.ShapeDtypeStruct((half, cols),...  6.66 us
    ppermute x3, starting transfers between devices, body(): blocks[step] = lax.ppermute(travelling, 'c', shift(NC, 1))  6.24 us
  transfers between devices with their start and end apart: 16, of which 9 were waited for; matrix products, arithmetic and copies ran while one was open for 4% of the time, Pallas kernels for 4%

profile of v2, /device:TPU:32, one launch (start us, length us, event | category | flops | bytes accessed | tf_op | source)
XLA Modules:
  0.0 179.6 jit_solution(12096735739804231796)
XLA Ops:
  0.6 20.7 %all-to-all-start = ((bf16[64,8,256]{2,1,0:T(8,128)(2,1)}), bf16[64,8,256]{2,1,0:T(8,128)(2,1)S(1)}, u32[]{:S(2)}, u32[]{:S(2)}) async-start(bf16[64,8,256]{2,1,0:T(8,128)(2,1)} %bitcast.39), calls=%async_computation | async-start | bytes 524288 | tf_op jit(solution)/shard_map/all_to_all | solution.py:112
  21.4 3.3 %collective-permute-start = (bf16[2,48,512]{2,1,0:T(8,128)(2,1)}, bf16[2,48,512]{2,1,0:T(8,128)(2,1)S(1)}, u32[]{:S(2)}, u32[]{:S(2)}) collective-permute-start(bf16[2,48,512]{2,1,0:T(8,128)(2,1)} %param.6), channel_id=1, source_target_pairs={{0,0},{1,128},{2,256},{3,384},{4,512},{5,640},{6,768},{7,896},{8,8... | collective-permute-start | bytes 294920 | tf_op jit(solution)/shard_map/ppermute | solution.py:113
  24.7 39.6 %collective-permute-done = bf16[2,48,512]{2,1,0:T(8,128)(2,1)S(1)} collective-permute-done((bf16[2,48,512]{2,1,0:T(8,128)(2,1)}, bf16[2,48,512]{2,1,0:T(8,128)(2,1)S(1)}, u32[]{:S(2)}, u32[]{:S(2)}) %collective-permute-start) | collective-permute-done | bytes 98336 | tf_op jit(solution)/shard_map/ppermute | solution.py:113
  64.3 1.9 %collective-permute-start.3 = (bf16[2,48,512]{2,1,0:T(8,128)(2,1)S(1)}, bf16[2,48,512]{2,1,0:T(8,128)(2,1)S(1)}, u32[]{:S(2)}, u32[]{:S(2)}) collective-permute-start(bf16[2,48,512]{2,1,0:T(8,128)(2,1)S(1)} %collective-permute-done), channel_id=1, source_target_pairs={{0,96},{32,64},{64,32},{96,0},{1,97},{33,65},{65,33},{97,1},{2,98}... | collective-permute-start | bytes 294920 | tf_op jit(solution)/shard_map/ppermute | solution.py:115
  66.2 10.5 %collective-permute-start.2 = (bf16[2,48,512]{2,1,0:T(8,128)(2,1)S(1)}, bf16[2,48,512]{2,1,0:T(8,128)(2,1)S(1)}, u32[]{:S(2)}, u32[]{:S(2)}) collective-permute-start(bf16[2,48,512]{2,1,0:T(8,128)(2,1)S(1)} %collective-permute-done), channel_id=1, source_target_pairs={{0,64},{32,96},{64,0},{96,32},{1,65},{33,97},{65,1},{97,33},{2,66}... | collective-permute-start | bytes 294920 | tf_op jit(solution)/shard_map/ppermute | solution.py:115
  76.8 1.9 %collective-permute-start.1 = (bf16[2,48,512]{2,1,0:T(8,128)(2,1)S(1)}, bf16[2,48,512]{2,1,0:T(8,128)(2,1)S(1)}, u32[]{:S(2)}, u32[]{:S(2)}) collective-permute-start(bf16[2,48,512]{2,1,0:T(8,128)(2,1)S(1)} %collective-permute-done), channel_id=1, source_target_pairs={{0,32},{32,0},{64,96},{96,64},{1,33},{33,1},{65,97},{97,65},{2,34}... | collective-permute-start | bytes 294920 | tf_op jit(solution)/shard_map/ppermute | solution.py:115
  78.7 1.0 collective-permute-done.2
  79.7 3.6 %collective-permute-done.1 = bf16[2,48,512]{2,1,0:T(8,128)(2,1)S(1)} collective-permute-done((bf16[2,48,512]{2,1,0:T(8,128)(2,1)S(1)}, bf16[2,48,512]{2,1,0:T(8,128)(2,1)S(1)}, u32[]{:S(2)}, u32[]{:S(2)}) %collective-permute-start.1) | collective-permute-done | bytes 98336 | tf_op jit(solution)/shard_map/ppermute | solution.py:115
  83.3 1.9 %collective-permute-start.4 = (bf16[384,512]{1,0:T(8,128)(2,1)S(1)}, bf16[384,512]{1,0:T(8,128)(2,1)S(1)}, u32[]{:S(2)}, u32[]{:S(2)}) collective-permute-start(bf16[384,512]{1,0:T(8,128)(2,1)S(1)} %bitcast.36), channel_id=1, source_target_pairs={{0,16},{16,0},{1,17},{17,1},{2,18},{18,2},{3,19},{19,3},{4,20},{20... | collective-permute-start | bytes 1179656 | tf_op jit(solution)/shard_map/ppermute | solution.py:119
  85.3 1.7 collective-permute-done.4
  87.1 1.9 %collective-permute-start.5 = (bf16[768,512]{1,0:T(8,128)(2,1)S(1)}, bf16[768,512]{1,0:T(8,128)(2,1)S(1)}, u32[]{:S(2)}, u32[]{:S(2)}) collective-permute-start(bf16[768,512]{1,0:T(8,128)(2,1)S(1)} %pad_maximum_fusion.refs_0_), channel_id=1, source_target_pairs={{0,128},{16,912},{128,256},{144,16},{256,384},{272,144},{384,512},... | collective-permute-start | bytes 2359304 | tf_op jit(solution)/shard_map/ppermute | solution.py:133
  89.8 1.4 broadcast_in_dim.2
  91.3 4.3 %all-to-all-start.1 = ((bf16[8,512,256]{2,1,0:T(8,128)(2,1)}), bf16[8,512,256]{2,1,0:T(8,128)(2,1)}, u32[]{:S(2)}, u32[]{:S(2)}) async-start(bf16[8,512,256]{2,1,0:T(8,128)(2,1)} %broadcast_in_dim.2), calls=%async_computation.1 | async-start | bytes 4194304 | tf_op jit(solution)/shard_map/all_to_all | solution.py:126
  95.6 6.5 %collective-permute-done.5.refs_7_ = bf16[768,512]{1,0:T(8,128)(2,1)S(1)} collective-permute-done((bf16[768,512]{1,0:T(8,128)(2,1)S(1)}, bf16[768,512]{1,0:T(8,128)(2,1)S(1)}, u32[]{:S(2)}, u32[]{:S(2)}) %collective-permute-start.5) | collective-permute-done | bytes 786464 | tf_op jit(solution)/shard_map/ppermute | solution.py:133
  102.2 1.9 %collective-permute-start.7 = (bf16[768,512]{1,0:T(8,128)(2,1)S(1)}, bf16[768,512]{1,0:T(8,128)(2,1)S(1)}, u32[]{:S(2)}, u32[]{:S(2)}) collective-permute-start(bf16[768,512]{1,0:T(8,128)(2,1)S(1)} %collective-permute-done.5.refs_7_), channel_id=1, source_target_pairs={{0,128},{16,912},{128,256},{144,16},{256,384},{272,144},{384,512},... | collective-permute-start | bytes 2359304 | tf_op jit(solution)/shard_map/ppermute | solution.py:133
  104.1 13.2 %collective-permute-done.7.refs_6_ = bf16[768,512]{1,0:T(8,128)(2,1)S(1)} collective-permute-done((bf16[768,512]{1,0:T(8,128)(2,1)S(1)}, bf16[768,512]{1,0:T(8,128)(2,1)S(1)}, u32[]{:S(2)}, u32[]{:S(2)}) %collective-permute-start.7) | collective-permute-done | bytes 786464 | tf_op jit(solution)/shard_map/ppermute | solution.py:133
  117.3 1.9 %collective-permute-start.9 = (bf16[768,512]{1,0:T(8,128)(2,1)S(1)}, bf16[768,512]{1,0:T(8,128)(2,1)S(1)}, u32[]{:S(2)}, u32[]{:S(2)}) collective-permute-start(bf16[768,512]{1,0:T(8,128)(2,1)S(1)} %collective-permute-done.7.refs_6_), channel_id=1, source_target_pairs={{0,128},{16,912},{128,256},{144,16},{256,384},{272,144},{384,512},... | collective-permute-start | bytes 2359304 | tf_op jit(solution)/shard_map/ppermute | solution.py:133
  119.2 1.9 %collective-permute-start.6 = (bf16[768,512]{1,0:T(8,128)(2,1)}, bf16[768,512]{1,0:T(8,128)(2,1)S(1)}, u32[]{:S(2)}, u32[]{:S(2)}) collective-permute-start(bf16[768,512]{1,0:T(8,128)(2,1)} %copy-done.7), channel_id=1, source_target_pairs={{0,16},{16,0},{1,17},{17,1},{2,18},{18,2},{3,19},{19,3},{4,20},{20... | collective-permute-start | bytes 2359304 | tf_op jit(solution)/shard_map/ppermute | solution.py:136
  121.4 2.4 %collective-permute-start.8 = (bf16[768,512]{1,0:T(8,128)(2,1)S(1)}, bf16[768,512]{1,0:T(8,128)(2,1)S(1)}, u32[]{:S(2)}, u32[]{:S(2)}) collective-permute-start(bf16[768,512]{1,0:T(8,128)(2,1)S(1)} %collective-permute-done.7.refs_6_), channel_id=1, source_target_pairs={{0,16},{16,0},{1,17},{17,1},{2,18},{18,2},{3,19},{19,3},{4,20},{20... | collective-permute-start | bytes 2359304 | tf_op jit(solution)/shard_map/ppermute | solution.py:136
  123.9 1.2 multiply_reduce_fusion.7
  125.1 7.3 %collective-permute-done.9.refs_5_ = bf16[768,512]{1,0:T(8,128)(2,1)S(1)} collective-permute-done((bf16[768,512]{1,0:T(8,128)(2,1)S(1)}, bf16[768,512]{1,0:T(8,128)(2,1)S(1)}, u32[]{:S(2)}, u32[]{:S(2)}) %collective-permute-start.9) | collective-permute-done | bytes 786464 | tf_op jit(solution)/shard_map/ppermute | solution.py:133
  132.3 1.9 %collective-permute-start.11 = (bf16[768,512]{1,0:T(8,128)(2,1)S(1)}, bf16[768,512]{1,0:T(8,128)(2,1)S(1)}, u32[]{:S(2)}, u32[]{:S(2)}) collective-permute-start(bf16[768,512]{1,0:T(8,128)(2,1)S(1)} %collective-permute-done.9.refs_5_), channel_id=1, source_target_pairs={{0,128},{16,912},{128,256},{144,16},{256,384},{272,144},{384,512},... | collective-permute-start | bytes 2359304 | tf_op jit(solution)/shard_map/ppermute | solution.py:133
  134.3 1.4 multiply_reduce_fusion
  135.6 1.9 %collective-permute-start.10 = (bf16[768,512]{1,0:T(8,128)(2,1)S(1)}, bf16[768,512]{1,0:T(8,128)(2,1)S(1)}, u32[]{:S(2)}, u32[]{:S(2)}) collective-permute-start(bf16[768,512]{1,0:T(8,128)(2,1)S(1)} %collective-permute-done.9.refs_5_), channel_id=1, source_target_pairs={{0,16},{16,0},{1,17},{17,1},{2,18},{18,2},{3,19},{19,3},{4,20},{20... | collective-permute-start | bytes 2359304 | tf_op jit(solution)/shard_map/ppermute | solution.py:136
  138.5 9.0 %collective-permute-done.11.refs_4_ = bf16[768,512]{1,0:T(8,128)(2,1)S(1)} collective-permute-done((bf16[768,512]{1,0:T(8,128)(2,1)S(1)}, bf16[768,512]{1,0:T(8,128)(2,1)S(1)}, u32[]{:S(2)}, u32[]{:S(2)}) %collective-permute-start.11) | collective-permute-done | bytes 786464 | tf_op jit(solution)/shard_map/ppermute | solution.py:133
  149.3 5.5 %collective-permute-start.13 = (f32[1,384]{1,0:T(1,128)}, f32[1,384]{1,0:T(1,128)}, u32[]{:S(2)}, u32[]{:S(2)}) collective-permute-start(f32[1,384]{1,0:T(1,128)} %reshape.137), channel_id=1, source_target_pairs={{0,8},{8,0},{1,9},{9,1},{2,10},{10,2},{3,11},{11,3},{4,12},{12,4},... | collective-permute-start | bytes 4616 | tf_op jit(solution)/shard_map/ppermute | solution.py:152
  154.9 1.1 copy-done.1
  156.0 1.1 copy-done.3
  157.1 1.1 copy-done.5
  158.2 6.7 %shard_map.59 = (f32[384,256]{1,0:T(8,128)S(1)}, bf16[384,256]{1,0:T(8,128)(2,1)}) custom-call(s32[8]{0:T(128)S(1)} %stack.88.place, s32[4]{0:T(128)S(1)} %pad_add_fusion.rows_of, bf16[768,512]{1,0:T(8,128)(2,1)S(1)} %pad_maximum_fusion.refs_0_, bf16[768,512]{1,0:T(8,128)(2,1)S(1)} %collective-permute-done.6.refs_1_, bf16[768,512]{1,0:T(8,128)(2,1)S(1)} %copy-done.1, ...), custom_call_target="tpu_custom_call" | custom-call | flops 1610612736 | bytes 8388608 | tf_op jit(solution)/shard_map/pallas_call | solution.py:84
  164.9 4.3 %collective-permute-start.12 = (bf16[384,256]{1,0:T(8,128)(2,1)}, bf16[384,256]{1,0:T(8,128)(2,1)S(1)}, u32[]{:S(2)}, u32[]{:S(2)}) collective-permute-start(bf16[384,256]{1,0:T(8,128)(2,1)} %get-tuple-element.9), channel_id=1, source_target_pairs={{0,8},{8,0},{1,9},{9,1},{2,10},{10,2},{3,11},{11,3},{4,12},{12,4},... | collective-permute-start | bytes 589832 | tf_op jit(solution)/shard_map/ppermute | solution.py:157
  170.0 8.7 %collective-permute-done.12 = bf16[384,256]{1,0:T(8,128)(2,1)S(1)} collective-permute-done((bf16[384,256]{1,0:T(8,128)(2,1)}, bf16[384,256]{1,0:T(8,128)(2,1)S(1)}, u32[]{:S(2)}, u32[]{:S(2)}) %collective-permute-start.12) | collective-permute-done | bytes 196640 | tf_op jit(solution)/shard_map/ppermute | solution.py:157
  (46 shorter events, 5.6 us)
Async XLA Ops:
  0.6 82.7 %all-to-all-start = ((bf16[64,8,256]{2,1,0:T(8,128)(2,1)}), bf16[64,8,256]{2,1,0:T(8,128)(2,1)S(1)}, u32[]{:S(2)}, u32[]{:S(2)}) async-start(bf16[64,8,256]{2,1,0:T(8,128)(2,1)} %bitcast.39), calls=%async_computation | async-start | bytes 524288 | tf_op jit(solution)/shard_map/all_to_all | solution.py:112
  21.4 42.9 %collective-permute-start = (bf16[2,48,512]{2,1,0:T(8,128)(2,1)}, bf16[2,48,512]{2,1,0:T(8,128)(2,1)S(1)}, u32[]{:S(2)}, u32[]{:S(2)}) collective-permute-start(bf16[2,48,512]{2,1,0:T(8,128)(2,1)} %param.6), channel_id=1, source_target_pairs={{0,0},{1,128},{2,256},{3,384},{4,512},{5,640},{6,768},{7,896},{8,8... | collective-permute-start | bytes 294920 | tf_op jit(solution)/shard_map/ppermute | solution.py:113
  64.3 14.4 %collective-permute-start.3 = (bf16[2,48,512]{2,1,0:T(8,128)(2,1)S(1)}, bf16[2,48,512]{2,1,0:T(8,128)(2,1)S(1)}, u32[]{:S(2)}, u32[]{:S(2)}) collective-permute-start(bf16[2,48,512]{2,1,0:T(8,128)(2,1)S(1)} %collective-permute-done), channel_id=1, source_target_pairs={{0,96},{32,64},{64,32},{96,0},{1,97},{33,65},{65,33},{97,1},{2,98}... | collective-permute-start | bytes 294920 | tf_op jit(solution)/shard_map/ppermute | solution.py:115
  66.2 13.4 %collective-permute-start.2 = (bf16[2,48,512]{2,1,0:T(8,128)(2,1)S(1)}, bf16[2,48,512]{2,1,0:T(8,128)(2,1)S(1)}, u32[]{:S(2)}, u32[]{:S(2)}) collective-permute-start(bf16[2,48,512]{2,1,0:T(8,128)(2,1)S(1)} %collective-permute-done), channel_id=1, source_target_pairs={{0,64},{32,96},{64,0},{96,32},{1,65},{33,97},{65,1},{97,33},{2,66}... | collective-permute-start | bytes 294920 | tf_op jit(solution)/shard_map/ppermute | solution.py:115
  76.8 6.5 %collective-permute-start.1 = (bf16[2,48,512]{2,1,0:T(8,128)(2,1)S(1)}, bf16[2,48,512]{2,1,0:T(8,128)(2,1)S(1)}, u32[]{:S(2)}, u32[]{:S(2)}) collective-permute-start(bf16[2,48,512]{2,1,0:T(8,128)(2,1)S(1)} %collective-permute-done), channel_id=1, source_target_pairs={{0,32},{32,0},{64,96},{96,64},{1,33},{33,1},{65,97},{97,65},{2,34}... | collective-permute-start | bytes 294920 | tf_op jit(solution)/shard_map/ppermute | solution.py:115
  83.3 3.6 %collective-permute-start.4 = (bf16[384,512]{1,0:T(8,128)(2,1)S(1)}, bf16[384,512]{1,0:T(8,128)(2,1)S(1)}, u32[]{:S(2)}, u32[]{:S(2)}) collective-permute-start(bf16[384,512]{1,0:T(8,128)(2,1)S(1)} %bitcast.36), channel_id=1, source_target_pairs={{0,16},{16,0},{1,17},{17,1},{2,18},{18,2},{3,19},{19,3},{4,20},{20... | collective-permute-start | bytes 1179656 | tf_op jit(solution)/shard_map/ppermute | solution.py:119
  85.3 3.7 %copy-start.8 = (bf16[512,256]{1,0:T(8,128)(2,1)S(1)}, bf16[512,256]{1,0:T(8,128)(2,1)}, u32[]{:S(2)}) copy-start(bf16[512,256]{1,0:T(8,128)(2,1)} %param.5) | copy-start | bytes 786436
  85.3 3.7 %copy-start.9 = (f32[512]{0:T(512)S(1)}, f32[512]{0:T(512)}, u32[]{:S(2)}) copy-start(f32[512]{0:T(512)} %param.7) | copy-start | bytes 6148
  87.0 4.3 %copy-start.6 = (bf16[384,512]{1,0:T(8,128)(2,1)}, bf16[384,512]{1,0:T(8,128)(2,1)S(1)}, u32[]{:S(2)}) copy-start(bf16[384,512]{1,0:T(8,128)(2,1)S(1)} %get-tuple-element.13) | copy-start | bytes 1179652
  87.1 15.1 %collective-permute-start.5 = (bf16[768,512]{1,0:T(8,128)(2,1)S(1)}, bf16[768,512]{1,0:T(8,128)(2,1)S(1)}, u32[]{:S(2)}, u32[]{:S(2)}) collective-permute-start(bf16[768,512]{1,0:T(8,128)(2,1)S(1)} %pad_maximum_fusion.refs_0_), channel_id=1, source_target_pairs={{0,128},{16,912},{128,256},{144,16},{256,384},{272,144},{384,512},... | collective-permute-start | bytes 2359304 | tf_op jit(solution)/shard_map/ppermute | solution.py:133
  91.3 63.6 %all-to-all-start.1 = ((bf16[8,512,256]{2,1,0:T(8,128)(2,1)}), bf16[8,512,256]{2,1,0:T(8,128)(2,1)}, u32[]{:S(2)}, u32[]{:S(2)}) async-start(bf16[8,512,256]{2,1,0:T(8,128)(2,1)} %broadcast_in_dim.2), calls=%async_computation.1 | async-start | bytes 4194304 | tf_op jit(solution)/shard_map/all_to_all | solution.py:126
  102.2 1.9 %copy-start.7 = (bf16[768,512]{1,0:T(8,128)(2,1)}, bf16[768,512]{1,0:T(8,128)(2,1)S(1)}, u32[]{:S(2)}) copy-start(bf16[768,512]{1,0:T(8,128)(2,1)S(1)} %collective-permute-done.5.refs_7_) | copy-start | bytes 2359300
  102.2 15.1 %collective-permute-start.7 = (bf16[768,512]{1,0:T(8,128)(2,1)S(1)}, bf16[768,512]{1,0:T(8,128)(2,1)S(1)}, u32[]{:S(2)}, u32[]{:S(2)}) collective-permute-start(bf16[768,512]{1,0:T(8,128)(2,1)S(1)} %collective-permute-done.5.refs_7_), channel_id=1, source_target_pairs={{0,128},{16,912},{128,256},{144,16},{256,384},{272,144},{384,512},... | collective-permute-start | bytes 2359304 | tf_op jit(solution)/shard_map/ppermute | solution.py:133
  117.3 15.1 %collective-permute-start.9 = (bf16[768,512]{1,0:T(8,128)(2,1)S(1)}, bf16[768,512]{1,0:T(8,128)(2,1)S(1)}, u32[]{:S(2)}, u32[]{:S(2)}) collective-permute-start(bf16[768,512]{1,0:T(8,128)(2,1)S(1)} %collective-permute-done.7.refs_6_), channel_id=1, source_target_pairs={{0,128},{16,912},{128,256},{144,16},{256,384},{272,144},{384,512},... | collective-permute-start | bytes 2359304 | tf_op jit(solution)/shard_map/ppermute | solution.py:133
  119.2 18.6 %collective-permute-start.6 = (bf16[768,512]{1,0:T(8,128)(2,1)}, bf16[768,512]{1,0:T(8,128)(2,1)S(1)}, u32[]{:S(2)}, u32[]{:S(2)}) collective-permute-start(bf16[768,512]{1,0:T(8,128)(2,1)} %copy-done.7), channel_id=1, source_target_pairs={{0,16},{16,0},{1,17},{17,1},{2,18},{18,2},{3,19},{19,3},{4,20},{20... | collective-permute-start | bytes 2359304 | tf_op jit(solution)/shard_map/ppermute | solution.py:136
  121.4 16.9 %collective-permute-start.8 = (bf16[768,512]{1,0:T(8,128)(2,1)S(1)}, bf16[768,512]{1,0:T(8,128)(2,1)S(1)}, u32[]{:S(2)}, u32[]{:S(2)}) collective-permute-start(bf16[768,512]{1,0:T(8,128)(2,1)S(1)} %collective-permute-done.7.refs_6_), channel_id=1, source_target_pairs={{0,16},{16,0},{1,17},{17,1},{2,18},{18,2},{3,19},{19,3},{4,20},{20... | collective-permute-start | bytes 2359304 | tf_op jit(solution)/shard_map/ppermute | solution.py:136
  132.3 15.1 %collective-permute-start.11 = (bf16[768,512]{1,0:T(8,128)(2,1)S(1)}, bf16[768,512]{1,0:T(8,128)(2,1)S(1)}, u32[]{:S(2)}, u32[]{:S(2)}) collective-permute-start(bf16[768,512]{1,0:T(8,128)(2,1)S(1)} %collective-permute-done.9.refs_5_), channel_id=1, source_target_pairs={{0,128},{16,912},{128,256},{144,16},{256,384},{272,144},{384,512},... | collective-permute-start | bytes 2359304 | tf_op jit(solution)/shard_map/ppermute | solution.py:133
  135.6 12.0 %collective-permute-start.10 = (bf16[768,512]{1,0:T(8,128)(2,1)S(1)}, bf16[768,512]{1,0:T(8,128)(2,1)S(1)}, u32[]{:S(2)}, u32[]{:S(2)}) collective-permute-start(bf16[768,512]{1,0:T(8,128)(2,1)S(1)} %collective-permute-done.9.refs_5_), channel_id=1, source_target_pairs={{0,16},{16,0},{1,17},{17,1},{2,18},{18,2},{3,19},{19,3},{4,20},{20... | collective-permute-start | bytes 2359304 | tf_op jit(solution)/shard_map/ppermute | solution.py:136
  138.2 9.4 %copy-start = (bf16[768,512]{1,0:T(8,128)(2,1)}, bf16[768,512]{1,0:T(8,128)(2,1)S(1)}, u32[]{:S(2)}) copy-start(bf16[768,512]{1,0:T(8,128)(2,1)S(1)} %collective-permute-done.8.refs_2_) | copy-start | bytes 2359300
  147.4 0.9 copy-start.2
  147.7 0.9 copy-start.4
  149.3 19.9 %collective-permute-start.13 = (f32[1,384]{1,0:T(1,128)}, f32[1,384]{1,0:T(1,128)}, u32[]{:S(2)}, u32[]{:S(2)}) collective-permute-start(f32[1,384]{1,0:T(1,128)} %reshape.137), channel_id=1, source_target_pairs={{0,8},{8,0},{1,9},{9,1},{2,10},{10,2},{3,11},{11,3},{4,12},{12,4},... | collective-permute-start | bytes 4616 | tf_op jit(solution)/shard_map/ppermute | solution.py:152
  154.8 1.1 copy-start.1
  156.0 1.1 copy-start.3
  157.1 1.1 copy-start.5
  164.9 13.8 %collective-permute-start.12 = (bf16[384,256]{1,0:T(8,128)(2,1)}, bf16[384,256]{1,0:T(8,128)(2,1)S(1)}, u32[]{:S(2)}, u32[]{:S(2)}) collective-permute-start(bf16[384,256]{1,0:T(8,128)(2,1)} %get-tuple-element.9), channel_id=1, source_target_pairs={{0,8},{8,0},{1,9},{9,1},{2,10},{10,2},{3,11},{11,3},{4,12},{12,4},... | collective-permute-start | bytes 589832 | tf_op jit(solution)/shard_map/ppermute | solution.py:157

commit v3 on v0

v3 whole, which is shorter than its diff:
```python
import math

import jax
import jax.numpy as jnp
from jax import lax
from jax.experimental import pallas as pl
from jax.experimental.pallas import tpu as pltpu
from jax.sharding import Mesh
from jax.sharding import PartitionSpec as P

D = 8192
AXES = ("zh", "zl", "y1", "y0", "c", "yh", "x")
SIZES = (2, 4, 2, 2, 2, 2, 8)
Z, YL, DP, TENSOR = ("zh", "zl"), ("y1", "y0"), ("zh", "zl", "y1", "y0", "c"), ("yh", "x")
NZ, NYL, NX, NZL = 8, 4, 8, 4
LANES = 128

ema_rate = 0.5
norm_eps = 1e-06


def shift(count, by):
    return [(i, (i + by) % count) for i in range(count)]


def spread(v, axes, count):
    return lax.all_to_all(jnp.broadcast_to(v[None], (count,) + v.shape), axes, 0, 0, tiled=True)


def gate_kernel(index, *refs):
    blocks, weights = refs[: 2 * NZ], refs[2 * NZ]
    kept, sent, a_buf, b_buf, acc, a_sem, b_sem = refs[2 * NZ + 1 :]
    b_copies = [
        pltpu.make_async_copy(weights.at[:, q], b_buf.at[q], b_sem.at[q]) for q in range(NZL)
    ]
    a_copies = [
        pltpu.make_async_copy(b, a_buf.at[index[s, 0], index[s, 1], index[s, 2]], a_sem.at[s])
        for s, b in enumerate(blocks)
    ]
    for copy in b_copies + a_copies:
        copy.start()
    for copy in a_copies:
        copy.wait()
    groups, cores, _, rows, depth = a_buf.shape
    cols = b_buf.shape[-1]
    for q in range(NZL):
        b_copies[q].wait()
        left = a_buf[:, :, q].reshape(groups * cores * rows, depth)
        part = jnp.dot(left, b_buf[q].reshape(depth, cols), preferred_element_type=jnp.float32)
        part = part.reshape(groups, cores * rows, cols)
        acc[...] = part if q == 0 else acc[...] + part
    mine = index[2 * NZ, 0]
    kept[...] = acc[mine]
    sent[...] = acc[1 - mine].astype(sent.dtype)


def gate_parts(index, blocks, weights):
    rows, depth = blocks[0].shape
    cols = weights.shape[-1]
    hbm = pl.BlockSpec(memory_space=pl.ANY)
    vmem = pl.BlockSpec(memory_space=pltpu.VMEM)
    return pl.pallas_call(
        gate_kernel,
        out_shape=(
            jax.ShapeDtypeStruct((2 * rows, cols), jnp.float32),
            jax.ShapeDtypeStruct((2 * rows, cols), jnp.bfloat16),
        ),
        in_specs=[pl.BlockSpec(memory_space=pltpu.SMEM)] + [hbm] * (2 * NZ + 1),
        out_specs=(vmem, vmem),
        scratch_shapes=[
            pltpu.VMEM((2, 2, NZL, rows, depth), jnp.bfloat16),
            pltpu.VMEM((NZL, NX, LANES, cols), jnp.bfloat16),
            pltpu.VMEM((2, 2 * rows, cols), jnp.float32),
            pltpu.SemaphoreType.DMA((2 * NZ,)),
            pltpu.SemaphoreType.DMA((NZL,)),
        ],
        compiler_params=pltpu.CompilerParams(vmem_limit_bytes=60 * 2**20),
        cost_estimate=pl.CostEstimate(
            flops=4 * NZ * rows * depth * cols,
            bytes_accessed=2 * NZ * depth * (2 * rows + cols),
            transcendentals=0,
        ),
    )(index, *blocks, weights)


def body(policy, ref_weight, tokens, gain):
    z, c, yh = lax.axis_index(Z), lax.axis_index("c"), lax.axis_index("yh")
    micro, toks, width = tokens.shape
    pieces = tokens.reshape(micro, toks, NZL, LANES).transpose(2, 0, 1, 3)
    pieces = pieces.reshape(NZL * micro, toks, LANES)
    pieces = lax.all_to_all(pieces, ("zl", "y1"), 0, 0, tiled=True)
    pieces = lax.all_to_all(pieces, "x", 0, 0, tiled=True)
    pieces, policy = lax.optimization_barrier((pieces, policy))
    arrived = lax.all_to_all(
        policy.reshape(8, 64, 256).transpose(1, 0, 2), DP, 0, 0, tiled=True
    )
    own = pieces.transpose(1, 0, 2).reshape(toks, NX * LANES)
    own = jnp.concatenate(
        [own] + [lax.ppermute(own, YL, [(i, i ^ e) for i in range(NYL)]) for e in range(1, NYL)]
    )
    rows = own.shape[0]
    own, arrived = lax.optimization_barrier((own, arrived))
    policy_slice = arrived.reshape(ref_weight.shape)
    ref_f = ref_weight.astype(jnp.float32)
    blended = (ref_f + ema_rate * (policy_slice.astype(jnp.float32) - ref_f)).astype(jnp.bfloat16)
    scaled = (blended.astype(jnp.float32) * gain[:, None]).astype(jnp.bfloat16)
    weights = spread(scaled, "x", NX)
    weights = weights.reshape(NX, NZL, LANES, weights.shape[-1])
    blocks, offsets = [own], [0]
    up = down = own
    for step in range(1, NZ // 2 + 1):
        up = lax.ppermute(up, Z, shift(NZ, 1))
        blocks.append(up)
        offsets.append(-step)
        if step < NZ // 2:
            down = lax.ppermute(down, Z, shift(NZ, -1))
            blocks.append(down)
            offsets.append(step)
    others = [lax.ppermute(b, "c", shift(2, 1)) for b in blocks]
    places = [(z + o) % NZ for o in offsets]
    sums = []
    for group in (yh, 1 - yh):
        pair = []
        for held in (blocks, others):
            total = 0.0
            for place, block in zip(places, held):
                block_f = block.astype(jnp.float32)
                part = jnp.sum(block_f * block_f, axis=1)
                total = total + jnp.where(place // NZL == group, part, 0.0)
            pair.append(total[None])
        first, second = pair
        sums.append(
            jnp.concatenate(
                [jnp.where(c == 0, first, second), jnp.where(c == 0, second, first)], axis=1
            )
        )
    swap = shift(2, 1)
    squares = sums[0] + lax.ppermute(sums[1], "yh", swap)
    index = [jnp.stack([p // NZL, core, p % NZL]) for core in (c, 1 - c) for p in places]
    index = jnp.stack(index + [jnp.stack([yh, yh, yh])]).astype(jnp.int32)
    kept, sent = gate_parts(index, blocks + others, weights)
    other = lax.ppermute(sent, "yh", swap)
    factor = lax.rsqrt(squares.reshape(-1, 1) / D + norm_eps) * (1.0 / math.sqrt(D))
    gate = (kept + other.astype(jnp.float32)) * factor
    activated = jax.nn.silu(gate).astype(jnp.bfloat16)
    activated = activated.reshape(2, 2, 2, toks, -1)
    y1, y0 = lax.axis_index("y1"), lax.axis_index("y0")
    activated = jnp.where(y1 == 0, activated, activated[:, ::-1])
    activated = jnp.where(y0 == 0, activated, activated[:, :, ::-1])
    activated = activated.transpose(1, 2, 0, 3, 4)
    return blended, activated.reshape(micro, 4 * toks, -1)


def solution(mesh):
    fine = Mesh(mesh.devices.reshape(SIZES), AXES)
    return jax.shard_map(
        body,
        mesh=fine,
        in_specs=(P(DP, TENSOR, None), P(TENSOR, DP), P(None, DP, TENSOR), P(TENSOR)),
        out_specs=(P(TENSOR, DP), P(None, TENSOR, DP)),
        check_vma=False,
    )
```

time: 797 us -> 175 us (0.22)
  the two profiles are of different devices: /device:TPU:1 before, /device:TPU:35 now
where the time goes in v3:
time: 175 us; the launch traced here: 174 us
  starting transfers between devices  88.4 us (51%)
  waiting for transfers between devices  34.1 us (19%)
  blocking collectives  29.6 us (17%)
  Pallas kernels  8.85 us (5%)
  local copies, waits for them, and re-layouts  6.28 us (4%)
  other arithmetic  5.45 us (3%)
    ppermute x8, starting transfers between devices, body(): others = [lax.ppermute(b, 'c', shift(2, 1)) for b in blocks]  26.3 us
    all_to_all x1, starting transfers between devices, body(): lax.all_to_all(policy.reshape(8, 64, 256).transpose(1, 0, 2), DP, 0, 0, t...  18.1 us
    all_to_all x1, blocking collectives, body(): pieces = lax.all_to_all(pieces, ('zl', 'y1'), 0, 0, tiled=True)  16.7 us
    ppermute x4, waiting for transfers between devices, body(): up = lax.ppermute(up, Z, shift(NZ, 1))  13.6 us
    all_to_all x1, blocking collectives, body(): pieces = lax.all_to_all(pieces, 'x', 0, 0, tiled=True)  12.9 us
    ppermute x3, starting transfers between devices, body(): down = lax.ppermute(down, Z, shift(NZ, -1))  12.9 us
    ppermute x1, waiting for transfers between devices, body(): other = lax.ppermute(sent, 'yh', swap)  12.4 us
    pallas_call x1, Pallas kernels, gate_parts(): pl.pallas_call(gate_kernel, out_shape=(jax.ShapeDtypeStruct((2 * rows, co...  8.85 us
  transfers between devices with their start and end apart: 22, of which 8 were waited for; matrix products, arithmetic and copies ran while one was open for 3% of the time, Pallas kernels for 5%

profile of v3, /device:TPU:35, one launch (start us, length us, event | category | flops | bytes accessed | tf_op | source)
XLA Modules:
  0.0 174.2 jit_solution(5938834945384542952)
XLA Ops:
  1.6 16.7 %all_to_all.20 = bf16[8,48,128]{2,1,0:T(8,128)(2,1)S(1)} all-to-all(bf16[8,48,128]{2,1,0:T(8,128)(2,1)S(1)} %bitcast.82), channel_id=1, replica_groups=mesh['zh'=2,'zl'=4,'y1'=2,'y0'=2,'c'=2,'yh'=2,'x'=8] {'zl','y1'}, dimensions={0} | all-to-all | bytes 196608 | tf_op jit(solution)/shard_map/all_to_all | solution.py:91
  18.2 12.9 %all_to_all.21 = bf16[8,48,128]{2,1,0:T(8,128)(2,1)S(1)} all-to-all(bf16[8,48,128]{2,1,0:T(8,128)(2,1)S(1)} %all_to_all.20), channel_id=1, replica_groups=mesh['zh'=2,'zl'=4,'y1'=2,'y0'=2,'c'=2,'yh'=2,'x'=8] {'x'}, dimensions={0} | all-to-all | bytes 196608 | tf_op jit(solution)/shard_map/all_to_all | solution.py:92
  31.2 18.1 %all-to-all-start.2 = ((bf16[64,8,256]{2,1,0:T(8,128)(2,1)}), bf16[64,8,256]{2,1,0:T(8,128)(2,1)S(1)}, u32[]{:S(2)}, u32[]{:S(2)}) async-start(bf16[64,8,256]{2,1,0:T(8,128)(2,1)} %bitcast.83), calls=%async_computation.2 | async-start | bytes 524288 | tf_op jit(solution)/shard_map/all_to_all | solution.py:94
  49.4 3.1 %collective-permute-start = (bf16[48,1024]{1,0:T(8,128)(2,1)S(1)}, bf16[48,1024]{1,0:T(8,128)(2,1)S(1)}, u32[]{:S(2)}, u32[]{:S(2)}) collective-permute-start(bf16[48,1024]{1,0:T(8,128)(2,1)S(1)} %copy_bitcast_fusion), channel_id=1, source_target_pairs={{0,32},{32,0},{64,96},{96,64},{1,33},{33,1},{65,97},{97,65},{2,34}... | collective-permute-start | bytes 294920 | tf_op jit(solution)/shard_map/ppermute | solution.py:99
  52.5 2.2 %collective-permute-start.1 = (bf16[48,1024]{1,0:T(8,128)(2,1)S(1)}, bf16[48,1024]{1,0:T(8,128)(2,1)S(1)}, u32[]{:S(2)}, u32[]{:S(2)}) collective-permute-start(bf16[48,1024]{1,0:T(8,128)(2,1)S(1)} %copy_bitcast_fusion), channel_id=1, source_target_pairs={{0,64},{32,96},{64,0},{96,32},{1,65},{33,97},{65,1},{97,33},{2,66}... | collective-permute-start | bytes 294920 | tf_op jit(solution)/shard_map/ppermute | solution.py:99
  54.7 3.1 %collective-permute-start.2 = (bf16[48,1024]{1,0:T(8,128)(2,1)S(1)}, bf16[48,1024]{1,0:T(8,128)(2,1)S(1)}, u32[]{:S(2)}, u32[]{:S(2)}) collective-permute-start(bf16[48,1024]{1,0:T(8,128)(2,1)S(1)} %copy_bitcast_fusion), channel_id=1, source_target_pairs={{0,96},{32,64},{64,32},{96,0},{1,97},{33,65},{65,33},{97,1},{2,98}... | collective-permute-start | bytes 294920 | tf_op jit(solution)/shard_map/ppermute | solution.py:99
  59.1 5.4 %collective-permute-done.2 = bf16[48,1024]{1,0:T(8,128)(2,1)S(1)} collective-permute-done((bf16[48,1024]{1,0:T(8,128)(2,1)S(1)}, bf16[48,1024]{1,0:T(8,128)(2,1)S(1)}, u32[]{:S(2)}, u32[]{:S(2)}) %collective-permute-start.2) | collective-permute-done | bytes 98336 | tf_op jit(solution)/shard_map/ppermute | solution.py:99
  65.4 1.5 broadcast_in_dim.46
  66.9 4.7 %all-to-all-start.3 = ((bf16[8,512,256]{2,1,0:T(8,128)(2,1)}), bf16[8,512,256]{2,1,0:T(8,128)(2,1)S(1)}, u32[]{:S(2)}, u32[]{:S(2)}) async-start(bf16[8,512,256]{2,1,0:T(8,128)(2,1)} %broadcast_in_dim.46), calls=%async_computation.3 | async-start | bytes 4194304 | tf_op jit(solution)/shard_map/all_to_all | solution.py:27
  72.0 3.1 %collective-permute-start.3 = (bf16[192,1024]{1,0:T(8,128)(2,1)S(1)}, bf16[192,1024]{1,0:T(8,128)(2,1)S(1)}, u32[]{:S(2)}, u32[]{:S(2)}) collective-permute-start(bf16[192,1024]{1,0:T(8,128)(2,1)S(1)} %pad_maximum_fusion.refs_0_), channel_id=1, source_target_pairs={{0,128},{128,256},{256,384},{384,512},{512,640},{640,768},{768,896... | collective-permute-start | bytes 1179656 | tf_op jit(solution)/shard_map/ppermute | solution.py:112
  75.1 3.4 %collective-permute-start.4 = (bf16[192,1024]{1,0:T(8,128)(2,1)S(1)}, bf16[192,1024]{1,0:T(8,128)(2,1)S(1)}, u32[]{:S(2)}, u32[]{:S(2)}) collective-permute-start(bf16[192,1024]{1,0:T(8,128)(2,1)S(1)} %pad_maximum_fusion.refs_0_), channel_id=1, source_target_pairs={{0,896},{128,0},{256,128},{384,256},{512,384},{640,512},{768,640},... | collective-permute-start | bytes 1179656 | tf_op jit(solution)/shard_map/ppermute | solution.py:116
  78.8 1.8 %stack.241.index = s32[17,3]{1,0:T(8,128)} concatenate(s32[1,3]{1,0:T(1,128)S(1)} %get-tuple-element.22, s32[1,3]{1,0:T(1,128)S(1)} %get-tuple-element.23, s32[1,3]{1,0:T(1,128)S(1)} %get-tuple-element.24, s32[1,3]{1,0:T(1,128)S(1)} %get-tuple-element.25, s32[1,3]{1,0:T(1,128)S(1)} %get-tuple-element.26, s32[1,3]{1,0:T(1,128)S(1)} %get-tuple-element.27, ...), dimensions={0} | concatenate | bytes 408 | tf_op jit(solution)/shard_map/stack | solution.py:140
  80.6 4.1 %collective-permute-start.10 = (bf16[192,1024]{1,0:T(8,128)(2,1)S(1)}, bf16[192,1024]{1,0:T(8,128)(2,1)S(1)}, u32[]{:S(2)}, u32[]{:S(2)}) collective-permute-start(bf16[192,1024]{1,0:T(8,128)(2,1)S(1)} %pad_maximum_fusion.refs_0_), channel_id=1, source_target_pairs={{0,16},{16,0},{1,17},{17,1},{2,18},{18,2},{3,19},{19,3},{4,20},{20... | collective-permute-start | bytes 1179656 | tf_op jit(solution)/shard_map/ppermute | solution.py:119
  85.6 4.6 %collective-permute-start.6 = (bf16[192,1024]{1,0:T(8,128)(2,1)S(1)}, bf16[192,1024]{1,0:T(8,128)(2,1)S(1)}, u32[]{:S(2)}, u32[]{:S(2)}) collective-permute-start(bf16[192,1024]{1,0:T(8,128)(2,1)S(1)} %collective-permute-done.4.refs_2_), channel_id=1, source_target_pairs={{0,896},{128,0},{256,128},{384,256},{512,384},{640,512},{768,640},... | collective-permute-start | bytes 1179656 | tf_op jit(solution)/shard_map/ppermute | solution.py:116
  90.2 5.1 %collective-permute-start.12 = (bf16[192,1024]{1,0:T(8,128)(2,1)S(1)}, bf16[192,1024]{1,0:T(8,128)(2,1)S(1)}, u32[]{:S(2)}, u32[]{:S(2)}) collective-permute-start(bf16[192,1024]{1,0:T(8,128)(2,1)S(1)} %collective-permute-done.4.refs_2_), channel_id=1, source_target_pairs={{0,16},{16,0},{1,17},{17,1},{2,18},{18,2},{3,19},{19,3},{4,20},{20... | collective-permute-start | bytes 1179656 | tf_op jit(solution)/shard_map/ppermute | solution.py:119
  95.3 1.9 %collective-permute-start.5 = (bf16[192,1024]{1,0:T(8,128)(2,1)S(1)}, bf16[192,1024]{1,0:T(8,128)(2,1)S(1)}, u32[]{:S(2)}, u32[]{:S(2)}) collective-permute-start(bf16[192,1024]{1,0:T(8,128)(2,1)S(1)} %collective-permute-done.3.refs_1_), channel_id=1, source_target_pairs={{0,128},{128,256},{256,384},{384,512},{512,640},{640,768},{768,896... | collective-permute-start | bytes 1179656 | tf_op jit(solution)/shard_map/ppermute | solution.py:112
  97.3 1.9 %collective-permute-start.11 = (bf16[192,1024]{1,0:T(8,128)(2,1)S(1)}, bf16[192,1024]{1,0:T(8,128)(2,1)S(1)}, u32[]{:S(2)}, u32[]{:S(2)}) collective-permute-start(bf16[192,1024]{1,0:T(8,128)(2,1)S(1)} %collective-permute-done.3.refs_1_), channel_id=1, source_target_pairs={{0,16},{16,0},{1,17},{17,1},{2,18},{18,2},{3,19},{19,3},{4,20},{20... | collective-permute-start | bytes 1179656 | tf_op jit(solution)/shard_map/ppermute | solution.py:119
  99.7 4.9 %collective-permute-start.8 = (bf16[192,1024]{1,0:T(8,128)(2,1)S(1)}, bf16[192,1024]{1,0:T(8,128)(2,1)S(1)}, u32[]{:S(2)}, u32[]{:S(2)}) collective-permute-start(bf16[192,1024]{1,0:T(8,128)(2,1)S(1)} %collective-permute-done.6.refs_4_), channel_id=1, source_target_pairs={{0,896},{128,0},{256,128},{384,256},{512,384},{640,512},{768,640},... | collective-permute-start | bytes 1179656 | tf_op jit(solution)/shard_map/ppermute | solution.py:116
  104.5 2.5 %collective-permute-start.14 = (bf16[192,1024]{1,0:T(8,128)(2,1)S(1)}, bf16[192,1024]{1,0:T(8,128)(2,1)S(1)}, u32[]{:S(2)}, u32[]{:S(2)}) collective-permute-start(bf16[192,1024]{1,0:T(8,128)(2,1)S(1)} %collective-permute-done.6.refs_4_), channel_id=1, source_target_pairs={{0,16},{16,0},{1,17},{17,1},{2,18},{18,2},{3,19},{19,3},{4,20},{20... | collective-permute-start | bytes 1179656 | tf_op jit(solution)/shard_map/ppermute | solution.py:119
  107.0 2.1 %collective-permute-done.5.refs_3_ = bf16[192,1024]{1,0:T(8,128)(2,1)S(1)} collective-permute-done((bf16[192,1024]{1,0:T(8,128)(2,1)S(1)}, bf16[192,1024]{1,0:T(8,128)(2,1)S(1)}, u32[]{:S(2)}, u32[]{:S(2)}) %collective-permute-start.5) | collective-permute-done | bytes 393248 | tf_op jit(solution)/shard_map/ppermute | solution.py:112
  109.2 1.9 %collective-permute-start.7 = (bf16[192,1024]{1,0:T(8,128)(2,1)S(1)}, bf16[192,1024]{1,0:T(8,128)(2,1)S(1)}, u32[]{:S(2)}, u32[]{:S(2)}) collective-permute-start(bf16[192,1024]{1,0:T(8,128)(2,1)S(1)} %collective-permute-done.5.refs_3_), channel_id=1, source_target_pairs={{0,128},{128,256},{256,384},{384,512},{512,640},{640,768},{768,896... | collective-permute-start | bytes 1179656 | tf_op jit(solution)/shard_map/ppermute | solution.py:112
  111.4 2.7 %collective-permute-start.13 = (bf16[192,1024]{1,0:T(8,128)(2,1)S(1)}, bf16[192,1024]{1,0:T(8,128)(2,1)S(1)}, u32[]{:S(2)}, u32[]{:S(2)}) collective-permute-start(bf16[192,1024]{1,0:T(8,128)(2,1)S(1)} %collective-permute-done.5.refs_3_), channel_id=1, source_target_pairs={{0,16},{16,0},{1,17},{17,1},{2,18},{18,2},{3,19},{19,3},{4,20},{20... | collective-permute-start | bytes 1179656 | tf_op jit(solution)/shard_map/ppermute | solution.py:119
  114.5 7.6 %collective-permute-done.7.refs_5_ = bf16[192,1024]{1,0:T(8,128)(2,1)S(1)} collective-permute-done((bf16[192,1024]{1,0:T(8,128)(2,1)S(1)}, bf16[192,1024]{1,0:T(8,128)(2,1)S(1)}, u32[]{:S(2)}, u32[]{:S(2)}) %collective-permute-start.7) | collective-permute-done | bytes 393248 | tf_op jit(solution)/shard_map/ppermute | solution.py:112
  122.1 1.9 %collective-permute-start.9 = (bf16[192,1024]{1,0:T(8,128)(2,1)S(1)}, bf16[192,1024]{1,0:T(8,128)(2,1)S(1)}, u32[]{:S(2)}, u32[]{:S(2)}) collective-permute-start(bf16[192,1024]{1,0:T(8,128)(2,1)S(1)} %collective-permute-done.7.refs_5_), channel_id=1, source_target_pairs={{0,128},{128,256},{256,384},{384,512},{512,640},{640,768},{768,896... | collective-permute-start | bytes 1179656 | tf_op jit(solution)/shard_map/ppermute | solution.py:112
  124.0 3.6 %collective-permute-start.15 = (bf16[192,1024]{1,0:T(8,128)(2,1)S(1)}, bf16[192,1024]{1,0:T(8,128)(2,1)S(1)}, u32[]{:S(2)}, u32[]{:S(2)}) collective-permute-start(bf16[192,1024]{1,0:T(8,128)(2,1)S(1)} %collective-permute-done.7.refs_5_), channel_id=1, source_target_pairs={{0,16},{16,0},{1,17},{17,1},{2,18},{18,2},{3,19},{19,3},{4,20},{20... | collective-permute-start | bytes 1179656 | tf_op jit(solution)/shard_map/ppermute | solution.py:119
  127.6 1.9 %collective-permute-start.16 = (bf16[192,1024]{1,0:T(8,128)(2,1)S(1)}, bf16[192,1024]{1,0:T(8,128)(2,1)S(1)}, u32[]{:S(2)}, u32[]{:S(2)}) collective-permute-start(bf16[192,1024]{1,0:T(8,128)(2,1)S(1)} %collective-permute-done.8.refs_6_), channel_id=1, source_target_pairs={{0,16},{16,0},{1,17},{17,1},{2,18},{18,2},{3,19},{19,3},{4,20},{20... | collective-permute-start | bytes 1179656 | tf_op jit(solution)/shard_map/ppermute | solution.py:119
  130.3 3.9 %collective-permute-done.9.refs_7_ = bf16[192,1024]{1,0:T(8,128)(2,1)S(1)} collective-permute-done((bf16[192,1024]{1,0:T(8,128)(2,1)S(1)}, bf16[192,1024]{1,0:T(8,128)(2,1)S(1)}, u32[]{:S(2)}, u32[]{:S(2)}) %collective-permute-start.9) | collective-permute-done | bytes 393248 | tf_op jit(solution)/shard_map/ppermute | solution.py:112
  134.1 4.5 %collective-permute-start.17 = (bf16[192,1024]{1,0:T(8,128)(2,1)S(1)}, bf16[192,1024]{1,0:T(8,128)(2,1)S(1)}, u32[]{:S(2)}, u32[]{:S(2)}) collective-permute-start(bf16[192,1024]{1,0:T(8,128)(2,1)S(1)} %collective-permute-done.9.refs_7_), channel_id=1, source_target_pairs={{0,16},{16,0},{1,17},{17,1},{2,18},{18,2},{3,19},{19,3},{4,20},{20... | collective-permute-start | bytes 1179656 | tf_op jit(solution)/shard_map/ppermute | solution.py:119
  140.2 5.4 %collective-permute-start.19 = (f32[1,384]{1,0:T(1,128)S(1)}, f32[1,384]{1,0:T(1,128)S(1)}, u32[]{:S(2)}, u32[]{:S(2)}) collective-permute-start(f32[1,384]{1,0:T(1,128)S(1)} %pad_maximum_fusion.1), channel_id=1, source_target_pairs={{0,8},{8,0},{1,9},{9,1},{2,10},{10,2},{3,11},{11,3},{4,12},{12,4},... | collective-permute-start | bytes 4616 | tf_op jit(solution)/shard_map/ppermute | solution.py:138
  147.1 8.8 %shard_map.59 = (f32[384,256]{1,0:T(8,128)}, bf16[384,256]{1,0:T(8,128)(2,1)}) custom-call(s32[17,3]{1,0:T(8,128)} %stack.241.index, bf16[192,1024]{1,0:T(8,128)(2,1)} %copy-done.2, bf16[192,1024]{1,0:T(8,128)(2,1)} %copy-done.3, bf16[192,1024]{1,0:T(8,128)(2,1)} %copy-done.4, bf16[192,1024]{1,0:T(8,128)(2,1)} %copy-done.8, bf16[192,1024]{1,0:T(8,128)(2,1)} %copy-done.6, ...), custom_call_target="tpu_custom_call" | custom-call | flops 1610612736 | bytes 10485760 | tf_op jit(solution)/shard_map/pallas_call | solution.py:62
  155.9 3.8 %collective-permute-start.18 = (bf16[384,256]{1,0:T(8,128)(2,1)}, bf16[384,256]{1,0:T(8,128)(2,1)S(1)}, u32[]{:S(2)}, u32[]{:S(2)}) collective-permute-start(bf16[384,256]{1,0:T(8,128)(2,1)} %get-tuple-element.13), channel_id=1, source_target_pairs={{0,8},{8,0},{1,9},{9,1},{2,10},{10,2},{3,11},{11,3},{4,12},{12,4},... | collective-permute-start | bytes 589832 | tf_op jit(solution)/shard_map/ppermute | solution.py:142
  159.9 12.4 %collective-permute-done.18 = bf16[384,256]{1,0:T(8,128)(2,1)S(1)} collective-permute-done((bf16[384,256]{1,0:T(8,128)(2,1)}, bf16[384,256]{1,0:T(8,128)(2,1)S(1)}, u32[]{:S(2)}, u32[]{:S(2)}) %collective-permute-start.18) | collective-permute-done | bytes 196640 | tf_op jit(solution)/shard_map/ppermute | solution.py:142
  (96 shorter events, 11.1 us)
Async XLA Ops:
  0.6 63.9 %copy-start.18 = (bf16[512,256]{1,0:T(8,128)(2,1)S(1)}, bf16[512,256]{1,0:T(8,128)(2,1)}, u32[]{:S(2)}) copy-start(bf16[512,256]{1,0:T(8,128)(2,1)} %param.5) | copy-start | bytes 786436
  1.5 63.1 %copy-start.19 = (f32[512]{0:T(512)S(1)}, f32[512]{0:T(512)}, u32[]{:S(2)}) copy-start(f32[512]{0:T(512)} %param.7) | copy-start | bytes 6148
  31.2 33.4 %all-to-all-start.2 = ((bf16[64,8,256]{2,1,0:T(8,128)(2,1)}), bf16[64,8,256]{2,1,0:T(8,128)(2,1)S(1)}, u32[]{:S(2)}, u32[]{:S(2)}) async-start(bf16[64,8,256]{2,1,0:T(8,128)(2,1)} %bitcast.83), calls=%async_computation.2 | async-start | bytes 524288 | tf_op jit(solution)/shard_map/all_to_all | solution.py:94
  49.4 8.5 %collective-permute-start = (bf16[48,1024]{1,0:T(8,128)(2,1)S(1)}, bf16[48,1024]{1,0:T(8,128)(2,1)S(1)}, u32[]{:S(2)}, u32[]{:S(2)}) collective-permute-start(bf16[48,1024]{1,0:T(8,128)(2,1)S(1)} %copy_bitcast_fusion), channel_id=1, source_target_pairs={{0,32},{32,0},{64,96},{96,64},{1,33},{33,1},{65,97},{97,65},{2,34}... | collective-permute-start | bytes 294920 | tf_op jit(solution)/shard_map/ppermute | solution.py:99
  52.5 6.6 %collective-permute-start.1 = (bf16[48,1024]{1,0:T(8,128)(2,1)S(1)}, bf16[48,1024]{1,0:T(8,128)(2,1)S(1)}, u32[]{:S(2)}, u32[]{:S(2)}) collective-permute-start(bf16[48,1024]{1,0:T(8,128)(2,1)S(1)} %copy_bitcast_fusion), channel_id=1, source_target_pairs={{0,64},{32,96},{64,0},{96,32},{1,65},{33,97},{65,1},{97,33},{2,66}... | collective-permute-start | bytes 294920 | tf_op jit(solution)/shard_map/ppermute | solution.py:99
  54.7 9.8 %collective-permute-start.2 = (bf16[48,1024]{1,0:T(8,128)(2,1)S(1)}, bf16[48,1024]{1,0:T(8,128)(2,1)S(1)}, u32[]{:S(2)}, u32[]{:S(2)}) collective-permute-start(bf16[48,1024]{1,0:T(8,128)(2,1)S(1)} %copy_bitcast_fusion), channel_id=1, source_target_pairs={{0,96},{32,64},{64,32},{96,0},{1,97},{33,65},{65,33},{97,1},{2,98}... | collective-permute-start | bytes 294920 | tf_op jit(solution)/shard_map/ppermute | solution.py:99
  66.9 78.8 %all-to-all-start.3 = ((bf16[8,512,256]{2,1,0:T(8,128)(2,1)}), bf16[8,512,256]{2,1,0:T(8,128)(2,1)S(1)}, u32[]{:S(2)}, u32[]{:S(2)}) async-start(bf16[8,512,256]{2,1,0:T(8,128)(2,1)} %broadcast_in_dim.46), calls=%async_computation.3 | async-start | bytes 4194304 | tf_op jit(solution)/shard_map/all_to_all | solution.py:27
  72.0 23.3 %collective-permute-start.3 = (bf16[192,1024]{1,0:T(8,128)(2,1)S(1)}, bf16[192,1024]{1,0:T(8,128)(2,1)S(1)}, u32[]{:S(2)}, u32[]{:S(2)}) collective-permute-start(bf16[192,1024]{1,0:T(8,128)(2,1)S(1)} %pad_maximum_fusion.refs_0_), channel_id=1, source_target_pairs={{0,128},{128,256},{256,384},{384,512},{512,640},{640,768},{768,896... | collective-permute-start | bytes 1179656 | tf_op jit(solution)/shard_map/ppermute | solution.py:112
  75.1 10.5 %collective-permute-start.4 = (bf16[192,1024]{1,0:T(8,128)(2,1)S(1)}, bf16[192,1024]{1,0:T(8,128)(2,1)S(1)}, u32[]{:S(2)}, u32[]{:S(2)}) collective-permute-start(bf16[192,1024]{1,0:T(8,128)(2,1)S(1)} %pad_maximum_fusion.refs_0_), channel_id=1, source_target_pairs={{0,896},{128,0},{256,128},{384,256},{512,384},{640,512},{768,640},... | collective-permute-start | bytes 1179656 | tf_op jit(solution)/shard_map/ppermute | solution.py:116
  80.6 18.9 %collective-permute-start.10 = (bf16[192,1024]{1,0:T(8,128)(2,1)S(1)}, bf16[192,1024]{1,0:T(8,128)(2,1)S(1)}, u32[]{:S(2)}, u32[]{:S(2)}) collective-permute-start(bf16[192,1024]{1,0:T(8,128)(2,1)S(1)} %pad_maximum_fusion.refs_0_), channel_id=1, source_target_pairs={{0,16},{16,0},{1,17},{17,1},{2,18},{18,2},{3,19},{19,3},{4,20},{20... | collective-permute-start | bytes 1179656 | tf_op jit(solution)/shard_map/ppermute | solution.py:119
  85.6 44.6 %copy-start.4 = (bf16[192,1024]{1,0:T(8,128)(2,1)}, bf16[192,1024]{1,0:T(8,128)(2,1)S(1)}, u32[]{:S(2)}) copy-start(bf16[192,1024]{1,0:T(8,128)(2,1)S(1)} %collective-permute-done.4.refs_2_) | copy-start | bytes 1179652
  85.6 14.1 %collective-permute-start.6 = (bf16[192,1024]{1,0:T(8,128)(2,1)S(1)}, bf16[192,1024]{1,0:T(8,128)(2,1)S(1)}, u32[]{:S(2)}, u32[]{:S(2)}) collective-permute-start(bf16[192,1024]{1,0:T(8,128)(2,1)S(1)} %collective-permute-done.4.refs_2_), channel_id=1, source_target_pairs={{0,896},{128,0},{256,128},{384,256},{512,384},{640,512},{768,640},... | collective-permute-start | bytes 1179656 | tf_op jit(solution)/shard_map/ppermute | solution.py:116
  90.2 21.2 %collective-permute-start.12 = (bf16[192,1024]{1,0:T(8,128)(2,1)S(1)}, bf16[192,1024]{1,0:T(8,128)(2,1)S(1)}, u32[]{:S(2)}, u32[]{:S(2)}) collective-permute-start(bf16[192,1024]{1,0:T(8,128)(2,1)S(1)} %collective-permute-done.4.refs_2_), channel_id=1, source_target_pairs={{0,16},{16,0},{1,17},{17,1},{2,18},{18,2},{3,19},{19,3},{4,20},{20... | collective-permute-start | bytes 1179656 | tf_op jit(solution)/shard_map/ppermute | solution.py:119
  95.3 34.9 %copy-start.3 = (bf16[192,1024]{1,0:T(8,128)(2,1)}, bf16[192,1024]{1,0:T(8,128)(2,1)S(1)}, u32[]{:S(2)}) copy-start(bf16[192,1024]{1,0:T(8,128)(2,1)S(1)} %collective-permute-done.3.refs_1_) | copy-start | bytes 1179652
  95.3 13.8 %collective-permute-start.5 = (bf16[192,1024]{1,0:T(8,128)(2,1)S(1)}, bf16[192,1024]{1,0:T(8,128)(2,1)S(1)}, u32[]{:S(2)}, u32[]{:S(2)}) collective-permute-start(bf16[192,1024]{1,0:T(8,128)(2,1)S(1)} %collective-permute-done.3.refs_1_), channel_id=1, source_target_pairs={{0,128},{128,256},{256,384},{384,512},{512,640},{640,768},{768,896... | collective-permute-start | bytes 1179656 | tf_op jit(solution)/shard_map/ppermute | solution.py:112
  97.3 17.0 %collective-permute-start.11 = (bf16[192,1024]{1,0:T(8,128)(2,1)S(1)}, bf16[192,1024]{1,0:T(8,128)(2,1)S(1)}, u32[]{:S(2)}, u32[]{:S(2)}) collective-permute-start(bf16[192,1024]{1,0:T(8,128)(2,1)S(1)} %collective-permute-done.3.refs_1_), channel_id=1, source_target_pairs={{0,16},{16,0},{1,17},{17,1},{2,18},{18,2},{3,19},{19,3},{4,20},{20... | collective-permute-start | bytes 1179656 | tf_op jit(solution)/shard_map/ppermute | solution.py:119
  99.5 39.5 %copy-start.5 = (bf16[192,1024]{1,0:T(8,128)(2,1)}, bf16[192,1024]{1,0:T(8,128)(2,1)S(1)}, u32[]{:S(2)}) copy-start(bf16[192,1024]{1,0:T(8,128)(2,1)S(1)} %collective-permute-done.10.refs_8_) | copy-start | bytes 1179652
  99.7 39.5 %copy-start.6 = (bf16[192,1024]{1,0:T(8,128)(2,1)}, bf16[192,1024]{1,0:T(8,128)(2,1)S(1)}, u32[]{:S(2)}) copy-start(bf16[192,1024]{1,0:T(8,128)(2,1)S(1)} %collective-permute-done.6.refs_4_) | copy-start | bytes 1179652
  99.7 27.9 %collective-permute-start.8 = (bf16[192,1024]{1,0:T(8,128)(2,1)S(1)}, bf16[192,1024]{1,0:T(8,128)(2,1)S(1)}, u32[]{:S(2)}, u32[]{:S(2)}) collective-permute-start(bf16[192,1024]{1,0:T(8,128)(2,1)S(1)} %collective-permute-done.6.refs_4_), channel_id=1, source_target_pairs={{0,896},{128,0},{256,128},{384,256},{512,384},{640,512},{768,640},... | collective-permute-start | bytes 1179656 | tf_op jit(solution)/shard_map/ppermute | solution.py:116
  104.5 25.3 %collective-permute-start.14 = (bf16[192,1024]{1,0:T(8,128)(2,1)S(1)}, bf16[192,1024]{1,0:T(8,128)(2,1)S(1)}, u32[]{:S(2)}, u32[]{:S(2)}) collective-permute-start(bf16[192,1024]{1,0:T(8,128)(2,1)S(1)} %collective-permute-done.6.refs_4_), channel_id=1, source_target_pairs={{0,16},{16,0},{1,17},{17,1},{2,18},{18,2},{3,19},{19,3},{4,20},{20... | collective-permute-start | bytes 1179656 | tf_op jit(solution)/shard_map/ppermute | solution.py:119
  109.2 30.0 %copy-start.8 = (bf16[192,1024]{1,0:T(8,128)(2,1)}, bf16[192,1024]{1,0:T(8,128)(2,1)S(1)}, u32[]{:S(2)}) copy-start(bf16[192,1024]{1,0:T(8,128)(2,1)S(1)} %collective-permute-done.5.refs_3_) | copy-start | bytes 1179652
  109.2 12.9 %collective-permute-start.7 = (bf16[192,1024]{1,0:T(8,128)(2,1)S(1)}, bf16[192,1024]{1,0:T(8,128)(2,1)S(1)}, u32[]{:S(2)}, u32[]{:S(2)}) collective-permute-start(bf16[192,1024]{1,0:T(8,128)(2,1)S(1)} %collective-permute-done.5.refs_3_), channel_id=1, source_target_pairs={{0,128},{128,256},{256,384},{384,512},{512,640},{640,768},{768,896... | collective-permute-start | bytes 1179656 | tf_op jit(solution)/shard_map/ppermute | solution.py:112
  111.4 34.2 %copy-start.7 = (bf16[192,1024]{1,0:T(8,128)(2,1)}, bf16[192,1024]{1,0:T(8,128)(2,1)S(1)}, u32[]{:S(2)}) copy-start(bf16[192,1024]{1,0:T(8,128)(2,1)S(1)} %collective-permute-done.12.refs_10_) | copy-start | bytes 1179652
  111.4 18.7 %collective-permute-start.13 = (bf16[192,1024]{1,0:T(8,128)(2,1)S(1)}, bf16[192,1024]{1,0:T(8,128)(2,1)S(1)}, u32[]{:S(2)}, u32[]{:S(2)}) collective-permute-start(bf16[192,1024]{1,0:T(8,128)(2,1)S(1)} %collective-permute-done.5.refs_3_), channel_id=1, source_target_pairs={{0,16},{16,0},{1,17},{17,1},{2,18},{18,2},{3,19},{19,3},{4,20},{20... | collective-permute-start | bytes 1179656 | tf_op jit(solution)/shard_map/ppermute | solution.py:119
  114.3 31.3 %copy-start.9 = (bf16[192,1024]{1,0:T(8,128)(2,1)}, bf16[192,1024]{1,0:T(8,128)(2,1)S(1)}, u32[]{:S(2)}) copy-start(bf16[192,1024]{1,0:T(8,128)(2,1)S(1)} %collective-permute-done.11.refs_9_) | copy-start | bytes 1179652
  122.1 23.5 %copy-start.12 = (bf16[192,1024]{1,0:T(8,128)(2,1)}, bf16[192,1024]{1,0:T(8,128)(2,1)S(1)}, u32[]{:S(2)}) copy-start(bf16[192,1024]{1,0:T(8,128)(2,1)S(1)} %collective-permute-done.7.refs_5_) | copy-start | bytes 1179652
  122.1 12.0 %collective-permute-start.9 = (bf16[192,1024]{1,0:T(8,128)(2,1)S(1)}, bf16[192,1024]{1,0:T(8,128)(2,1)S(1)}, u32[]{:S(2)}, u32[]{:S(2)}) collective-permute-start(bf16[192,1024]{1,0:T(8,128)(2,1)S(1)} %collective-permute-done.7.refs_5_), channel_id=1, source_target_pairs={{0,128},{128,256},{256,384},{384,512},{512,640},{640,768},{768,896... | collective-permute-start | bytes 1179656 | tf_op jit(solution)/shard_map/ppermute | solution.py:112
  124.0 14.8 %collective-permute-start.15 = (bf16[192,1024]{1,0:T(8,128)(2,1)S(1)}, bf16[192,1024]{1,0:T(8,128)(2,1)S(1)}, u32[]{:S(2)}, u32[]{:S(2)}) collective-permute-start(bf16[192,1024]{1,0:T(8,128)(2,1)S(1)} %collective-permute-done.7.refs_5_), channel_id=1, source_target_pairs={{0,16},{16,0},{1,17},{17,1},{2,18},{18,2},{3,19},{19,3},{4,20},{20... | collective-permute-start | bytes 1179656 | tf_op jit(solution)/shard_map/ppermute | solution.py:119
  127.6 11.3 %collective-permute-start.16 = (bf16[192,1024]{1,0:T(8,128)(2,1)S(1)}, bf16[192,1024]{1,0:T(8,128)(2,1)S(1)}, u32[]{:S(2)}, u32[]{:S(2)}) collective-permute-start(bf16[192,1024]{1,0:T(8,128)(2,1)S(1)} %collective-permute-done.8.refs_6_), channel_id=1, source_target_pairs={{0,16},{16,0},{1,17},{17,1},{2,18},{18,2},{3,19},{19,3},{4,20},{20... | collective-permute-start | bytes 1179656 | tf_op jit(solution)/shard_map/ppermute | solution.py:119
  134.1 5.8 %collective-permute-start.17 = (bf16[192,1024]{1,0:T(8,128)(2,1)S(1)}, bf16[192,1024]{1,0:T(8,128)(2,1)S(1)}, u32[]{:S(2)}, u32[]{:S(2)}) collective-permute-start(bf16[192,1024]{1,0:T(8,128)(2,1)S(1)} %collective-permute-done.9.refs_7_), channel_id=1, source_target_pairs={{0,16},{16,0},{1,17},{17,1},{2,18},{18,2},{3,19},{19,3},{4,20},{20... | collective-permute-start | bytes 1179656 | tf_op jit(solution)/shard_map/ppermute | solution.py:119
  140.2 19.5 %collective-permute-start.19 = (f32[1,384]{1,0:T(1,128)S(1)}, f32[1,384]{1,0:T(1,128)S(1)}, u32[]{:S(2)}, u32[]{:S(2)}) collective-permute-start(f32[1,384]{1,0:T(1,128)S(1)} %pad_maximum_fusion.1), channel_id=1, source_target_pairs={{0,8},{8,0},{1,9},{9,1},{2,10},{10,2},{3,11},{11,3},{4,12},{12,4},... | collective-permute-start | bytes 4616 | tf_op jit(solution)/shard_map/ppermute | solution.py:138
  155.9 16.3 %collective-permute-start.18 = (bf16[384,256]{1,0:T(8,128)(2,1)}, bf16[384,256]{1,0:T(8,128)(2,1)S(1)}, u32[]{:S(2)}, u32[]{:S(2)}) collective-permute-start(bf16[384,256]{1,0:T(8,128)(2,1)} %get-tuple-element.13), channel_id=1, source_target_pairs={{0,8},{8,0},{1,9},{9,1},{2,10},{10,2},{3,11},{11,3},{4,12},{12,4},... | collective-permute-start | bytes 589832 | tf_op jit(solution)/shard_map/ppermute | solution.py:142
  (10 other events, 102.8 us)

commit v4 on v3

v4 whole, which is shorter than its diff:
```python
import functools
import math

import jax
import jax.numpy as jnp
from jax import lax
from jax.experimental import pallas as pl
from jax.experimental.pallas import tpu as pltpu
from jax.sharding import Mesh
from jax.sharding import PartitionSpec as P

D = 8192
AXES = ("zh", "zl", "y1", "y0", "c", "yh", "x")
SIZES = (2, 4, 2, 2, 2, 2, 8)
Z, YL, DP, TENSOR = ("zh", "zl"), ("y1", "y0"), ("zh", "zl", "y1", "y0", "c"), ("yh", "x")
NZ, NYL, NX, NZL = 8, 4, 8, 4
LANES = 128
TAIL = 16

ema_rate = 0.5
norm_eps = 1e-06


def shift(count, by):
    return [(i, (i + by) % count) for i in range(count)]


def spread(v, axes, count):
    return lax.all_to_all(jnp.broadcast_to(v[None], (count,) + v.shape), axes, 0, 0, tiled=True)


def gate_kernel(first, index, *refs):
    blocks, weights, tail = refs[:NZ], refs[NZ], refs[NZ + 1]
    near, far, extra, a_buf, b_buf, acc, sums, a_sem, b_sem = refs[NZ + (1 if first else 2) :]
    b_copies = [
        pltpu.make_async_copy(weights.at[:, q], b_buf.at[q], b_sem.at[q]) for q in range(NZL)
    ]
    a_copies = [
        pltpu.make_async_copy(b, a_buf.at[index[s, 0], index[s, 1]], a_sem.at[s])
        for s, b in enumerate(blocks)
    ]
    for copy in b_copies + a_copies:
        copy.start()
    for copy in a_copies:
        copy.wait()
    groups, _, rows, depth = a_buf.shape
    cols = b_buf.shape[-1]
    if first:
        sums[...] = jnp.zeros_like(sums)
    for q in range(NZL):
        b_copies[q].wait()
        left = a_buf[:, q].reshape(groups * rows, depth)
        part = jnp.dot(left, b_buf[q].reshape(depth, cols), preferred_element_type=jnp.float32)
        part = part.reshape(groups, rows, cols)
        acc[...] = part if q == 0 else acc[...] + part
        if first:
            for g in range(groups):
                for lane in range(0, depth, LANES):
                    v = a_buf[g, q, :, lane : lane + LANES].astype(jnp.float32)
                    sums[g, :rows] += v * v
    if first:
        for g in range(groups):
            total = jnp.sum(jnp.transpose(sums[g]), axis=0, keepdims=True)
            high = total.astype(jnp.bfloat16).astype(jnp.float32)
            middle = (total - high).astype(jnp.bfloat16).astype(jnp.float32)
            low = total - high - middle
            row = lax.broadcasted_iota(jnp.int32, (TAIL, cols), 0)
            spread_rows = jnp.where(
                row == 0, high, jnp.where(row == 1, middle, jnp.where(row == 2, low, 0.0))
            )
            extra[g] = spread_rows.astype(extra.dtype)
    else:
        extra[...] = tail[...]
    mine = index[NZ, 0]
    for to, g in ((near, mine), (far, 1 - mine)):
        to[:rows] = acc[g].astype(to.dtype)
        to[rows:] = extra[g]


def gate_parts(index, blocks, weights, tail=None):
    rows, depth = blocks[0].shape
    cols = weights.shape[-1]
    hbm = pl.BlockSpec(memory_space=pl.ANY)
    vmem = pl.BlockSpec(memory_space=pltpu.VMEM)
    first = tail is None
    part = jax.ShapeDtypeStruct((rows + TAIL, cols), jnp.bfloat16)
    return pl.pallas_call(
        functools.partial(gate_kernel, first),
        out_shape=(part, part, jax.ShapeDtypeStruct((2, TAIL, cols), jnp.bfloat16)),
        in_specs=[pl.BlockSpec(memory_space=pltpu.SMEM)]
        + [hbm] * (NZ + 1)
        + ([] if first else [vmem]),
        out_specs=(vmem, vmem, vmem),
        scratch_shapes=[
            pltpu.VMEM((2, NZL, rows, depth), jnp.bfloat16),
            pltpu.VMEM((NZL, NX, LANES, cols), jnp.bfloat16),
            pltpu.VMEM((2, rows, cols), jnp.float32),
            pltpu.VMEM((2, cols, LANES), jnp.float32),
            pltpu.SemaphoreType.DMA((NZ,)),
            pltpu.SemaphoreType.DMA((NZL,)),
        ],
        compiler_params=pltpu.CompilerParams(vmem_limit_bytes=60 * 2**20),
        cost_estimate=pl.CostEstimate(
            flops=2 * NZ * rows * depth * cols,
            bytes_accessed=2 * NZ * depth * (rows + cols),
            transcendentals=0,
        ),
    )(index, *blocks, weights, *([] if first else [tail]))


def body(policy, ref_weight, tokens, gain):
    z, c, yh = lax.axis_index(Z), lax.axis_index("c"), lax.axis_index("yh")
    micro, toks, width = tokens.shape
    pieces = tokens.reshape(micro, toks, NZL, LANES).transpose(2, 0, 1, 3)
    pieces = pieces.reshape(NZL * micro, toks, LANES)
    pieces = lax.all_to_all(pieces, ("zl", "y1"), 0, 0, tiled=True)
    pieces = lax.all_to_all(pieces, "x", 0, 0, tiled=True)
    pieces, policy = lax.optimization_barrier((pieces, policy))
    arrived = lax.all_to_all(
        policy.reshape(8, 64, 256).transpose(1, 0, 2), DP, 0, 0, tiled=True
    )
    own = pieces.transpose(1, 0, 2).reshape(toks, NX * LANES)
    own = jnp.concatenate(
        [own] + [lax.ppermute(own, YL, [(i, i ^ e) for i in range(NYL)]) for e in range(1, NYL)]
    )
    rows = own.shape[0]
    own, arrived = lax.optimization_barrier((own, arrived))
    policy_slice = arrived.reshape(ref_weight.shape)
    ref_f = ref_weight.astype(jnp.float32)
    blended = (ref_f + ema_rate * (policy_slice.astype(jnp.float32) - ref_f)).astype(jnp.bfloat16)
    scaled = (blended.astype(jnp.float32) * gain[:, None]).astype(jnp.bfloat16)
    weights = spread(scaled, "x", NX)
    weights = weights.reshape(NX, NZL, LANES, weights.shape[-1])
    blocks, offsets = [own], [0]
    up = down = own
    for step in range(1, NZ // 2 + 1):
        if step > 1:
            up, down = lax.optimization_barrier((up, down))
        up = lax.ppermute(up, Z, shift(NZ, 1))
        blocks.append(up)
        offsets.append(-step)
        if step < NZ // 2:
            down = lax.ppermute(down, Z, shift(NZ, -1))
            blocks.append(down)
            offsets.append(step)
    weights, *blocks[-2:] = lax.optimization_barrier((weights, *blocks[-2:]))
    others = lax.ppermute(weights, "c", shift(2, 1))
    places = [(z + o) % NZ for o in offsets]
    index = [jnp.stack([p // NZL, p % NZL]) for p in places] + [jnp.stack([yh, yh])]
    index = jnp.stack(index).astype(jnp.int32)
    near, far, tail = gate_parts(index, blocks, weights)
    mine = near, lax.ppermute(far, "yh", shift(2, 1))
    near, far, _ = gate_parts(index, blocks, others, tail)
    across = lax.ppermute(far, ("c", "yh"), [(i, 3 - i) for i in range(4)])
    theirs = lax.ppermute(near, "c", shift(2, 1)), across

    def finish(pair):
        total = pair[0].astype(jnp.float32) + pair[1].astype(jnp.float32)
        squares = jnp.sum(total[rows : rows + 3], axis=0)[:rows]
        factor = lax.rsqrt(squares / D + norm_eps) * (1.0 / math.sqrt(D))
        return jax.nn.silu(total[:rows] * factor[:, None]).astype(jnp.bfloat16)

    mine, theirs = finish(mine), finish(theirs)
    activated = jnp.stack([jnp.where(c == 0, mine, theirs), jnp.where(c == 0, theirs, mine)])
    activated = activated.reshape(2, 2, 2, toks, -1)
    y1, y0 = lax.axis_index("y1"), lax.axis_index("y0")
    activated = jnp.where(y1 == 0, activated, activated[:, ::-1])
    activated = jnp.where(y0 == 0, activated, activated[:, :, ::-1])
    activated = activated.transpose(1, 2, 0, 3, 4)
    return blended, activated.reshape(micro, 4 * toks, -1)


def solution(mesh):
    fine = Mesh(mesh.devices.reshape(SIZES), AXES)
    return jax.shard_map(
        body,
        mesh=fine,
        in_specs=(P(DP, TENSOR, None), P(TENSOR, DP), P(None, DP, TENSOR), P(TENSOR)),
        out_specs=(P(TENSOR, DP), P(None, TENSOR, DP)),
        check_vma=False,
    )
```

time: 175 us -> 174 us (level)
  the two profiles are of different devices: /device:TPU:35 before, /device:TPU:1 now
where the time goes in v4:
time: 174 us; the launch traced here: 171 us
  starting transfers between devices  72.1 us (41%)
  waiting for transfers between devices  44.5 us (26%)
  blocking collectives  33.2 us (19%)
  Pallas kernels  12.6 us (7%)
  local copies, waits for them, and re-layouts  4.35 us (2%)
  other arithmetic  2.52 us (1%)
    ppermute x4, waiting for transfers between devices, body(): up = lax.ppermute(up, Z, shift(NZ, 1))  19.7 us
    all_to_all x1, blocking collectives, body(): pieces = lax.all_to_all(pieces, ('zl', 'y1'), 0, 0, tiled=True)  19.3 us
    all_to_all x1, starting transfers between devices, body(): lax.all_to_all(policy.reshape(8, 64, 256).transpose(1, 0, 2), DP, 0, 0, t...  16.6 us
    all_to_all x1, blocking collectives, body(): pieces = lax.all_to_all(pieces, 'x', 0, 0, tiled=True)  13.8 us
    ppermute x4, starting transfers between devices, body(): up = lax.ppermute(up, Z, shift(NZ, 1))  13.3 us
    pallas_call x2, Pallas kernels, gate_parts(): pl.pallas_call(functools.partial(gate_kernel, first), out_shape=(part, pa...  12.6 us
    ppermute x3, starting transfers between devices, body(): down = lax.ppermute(down, Z, shift(NZ, -1))  9.39 us
    ppermute x3, starting transfers between devices, body(): lax.ppermute(own, YL, [(i, i ^ e) for i in range(NYL)])  9.27 us
  transfers between devices with their start and end apart: 16, of which 12 were waited for; matrix products, arithmetic and copies ran while one was open for 2% of the time, Pallas kernels for 4%

profile of v4, /device:TPU:1, one launch (start us, length us, event | category | flops | bytes accessed | tf_op | source)
XLA Modules:
  0.0 170.6 jit_solution(10803627584595622902)
XLA Ops:
  1.6 19.3 %all_to_all.20 = bf16[8,48,128]{2,1,0:T(8,128)(2,1)S(1)} all-to-all(bf16[8,48,128]{2,1,0:T(8,128)(2,1)S(1)} %bitcast.65), channel_id=1, replica_groups=mesh['zh'=2,'zl'=4,'y1'=2,'y0'=2,'c'=2,'yh'=2,'x'=8] {'zl','y1'}, dimensions={0} | all-to-all | bytes 196608 | tf_op jit(solution)/shard_map/all_to_all | solution.py:116
  20.9 13.8 %all_to_all.21 = bf16[8,48,128]{2,1,0:T(8,128)(2,1)S(1)} all-to-all(bf16[8,48,128]{2,1,0:T(8,128)(2,1)S(1)} %all_to_all.20), channel_id=1, replica_groups=mesh['zh'=2,'zl'=4,'y1'=2,'y0'=2,'c'=2,'yh'=2,'x'=8] {'x'}, dimensions={0} | all-to-all | bytes 196608 | tf_op jit(solution)/shard_map/all_to_all | solution.py:117
  34.7 16.6 %all-to-all-start.2 = ((bf16[64,8,256]{2,1,0:T(8,128)(2,1)}), bf16[64,8,256]{2,1,0:T(8,128)(2,1)S(1)}, u32[]{:S(2)}, u32[]{:S(2)}) async-start(bf16[64,8,256]{2,1,0:T(8,128)(2,1)} %bitcast.67), calls=%async_computation.2 | async-start | bytes 524288 | tf_op jit(solution)/shard_map/all_to_all | solution.py:119
  51.3 3.3 %collective-permute-start = (bf16[48,1024]{1,0:T(8,128)(2,1)S(1)}, bf16[48,1024]{1,0:T(8,128)(2,1)S(1)}, u32[]{:S(2)}, u32[]{:S(2)}) collective-permute-start(bf16[48,1024]{1,0:T(8,128)(2,1)S(1)} %copy_bitcast_fusion), channel_id=1, source_target_pairs={{0,32},{32,0},{64,96},{96,64},{1,33},{33,1},{65,97},{97,65},{2,34}... | collective-permute-start | bytes 294920 | tf_op jit(solution)/shard_map/ppermute | solution.py:124
  54.6 4.0 %collective-permute-start.1 = (bf16[48,1024]{1,0:T(8,128)(2,1)S(1)}, bf16[48,1024]{1,0:T(8,128)(2,1)S(1)}, u32[]{:S(2)}, u32[]{:S(2)}) collective-permute-start(bf16[48,1024]{1,0:T(8,128)(2,1)S(1)} %copy_bitcast_fusion), channel_id=1, source_target_pairs={{0,64},{32,96},{64,0},{96,32},{1,65},{33,97},{65,1},{97,33},{2,66}... | collective-permute-start | bytes 294920 | tf_op jit(solution)/shard_map/ppermute | solution.py:124
  58.6 2.0 %collective-permute-start.2 = (bf16[48,1024]{1,0:T(8,128)(2,1)S(1)}, bf16[48,1024]{1,0:T(8,128)(2,1)S(1)}, u32[]{:S(2)}, u32[]{:S(2)}) collective-permute-start(bf16[48,1024]{1,0:T(8,128)(2,1)S(1)} %copy_bitcast_fusion), channel_id=1, source_target_pairs={{0,96},{32,64},{64,32},{96,0},{1,97},{33,65},{65,33},{97,1},{2,98}... | collective-permute-start | bytes 294920 | tf_op jit(solution)/shard_map/ppermute | solution.py:124
  61.5 4.4 %collective-permute-done.2 = bf16[48,1024]{1,0:T(8,128)(2,1)S(1)} collective-permute-done((bf16[48,1024]{1,0:T(8,128)(2,1)S(1)}, bf16[48,1024]{1,0:T(8,128)(2,1)S(1)}, u32[]{:S(2)}, u32[]{:S(2)}) %collective-permute-start.2) | collective-permute-done | bytes 98336 | tf_op jit(solution)/shard_map/ppermute | solution.py:124
  66.8 1.5 broadcast_in_dim.2
  68.3 3.6 %all-to-all-start.3 = ((bf16[8,512,256]{2,1,0:T(8,128)(2,1)}), bf16[8,512,256]{2,1,0:T(8,128)(2,1)S(1)}, u32[]{:S(2)}, u32[]{:S(2)}) async-start(bf16[8,512,256]{2,1,0:T(8,128)(2,1)} %broadcast_in_dim.2), calls=%async_computation.3 | async-start | bytes 4194304 | tf_op jit(solution)/shard_map/all_to_all | solution.py:29
  71.9 3.1 %collective-permute-start.3 = (bf16[192,1024]{1,0:T(8,128)(2,1)S(1)}, bf16[192,1024]{1,0:T(8,128)(2,1)S(1)}, u32[]{:S(2)}, u32[]{:S(2)}) collective-permute-start(bf16[192,1024]{1,0:T(8,128)(2,1)S(1)} %pad_maximum_fusion.refs_0_), channel_id=1, source_target_pairs={{0,128},{128,256},{256,384},{384,512},{512,640},{640,768},{768,896... | collective-permute-start | bytes 1179656 | tf_op jit(solution)/shard_map/ppermute | solution.py:139
  75.0 3.4 %collective-permute-start.4 = (bf16[192,1024]{1,0:T(8,128)(2,1)S(1)}, bf16[192,1024]{1,0:T(8,128)(2,1)S(1)}, u32[]{:S(2)}, u32[]{:S(2)}) collective-permute-start(bf16[192,1024]{1,0:T(8,128)(2,1)S(1)} %pad_maximum_fusion.refs_0_), channel_id=1, source_target_pairs={{0,896},{128,0},{256,128},{384,256},{512,384},{640,512},{768,640},... | collective-permute-start | bytes 1179656 | tf_op jit(solution)/shard_map/ppermute | solution.py:143
  78.4 5.2 %collective-permute-done.3.refs_1_ = bf16[192,1024]{1,0:T(8,128)(2,1)S(1)} collective-permute-done((bf16[192,1024]{1,0:T(8,128)(2,1)S(1)}, bf16[192,1024]{1,0:T(8,128)(2,1)S(1)}, u32[]{:S(2)}, u32[]{:S(2)}) %collective-permute-start.3) | collective-permute-done | bytes 393248 | tf_op jit(solution)/shard_map/ppermute | solution.py:139
  83.6 1.6 collective-permute-done.4.refs_2_
  85.2 3.1 %collective-permute-start.5 = (bf16[192,1024]{1,0:T(8,128)(2,1)S(1)}, bf16[192,1024]{1,0:T(8,128)(2,1)S(1)}, u32[]{:S(2)}, u32[]{:S(2)}) collective-permute-start(bf16[192,1024]{1,0:T(8,128)(2,1)S(1)} %collective-permute-done.3.refs_1_), channel_id=1, source_target_pairs={{0,128},{128,256},{256,384},{384,512},{512,640},{640,768},{768,896... | collective-permute-start | bytes 1179656 | tf_op jit(solution)/shard_map/ppermute | solution.py:139
  88.3 3.5 %collective-permute-start.6 = (bf16[192,1024]{1,0:T(8,128)(2,1)S(1)}, bf16[192,1024]{1,0:T(8,128)(2,1)S(1)}, u32[]{:S(2)}, u32[]{:S(2)}) collective-permute-start(bf16[192,1024]{1,0:T(8,128)(2,1)S(1)} %collective-permute-done.4.refs_2_), channel_id=1, source_target_pairs={{0,896},{128,0},{256,128},{384,256},{512,384},{640,512},{768,640},... | collective-permute-start | bytes 1179656 | tf_op jit(solution)/shard_map/ppermute | solution.py:143
  91.8 4.1 %collective-permute-done.5.refs_3_ = bf16[192,1024]{1,0:T(8,128)(2,1)S(1)} collective-permute-done((bf16[192,1024]{1,0:T(8,128)(2,1)S(1)}, bf16[192,1024]{1,0:T(8,128)(2,1)S(1)}, u32[]{:S(2)}, u32[]{:S(2)}) %collective-permute-start.5) | collective-permute-done | bytes 393248 | tf_op jit(solution)/shard_map/ppermute | solution.py:139
  95.9 3.1 %collective-permute-done.6.refs_4_ = bf16[192,1024]{1,0:T(8,128)(2,1)S(1)} collective-permute-done((bf16[192,1024]{1,0:T(8,128)(2,1)S(1)}, bf16[192,1024]{1,0:T(8,128)(2,1)S(1)}, u32[]{:S(2)}, u32[]{:S(2)}) %collective-permute-start.6) | collective-permute-done | bytes 393248 | tf_op jit(solution)/shard_map/ppermute | solution.py:143
  98.9 4.0 %collective-permute-start.7 = (bf16[192,1024]{1,0:T(8,128)(2,1)S(1)}, bf16[192,1024]{1,0:T(8,128)(2,1)S(1)}, u32[]{:S(2)}, u32[]{:S(2)}) collective-permute-start(bf16[192,1024]{1,0:T(8,128)(2,1)S(1)} %collective-permute-done.5.refs_3_), channel_id=1, source_target_pairs={{0,128},{128,256},{256,384},{384,512},{512,640},{640,768},{768,896... | collective-permute-start | bytes 1179656 | tf_op jit(solution)/shard_map/ppermute | solution.py:139
  103.0 2.5 %collective-permute-start.8 = (bf16[192,1024]{1,0:T(8,128)(2,1)S(1)}, bf16[192,1024]{1,0:T(8,128)(2,1)S(1)}, u32[]{:S(2)}, u32[]{:S(2)}) collective-permute-start(bf16[192,1024]{1,0:T(8,128)(2,1)S(1)} %collective-permute-done.6.refs_4_), channel_id=1, source_target_pairs={{0,896},{128,0},{256,128},{384,256},{512,384},{640,512},{768,640},... | collective-permute-start | bytes 1179656 | tf_op jit(solution)/shard_map/ppermute | solution.py:143
  105.4 3.5 %collective-permute-done.7.refs_5_ = bf16[192,1024]{1,0:T(8,128)(2,1)S(1)} collective-permute-done((bf16[192,1024]{1,0:T(8,128)(2,1)S(1)}, bf16[192,1024]{1,0:T(8,128)(2,1)S(1)}, u32[]{:S(2)}, u32[]{:S(2)}) %collective-permute-start.7) | collective-permute-done | bytes 393248 | tf_op jit(solution)/shard_map/ppermute | solution.py:139
  109.0 2.8 %collective-permute-done.8.refs_6_ = bf16[192,1024]{1,0:T(8,128)(2,1)S(1)} collective-permute-done((bf16[192,1024]{1,0:T(8,128)(2,1)S(1)}, bf16[192,1024]{1,0:T(8,128)(2,1)S(1)}, u32[]{:S(2)}, u32[]{:S(2)}) %collective-permute-start.8) | collective-permute-done | bytes 393248 | tf_op jit(solution)/shard_map/ppermute | solution.py:143
  111.8 3.1 %collective-permute-start.9 = (bf16[192,1024]{1,0:T(8,128)(2,1)S(1)}, bf16[192,1024]{1,0:T(8,128)(2,1)}, u32[]{:S(2)}, u32[]{:S(2)}) collective-permute-start(bf16[192,1024]{1,0:T(8,128)(2,1)S(1)} %collective-permute-done.7.refs_5_), channel_id=1, source_target_pairs={{0,128},{128,256},{256,384},{384,512},{512,640},{640,768},{768,896... | collective-permute-start | bytes 1179656 | tf_op jit(solution)/shard_map/ppermute | solution.py:139
  114.9 6.9 %collective-permute-done.9.refs_7_ = bf16[192,1024]{1,0:T(8,128)(2,1)} collective-permute-done((bf16[192,1024]{1,0:T(8,128)(2,1)S(1)}, bf16[192,1024]{1,0:T(8,128)(2,1)}, u32[]{:S(2)}, u32[]{:S(2)}) %collective-permute-start.9) | collective-permute-done | bytes 393248 | tf_op jit(solution)/shard_map/ppermute | solution.py:139
  121.8 1.7 all-to-all-done.3
  123.5 6.5 %collective-permute-start.11 = (bf16[8,4,128,256]{3,2,1,0:T(8,128)(2,1)S(1)}, bf16[8,4,128,256]{3,2,1,0:T(8,128)(2,1)}, u32[]{:S(2)}, u32[]{:S(2)}) collective-permute-start(bf16[8,4,128,256]{3,2,1,0:T(8,128)(2,1)S(1)} %bitcast.62), channel_id=1, source_target_pairs={{0,16},{16,0},{1,17},{17,1},{2,18},{18,2},{3,19},{19,3},{4,20},{20... | collective-permute-start | bytes 6291464 | tf_op jit(solution)/shard_map/ppermute | solution.py:147
  132.0 6.5 %shard_map.59 = (bf16[208,256]{1,0:T(8,128)(2,1)}, bf16[208,256]{1,0:T(8,128)(2,1)}, bf16[2,16,256]{2,1,0:T(8,128)(2,1)}) custom-call(s32[9,2]{1,0:T(8,128)} %stack.153.index, bf16[192,1024]{1,0:T(8,128)(2,1)} %copy-done.2, bf16[192,1024]{1,0:T(8,128)(2,1)} %copy-done.3, bf16[192,1024]{1,0:T(8,128)(2,1)} %copy-done.4, bf16[192,1024]{1,0:T(8,128)(2,1)} %copy-done.5, ...), custom_call_target="tpu_custom_call" | custom-call | flops 805306368 | bytes 7340032 | tf_op jit(solution)/shard_map/pallas_call | solution.py:87
  138.5 5.4 %collective-permute-start.10 = (bf16[208,256]{1,0:T(8,128)(2,1)}, bf16[208,256]{1,0:T(8,128)(2,1)S(1)}, u32[]{:S(2)}, u32[]{:S(2)}) collective-permute-start(bf16[208,256]{1,0:T(8,128)(2,1)} %get-tuple-element.32), channel_id=1, source_target_pairs={{0,8},{8,0},{1,9},{9,1},{2,10},{10,2},{3,11},{11,3},{4,12},{12,4},... | collective-permute-start | bytes 319496 | tf_op jit(solution)/shard_map/ppermute | solution.py:152
  143.9 5.2 %collective-permute-done.10 = bf16[208,256]{1,0:T(8,128)(2,1)S(1)} collective-permute-done((bf16[208,256]{1,0:T(8,128)(2,1)}, bf16[208,256]{1,0:T(8,128)(2,1)S(1)}, u32[]{:S(2)}, u32[]{:S(2)}) %collective-permute-start.10) | collective-permute-done | bytes 106528 | tf_op jit(solution)/shard_map/ppermute | solution.py:152
  150.0 6.1 %shard_map.60 = (bf16[208,256]{1,0:T(8,128)(2,1)}, bf16[208,256]{1,0:T(8,128)(2,1)}, bf16[2,16,256]{2,1,0:T(8,128)(2,1)}) custom-call(s32[9,2]{1,0:T(8,128)} %stack.153.index, bf16[192,1024]{1,0:T(8,128)(2,1)} %copy-done.2, bf16[192,1024]{1,0:T(8,128)(2,1)} %copy-done.3, bf16[192,1024]{1,0:T(8,128)(2,1)} %copy-done.4, bf16[192,1024]{1,0:T(8,128)(2,1)} %copy-done.5, ...), custom_call_target="tpu_custom_call" | custom-call | flops 805306368 | bytes 7340032 | tf_op jit(solution)/shard_map/pallas_call | solution.py:87
  156.1 2.8 %collective-permute-start.12 = (bf16[208,256]{1,0:T(8,128)(2,1)}, bf16[208,256]{1,0:T(8,128)(2,1)S(1)}, u32[]{:S(2)}, u32[]{:S(2)}) collective-permute-start(bf16[208,256]{1,0:T(8,128)(2,1)} %get-tuple-element.34), channel_id=1, source_target_pairs={{0,16},{16,0},{1,17},{17,1},{2,18},{18,2},{3,19},{19,3},{4,20},{20... | collective-permute-start | bytes 319496 | tf_op jit(solution)/shard_map/ppermute | solution.py:155
  158.9 5.3 %collective-permute-start.13 = (bf16[208,256]{1,0:T(8,128)(2,1)}, bf16[208,256]{1,0:T(8,128)(2,1)S(1)}, u32[]{:S(2)}, u32[]{:S(2)}) collective-permute-start(bf16[208,256]{1,0:T(8,128)(2,1)} %get-tuple-element.35), channel_id=1, source_target_pairs={{0,24},{8,16},{16,8},{24,0},{1,25},{9,17},{17,9},{25,1},{2,26},{10... | collective-permute-start | bytes 319496 | tf_op jit(solution)/shard_map/ppermute | solution.py:154
  164.2 5.3 %collective-permute-done.13 = bf16[208,256]{1,0:T(8,128)(2,1)S(1)} collective-permute-done((bf16[208,256]{1,0:T(8,128)(2,1)}, bf16[208,256]{1,0:T(8,128)(2,1)S(1)}, u32[]{:S(2)}, u32[]{:S(2)}) %collective-permute-start.13) | collective-permute-done | bytes 106528 | tf_op jit(solution)/shard_map/ppermute | solution.py:154
  (49 shorter events, 6.3 us)
Async XLA Ops:
  0.6 0.9 copy-start
  0.6 65.3 %copy-start.9 = (bf16[512,256]{1,0:T(8,128)(2,1)S(1)}, bf16[512,256]{1,0:T(8,128)(2,1)}, u32[]{:S(2)}) copy-start(bf16[512,256]{1,0:T(8,128)(2,1)} %param.5) | copy-start | bytes 786436
  1.5 64.4 %copy-start.10 = (f32[512]{0:T(512)S(1)}, f32[512]{0:T(512)}, u32[]{:S(2)}) copy-start(f32[512]{0:T(512)} %param.7) | copy-start | bytes 6148
  34.7 31.2 %all-to-all-start.2 = ((bf16[64,8,256]{2,1,0:T(8,128)(2,1)}), bf16[64,8,256]{2,1,0:T(8,128)(2,1)S(1)}, u32[]{:S(2)}, u32[]{:S(2)}) async-start(bf16[64,8,256]{2,1,0:T(8,128)(2,1)} %bitcast.67), calls=%async_computation.2 | async-start | bytes 524288 | tf_op jit(solution)/shard_map/all_to_all | solution.py:119
  51.3 9.3 %collective-permute-start = (bf16[48,1024]{1,0:T(8,128)(2,1)S(1)}, bf16[48,1024]{1,0:T(8,128)(2,1)S(1)}, u32[]{:S(2)}, u32[]{:S(2)}) collective-permute-start(bf16[48,1024]{1,0:T(8,128)(2,1)S(1)} %copy_bitcast_fusion), channel_id=1, source_target_pairs={{0,32},{32,0},{64,96},{96,64},{1,33},{33,1},{65,97},{97,65},{2,34}... | collective-permute-start | bytes 294920 | tf_op jit(solution)/shard_map/ppermute | solution.py:124
  54.6 6.9 %collective-permute-start.1 = (bf16[48,1024]{1,0:T(8,128)(2,1)S(1)}, bf16[48,1024]{1,0:T(8,128)(2,1)S(1)}, u32[]{:S(2)}, u32[]{:S(2)}) collective-permute-start(bf16[48,1024]{1,0:T(8,128)(2,1)S(1)} %copy_bitcast_fusion), channel_id=1, source_target_pairs={{0,64},{32,96},{64,0},{96,32},{1,65},{33,97},{65,1},{97,33},{2,66}... | collective-permute-start | bytes 294920 | tf_op jit(solution)/shard_map/ppermute | solution.py:124
  58.6 7.3 %collective-permute-start.2 = (bf16[48,1024]{1,0:T(8,128)(2,1)S(1)}, bf16[48,1024]{1,0:T(8,128)(2,1)S(1)}, u32[]{:S(2)}, u32[]{:S(2)}) collective-permute-start(bf16[48,1024]{1,0:T(8,128)(2,1)S(1)} %copy_bitcast_fusion), channel_id=1, source_target_pairs={{0,96},{32,64},{64,32},{96,0},{1,97},{33,65},{65,33},{97,1},{2,98}... | collective-permute-start | bytes 294920 | tf_op jit(solution)/shard_map/ppermute | solution.py:124
  65.9 9.1 %copy-start.2 = (bf16[192,1024]{1,0:T(8,128)(2,1)}, bf16[192,1024]{1,0:T(8,128)(2,1)S(1)}, u32[]{:S(2)}) copy-start(bf16[192,1024]{1,0:T(8,128)(2,1)S(1)} %pad_maximum_fusion.refs_0_) | copy-start | bytes 1179652
  68.3 55.2 %all-to-all-start.3 = ((bf16[8,512,256]{2,1,0:T(8,128)(2,1)}), bf16[8,512,256]{2,1,0:T(8,128)(2,1)S(1)}, u32[]{:S(2)}, u32[]{:S(2)}) async-start(bf16[8,512,256]{2,1,0:T(8,128)(2,1)} %broadcast_in_dim.2), calls=%async_computation.3 | async-start | bytes 4194304 | tf_op jit(solution)/shard_map/all_to_all | solution.py:29
  71.9 11.8 %collective-permute-start.3 = (bf16[192,1024]{1,0:T(8,128)(2,1)S(1)}, bf16[192,1024]{1,0:T(8,128)(2,1)S(1)}, u32[]{:S(2)}, u32[]{:S(2)}) collective-permute-start(bf16[192,1024]{1,0:T(8,128)(2,1)S(1)} %pad_maximum_fusion.refs_0_), channel_id=1, source_target_pairs={{0,128},{128,256},{256,384},{384,512},{512,640},{640,768},{768,896... | collective-permute-start | bytes 1179656 | tf_op jit(solution)/shard_map/ppermute | solution.py:139
  75.0 10.2 %collective-permute-start.4 = (bf16[192,1024]{1,0:T(8,128)(2,1)S(1)}, bf16[192,1024]{1,0:T(8,128)(2,1)S(1)}, u32[]{:S(2)}, u32[]{:S(2)}) collective-permute-start(bf16[192,1024]{1,0:T(8,128)(2,1)S(1)} %pad_maximum_fusion.refs_0_), channel_id=1, source_target_pairs={{0,896},{128,0},{256,128},{384,256},{512,384},{640,512},{768,640},... | collective-permute-start | bytes 1179656 | tf_op jit(solution)/shard_map/ppermute | solution.py:143
  83.6 48.3 %copy-start.3 = (bf16[192,1024]{1,0:T(8,128)(2,1)}, bf16[192,1024]{1,0:T(8,128)(2,1)S(1)}, u32[]{:S(2)}) copy-start(bf16[192,1024]{1,0:T(8,128)(2,1)S(1)} %collective-permute-done.3.refs_1_) | copy-start | bytes 1179652
  85.2 46.8 %copy-start.4 = (bf16[192,1024]{1,0:T(8,128)(2,1)}, bf16[192,1024]{1,0:T(8,128)(2,1)S(1)}, u32[]{:S(2)}) copy-start(bf16[192,1024]{1,0:T(8,128)(2,1)S(1)} %collective-permute-done.4.refs_2_) | copy-start | bytes 1179652
  85.2 10.7 %collective-permute-start.5 = (bf16[192,1024]{1,0:T(8,128)(2,1)S(1)}, bf16[192,1024]{1,0:T(8,128)(2,1)S(1)}, u32[]{:S(2)}, u32[]{:S(2)}) collective-permute-start(bf16[192,1024]{1,0:T(8,128)(2,1)S(1)} %collective-permute-done.3.refs_1_), channel_id=1, source_target_pairs={{0,128},{128,256},{256,384},{384,512},{512,640},{640,768},{768,896... | collective-permute-start | bytes 1179656 | tf_op jit(solution)/shard_map/ppermute | solution.py:139
  88.3 10.6 %collective-permute-start.6 = (bf16[192,1024]{1,0:T(8,128)(2,1)S(1)}, bf16[192,1024]{1,0:T(8,128)(2,1)S(1)}, u32[]{:S(2)}, u32[]{:S(2)}) collective-permute-start(bf16[192,1024]{1,0:T(8,128)(2,1)S(1)} %collective-permute-done.4.refs_2_), channel_id=1, source_target_pairs={{0,896},{128,0},{256,128},{384,256},{512,384},{640,512},{768,640},... | collective-permute-start | bytes 1179656 | tf_op jit(solution)/shard_map/ppermute | solution.py:143
  95.9 36.1 %copy-start.5 = (bf16[192,1024]{1,0:T(8,128)(2,1)}, bf16[192,1024]{1,0:T(8,128)(2,1)S(1)}, u32[]{:S(2)}) copy-start(bf16[192,1024]{1,0:T(8,128)(2,1)S(1)} %collective-permute-done.5.refs_3_) | copy-start | bytes 1179652
  98.9 16.0 %copy-start.6 = (bf16[192,1024]{1,0:T(8,128)(2,1)}, bf16[192,1024]{1,0:T(8,128)(2,1)S(1)}, u32[]{:S(2)}) copy-start(bf16[192,1024]{1,0:T(8,128)(2,1)S(1)} %collective-permute-done.6.refs_4_) | copy-start | bytes 1179652
  98.9 10.0 %collective-permute-start.7 = (bf16[192,1024]{1,0:T(8,128)(2,1)S(1)}, bf16[192,1024]{1,0:T(8,128)(2,1)S(1)}, u32[]{:S(2)}, u32[]{:S(2)}) collective-permute-start(bf16[192,1024]{1,0:T(8,128)(2,1)S(1)} %collective-permute-done.5.refs_3_), channel_id=1, source_target_pairs={{0,128},{128,256},{256,384},{384,512},{512,640},{640,768},{768,896... | collective-permute-start | bytes 1179656 | tf_op jit(solution)/shard_map/ppermute | solution.py:139
  103.0 8.8 %collective-permute-start.8 = (bf16[192,1024]{1,0:T(8,128)(2,1)S(1)}, bf16[192,1024]{1,0:T(8,128)(2,1)S(1)}, u32[]{:S(2)}, u32[]{:S(2)}) collective-permute-start(bf16[192,1024]{1,0:T(8,128)(2,1)S(1)} %collective-permute-done.6.refs_4_), channel_id=1, source_target_pairs={{0,896},{128,0},{256,128},{384,256},{512,384},{640,512},{768,640},... | collective-permute-start | bytes 1179656 | tf_op jit(solution)/shard_map/ppermute | solution.py:143
  109.0 6.0 %copy-start.7 = (bf16[192,1024]{1,0:T(8,128)(2,1)}, bf16[192,1024]{1,0:T(8,128)(2,1)S(1)}, u32[]{:S(2)}) copy-start(bf16[192,1024]{1,0:T(8,128)(2,1)S(1)} %collective-permute-done.7.refs_5_) | copy-start | bytes 1179652
  111.8 3.2 %copy-start.8 = (bf16[192,1024]{1,0:T(8,128)(2,1)}, bf16[192,1024]{1,0:T(8,128)(2,1)S(1)}, u32[]{:S(2)}) copy-start(bf16[192,1024]{1,0:T(8,128)(2,1)S(1)} %collective-permute-done.8.refs_6_) | copy-start | bytes 1179652
  111.8 10.0 %collective-permute-start.9 = (bf16[192,1024]{1,0:T(8,128)(2,1)S(1)}, bf16[192,1024]{1,0:T(8,128)(2,1)}, u32[]{:S(2)}, u32[]{:S(2)}) collective-permute-start(bf16[192,1024]{1,0:T(8,128)(2,1)S(1)} %collective-permute-done.7.refs_5_), channel_id=1, source_target_pairs={{0,128},{128,256},{256,384},{384,512},{512,640},{640,768},{768,896... | collective-permute-start | bytes 1179656 | tf_op jit(solution)/shard_map/ppermute | solution.py:139
  123.5 8.5 %copy-start.1 = (bf16[8,512,256]{2,1,0:T(8,128)(2,1)}, bf16[8,512,256]{2,1,0:T(8,128)(2,1)S(1)}, u32[]{:S(2)}) copy-start(bf16[8,512,256]{2,1,0:T(8,128)(2,1)S(1)} %all-to-all-done.3) | copy-start | bytes 6291460
  123.5 26.6 %collective-permute-start.11 = (bf16[8,4,128,256]{3,2,1,0:T(8,128)(2,1)S(1)}, bf16[8,4,128,256]{3,2,1,0:T(8,128)(2,1)}, u32[]{:S(2)}, u32[]{:S(2)}) collective-permute-start(bf16[8,4,128,256]{3,2,1,0:T(8,128)(2,1)S(1)} %bitcast.62), channel_id=1, source_target_pairs={{0,16},{16,0},{1,17},{17,1},{2,18},{18,2},{3,19},{19,3},{4,20},{20... | collective-permute-start | bytes 6291464 | tf_op jit(solution)/shard_map/ppermute | solution.py:147
  138.5 10.6 %collective-permute-start.10 = (bf16[208,256]{1,0:T(8,128)(2,1)}, bf16[208,256]{1,0:T(8,128)(2,1)S(1)}, u32[]{:S(2)}, u32[]{:S(2)}) collective-permute-start(bf16[208,256]{1,0:T(8,128)(2,1)} %get-tuple-element.32), channel_id=1, source_target_pairs={{0,8},{8,0},{1,9},{9,1},{2,10},{10,2},{3,11},{11,3},{4,12},{12,4},... | collective-permute-start | bytes 319496 | tf_op jit(solution)/shard_map/ppermute | solution.py:152
  156.1 8.1 %collective-permute-start.12 = (bf16[208,256]{1,0:T(8,128)(2,1)}, bf16[208,256]{1,0:T(8,128)(2,1)S(1)}, u32[]{:S(2)}, u32[]{:S(2)}) collective-permute-start(bf16[208,256]{1,0:T(8,128)(2,1)} %get-tuple-element.34), channel_id=1, source_target_pairs={{0,16},{16,0},{1,17},{17,1},{2,18},{18,2},{3,19},{19,3},{4,20},{20... | collective-permute-start | bytes 319496 | tf_op jit(solution)/shard_map/ppermute | solution.py:155
  158.9 10.6 %collective-permute-start.13 = (bf16[208,256]{1,0:T(8,128)(2,1)}, bf16[208,256]{1,0:T(8,128)(2,1)S(1)}, u32[]{:S(2)}, u32[]{:S(2)}) collective-permute-start(bf16[208,256]{1,0:T(8,128)(2,1)} %get-tuple-element.35), channel_id=1, source_target_pairs={{0,24},{8,16},{16,8},{24,0},{1,25},{9,17},{17,9},{25,1},{2,26},{10... | collective-permute-start | bytes 319496 | tf_op jit(solution)/shard_map/ppermute | solution.py:154

commit v5 on v4

v5 whole, which is shorter than its diff:
```python
import functools
import math

import jax
import jax.numpy as jnp
from jax import lax
from jax.experimental import pallas as pl
from jax.experimental.pallas import tpu as pltpu
from jax.sharding import Mesh
from jax.sharding import PartitionSpec as P

D = 8192
AXES = ("zh", "zl", "y1", "y0", "c", "yh", "x")
SIZES = (2, 4, 2, 2, 2, 2, 8)
Z, YL, DP, TENSOR = ("zh", "zl"), ("y1", "y0"), ("zh", "zl", "y1", "y0", "c"), ("yh", "x")
NZ, NYL, NX, NZL = 8, 4, 8, 4
LANES = 128
TAIL = 16

ema_rate = 0.5
norm_eps = 1e-06


def shift(count, by):
    return [(i, (i + by) % count) for i in range(count)]


def spread(v, axes, count):
    return lax.all_to_all(jnp.broadcast_to(v[None], (count,) + v.shape), axes, 0, 0, tiled=True)


def gate_kernel(step, index, *refs):
    held = refs[: (NZ - 1, 1, NZ)[step]]
    weights, refs = refs[len(held)], refs[len(held) + 1 :]
    base = NZ - 1 if step == 1 else 0
    if step == 0:
        acc, sums, a_buf, b_buf, a_sem, b_sem = refs
    elif step == 1:
        acc_in, sums_in, near, far, extra, a_buf, b_buf, acc, sums, a_sem, b_sem = refs
    else:
        tail, near, far, a_buf, b_buf, acc, a_sem, b_sem = refs
    a_copies = [
        pltpu.make_async_copy(h, a_buf.at[s], a_sem.at[s]) for s, h in enumerate(held)
    ]
    if step == 1:
        last = index[NZ + base]
        b_copies = [pltpu.make_async_copy(weights.at[:, last], b_buf.at[last], b_sem.at[0])]
    else:
        b_copies = [
            pltpu.make_async_copy(weights.at[:, q], b_buf.at[q], b_sem.at[q]) for q in range(NZL)
        ]
    for copy in b_copies + a_copies:
        copy.start()
    if step == 1:
        acc[...] = acc_in[...]
        sums[...] = sums_in[...]
    else:
        acc[...] = jnp.zeros_like(acc)
    if step == 0:
        sums[...] = jnp.zeros_like(sums)
    rows, depth = a_buf.shape[1:]
    cols = b_buf.shape[-1]
    for copy in b_copies:
        copy.wait()
    for s, copy in enumerate(a_copies):
        copy.wait()
        g, q = index[base + s], index[NZ + base + s]
        right = b_buf[q].reshape(depth, cols)
        acc[g] += jnp.dot(a_buf[s], right, preferred_element_type=jnp.float32)
        if step < 2:
            total = jnp.zeros((rows, LANES), jnp.float32)
            for lane in range(0, depth, LANES):
                v = a_buf[s, :, lane : lane + LANES].astype(jnp.float32)
                total += v * v
            sums[g, :rows] += total
    if step == 0:
        return
    if step == 1:
        for g in range(2):
            total = jnp.sum(jnp.transpose(sums[g]), axis=0, keepdims=True)
            high = total.astype(jnp.bfloat16).astype(jnp.float32)
            middle = (total - high).astype(jnp.bfloat16).astype(jnp.float32)
            low = total - high - middle
            row = lax.broadcasted_iota(jnp.int32, (TAIL, cols), 0)
            spread_rows = jnp.where(
                row == 0, high, jnp.where(row == 1, middle, jnp.where(row == 2, low, 0.0))
            )
            extra[g] = spread_rows.astype(extra.dtype)
        tail = extra
    mine = index[2 * NZ]
    for to, g in ((near, mine), (far, 1 - mine)):
        to[:rows] = acc[g].astype(to.dtype)
        to[rows:] = tail[g]


def gate_parts(step, index, blocks, weights, *more):
    rows, depth = blocks[0].shape
    cols = weights.shape[-1]
    hbm = pl.BlockSpec(memory_space=pl.ANY)
    vmem = pl.BlockSpec(memory_space=pltpu.VMEM)
    part = jax.ShapeDtypeStruct((rows + TAIL, cols), jnp.bfloat16)
    tail = jax.ShapeDtypeStruct((2, TAIL, cols), jnp.bfloat16)
    acc, sums = (2, rows, cols), (2, cols, LANES)
    totals = [pltpu.VMEM(acc, jnp.float32), pltpu.VMEM(sums, jnp.float32)]
    outs = (
        (jax.ShapeDtypeStruct(acc, jnp.float32), jax.ShapeDtypeStruct(sums, jnp.float32)),
        (part, part, tail),
        (part, part),
    )[step]
    return pl.pallas_call(
        functools.partial(gate_kernel, step),
        out_shape=outs,
        in_specs=[pl.BlockSpec(memory_space=pltpu.SMEM)]
        + [hbm] * (len(blocks) + 1)
        + [vmem] * len(more),
        out_specs=(vmem,) * len(outs),
        scratch_shapes=[
            pltpu.VMEM((len(blocks), rows, depth), jnp.bfloat16),
            pltpu.VMEM((NZL, NX, LANES, cols), jnp.bfloat16),
        ]
        + ([], totals, totals[:1])[step]
        + [pltpu.SemaphoreType.DMA((len(blocks),)), pltpu.SemaphoreType.DMA((NZL,))],
        compiler_params=pltpu.CompilerParams(vmem_limit_bytes=60 * 2**20),
        cost_estimate=pl.CostEstimate(
            flops=2 * len(blocks) * rows * depth * cols,
            bytes_accessed=2 * len(blocks) * depth * (rows + cols),
            transcendentals=0,
        ),
    )(index, *blocks, weights, *more)


def finish_kernel(index, near, far, near_other, far_other, out):
    rows = near.shape[0] - TAIL
    toks = rows // NYL
    core, place = index[2 * NZ + 1], index[2 * NZ + 2]
    for first, second, col in ((near, far, core), (near_other, far_other, 1 - core)):
        squares = first[rows:].astype(jnp.float32) + second[rows:].astype(jnp.float32)
        squares = jnp.sum(squares, axis=0, keepdims=True)
        factor = lax.rsqrt(squares / D + norm_eps) * (1.0 / math.sqrt(D))
        factor = jnp.transpose(jnp.broadcast_to(factor, (LANES, factor.shape[1])))
        for e in range(NYL):
            y = place ^ e
            to = pl.multiple_of(((y % 2) * 2 + col) * toks, 16)
            for lane in range(0, out.shape[2], LANES):
                at = slice(e * toks, (e + 1) * toks), slice(lane, lane + LANES)
                gate = first[at].astype(jnp.float32) + second[at].astype(jnp.float32)
                gate = gate * factor[e * toks : (e + 1) * toks]
                gate = gate / (1.0 + jnp.exp(-gate))
                out[y // 2, pl.ds(to, toks), lane : lane + LANES] = gate.astype(out.dtype)


def finish(index, parts, micro):
    rows, cols = parts[0].shape
    vmem = pl.BlockSpec(memory_space=pltpu.VMEM)
    return pl.pallas_call(
        finish_kernel,
        out_shape=jax.ShapeDtypeStruct((micro, rows - TAIL, cols), jnp.bfloat16),
        in_specs=[pl.BlockSpec(memory_space=pltpu.SMEM)] + [vmem] * 4,
        out_specs=vmem,
        compiler_params=pltpu.CompilerParams(vmem_limit_bytes=8 * 2**20),
    )(index, *parts)


def body(policy, ref_weight, tokens, gain):
    z, c, yh = lax.axis_index(Z), lax.axis_index("c"), lax.axis_index("yh")
    micro, toks, width = tokens.shape
    pieces = tokens.reshape(micro, toks, NZL, LANES).transpose(2, 0, 1, 3)
    pieces = pieces.reshape(NZL * micro, toks, LANES)
    pieces = lax.all_to_all(pieces, ("zl", "y1"), 0, 0, tiled=True)
    pieces = lax.all_to_all(pieces, "x", 0, 0, tiled=True)
    pieces, policy = lax.optimization_barrier((pieces, policy))
    arrived = lax.all_to_all(
        policy.reshape(8, 64, 256).transpose(1, 0, 2), DP, 0, 0, tiled=True
    )
    own = pieces.transpose(1, 0, 2).reshape(toks, NX * LANES)
    own = jnp.concatenate(
        [own] + [lax.ppermute(own, YL, [(i, i ^ e) for i in range(NYL)]) for e in range(1, NYL)]
    )
    rows = own.shape[0]
    own, arrived = lax.optimization_barrier((own, arrived))
    policy_slice = arrived.reshape(ref_weight.shape)
    ref_f = ref_weight.astype(jnp.float32)
    blended = (ref_f + ema_rate * (policy_slice.astype(jnp.float32) - ref_f)).astype(jnp.bfloat16)
    scaled = (blended.astype(jnp.float32) * gain[:, None]).astype(jnp.bfloat16)
    weights = spread(scaled, "x", NX)
    weights = weights.reshape(NX, NZL, LANES, weights.shape[-1])
    blocks, offsets = [own], [0]
    up = down = own
    for step in range(1, NZ // 2 + 1):
        if step > 1:
            up, down = lax.optimization_barrier((up, down))
        up = lax.ppermute(up, Z, shift(NZ, 1))
        blocks.append(up)
        offsets.append(-step)
        if step < NZ // 2:
            down = lax.ppermute(down, Z, shift(NZ, -1))
            blocks.append(down)
            offsets.append(step)
    place = lax.axis_index(YL)
    places = (z + jnp.array(offsets, jnp.int32)) & (NZ - 1)
    index = jnp.concatenate([places // NZL, places % NZL, jnp.stack([yh, c, place])])
    weights, *blocks[-3:-1] = lax.optimization_barrier((weights, *blocks[-3:-1]))
    others = lax.ppermute(weights, "c", shift(2, 1))
    acc, sums = gate_parts(0, index, blocks[:-1], weights)
    acc, blocks[-1] = lax.optimization_barrier((acc, blocks[-1]))
    near, far, tail = gate_parts(1, index, blocks[-1:], weights, acc, sums)
    far = lax.ppermute(far, "yh", shift(2, 1))
    near_other, far_other = gate_parts(2, index, blocks, others, tail)
    far_other = lax.ppermute(far_other, ("c", "yh"), [(i, 3 - i) for i in range(4)])
    near_other = lax.ppermute(near_other, "c", shift(2, 1))
    activated = finish(index, (near, far, near_other, far_other), micro)
    return blended, activated


def solution(mesh):
    fine = Mesh(mesh.devices.reshape(SIZES), AXES)
    return jax.shard_map(
        body,
        mesh=fine,
        in_specs=(P(DP, TENSOR, None), P(TENSOR, DP), P(None, DP, TENSOR), P(TENSOR)),
        out_specs=(P(TENSOR, DP), P(None, TENSOR, DP)),
        check_vma=False,
    )
```

time: 174 us -> 175 us (level); the launches traced: 171 us -> 174 us
  Pallas kernels: 12.6 us -> 18.3 us
  waiting for transfers between devices: 44.5 us -> 48.2 us
  starting transfers between devices: 72.1 us -> 68.8 us
    pallas_call x2 -> x4, Pallas kernels: 12.6 us -> 18.3 us  [the longest x3 16.8 us: gate_parts(): pl.pallas_call(functools.partial(gate_kernel, step), out_shape=outs, in_s...]
    ppermute x4, starting transfers between devices: 13.3 us -> 7.66 us  [body(): up = lax.ppermute(up, Z, shift(NZ, 1))]
    all_to_all x1, waiting for transfers between devices: 1.67 us -> 6.99 us  [spread(): lax.all_to_all(jnp.broadcast_to(v[None], (count,) + v.shape), axes, 0, 0,...]
    ppermute x3, starting transfers between devices: 9.39 us -> 13.7 us  [body(): down = lax.ppermute(down, Z, shift(NZ, -1))]
    ppermute x3, waiting for transfers between devices: 10.5 us -> 6.87 us  [the longest x1 6.87 us: body(): lax.ppermute(far_other, ('c', 'yh'), [(i, 3 - i) for i in range(4)])]
    ppermute x3, waiting for transfers between devices: 5.26 us -> 7.63 us  [body(): lax.ppermute(own, YL, [(i, i ^ e) for i in range(NYL)])]
  transfers between devices with their start and end apart: 16 -> 16, of which waited for: 12 -> 12; matrix products, arithmetic and copies ran while one was open for 2% -> 0% of each run, Pallas kernels for 4% -> 10%
where the time goes in v5:
time: 175 us; the launch traced here: 174 us
  starting transfers between devices  68.8 us (39%)
  waiting for transfers between devices  48.2 us (28%)
  blocking collectives  33.3 us (19%)
  Pallas kernels  18.3 us (10%)
  local copies, waits for them, and re-layouts  3.81 us (2%)
    all_to_all x1, blocking collectives, body(): pieces = lax.all_to_all(pieces, ('zl', 'y1'), 0, 0, tiled=True)  19.5 us
    ppermute x4, waiting for transfers between devices, body(): up = lax.ppermute(up, Z, shift(NZ, 1))  18.4 us
    pallas_call x3, Pallas kernels, gate_parts(): pl.pallas_call(functools.partial(gate_kernel, step), out_shape=outs, in_s...  16.8 us
    all_to_all x1, starting transfers between devices, body(): lax.all_to_all(policy.reshape(8, 64, 256).transpose(1, 0, 2), DP, 0, 0, t...  16.6 us
    all_to_all x1, blocking collectives, body(): pieces = lax.all_to_all(pieces, 'x', 0, 0, tiled=True)  13.8 us
    ppermute x3, starting transfers between devices, body(): down = lax.ppermute(down, Z, shift(NZ, -1))  13.7 us
    ppermute x3, starting transfers between devices, body(): lax.ppermute(own, YL, [(i, i ^ e) for i in range(NYL)])  9.27 us
    ppermute x4, starting transfers between devices, body(): up = lax.ppermute(up, Z, shift(NZ, 1))  7.66 us
  transfers between devices with their start and end apart: 16, of which 12 were waited for; matrix products, arithmetic and copies ran while one was open for 0% of the time, Pallas kernels for 10%

profile of v5, /device:TPU:1, one launch (start us, length us, event | category | flops | bytes accessed | tf_op | source)
XLA Modules:
  0.0 174.1 jit_solution(14017983519462375437)
XLA Ops:
  1.6 19.5 %all_to_all.20 = bf16[8,48,128]{2,1,0:T(8,128)(2,1)S(1)} all-to-all(bf16[8,48,128]{2,1,0:T(8,128)(2,1)S(1)} %bitcast.28), channel_id=1, replica_groups=mesh['zh'=2,'zl'=4,'y1'=2,'y0'=2,'c'=2,'yh'=2,'x'=8] {'zl','y1'}, dimensions={0} | all-to-all | bytes 196608 | tf_op jit(solution)/shard_map/all_to_all | solution.py:169
  21.0 13.8 %all_to_all.21 = bf16[8,48,128]{2,1,0:T(8,128)(2,1)S(1)} all-to-all(bf16[8,48,128]{2,1,0:T(8,128)(2,1)S(1)} %all_to_all.20), channel_id=1, replica_groups=mesh['zh'=2,'zl'=4,'y1'=2,'y0'=2,'c'=2,'yh'=2,'x'=8] {'x'}, dimensions={0} | all-to-all | bytes 196608 | tf_op jit(solution)/shard_map/all_to_all | solution.py:170
  34.9 16.6 %all-to-all-start.2 = ((bf16[64,8,256]{2,1,0:T(8,128)(2,1)}), bf16[64,8,256]{2,1,0:T(8,128)(2,1)S(1)}, u32[]{:S(2)}, u32[]{:S(2)}) async-start(bf16[64,8,256]{2,1,0:T(8,128)(2,1)} %bitcast.29), calls=%async_computation.2 | async-start | bytes 524288 | tf_op jit(solution)/shard_map/all_to_all | solution.py:172
  51.5 5.1 %collective-permute-start.2 = (bf16[48,1024]{1,0:T(8,128)(2,1)S(1)}, bf16[48,1024]{1,0:T(8,128)(2,1)S(1)}, u32[]{:S(2)}, u32[]{:S(2)}) collective-permute-start(bf16[48,1024]{1,0:T(8,128)(2,1)S(1)} %copy_bitcast_fusion), channel_id=1, source_target_pairs={{0,96},{32,64},{64,32},{96,0},{1,97},{33,65},{65,33},{97,1},{2,98}... | collective-permute-start | bytes 294920 | tf_op jit(solution)/shard_map/ppermute | solution.py:177
  56.6 1.9 %collective-permute-start.1 = (bf16[48,1024]{1,0:T(8,128)(2,1)S(1)}, bf16[48,1024]{1,0:T(8,128)(2,1)S(1)}, u32[]{:S(2)}, u32[]{:S(2)}) collective-permute-start(bf16[48,1024]{1,0:T(8,128)(2,1)S(1)} %copy_bitcast_fusion), channel_id=1, source_target_pairs={{0,64},{32,96},{64,0},{96,32},{1,65},{33,97},{65,1},{97,33},{2,66}... | collective-permute-start | bytes 294920 | tf_op jit(solution)/shard_map/ppermute | solution.py:177
  58.5 2.3 %collective-permute-start = (bf16[48,1024]{1,0:T(8,128)(2,1)S(1)}, bf16[48,1024]{1,0:T(8,128)(2,1)S(1)}, u32[]{:S(2)}, u32[]{:S(2)}) collective-permute-start(bf16[48,1024]{1,0:T(8,128)(2,1)S(1)} %copy_bitcast_fusion), channel_id=1, source_target_pairs={{0,32},{32,0},{64,96},{96,64},{1,33},{33,1},{65,97},{97,65},{2,34}... | collective-permute-start | bytes 294920 | tf_op jit(solution)/shard_map/ppermute | solution.py:177
  61.6 6.8 %collective-permute-done.1 = bf16[48,1024]{1,0:T(8,128)(2,1)S(1)} collective-permute-done((bf16[48,1024]{1,0:T(8,128)(2,1)S(1)}, bf16[48,1024]{1,0:T(8,128)(2,1)S(1)}, u32[]{:S(2)}, u32[]{:S(2)}) %collective-permute-start.1) | collective-permute-done | bytes 98336 | tf_op jit(solution)/shard_map/ppermute | solution.py:177
  70.1 1.5 broadcast_in_dim.2
  71.6 3.7 %all-to-all-start.3 = ((bf16[8,512,256]{2,1,0:T(8,128)(2,1)}), bf16[8,512,256]{2,1,0:T(8,128)(2,1)S(1)}, u32[]{:S(2)}, u32[]{:S(2)}) async-start(bf16[8,512,256]{2,1,0:T(8,128)(2,1)} %broadcast_in_dim.2), calls=%async_computation.3 | async-start | bytes 4194304 | tf_op jit(solution)/shard_map/all_to_all | solution.py:29
  75.3 3.8 %collective-permute-start.4 = (bf16[192,1024]{1,0:T(8,128)(2,1)S(1)}, bf16[192,1024]{1,0:T(8,128)(2,1)S(1)}, u32[]{:S(2)}, u32[]{:S(2)}) collective-permute-start(bf16[192,1024]{1,0:T(8,128)(2,1)S(1)} %pad_maximum_fusion.refs_0_), channel_id=1, source_target_pairs={{0,896},{128,0},{256,128},{384,256},{512,384},{640,512},{768,640},... | collective-permute-start | bytes 1179656 | tf_op jit(solution)/shard_map/ppermute | solution.py:196
  79.1 1.9 %collective-permute-start.3 = (bf16[192,1024]{1,0:T(8,128)(2,1)S(1)}, bf16[192,1024]{1,0:T(8,128)(2,1)S(1)}, u32[]{:S(2)}, u32[]{:S(2)}) collective-permute-start(bf16[192,1024]{1,0:T(8,128)(2,1)S(1)} %pad_maximum_fusion.refs_0_), channel_id=1, source_target_pairs={{0,128},{128,256},{256,384},{384,512},{512,640},{640,768},{768,896... | collective-permute-start | bytes 1179656 | tf_op jit(solution)/shard_map/ppermute | solution.py:192
  81.0 6.5 %collective-permute-done.4.refs_2_ = bf16[192,1024]{1,0:T(8,128)(2,1)S(1)} collective-permute-done((bf16[192,1024]{1,0:T(8,128)(2,1)S(1)}, bf16[192,1024]{1,0:T(8,128)(2,1)S(1)}, u32[]{:S(2)}, u32[]{:S(2)}) %collective-permute-start.4) | collective-permute-done | bytes 393248 | tf_op jit(solution)/shard_map/ppermute | solution.py:196
  87.5 4.2 %collective-permute-done.3.refs_1_ = bf16[192,1024]{1,0:T(8,128)(2,1)S(1)} collective-permute-done((bf16[192,1024]{1,0:T(8,128)(2,1)S(1)}, bf16[192,1024]{1,0:T(8,128)(2,1)S(1)}, u32[]{:S(2)}, u32[]{:S(2)}) %collective-permute-start.3) | collective-permute-done | bytes 393248 | tf_op jit(solution)/shard_map/ppermute | solution.py:192
  91.7 1.9 %collective-permute-start.5 = (bf16[192,1024]{1,0:T(8,128)(2,1)S(1)}, bf16[192,1024]{1,0:T(8,128)(2,1)S(1)}, u32[]{:S(2)}, u32[]{:S(2)}) collective-permute-start(bf16[192,1024]{1,0:T(8,128)(2,1)S(1)} %collective-permute-done.3.refs_1_), channel_id=1, source_target_pairs={{0,128},{128,256},{256,384},{384,512},{512,640},{640,768},{768,896... | collective-permute-start | bytes 1179656 | tf_op jit(solution)/shard_map/ppermute | solution.py:192
  93.6 4.6 %collective-permute-start.6 = (bf16[192,1024]{1,0:T(8,128)(2,1)S(1)}, bf16[192,1024]{1,0:T(8,128)(2,1)S(1)}, u32[]{:S(2)}, u32[]{:S(2)}) collective-permute-start(bf16[192,1024]{1,0:T(8,128)(2,1)S(1)} %collective-permute-done.4.refs_2_), channel_id=1, source_target_pairs={{0,896},{128,0},{256,128},{384,256},{512,384},{640,512},{768,640},... | collective-permute-start | bytes 1179656 | tf_op jit(solution)/shard_map/ppermute | solution.py:196
  98.2 5.1 %collective-permute-done.5.refs_3_ = bf16[192,1024]{1,0:T(8,128)(2,1)S(1)} collective-permute-done((bf16[192,1024]{1,0:T(8,128)(2,1)S(1)}, bf16[192,1024]{1,0:T(8,128)(2,1)S(1)}, u32[]{:S(2)}, u32[]{:S(2)}) %collective-permute-start.5) | collective-permute-done | bytes 393248 | tf_op jit(solution)/shard_map/ppermute | solution.py:192
  103.3 0.9 collective-permute-done.6.refs_4_
  104.2 1.9 %collective-permute-start.7 = (bf16[192,1024]{1,0:T(8,128)(2,1)S(1)}, bf16[192,1024]{1,0:T(8,128)(2,1)S(1)}, u32[]{:S(2)}, u32[]{:S(2)}) collective-permute-start(bf16[192,1024]{1,0:T(8,128)(2,1)S(1)} %collective-permute-done.5.refs_3_), channel_id=1, source_target_pairs={{0,128},{128,256},{256,384},{384,512},{512,640},{640,768},{768,896... | collective-permute-start | bytes 1179656 | tf_op jit(solution)/shard_map/ppermute | solution.py:192
  106.1 5.3 %collective-permute-start.8 = (bf16[192,1024]{1,0:T(8,128)(2,1)S(1)}, bf16[192,1024]{1,0:T(8,128)(2,1)}, u32[]{:S(2)}, u32[]{:S(2)}) collective-permute-start(bf16[192,1024]{1,0:T(8,128)(2,1)S(1)} %collective-permute-done.6.refs_4_), channel_id=1, source_target_pairs={{0,896},{128,0},{256,128},{384,256},{512,384},{640,512},{768,640},... | collective-permute-start | bytes 1179656 | tf_op jit(solution)/shard_map/ppermute | solution.py:196
  111.5 4.2 %collective-permute-done.7.refs_5_ = bf16[192,1024]{1,0:T(8,128)(2,1)S(1)} collective-permute-done((bf16[192,1024]{1,0:T(8,128)(2,1)S(1)}, bf16[192,1024]{1,0:T(8,128)(2,1)S(1)}, u32[]{:S(2)}, u32[]{:S(2)}) %collective-permute-start.7) | collective-permute-done | bytes 393248 | tf_op jit(solution)/shard_map/ppermute | solution.py:192
  116.6 7.0 %all-to-all-done.3 = bf16[8,512,256]{2,1,0:T(8,128)(2,1)S(1)} async-done(((bf16[8,512,256]{2,1,0:T(8,128)(2,1)}), bf16[8,512,256]{2,1,0:T(8,128)(2,1)S(1)}, u32[]{:S(2)}, u32[]{:S(2)}) %all-to-all-start.3) | async-done | bytes 2097184 | tf_op jit(solution)/shard_map/all_to_all | solution.py:29
  123.6 5.8 %collective-permute-start.11 = (bf16[8,4,128,256]{3,2,1,0:T(8,128)(2,1)S(1)}, bf16[8,4,128,256]{3,2,1,0:T(8,128)(2,1)}, u32[]{:S(2)}, u32[]{:S(2)}) collective-permute-start(bf16[8,4,128,256]{3,2,1,0:T(8,128)(2,1)S(1)} %bitcast.25), channel_id=1, source_target_pairs={{0,16},{16,0},{1,17},{17,1},{2,18},{18,2},{3,19},{19,3},{4,20},{20... | collective-permute-start | bytes 6291464 | tf_op jit(solution)/shard_map/ppermute | solution.py:203
  129.3 1.9 %collective-permute-start.9 = (bf16[192,1024]{1,0:T(8,128)(2,1)}, bf16[192,1024]{1,0:T(8,128)(2,1)}, u32[]{:S(2)}, u32[]{:S(2)}) collective-permute-start(bf16[192,1024]{1,0:T(8,128)(2,1)} %copy-done.9), channel_id=1, source_target_pairs={{0,128},{128,256},{256,384},{384,512},{512,640},{640,768},{768,896... | collective-permute-start | bytes 1179656 | tf_op jit(solution)/shard_map/ppermute | solution.py:192
  132.0 6.7 %shard_map.68 = (f32[2,192,256]{2,1,0:T(8,128)}, f32[2,256,128]{2,1,0:T(8,128)}) custom-call(s32[19]{0:T(128)} %concatenate.7.index, bf16[192,1024]{1,0:T(8,128)(2,1)} %copy-done.4, bf16[192,1024]{1,0:T(8,128)(2,1)} %copy-done.6, bf16[192,1024]{1,0:T(8,128)(2,1)} %copy-done.5, bf16[192,1024]{1,0:T(8,128)(2,1)} %copy-done.7, bf16[192,1024]{1,0:T(8,128)(2,1)} %copy-done.8, ...), custom_call_target="tpu_custom_call" | custom-call | flops 704643072 | bytes 6422528 | tf_op jit(solution)/shard_map/pallas_call | solution.py:110
  138.6 4.9 %collective-permute-done.9.refs_0_.refs_7_ = bf16[192,1024]{1,0:T(8,128)(2,1)} collective-permute-done((bf16[192,1024]{1,0:T(8,128)(2,1)}, bf16[192,1024]{1,0:T(8,128)(2,1)}, u32[]{:S(2)}, u32[]{:S(2)}) %collective-permute-start.9) | collective-permute-done | bytes 393248 | tf_op jit(solution)/shard_map/ppermute | solution.py:192
  143.5 3.4 %shard_map.69 = (bf16[208,256]{1,0:T(8,128)(2,1)}, bf16[208,256]{1,0:T(8,128)(2,1)}, bf16[2,16,256]{2,1,0:T(8,128)(2,1)}) custom-call(s32[19]{0:T(128)} %concatenate.7.index, bf16[192,1024]{1,0:T(8,128)(2,1)} %collective-permute-done.9.refs_0_.refs_7_, bf16[8,4,128,256]{3,2,1,0:T(8,128)(2,1)} %bitcast.27, f32[2,192,256]{2,1,0:T(8,128)} %get-tuple-element.37.refs_2_, ...), custom_call_target="tpu_custom_call" | custom-call | flops 100663296 | bytes 917504 | tf_op jit(solution)/shard_map/pallas_call | solution.py:110
  146.9 5.4 %collective-permute-start.10 = (bf16[208,256]{1,0:T(8,128)(2,1)}, bf16[208,256]{1,0:T(8,128)(2,1)S(1)}, u32[]{:S(2)}, u32[]{:S(2)}) collective-permute-start(bf16[208,256]{1,0:T(8,128)(2,1)} %get-tuple-element.40), channel_id=1, source_target_pairs={{0,8},{8,0},{1,9},{9,1},{2,10},{10,2},{3,11},{11,3},{4,12},{12,4},... | collective-permute-start | bytes 319496 | tf_op jit(solution)/shard_map/ppermute | solution.py:207
  152.3 6.8 %shard_map.70 = (bf16[208,256]{1,0:T(8,128)(2,1)}, bf16[208,256]{1,0:T(8,128)(2,1)}) custom-call(s32[19]{0:T(128)} %concatenate.7.index, bf16[192,1024]{1,0:T(8,128)(2,1)} %copy-done.4, bf16[192,1024]{1,0:T(8,128)(2,1)} %copy-done.6, bf16[192,1024]{1,0:T(8,128)(2,1)} %copy-done.5, bf16[192,1024]{1,0:T(8,128)(2,1)} %copy-done.7, bf16[192,1024]{1,0:T(8,128)(2,1)} %copy-done.8, ...), custom_call_target="tpu_custom_call" | custom-call | flops 805306368 | bytes 7340032 | tf_op jit(solution)/shard_map/pallas_call | solution.py:110
  159.1 3.0 %collective-permute-start.12 = (bf16[208,256]{1,0:T(8,128)(2,1)}, bf16[208,256]{1,0:T(8,128)(2,1)S(1)}, u32[]{:S(2)}, u32[]{:S(2)}) collective-permute-start(bf16[208,256]{1,0:T(8,128)(2,1)} %get-tuple-element.42), channel_id=1, source_target_pairs={{0,16},{16,0},{1,17},{17,1},{2,18},{18,2},{3,19},{19,3},{4,20},{20... | collective-permute-start | bytes 319496 | tf_op jit(solution)/shard_map/ppermute | solution.py:210
  162.1 3.7 %collective-permute-start.13 = (bf16[208,256]{1,0:T(8,128)(2,1)}, bf16[208,256]{1,0:T(8,128)(2,1)S(1)}, u32[]{:S(2)}, u32[]{:S(2)}) collective-permute-start(bf16[208,256]{1,0:T(8,128)(2,1)} %get-tuple-element.43), channel_id=1, source_target_pairs={{0,24},{8,16},{16,8},{24,0},{1,25},{9,17},{17,9},{25,1},{2,26},{10... | collective-permute-start | bytes 319496 | tf_op jit(solution)/shard_map/ppermute | solution.py:209
  165.8 6.9 %collective-permute-done.13.far_other = bf16[208,256]{1,0:T(8,128)(2,1)S(1)} collective-permute-done((bf16[208,256]{1,0:T(8,128)(2,1)}, bf16[208,256]{1,0:T(8,128)(2,1)S(1)}, u32[]{:S(2)}, u32[]{:S(2)}) %collective-permute-start.13) | collective-permute-done | bytes 106528 | tf_op jit(solution)/shard_map/ppermute | solution.py:209
  172.7 1.4 shard_map.71
  (40 shorter events, 5.0 us)
Async XLA Ops:
  0.6 0.9 copy-start
  0.6 68.6 %copy-start.11 = (f32[512]{0:T(512)S(1)}, f32[512]{0:T(512)}, u32[]{:S(2)}) copy-start(f32[512]{0:T(512)} %param.8) | copy-start | bytes 6148
  1.5 67.7 %copy-start.10 = (bf16[512,256]{1,0:T(8,128)(2,1)S(1)}, bf16[512,256]{1,0:T(8,128)(2,1)}, u32[]{:S(2)}) copy-start(bf16[512,256]{1,0:T(8,128)(2,1)} %param.6) | copy-start | bytes 786436
  34.9 34.4 %all-to-all-start.2 = ((bf16[64,8,256]{2,1,0:T(8,128)(2,1)}), bf16[64,8,256]{2,1,0:T(8,128)(2,1)S(1)}, u32[]{:S(2)}, u32[]{:S(2)}) async-start(bf16[64,8,256]{2,1,0:T(8,128)(2,1)} %bitcast.29), calls=%async_computation.2 | async-start | bytes 524288 | tf_op jit(solution)/shard_map/all_to_all | solution.py:172
  51.5 10.1 %collective-permute-start.2 = (bf16[48,1024]{1,0:T(8,128)(2,1)S(1)}, bf16[48,1024]{1,0:T(8,128)(2,1)S(1)}, u32[]{:S(2)}, u32[]{:S(2)}) collective-permute-start(bf16[48,1024]{1,0:T(8,128)(2,1)S(1)} %copy_bitcast_fusion), channel_id=1, source_target_pairs={{0,96},{32,64},{64,32},{96,0},{1,97},{33,65},{65,33},{97,1},{2,98}... | collective-permute-start | bytes 294920 | tf_op jit(solution)/shard_map/ppermute | solution.py:177
  56.6 11.8 %collective-permute-start.1 = (bf16[48,1024]{1,0:T(8,128)(2,1)S(1)}, bf16[48,1024]{1,0:T(8,128)(2,1)S(1)}, u32[]{:S(2)}, u32[]{:S(2)}) collective-permute-start(bf16[48,1024]{1,0:T(8,128)(2,1)S(1)} %copy_bitcast_fusion), channel_id=1, source_target_pairs={{0,64},{32,96},{64,0},{96,32},{1,65},{33,97},{65,1},{97,33},{2,66}... | collective-permute-start | bytes 294920 | tf_op jit(solution)/shard_map/ppermute | solution.py:177
  58.5 9.9 %collective-permute-start = (bf16[48,1024]{1,0:T(8,128)(2,1)S(1)}, bf16[48,1024]{1,0:T(8,128)(2,1)S(1)}, u32[]{:S(2)}, u32[]{:S(2)}) collective-permute-start(bf16[48,1024]{1,0:T(8,128)(2,1)S(1)} %copy_bitcast_fusion), channel_id=1, source_target_pairs={{0,32},{32,0},{64,96},{96,64},{1,33},{33,1},{65,97},{97,65},{2,34}... | collective-permute-start | bytes 294920 | tf_op jit(solution)/shard_map/ppermute | solution.py:177
  68.4 10.7 %copy-start.4 = (bf16[192,1024]{1,0:T(8,128)(2,1)}, bf16[192,1024]{1,0:T(8,128)(2,1)S(1)}, u32[]{:S(2)}) copy-start(bf16[192,1024]{1,0:T(8,128)(2,1)S(1)} %pad_maximum_fusion.refs_0_) | copy-start | bytes 1179652
  71.6 59.7 %copy-start.12 = (s32[8]{0:T(128)S(1)}, s32[8]{0:T(128)}, u32[]{:S(2)}) copy-start(s32[8]{0:T(128)} %constant.62.clone) | copy-start | bytes 100
  71.6 52.0 %all-to-all-start.3 = ((bf16[8,512,256]{2,1,0:T(8,128)(2,1)}), bf16[8,512,256]{2,1,0:T(8,128)(2,1)S(1)}, u32[]{:S(2)}, u32[]{:S(2)}) async-start(bf16[8,512,256]{2,1,0:T(8,128)(2,1)} %broadcast_in_dim.2), calls=%async_computation.3 | async-start | bytes 4194304 | tf_op jit(solution)/shard_map/all_to_all | solution.py:29
  75.3 12.2 %collective-permute-start.4 = (bf16[192,1024]{1,0:T(8,128)(2,1)S(1)}, bf16[192,1024]{1,0:T(8,128)(2,1)S(1)}, u32[]{:S(2)}, u32[]{:S(2)}) collective-permute-start(bf16[192,1024]{1,0:T(8,128)(2,1)S(1)} %pad_maximum_fusion.refs_0_), channel_id=1, source_target_pairs={{0,896},{128,0},{256,128},{384,256},{512,384},{640,512},{768,640},... | collective-permute-start | bytes 1179656 | tf_op jit(solution)/shard_map/ppermute | solution.py:196
  79.1 12.6 %collective-permute-start.3 = (bf16[192,1024]{1,0:T(8,128)(2,1)S(1)}, bf16[192,1024]{1,0:T(8,128)(2,1)S(1)}, u32[]{:S(2)}, u32[]{:S(2)}) collective-permute-start(bf16[192,1024]{1,0:T(8,128)(2,1)S(1)} %pad_maximum_fusion.refs_0_), channel_id=1, source_target_pairs={{0,128},{128,256},{256,384},{384,512},{512,640},{640,768},{768,896... | collective-permute-start | bytes 1179656 | tf_op jit(solution)/shard_map/ppermute | solution.py:192
  87.5 44.4 %copy-start.5 = (bf16[192,1024]{1,0:T(8,128)(2,1)}, bf16[192,1024]{1,0:T(8,128)(2,1)S(1)}, u32[]{:S(2)}) copy-start(bf16[192,1024]{1,0:T(8,128)(2,1)S(1)} %collective-permute-done.4.refs_2_) | copy-start | bytes 1179652
  91.7 40.3 %copy-start.6 = (bf16[192,1024]{1,0:T(8,128)(2,1)}, bf16[192,1024]{1,0:T(8,128)(2,1)S(1)}, u32[]{:S(2)}) copy-start(bf16[192,1024]{1,0:T(8,128)(2,1)S(1)} %collective-permute-done.3.refs_1_) | copy-start | bytes 1179652
  91.7 11.6 %collective-permute-start.5 = (bf16[192,1024]{1,0:T(8,128)(2,1)S(1)}, bf16[192,1024]{1,0:T(8,128)(2,1)S(1)}, u32[]{:S(2)}, u32[]{:S(2)}) collective-permute-start(bf16[192,1024]{1,0:T(8,128)(2,1)S(1)} %collective-permute-done.3.refs_1_), channel_id=1, source_target_pairs={{0,128},{128,256},{256,384},{384,512},{512,640},{640,768},{768,896... | collective-permute-start | bytes 1179656 | tf_op jit(solution)/shard_map/ppermute | solution.py:192
  93.6 10.6 %collective-permute-start.6 = (bf16[192,1024]{1,0:T(8,128)(2,1)S(1)}, bf16[192,1024]{1,0:T(8,128)(2,1)S(1)}, u32[]{:S(2)}, u32[]{:S(2)}) collective-permute-start(bf16[192,1024]{1,0:T(8,128)(2,1)S(1)} %collective-permute-done.4.refs_2_), channel_id=1, source_target_pairs={{0,896},{128,0},{256,128},{384,256},{512,384},{640,512},{768,640},... | collective-permute-start | bytes 1179656 | tf_op jit(solution)/shard_map/ppermute | solution.py:196
  103.3 28.7 %copy-start.7 = (bf16[192,1024]{1,0:T(8,128)(2,1)}, bf16[192,1024]{1,0:T(8,128)(2,1)S(1)}, u32[]{:S(2)}) copy-start(bf16[192,1024]{1,0:T(8,128)(2,1)S(1)} %collective-permute-done.5.refs_3_) | copy-start | bytes 1179652
  104.2 11.5 %copy-start.8 = (bf16[192,1024]{1,0:T(8,128)(2,1)}, bf16[192,1024]{1,0:T(8,128)(2,1)S(1)}, u32[]{:S(2)}) copy-start(bf16[192,1024]{1,0:T(8,128)(2,1)S(1)} %collective-permute-done.6.refs_4_) | copy-start | bytes 1179652
  104.2 11.5 %collective-permute-start.7 = (bf16[192,1024]{1,0:T(8,128)(2,1)S(1)}, bf16[192,1024]{1,0:T(8,128)(2,1)S(1)}, u32[]{:S(2)}, u32[]{:S(2)}) collective-permute-start(bf16[192,1024]{1,0:T(8,128)(2,1)S(1)} %collective-permute-done.5.refs_3_), channel_id=1, source_target_pairs={{0,128},{128,256},{256,384},{384,512},{512,640},{640,768},{768,896... | collective-permute-start | bytes 1179656 | tf_op jit(solution)/shard_map/ppermute | solution.py:192
  106.1 10.4 %collective-permute-start.8 = (bf16[192,1024]{1,0:T(8,128)(2,1)S(1)}, bf16[192,1024]{1,0:T(8,128)(2,1)}, u32[]{:S(2)}, u32[]{:S(2)}) collective-permute-start(bf16[192,1024]{1,0:T(8,128)(2,1)S(1)} %collective-permute-done.6.refs_4_), channel_id=1, source_target_pairs={{0,896},{128,0},{256,128},{384,256},{512,384},{640,512},{768,640},... | collective-permute-start | bytes 1179656 | tf_op jit(solution)/shard_map/ppermute | solution.py:196
  115.7 0.8 copy-start.9
  123.6 8.4 %copy-start.3 = (bf16[8,512,256]{2,1,0:T(8,128)(2,1)}, bf16[8,512,256]{2,1,0:T(8,128)(2,1)S(1)}, u32[]{:S(2)}) copy-start(bf16[8,512,256]{2,1,0:T(8,128)(2,1)S(1)} %all-to-all-done.3) | copy-start | bytes 6291460
  123.6 28.7 %collective-permute-start.11 = (bf16[8,4,128,256]{3,2,1,0:T(8,128)(2,1)S(1)}, bf16[8,4,128,256]{3,2,1,0:T(8,128)(2,1)}, u32[]{:S(2)}, u32[]{:S(2)}) collective-permute-start(bf16[8,4,128,256]{3,2,1,0:T(8,128)(2,1)S(1)} %bitcast.25), channel_id=1, source_target_pairs={{0,16},{16,0},{1,17},{17,1},{2,18},{18,2},{3,19},{19,3},{4,20},{20... | collective-permute-start | bytes 6291464 | tf_op jit(solution)/shard_map/ppermute | solution.py:203
  129.3 14.2 %collective-permute-start.9 = (bf16[192,1024]{1,0:T(8,128)(2,1)}, bf16[192,1024]{1,0:T(8,128)(2,1)}, u32[]{:S(2)}, u32[]{:S(2)}) collective-permute-start(bf16[192,1024]{1,0:T(8,128)(2,1)} %copy-done.9), channel_id=1, source_target_pairs={{0,128},{128,256},{256,384},{384,512},{512,640},{640,768},{768,896... | collective-permute-start | bytes 1179656 | tf_op jit(solution)/shard_map/ppermute | solution.py:192
  146.9 18.9 %collective-permute-start.10 = (bf16[208,256]{1,0:T(8,128)(2,1)}, bf16[208,256]{1,0:T(8,128)(2,1)S(1)}, u32[]{:S(2)}, u32[]{:S(2)}) collective-permute-start(bf16[208,256]{1,0:T(8,128)(2,1)} %get-tuple-element.40), channel_id=1, source_target_pairs={{0,8},{8,0},{1,9},{9,1},{2,10},{10,2},{3,11},{11,3},{4,12},{12,4},... | collective-permute-start | bytes 319496 | tf_op jit(solution)/shard_map/ppermute | solution.py:207
  152.3 20.4 %copy-start.1 = (bf16[208,256]{1,0:T(8,128)(2,1)S(1)}, bf16[208,256]{1,0:T(8,128)(2,1)}, u32[]{:S(2)}) copy-start(bf16[208,256]{1,0:T(8,128)(2,1)} %get-tuple-element.39.near) | copy-start | bytes 319492
  152.3 20.4 %copy-start.2 = (s32[19]{0:T(128)S(1)}, s32[19]{0:T(128)}, u32[]{:S(2)}) copy-start(s32[19]{0:T(128)} %concatenate.7.index) | copy-start | bytes 232
  159.1 6.7 %collective-permute-start.12 = (bf16[208,256]{1,0:T(8,128)(2,1)}, bf16[208,256]{1,0:T(8,128)(2,1)S(1)}, u32[]{:S(2)}, u32[]{:S(2)}) collective-permute-start(bf16[208,256]{1,0:T(8,128)(2,1)} %get-tuple-element.42), channel_id=1, source_target_pairs={{0,16},{16,0},{1,17},{17,1},{2,18},{18,2},{3,19},{19,3},{4,20},{20... | collective-permute-start | bytes 319496 | tf_op jit(solution)/shard_map/ppermute | solution.py:210
  162.1 10.6 %collective-permute-start.13 = (bf16[208,256]{1,0:T(8,128)(2,1)}, bf16[208,256]{1,0:T(8,128)(2,1)S(1)}, u32[]{:S(2)}, u32[]{:S(2)}) collective-permute-start(bf16[208,256]{1,0:T(8,128)(2,1)} %get-tuple-element.43), channel_id=1, source_target_pairs={{0,24},{8,16},{16,8},{24,0},{1,25},{9,17},{17,9},{25,1},{2,26},{10... | collective-permute-start | bytes 319496 | tf_op jit(solution)/shard_map/ppermute | solution.py:209

commit v6 on v4

v6 whole, which is shorter than its diff:
```python
import functools
import math

import jax
import jax.numpy as jnp
from jax import lax
from jax.experimental import pallas as pl
from jax.experimental.pallas import tpu as pltpu
from jax.sharding import Mesh
from jax.sharding import PartitionSpec as P

D = 8192
AXES = ("zh", "zl", "y1", "y0", "c", "yh", "x")
SIZES = (2, 4, 2, 2, 2, 2, 8)
Z, YL, DP, TENSOR = ("zh", "zl"), ("y1", "y0"), ("zh", "zl", "y1", "y0", "c"), ("yh", "x")
NZ, NYL, NX, NZL = 8, 4, 8, 4
LANES = 128
TAIL = 16

ema_rate = 0.5
norm_eps = 1e-06


def shift(count, by):
    return [(i, (i + by) % count) for i in range(count)]


def spread(v, axes, count):
    return lax.all_to_all(jnp.broadcast_to(v[None], (count,) + v.shape), axes, 0, 0, tiled=True)


def gate_kernel(first, index, *refs):
    blocks, weights, refs = refs[: NZ + 1], refs[NZ + 1], refs[NZ + 2 :]
    if first:
        parts, a_buf, b_buf, acc, sums, a_sem, b_sem = refs
    else:
        before, out, a_buf, b_buf, acc, a_sem, b_sem = refs
    groups, _, rows, depth = a_buf.shape
    cols = b_buf.shape[-1]
    b_copies = [
        pltpu.make_async_copy(weights.at[:, q], b_buf.at[q], b_sem.at[q]) for q in range(NZL)
    ]
    places = [a_buf.at[index[s], index[NZ + s]] for s in range(NZ)]
    places[-1:] = [places[-1].at[: rows // 2], places[-1].at[rows // 2 :]]
    a_copies = [
        pltpu.make_async_copy(h, to, a_sem.at[s]) for s, (h, to) in enumerate(zip(blocks, places))
    ]
    for copy in a_copies + b_copies:
        copy.start()
    if first:
        sums[...] = jnp.zeros_like(sums)
    for copy in a_copies:
        copy.wait()
    for q in range(NZL):
        b_copies[q].wait()
        left = a_buf[:, q].reshape(groups * rows, depth)
        part = jnp.dot(left, b_buf[q].reshape(depth, cols), preferred_element_type=jnp.float32)
        part = part.reshape(groups, rows, cols)
        acc[...] = part if q == 0 else acc[...] + part
        if first:
            for g in range(groups):
                total = jnp.zeros((rows, LANES), jnp.float32)
                for lane in range(0, depth, LANES):
                    v = a_buf[g, q, :, lane : lane + LANES].astype(jnp.float32)
                    total += v * v
                sums[g, :rows] += total
    if first:
        for g in range(groups):
            total = jnp.sum(jnp.transpose(sums[g]), axis=0, keepdims=True)
            high = total.astype(jnp.bfloat16).astype(jnp.float32)
            middle = (total - high).astype(jnp.bfloat16).astype(jnp.float32)
            low = total - high - middle
            row = lax.broadcasted_iota(jnp.int32, (TAIL, cols), 0)
            spread_rows = jnp.where(
                row == 0, high, jnp.where(row == 1, middle, jnp.where(row == 2, low, 0.0))
            )
            parts[g, :rows] = acc[g].astype(parts.dtype)
            parts[g, rows:] = spread_rows.astype(parts.dtype)
    else:
        core = index[2 * NZ]
        out[core] = before[...]
        for g in range(groups):
            out[1 - core, g, :rows] = acc[g].astype(out.dtype)
            out[1 - core, g, rows:] = before[g, rows:]


def gate_parts(index, blocks, weights, *before):
    rows, depth = blocks[0].shape
    cols = weights.shape[-1]
    hbm = pl.BlockSpec(memory_space=pl.ANY)
    vmem = pl.BlockSpec(memory_space=pltpu.VMEM)
    first = not before
    parts = (2, rows + TAIL, cols)
    totals = [pltpu.VMEM((2, rows, cols), jnp.float32), pltpu.VMEM((2, cols, LANES), jnp.float32)]
    return pl.pallas_call(
        functools.partial(gate_kernel, first),
        out_shape=jax.ShapeDtypeStruct(parts if first else (2,) + parts, jnp.bfloat16),
        in_specs=[pl.BlockSpec(memory_space=pltpu.SMEM)]
        + [hbm] * (len(blocks) + 1)
        + [vmem] * len(before),
        out_specs=vmem,
        scratch_shapes=[
            pltpu.VMEM((2, NZL, rows, depth), jnp.bfloat16),
            pltpu.VMEM((NZL, NX, LANES, cols), jnp.bfloat16),
        ]
        + (totals if first else totals[:1])
        + [pltpu.SemaphoreType.DMA((len(blocks),)), pltpu.SemaphoreType.DMA((NZL,))],
        compiler_params=pltpu.CompilerParams(vmem_limit_bytes=60 * 2**20),
        cost_estimate=pl.CostEstimate(
            flops=2 * NZ * rows * depth * cols,
            bytes_accessed=2 * NZ * depth * (rows + cols),
            transcendentals=0,
        ),
    )(index, *blocks, weights, *before)


def finish_kernel(index, parts, out):
    rows = parts.shape[1] - TAIL
    toks = rows // NYL
    place = index[2 * NZ + 1]
    for core in range(2):
        a, b = 2 * core, 2 * core + 1
        squares = parts[a, rows:].astype(jnp.float32) + parts[b, rows:].astype(jnp.float32)
        squares = jnp.sum(squares, axis=0, keepdims=True)
        factor = lax.rsqrt(squares / D + norm_eps) * (1.0 / math.sqrt(D))
        factor = jnp.transpose(jnp.broadcast_to(factor, (LANES, factor.shape[1])))
        for e in range(NYL):
            y = place ^ e
            to = pl.multiple_of(((y % 2) * 2 + core) * toks, 16)
            for lane in range(0, out.shape[2], LANES):
                at = slice(e * toks, (e + 1) * toks), slice(lane, lane + LANES)
                gate = parts[(a,) + at].astype(jnp.float32) + parts[(b,) + at].astype(jnp.float32)
                gate = gate * factor[e * toks : (e + 1) * toks]
                gate = gate / (1.0 + jnp.exp(-gate))
                out[y // 2, pl.ds(to, toks), lane : lane + LANES] = gate.astype(out.dtype)


def finish(index, parts, micro):
    _, rows, cols = parts.shape
    vmem = pl.BlockSpec(memory_space=pltpu.VMEM)
    return pl.pallas_call(
        finish_kernel,
        out_shape=jax.ShapeDtypeStruct((micro, rows - TAIL, cols), jnp.bfloat16),
        in_specs=[pl.BlockSpec(memory_space=pltpu.SMEM), vmem],
        out_specs=vmem,
        compiler_params=pltpu.CompilerParams(vmem_limit_bytes=8 * 2**20),
    )(index, parts)


def body(policy, ref_weight, tokens, gain):
    z, c, yh = lax.axis_index(Z), lax.axis_index("c"), lax.axis_index("yh")
    micro, toks, width = tokens.shape
    pieces = tokens.reshape(micro, toks, NZL, LANES).transpose(2, 0, 1, 3)
    pieces = pieces.reshape(NZL * micro, toks, LANES)
    pieces = lax.all_to_all(pieces, ("zl", "y1"), 0, 0, tiled=True)
    pieces = lax.all_to_all(pieces, "x", 0, 0, tiled=True)
    pieces, policy = lax.optimization_barrier((pieces, policy))
    arrived = lax.all_to_all(
        policy.reshape(8, 64, 256).transpose(1, 0, 2), DP, 0, 0, tiled=True
    )
    own = pieces.transpose(1, 0, 2).reshape(toks, NX * LANES)
    own = jnp.concatenate(
        [own] + [lax.ppermute(own, YL, [(i, i ^ e) for i in range(NYL)]) for e in range(1, NYL)]
    )
    rows = own.shape[0]
    own, arrived = lax.optimization_barrier((own, arrived))
    policy_slice = arrived.reshape(ref_weight.shape)
    ref_f = ref_weight.astype(jnp.float32)
    blended = (ref_f + ema_rate * (policy_slice.astype(jnp.float32) - ref_f)).astype(jnp.bfloat16)
    scaled = (blended.astype(jnp.float32) * gain[:, None]).astype(jnp.bfloat16)
    weights = spread(scaled, "x", NX)
    weights = weights.reshape(NX, NZL, LANES, weights.shape[-1])
    blocks, offsets = [own], [0]
    up = down = own
    for step in range(1, NZ // 2):
        if step == NZ // 2 - 1:
            halves = (
                lax.ppermute(up[: rows // 2], Z, shift(NZ, 2)),
                lax.ppermute(down[rows // 2 :], Z, shift(NZ, -2)),
            )
        up = lax.ppermute(up, Z, shift(NZ, 1))
        down = lax.ppermute(down, Z, shift(NZ, -1))
        blocks += [up, down]
        offsets += [-step, step]
    blocks += halves
    offsets.append(NZ // 2)
    places = (z + jnp.array(offsets, jnp.int32)) & (NZ - 1)
    index = jnp.concatenate([places // NZL, places % NZL, jnp.stack([c, lax.axis_index(YL)])])
    weights, index, *blocks[-4:] = lax.optimization_barrier((weights, index, *blocks[-4:]))
    others = lax.ppermute(weights, "c", shift(2, 1))
    parts = gate_parts(index, blocks, weights)
    parts = gate_parts(index, blocks, others, parts)
    parts = lax.all_to_all(parts.reshape(4, *parts.shape[2:]), ("c", "yh"), 0, 0, tiled=True)
    return blended, finish(index, parts, micro)


def solution(mesh):
    fine = Mesh(mesh.devices.reshape(SIZES), AXES)
    return jax.shard_map(
        body,
        mesh=fine,
        in_specs=(P(DP, TENSOR, None), P(TENSOR, DP), P(None, DP, TENSOR), P(TENSOR)),
        out_specs=(P(TENSOR, DP), P(None, TENSOR, DP)),
        check_vma=False,
    )
```

time: 174 us -> 163 us (0.937)
  blocking collectives: 33.2 us -> 50.6 us
  waiting for transfers between devices: 44.5 us -> 28.9 us
  starting transfers between devices: 72.1 us -> 60.9 us
    all_to_all x0 -> x1, blocking collectives: none -> 17.3 us  [body(): lax.all_to_all(parts.reshape(4, *parts.shape[2:]), ('c', 'yh'), 0, 0, til...]
    ppermute x3, waiting for transfers between devices: 7.41 us -> 0.01 us  [body(): down = lax.ppermute(down, Z, shift(NZ, -1))]
    ppermute x4 -> x3, starting transfers between devices: 13.3 us -> 6.11 us  [body(): up = lax.ppermute(up, Z, shift(NZ, 1))]
    ppermute x4 -> x3, waiting for transfers between devices: 19.7 us -> 12.8 us  [body(): up = lax.ppermute(up, Z, shift(NZ, 1))]
    ppermute x3 -> x2, starting transfers between devices: 13.4 us -> 7.37 us  [the longest x1 5.46 us: body(): lax.ppermute(down[rows // 2:], Z, shift(NZ, -2))]
    ppermute x3, starting transfers between devices: 9.39 us -> 13.4 us  [body(): down = lax.ppermute(down, Z, shift(NZ, -1))]
    ppermute x3 -> x2, waiting for transfers between devices: 10.5 us -> 7.61 us  [the longest x1 3.92 us: body(): lax.ppermute(up[:rows // 2], Z, shift(NZ, 2))]
    ppermute x3, waiting for transfers between devices: 5.26 us -> 7.63 us  [body(): lax.ppermute(own, YL, [(i, i ^ e) for i in range(NYL)])]
  transfers between devices with their start and end apart: 16 -> 14, of which waited for: 12 -> 7; matrix products, arithmetic and copies ran while one was open for 2% -> 1% of each run, Pallas kernels for 4% -> 4%
where the time goes in v6:
time: 163 us; the launch traced here: 161 us
  starting transfers between devices  60.9 us (37%)
  blocking collectives  50.6 us (31%)
  waiting for transfers between devices  28.9 us (18%)
  Pallas kernels  13.9 us (9%)
  local copies, waits for them, and re-layouts  3.78 us (2%)
    all_to_all x1, blocking collectives, body(): pieces = lax.all_to_all(pieces, ('zl', 'y1'), 0, 0, tiled=True)  19.5 us
    all_to_all x1, blocking collectives, body(): lax.all_to_all(parts.reshape(4, *parts.shape[2:]), ('c', 'yh'), 0, 0, til...  17.3 us
    all_to_all x1, starting transfers between devices, body(): lax.all_to_all(policy.reshape(8, 64, 256).transpose(1, 0, 2), DP, 0, 0, t...  16.6 us
    all_to_all x1, blocking collectives, body(): pieces = lax.all_to_all(pieces, 'x', 0, 0, tiled=True)  13.8 us
    ppermute x3, starting transfers between devices, body(): down = lax.ppermute(down, Z, shift(NZ, -1))  13.4 us
    ppermute x3, waiting for transfers between devices, body(): up = lax.ppermute(up, Z, shift(NZ, 1))  12.8 us
    pallas_call x2, Pallas kernels, gate_parts(): pl.pallas_call(functools.partial(gate_kernel, first), out_shape=jax.Shape...  12.5 us
    ppermute x3, starting transfers between devices, body(): lax.ppermute(own, YL, [(i, i ^ e) for i in range(NYL)])  9.27 us
  transfers between devices with their start and end apart: 14, of which 7 were waited for; matrix products, arithmetic and copies ran while one was open for 1% of the time, Pallas kernels for 4%

profile of v6, /device:TPU:1, one launch (start us, length us, event | category | flops | bytes accessed | tf_op | source)
XLA Modules:
  0.0 160.6 jit_solution(15133094298649432507)
XLA Ops:
  0.7 0.9 copy-done
  1.6 19.5 %all_to_all.25 = bf16[8,48,128]{2,1,0:T(8,128)(2,1)S(1)} all-to-all(bf16[8,48,128]{2,1,0:T(8,128)(2,1)S(1)} %bitcast.28), channel_id=1, replica_groups=mesh['zh'=2,'zl'=4,'y1'=2,'y0'=2,'c'=2,'yh'=2,'x'=8] {'zl','y1'}, dimensions={0} | all-to-all | bytes 196608 | tf_op jit(solution)/shard_map/all_to_all | solution.py:155
  21.0 13.8 %all_to_all.26 = bf16[8,48,128]{2,1,0:T(8,128)(2,1)S(1)} all-to-all(bf16[8,48,128]{2,1,0:T(8,128)(2,1)S(1)} %all_to_all.25), channel_id=1, replica_groups=mesh['zh'=2,'zl'=4,'y1'=2,'y0'=2,'c'=2,'yh'=2,'x'=8] {'x'}, dimensions={0} | all-to-all | bytes 196608 | tf_op jit(solution)/shard_map/all_to_all | solution.py:156
  34.9 16.6 %all-to-all-start.2 = ((bf16[64,8,256]{2,1,0:T(8,128)(2,1)}), bf16[64,8,256]{2,1,0:T(8,128)(2,1)S(1)}, u32[]{:S(2)}, u32[]{:S(2)}) async-start(bf16[64,8,256]{2,1,0:T(8,128)(2,1)} %bitcast.29), calls=%async_computation.2 | async-start | bytes 524288 | tf_op jit(solution)/shard_map/all_to_all | solution.py:158
  51.5 5.1 %collective-permute-start.2 = (bf16[48,1024]{1,0:T(8,128)(2,1)S(1)}, bf16[48,1024]{1,0:T(8,128)(2,1)S(1)}, u32[]{:S(2)}, u32[]{:S(2)}) collective-permute-start(bf16[48,1024]{1,0:T(8,128)(2,1)S(1)} %copy_bitcast_fusion), channel_id=1, source_target_pairs={{0,96},{32,64},{64,32},{96,0},{1,97},{33,65},{65,33},{97,1},{2,98}... | collective-permute-start | bytes 294920 | tf_op jit(solution)/shard_map/ppermute | solution.py:163
  56.6 1.9 %collective-permute-start.1 = (bf16[48,1024]{1,0:T(8,128)(2,1)S(1)}, bf16[48,1024]{1,0:T(8,128)(2,1)S(1)}, u32[]{:S(2)}, u32[]{:S(2)}) collective-permute-start(bf16[48,1024]{1,0:T(8,128)(2,1)S(1)} %copy_bitcast_fusion), channel_id=1, source_target_pairs={{0,64},{32,96},{64,0},{96,32},{1,65},{33,97},{65,1},{97,33},{2,66}... | collective-permute-start | bytes 294920 | tf_op jit(solution)/shard_map/ppermute | solution.py:163
  58.5 2.3 %collective-permute-start = (bf16[48,1024]{1,0:T(8,128)(2,1)S(1)}, bf16[48,1024]{1,0:T(8,128)(2,1)S(1)}, u32[]{:S(2)}, u32[]{:S(2)}) collective-permute-start(bf16[48,1024]{1,0:T(8,128)(2,1)S(1)} %copy_bitcast_fusion), channel_id=1, source_target_pairs={{0,32},{32,0},{64,96},{96,64},{1,33},{33,1},{65,97},{97,65},{2,34}... | collective-permute-start | bytes 294920 | tf_op jit(solution)/shard_map/ppermute | solution.py:163
  60.8 0.8 collective-permute-done.2
  61.6 6.8 %collective-permute-done.1 = bf16[48,1024]{1,0:T(8,128)(2,1)S(1)} collective-permute-done((bf16[48,1024]{1,0:T(8,128)(2,1)S(1)}, bf16[48,1024]{1,0:T(8,128)(2,1)S(1)}, u32[]{:S(2)}, u32[]{:S(2)}) %collective-permute-start.1) | collective-permute-done | bytes 98336 | tf_op jit(solution)/shard_map/ppermute | solution.py:163
  68.4 0.8 all-to-all-done.2
  69.3 0.8 multiply_convert_fusion
  70.1 1.5 broadcast_in_dim.2
  71.6 3.7 %all-to-all-start.3 = ((bf16[8,512,256]{2,1,0:T(8,128)(2,1)}), bf16[8,512,256]{2,1,0:T(8,128)(2,1)S(1)}, u32[]{:S(2)}, u32[]{:S(2)}) async-start(bf16[8,512,256]{2,1,0:T(8,128)(2,1)} %broadcast_in_dim.2), calls=%async_computation.3 | async-start | bytes 4194304 | tf_op jit(solution)/shard_map/all_to_all | solution.py:29
  75.3 2.3 %collective-permute-start.3 = (bf16[192,1024]{1,0:T(8,128)(2,1)S(1)}, bf16[192,1024]{1,0:T(8,128)(2,1)S(1)}, u32[]{:S(2)}, u32[]{:S(2)}) collective-permute-start(bf16[192,1024]{1,0:T(8,128)(2,1)S(1)} %pad_maximum_fusion.refs_0_), channel_id=1, source_target_pairs={{0,128},{128,256},{256,384},{384,512},{512,640},{640,768},{768,896... | collective-permute-start | bytes 1179656 | tf_op jit(solution)/shard_map/ppermute | solution.py:181
  77.6 4.2 %collective-permute-start.6 = (bf16[192,1024]{1,0:T(8,128)(2,1)S(1)}, bf16[192,1024]{1,0:T(8,128)(2,1)}, u32[]{:S(2)}, u32[]{:S(2)}) collective-permute-start(bf16[192,1024]{1,0:T(8,128)(2,1)S(1)} %pad_maximum_fusion.refs_0_), channel_id=1, source_target_pairs={{0,896},{128,0},{256,128},{384,256},{512,384},{640,512},{768,640},... | collective-permute-start | bytes 1179656 | tf_op jit(solution)/shard_map/ppermute | solution.py:182
  81.8 6.9 %collective-permute-done.3.refs_1_ = bf16[192,1024]{1,0:T(8,128)(2,1)S(1)} collective-permute-done((bf16[192,1024]{1,0:T(8,128)(2,1)S(1)}, bf16[192,1024]{1,0:T(8,128)(2,1)S(1)}, u32[]{:S(2)}, u32[]{:S(2)}) %collective-permute-start.3) | collective-permute-done | bytes 393248 | tf_op jit(solution)/shard_map/ppermute | solution.py:181
  88.7 1.9 %collective-permute-start.4 = (bf16[192,1024]{1,0:T(8,128)(2,1)S(1)}, bf16[192,1024]{1,0:T(8,128)(2,1)S(1)}, u32[]{:S(2)}, u32[]{:S(2)}) collective-permute-start(bf16[192,1024]{1,0:T(8,128)(2,1)S(1)} %collective-permute-done.3.refs_1_), channel_id=1, source_target_pairs={{0,128},{128,256},{256,384},{384,512},{512,640},{640,768},{768,896... | collective-permute-start | bytes 1179656 | tf_op jit(solution)/shard_map/ppermute | solution.py:181
  90.6 4.6 %collective-permute-start.7 = (bf16[192,1024]{1,0:T(8,128)(2,1)}, bf16[192,1024]{1,0:T(8,128)(2,1)S(1)}, u32[]{:S(2)}, u32[]{:S(2)}) collective-permute-start(bf16[192,1024]{1,0:T(8,128)(2,1)} %collective-permute-done.6.refs_2_), channel_id=1, source_target_pairs={{0,896},{128,0},{256,128},{384,256},{512,384},{640,512},{768,640},... | collective-permute-start | bytes 1179656 | tf_op jit(solution)/shard_map/ppermute | solution.py:182
  95.2 6.0 %collective-permute-done.4.refs_3_ = bf16[192,1024]{1,0:T(8,128)(2,1)S(1)} collective-permute-done((bf16[192,1024]{1,0:T(8,128)(2,1)S(1)}, bf16[192,1024]{1,0:T(8,128)(2,1)S(1)}, u32[]{:S(2)}, u32[]{:S(2)}) %collective-permute-start.4) | collective-permute-done | bytes 393248 | tf_op jit(solution)/shard_map/ppermute | solution.py:181
  101.2 1.9 %collective-permute-start.5 = (bf16[192,1024]{1,0:T(8,128)(2,1)S(1)}, bf16[192,1024]{1,0:T(8,128)(2,1)}, u32[]{:S(2)}, u32[]{:S(2)}) collective-permute-start(bf16[192,1024]{1,0:T(8,128)(2,1)S(1)} %collective-permute-done.4.refs_3_), channel_id=1, source_target_pairs={{0,128},{128,256},{256,384},{384,512},{512,640},{640,768},{768,896... | collective-permute-start | bytes 1179656 | tf_op jit(solution)/shard_map/ppermute | solution.py:181
  103.1 4.6 %collective-permute-start.8 = (bf16[192,1024]{1,0:T(8,128)(2,1)S(1)}, bf16[192,1024]{1,0:T(8,128)(2,1)}, u32[]{:S(2)}, u32[]{:S(2)}) collective-permute-start(bf16[192,1024]{1,0:T(8,128)(2,1)S(1)} %collective-permute-done.7.refs_4_), channel_id=1, source_target_pairs={{0,896},{128,0},{256,128},{384,256},{512,384},{640,512},{768,640},... | collective-permute-start | bytes 1179656 | tf_op jit(solution)/shard_map/ppermute | solution.py:182
  107.7 0.7 slice.8
  108.4 1.9 %collective-permute-start.9 = (bf16[96,1024]{1,0:T(8,128)(2,1)}, bf16[96,1024]{1,0:T(8,128)(2,1)}, u32[]{:S(2)}, u32[]{:S(2)}) collective-permute-start(bf16[96,1024]{1,0:T(8,128)(2,1)} %slice.8), channel_id=1, source_target_pairs={{0,256},{128,384},{256,512},{384,640},{512,768},{640,896},{768,0},... | collective-permute-start | bytes 589832 | tf_op jit(solution)/shard_map/ppermute | solution.py:178
  110.3 0.7 slice.9
  111.0 5.5 %collective-permute-start.10 = (bf16[96,1024]{1,0:T(8,128)(2,1)}, bf16[96,1024]{1,0:T(8,128)(2,1)}, u32[]{:S(2)}, u32[]{:S(2)}) collective-permute-start(bf16[96,1024]{1,0:T(8,128)(2,1)} %slice.9), channel_id=1, source_target_pairs={{0,768},{128,896},{256,0},{384,128},{512,256},{640,384},{768,512},... | collective-permute-start | bytes 589832 | tf_op jit(solution)/shard_map/ppermute | solution.py:179
  117.2 3.9 %collective-permute-done.9.refs_7_ = bf16[96,1024]{1,0:T(8,128)(2,1)} collective-permute-done((bf16[96,1024]{1,0:T(8,128)(2,1)}, bf16[96,1024]{1,0:T(8,128)(2,1)}, u32[]{:S(2)}, u32[]{:S(2)}) %collective-permute-start.9) | collective-permute-done | bytes 196640 | tf_op jit(solution)/shard_map/ppermute | solution.py:178
  121.1 3.7 %collective-permute-done.10.refs_8_ = bf16[96,1024]{1,0:T(8,128)(2,1)} collective-permute-done((bf16[96,1024]{1,0:T(8,128)(2,1)}, bf16[96,1024]{1,0:T(8,128)(2,1)}, u32[]{:S(2)}, u32[]{:S(2)}) %collective-permute-start.10) | collective-permute-done | bytes 196640 | tf_op jit(solution)/shard_map/ppermute | solution.py:179
  124.8 4.5 %collective-permute-start.11 = (bf16[8,4,128,256]{3,2,1,0:T(8,128)(2,1)S(1)}, bf16[8,4,128,256]{3,2,1,0:T(8,128)(2,1)}, u32[]{:S(2)}, u32[]{:S(2)}) collective-permute-start(bf16[8,4,128,256]{3,2,1,0:T(8,128)(2,1)S(1)} %bitcast.25), channel_id=1, source_target_pairs={{0,16},{16,0},{1,17},{17,1},{2,18},{18,2},{3,19},{19,3},{4,20},{20... | collective-permute-start | bytes 6291464 | tf_op jit(solution)/shard_map/ppermute | solution.py:190
  129.4 6.4 %shard_map.68.refs_10_ = bf16[2,208,256]{2,1,0:T(8,128)(2,1)} custom-call(s32[18]{0:T(128)} %pad_add_fusion.index, bf16[192,1024]{1,0:T(8,128)(2,1)} %copy-done.3, bf16[192,1024]{1,0:T(8,128)(2,1)} %copy-done.6, bf16[192,1024]{1,0:T(8,128)(2,1)} %collective-permute-done.6.refs_2_, bf16[192,1024]{1,0:T(8,128)(2,1)} %copy-done.4, bf16[192,1024]{1,0:T(8,128)(2,1)} %copy-done.5, ...), custom_call_target="tpu_custom_call" | custom-call | flops 805306368 | bytes 7340032 | tf_op jit(solution)/shard_map/pallas_call | solution.py:95
  135.8 6.1 %shard_map.69 = bf16[2,2,208,256]{3,2,1,0:T(8,128)(2,1)} custom-call(s32[18]{0:T(128)} %pad_add_fusion.index, bf16[192,1024]{1,0:T(8,128)(2,1)} %copy-done.3, bf16[192,1024]{1,0:T(8,128)(2,1)} %copy-done.6, bf16[192,1024]{1,0:T(8,128)(2,1)} %collective-permute-done.6.refs_2_, bf16[192,1024]{1,0:T(8,128)(2,1)} %copy-done.4, bf16[192,1024]{1,0:T(8,128)(2,1)} %copy-done.5, ...), custom_call_target="tpu_custom_call" | custom-call | flops 805306368 | bytes 7340032 | tf_op jit(solution)/shard_map/pallas_call | solution.py:95
  141.9 17.3 %all_to_all.27.parts = bf16[4,208,256]{2,1,0:T(8,128)(2,1)S(1)} all-to-all(bf16[4,208,256]{2,1,0:T(8,128)(2,1)} %bitcast.27), channel_id=1, replica_groups=mesh['zh'=2,'zl'=4,'y1'=2,'y0'=2,'c'=2,'yh'=2,'x'=8] {'c','yh'}, dimensions={0} | all-to-all | bytes 851968 | tf_op jit(solution)/shard_map/all_to_all | solution.py:193
  159.2 1.4 shard_map.70
  (32 shorter events, 0.8 us)
Async XLA Ops:
  0.6 0.9 copy-start
  0.6 68.6 %copy-start.8 = (f32[512]{0:T(512)S(1)}, f32[512]{0:T(512)}, u32[]{:S(2)}) copy-start(f32[512]{0:T(512)} %param.8) | copy-start | bytes 6148
  1.5 67.7 %copy-start.7 = (bf16[512,256]{1,0:T(8,128)(2,1)S(1)}, bf16[512,256]{1,0:T(8,128)(2,1)}, u32[]{:S(2)}) copy-start(bf16[512,256]{1,0:T(8,128)(2,1)} %param.6) | copy-start | bytes 786436
  34.9 34.4 %all-to-all-start.2 = ((bf16[64,8,256]{2,1,0:T(8,128)(2,1)}), bf16[64,8,256]{2,1,0:T(8,128)(2,1)S(1)}, u32[]{:S(2)}, u32[]{:S(2)}) async-start(bf16[64,8,256]{2,1,0:T(8,128)(2,1)} %bitcast.29), calls=%async_computation.2 | async-start | bytes 524288 | tf_op jit(solution)/shard_map/all_to_all | solution.py:158
  51.5 10.1 %collective-permute-start.2 = (bf16[48,1024]{1,0:T(8,128)(2,1)S(1)}, bf16[48,1024]{1,0:T(8,128)(2,1)S(1)}, u32[]{:S(2)}, u32[]{:S(2)}) collective-permute-start(bf16[48,1024]{1,0:T(8,128)(2,1)S(1)} %copy_bitcast_fusion), channel_id=1, source_target_pairs={{0,96},{32,64},{64,32},{96,0},{1,97},{33,65},{65,33},{97,1},{2,98}... | collective-permute-start | bytes 294920 | tf_op jit(solution)/shard_map/ppermute | solution.py:163
  56.6 11.8 %collective-permute-start.1 = (bf16[48,1024]{1,0:T(8,128)(2,1)S(1)}, bf16[48,1024]{1,0:T(8,128)(2,1)S(1)}, u32[]{:S(2)}, u32[]{:S(2)}) collective-permute-start(bf16[48,1024]{1,0:T(8,128)(2,1)S(1)} %copy_bitcast_fusion), channel_id=1, source_target_pairs={{0,64},{32,96},{64,0},{96,32},{1,65},{33,97},{65,1},{97,33},{2,66}... | collective-permute-start | bytes 294920 | tf_op jit(solution)/shard_map/ppermute | solution.py:163
  58.5 9.9 %collective-permute-start = (bf16[48,1024]{1,0:T(8,128)(2,1)S(1)}, bf16[48,1024]{1,0:T(8,128)(2,1)S(1)}, u32[]{:S(2)}, u32[]{:S(2)}) collective-permute-start(bf16[48,1024]{1,0:T(8,128)(2,1)S(1)} %copy_bitcast_fusion), channel_id=1, source_target_pairs={{0,32},{32,0},{64,96},{96,64},{1,33},{33,1},{65,97},{97,65},{2,34}... | collective-permute-start | bytes 294920 | tf_op jit(solution)/shard_map/ppermute | solution.py:163
  68.4 9.2 %copy-start.3 = (bf16[192,1024]{1,0:T(8,128)(2,1)}, bf16[192,1024]{1,0:T(8,128)(2,1)S(1)}, u32[]{:S(2)}) copy-start(bf16[192,1024]{1,0:T(8,128)(2,1)S(1)} %pad_maximum_fusion.refs_0_) | copy-start | bytes 1179652
  71.6 36.1 %copy-start.9 = (s32[8]{0:T(128)S(1)}, s32[8]{0:T(128)}, u32[]{:S(2)}) copy-start(s32[8]{0:T(128)} %constant.59.clone) | copy-start | bytes 100
  71.6 53.2 %all-to-all-start.3 = ((bf16[8,512,256]{2,1,0:T(8,128)(2,1)}), bf16[8,512,256]{2,1,0:T(8,128)(2,1)S(1)}, u32[]{:S(2)}, u32[]{:S(2)}) async-start(bf16[8,512,256]{2,1,0:T(8,128)(2,1)} %broadcast_in_dim.2), calls=%async_computation.3 | async-start | bytes 4194304 | tf_op jit(solution)/shard_map/all_to_all | solution.py:29
  75.3 13.4 %collective-permute-start.3 = (bf16[192,1024]{1,0:T(8,128)(2,1)S(1)}, bf16[192,1024]{1,0:T(8,128)(2,1)S(1)}, u32[]{:S(2)}, u32[]{:S(2)}) collective-permute-start(bf16[192,1024]{1,0:T(8,128)(2,1)S(1)} %pad_maximum_fusion.refs_0_), channel_id=1, source_target_pairs={{0,128},{128,256},{256,384},{384,512},{512,640},{640,768},{768,896... | collective-permute-start | bytes 1179656 | tf_op jit(solution)/shard_map/ppermute | solution.py:181
  77.6 13.0 %collective-permute-start.6 = (bf16[192,1024]{1,0:T(8,128)(2,1)S(1)}, bf16[192,1024]{1,0:T(8,128)(2,1)}, u32[]{:S(2)}, u32[]{:S(2)}) collective-permute-start(bf16[192,1024]{1,0:T(8,128)(2,1)S(1)} %pad_maximum_fusion.refs_0_), channel_id=1, source_target_pairs={{0,896},{128,0},{256,128},{384,256},{512,384},{640,512},{768,640},... | collective-permute-start | bytes 1179656 | tf_op jit(solution)/shard_map/ppermute | solution.py:182
  88.7 40.6 %copy-start.6 = (bf16[192,1024]{1,0:T(8,128)(2,1)}, bf16[192,1024]{1,0:T(8,128)(2,1)S(1)}, u32[]{:S(2)}) copy-start(bf16[192,1024]{1,0:T(8,128)(2,1)S(1)} %collective-permute-done.3.refs_1_) | copy-start | bytes 1179652
  88.7 12.5 %collective-permute-start.4 = (bf16[192,1024]{1,0:T(8,128)(2,1)S(1)}, bf16[192,1024]{1,0:T(8,128)(2,1)S(1)}, u32[]{:S(2)}, u32[]{:S(2)}) collective-permute-start(bf16[192,1024]{1,0:T(8,128)(2,1)S(1)} %collective-permute-done.3.refs_1_), channel_id=1, source_target_pairs={{0,128},{128,256},{256,384},{384,512},{512,640},{640,768},{768,896... | collective-permute-start | bytes 1179656 | tf_op jit(solution)/shard_map/ppermute | solution.py:181
  90.6 12.5 %collective-permute-start.7 = (bf16[192,1024]{1,0:T(8,128)(2,1)}, bf16[192,1024]{1,0:T(8,128)(2,1)S(1)}, u32[]{:S(2)}, u32[]{:S(2)}) collective-permute-start(bf16[192,1024]{1,0:T(8,128)(2,1)} %collective-permute-done.6.refs_2_), channel_id=1, source_target_pairs={{0,896},{128,0},{256,128},{384,256},{512,384},{640,512},{768,640},... | collective-permute-start | bytes 1179656 | tf_op jit(solution)/shard_map/ppermute | solution.py:182
  101.2 28.2 %copy-start.4 = (bf16[192,1024]{1,0:T(8,128)(2,1)}, bf16[192,1024]{1,0:T(8,128)(2,1)S(1)}, u32[]{:S(2)}) copy-start(bf16[192,1024]{1,0:T(8,128)(2,1)S(1)} %collective-permute-done.4.refs_3_) | copy-start | bytes 1179652
  101.2 23.6 %collective-permute-start.5 = (bf16[192,1024]{1,0:T(8,128)(2,1)S(1)}, bf16[192,1024]{1,0:T(8,128)(2,1)}, u32[]{:S(2)}, u32[]{:S(2)}) collective-permute-start(bf16[192,1024]{1,0:T(8,128)(2,1)S(1)} %collective-permute-done.4.refs_3_), channel_id=1, source_target_pairs={{0,128},{128,256},{256,384},{384,512},{512,640},{640,768},{768,896... | collective-permute-start | bytes 1179656 | tf_op jit(solution)/shard_map/ppermute | solution.py:181
  103.1 26.2 %copy-start.5 = (bf16[192,1024]{1,0:T(8,128)(2,1)}, bf16[192,1024]{1,0:T(8,128)(2,1)S(1)}, u32[]{:S(2)}) copy-start(bf16[192,1024]{1,0:T(8,128)(2,1)S(1)} %collective-permute-done.7.refs_4_) | copy-start | bytes 1179652
  103.1 21.7 %collective-permute-start.8 = (bf16[192,1024]{1,0:T(8,128)(2,1)S(1)}, bf16[192,1024]{1,0:T(8,128)(2,1)}, u32[]{:S(2)}, u32[]{:S(2)}) collective-permute-start(bf16[192,1024]{1,0:T(8,128)(2,1)S(1)} %collective-permute-done.7.refs_4_), channel_id=1, source_target_pairs={{0,896},{128,0},{256,128},{384,256},{512,384},{640,512},{768,640},... | collective-permute-start | bytes 1179656 | tf_op jit(solution)/shard_map/ppermute | solution.py:182
  108.4 12.7 %collective-permute-start.9 = (bf16[96,1024]{1,0:T(8,128)(2,1)}, bf16[96,1024]{1,0:T(8,128)(2,1)}, u32[]{:S(2)}, u32[]{:S(2)}) collective-permute-start(bf16[96,1024]{1,0:T(8,128)(2,1)} %slice.8), channel_id=1, source_target_pairs={{0,256},{128,384},{256,512},{384,640},{512,768},{640,896},{768,0},... | collective-permute-start | bytes 589832 | tf_op jit(solution)/shard_map/ppermute | solution.py:178
  111.0 13.8 %collective-permute-start.10 = (bf16[96,1024]{1,0:T(8,128)(2,1)}, bf16[96,1024]{1,0:T(8,128)(2,1)}, u32[]{:S(2)}, u32[]{:S(2)}) collective-permute-start(bf16[96,1024]{1,0:T(8,128)(2,1)} %slice.9), channel_id=1, source_target_pairs={{0,768},{128,896},{256,0},{384,128},{512,256},{640,384},{768,512},... | collective-permute-start | bytes 589832 | tf_op jit(solution)/shard_map/ppermute | solution.py:179
  124.8 4.6 %copy-start.2 = (bf16[8,512,256]{2,1,0:T(8,128)(2,1)}, bf16[8,512,256]{2,1,0:T(8,128)(2,1)S(1)}, u32[]{:S(2)}) copy-start(bf16[8,512,256]{2,1,0:T(8,128)(2,1)S(1)} %all-to-all-done.3) | copy-start | bytes 6291460
  124.8 10.9 %collective-permute-start.11 = (bf16[8,4,128,256]{3,2,1,0:T(8,128)(2,1)S(1)}, bf16[8,4,128,256]{3,2,1,0:T(8,128)(2,1)}, u32[]{:S(2)}, u32[]{:S(2)}) collective-permute-start(bf16[8,4,128,256]{3,2,1,0:T(8,128)(2,1)S(1)} %bitcast.25), channel_id=1, source_target_pairs={{0,16},{16,0},{1,17},{17,1},{2,18},{18,2},{3,19},{19,3},{4,20},{20... | collective-permute-start | bytes 6291464 | tf_op jit(solution)/shard_map/ppermute | solution.py:190
  135.7 23.4 %copy-start.1 = (s32[18]{0:T(128)S(1)}, s32[18]{0:T(128)}, u32[]{:S(2)}) copy-start(s32[18]{0:T(128)} %pad_add_fusion.index) | copy-start | bytes 220

commit v7 on v6

--- a/solution.py
+++ b/solution.py
@@ -37,8 +37,9 @@
         before, out, a_buf, b_buf, acc, a_sem, b_sem = refs
     groups, _, rows, depth = a_buf.shape
     cols = b_buf.shape[-1]
+    x = index[2 * NZ + 2]
     b_copies = [
-        pltpu.make_async_copy(weights.at[:, q], b_buf.at[q], b_sem.at[q]) for q in range(NZL)
+        pltpu.make_async_copy(weights.at[x ^ e], b_buf.at[:, e], b_sem.at[e]) for e in range(NX)
     ]
     places = [a_buf.at[index[s], index[NZ + s]] for s in range(NZ)]
     places[-1:] = [places[-1].at[: rows // 2], places[-1].at[rows // 2 :]]
@@ -49,10 +50,9 @@
         copy.start()
     if first:
         sums[...] = jnp.zeros_like(sums)
-    for copy in a_copies:
+    for copy in a_copies + b_copies:
         copy.wait()
     for q in range(NZL):
-        b_copies[q].wait()
         left = a_buf[:, q].reshape(groups * rows, depth)
         part = jnp.dot(left, b_buf[q].reshape(depth, cols), preferred_element_type=jnp.float32)
         part = part.reshape(groups, rows, cols)
@@ -104,7 +104,7 @@
             pltpu.VMEM((NZL, NX, LANES, cols), jnp.bfloat16),
         ]
         + (totals if first else totals[:1])
-        + [pltpu.SemaphoreType.DMA((len(blocks),)), pltpu.SemaphoreType.DMA((NZL,))],
+        + [pltpu.SemaphoreType.DMA((len(blocks),)), pltpu.SemaphoreType.DMA((NX,))],
         compiler_params=pltpu.CompilerParams(vmem_limit_bytes=60 * 2**20),
         cost_estimate=pl.CostEstimate(
             flops=2 * NZ * rows * depth * cols,
@@ -148,22 +148,25 @@
 
 
 def body(policy, ref_weight, tokens, gain):
-    z, c, yh = lax.axis_index(Z), lax.axis_index("c"), lax.axis_index("yh")
+    z, c, x = lax.axis_index(Z), lax.axis_index("c"), lax.axis_index("x")
     micro, toks, width = tokens.shape
     pieces = tokens.reshape(micro, toks, NZL, LANES).transpose(2, 0, 1, 3)
     pieces = pieces.reshape(NZL * micro, toks, LANES)
     pieces = lax.all_to_all(pieces, ("zl", "y1"), 0, 0, tiled=True)
-    pieces = lax.all_to_all(pieces, "x", 0, 0, tiled=True)
     pieces, policy = lax.optimization_barrier((pieces, policy))
     arrived = lax.all_to_all(
         policy.reshape(8, 64, 256).transpose(1, 0, 2), DP, 0, 0, tiled=True
     )
-    own = pieces.transpose(1, 0, 2).reshape(toks, NX * LANES)
+    own = []
+    for e in range(NX):
+        piece = lax.dynamic_index_in_dim(pieces, x ^ e, 0, keepdims=False)
+        own.append(lax.ppermute(piece, "x", [(i, i ^ e) for i in range(NX)]) if e else piece)
+    own = jnp.concatenate(own, axis=1)
+    own, arrived = lax.optimization_barrier((own, arrived))
     own = jnp.concatenate(
         [own] + [lax.ppermute(own, YL, [(i, i ^ e) for i in range(NYL)]) for e in range(1, NYL)]
     )
     rows = own.shape[0]
-    own, arrived = lax.optimization_barrier((own, arrived))
     policy_slice = arrived.reshape(ref_weight.shape)
     ref_f = ref_weight.astype(jnp.float32)
     blended = (ref_f + ema_rate * (policy_slice.astype(jnp.float32) - ref_f)).astype(jnp.bfloat16)
@@ -185,7 +188,7 @@
     blocks += halves
     offsets.append(NZ // 2)
     places = (z + jnp.array(offsets, jnp.int32)) & (NZ - 1)
-    index = jnp.concatenate([places // NZL, places % NZL, jnp.stack([c, lax.axis_index(YL)])])
+    index = jnp.concatenate([places // NZL, places % NZL, jnp.stack([c, lax.axis_index(YL), x])])
     weights, index, *blocks[-4:] = lax.optimization_barrier((weights, index, *blocks[-4:]))
     others = lax.ppermute(weights, "c", shift(2, 1))
     parts = gate_parts(index, blocks, weights)

time: 163 us -> 176 us (1.080)
  starting transfers between devices: 60.9 us -> 102 us
  blocking collectives: 50.6 us -> 20.6 us
  waiting for transfers between devices: 28.9 us -> 31.7 us
  Pallas kernels: 13.9 us -> 12.1 us
    all_to_all x2 -> x0, blocking collectives: 33.3 us -> none  [the longest x1 19.5 us: body(): pieces = lax.all_to_all(pieces, ('zl', 'y1'), 0, 0, tiled=True)]
    ppermute x0 -> x7, starting transfers between devices: none -> 25.2 us  [body(): lax.ppermute(piece, 'x', [(i, i ^ e) for i in range(NX)])]
    all_to_all x0 -> x1, starting transfers between devices: none -> 12.8 us  [body(): pieces = lax.all_to_all(pieces, ('zl', 'y1'), 0, 0, tiled=True)]
    all_to_all x0 -> x1, waiting for transfers between devices: none -> 6.74 us  [body(): pieces = lax.all_to_all(pieces, ('zl', 'y1'), 0, 0, tiled=True)]
    ppermute x3, waiting for transfers between devices: 12.8 us -> 7.89 us  [body(): up = lax.ppermute(up, Z, shift(NZ, 1))]
    ppermute x3, waiting for transfers between devices: 7.63 us -> 3.01 us  [body(): lax.ppermute(own, YL, [(i, i ^ e) for i in range(NYL)])]
    ppermute x0 -> x7, waiting for transfers between devices: none -> 3.85 us  [body(): lax.ppermute(piece, 'x', [(i, i ^ e) for i in range(NX)])]
    all_to_all x1, blocking collectives: 17.3 us -> 20.6 us  [body(): lax.all_to_all(parts.reshape(4, *parts.shape[2:]), ('c', 'yh'), 0, 0, til...]
  transfers between devices with their start and end apart: 14 -> 22, of which waited for: 7 -> 8; matrix products, arithmetic and copies ran while one was open for 1% -> 1% of each run, Pallas kernels for 4% -> 3%
where the time goes in v7:
time: 176 us; the launch traced here: 175 us
  starting transfers between devices  102 us (58%)
  waiting for transfers between devices  31.7 us (18%)
  blocking collectives  20.6 us (12%)
  Pallas kernels  12.1 us (7%)
  local copies, waits for them, and re-layouts  5.26 us (3%)
  other arithmetic  1.81 us (1%)
    ppermute x7, starting transfers between devices, body(): lax.ppermute(piece, 'x', [(i, i ^ e) for i in range(NX)])  25.2 us
    all_to_all x1, blocking collectives, body(): lax.all_to_all(parts.reshape(4, *parts.shape[2:]), ('c', 'yh'), 0, 0, til...  20.6 us
    all_to_all x1, starting transfers between devices, body(): lax.all_to_all(policy.reshape(8, 64, 256).transpose(1, 0, 2), DP, 0, 0, t...  16.3 us
    all_to_all x1, starting transfers between devices, body(): pieces = lax.all_to_all(pieces, ('zl', 'y1'), 0, 0, tiled=True)  12.8 us
    ppermute x3, starting transfers between devices, body(): down = lax.ppermute(down, Z, shift(NZ, -1))  12.4 us
    pallas_call x2, Pallas kernels, gate_parts(): pl.pallas_call(functools.partial(gate_kernel, first), out_shape=jax.Shape...  10.7 us
    ppermute x3, starting transfers between devices, body(): lax.ppermute(own, YL, [(i, i ^ e) for i in range(NYL)])  9.26 us
    ppermute x3, waiting for transfers between devices, body(): up = lax.ppermute(up, Z, shift(NZ, 1))  7.89 us
  transfers between devices with their start and end apart: 22, of which 8 were waited for; matrix products, arithmetic and copies ran while one was open for 1% of the time, Pallas kernels for 3%

profile of v7, /device:TPU:1, one launch (start us, length us, event | category | flops | bytes accessed | tf_op | source)
XLA Modules:
  0.0 174.8 jit_solution(17588163043158100704)
XLA Ops:
  2.2 12.8 %all-to-all-start = ((bf16[8,48,128]{2,1,0:T(8,128)(2,1)}), bf16[8,48,128]{2,1,0:T(8,128)(2,1)S(1)}, u32[]{:S(2)}, u32[]{:S(2)}) async-start(bf16[8,48,128]{2,1,0:T(8,128)(2,1)} %bitcast.1), calls=%async_computation | async-start | bytes 196608 | tf_op jit(solution)/shard_map/all_to_all | solution.py:155
  15.0 6.7 %all-to-all-done = bf16[8,48,128]{2,1,0:T(8,128)(2,1)S(1)} async-done(((bf16[8,48,128]{2,1,0:T(8,128)(2,1)}), bf16[8,48,128]{2,1,0:T(8,128)(2,1)S(1)}, u32[]{:S(2)}, u32[]{:S(2)}) %all-to-all-start) | async-done | bytes 98336 | tf_op jit(solution)/shard_map/all_to_all | solution.py:155
  21.8 3.1 %collective-permute-start = (bf16[48,128]{1,0:T(8,128)(2,1)S(1)}, bf16[48,128]{1,0:T(8,128)(2,1)S(1)}, u32[]{:S(2)}, u32[]{:S(2)}) collective-permute-start(bf16[48,128]{1,0:T(8,128)(2,1)S(1)} %get-tuple-element.32), channel_id=1, source_target_pairs={{0,1},{1,0},{2,3},{3,2},{4,5},{5,4},{6,7},{7,6},{8,9},{9,8},{10,11... | collective-permute-start | bytes 36872 | tf_op jit(solution)/shard_map/ppermute | solution.py:163
  24.9 4.0 %collective-permute-start.1 = (bf16[48,128]{1,0:T(8,128)(2,1)S(1)}, bf16[48,128]{1,0:T(8,128)(2,1)S(1)}, u32[]{:S(2)}, u32[]{:S(2)}) collective-permute-start(bf16[48,128]{1,0:T(8,128)(2,1)S(1)} %get-tuple-element.31), channel_id=1, source_target_pairs={{0,2},{1,3},{2,0},{3,1},{4,6},{5,7},{6,4},{7,5},{8,10},{9,11},{10,... | collective-permute-start | bytes 36872 | tf_op jit(solution)/shard_map/ppermute | solution.py:163
  29.0 2.1 %collective-permute-start.2 = (bf16[48,128]{1,0:T(8,128)(2,1)S(1)}, bf16[48,128]{1,0:T(8,128)(2,1)S(1)}, u32[]{:S(2)}, u32[]{:S(2)}) collective-permute-start(bf16[48,128]{1,0:T(8,128)(2,1)S(1)} %get-tuple-element.30), channel_id=1, source_target_pairs={{0,3},{1,2},{2,1},{3,0},{4,7},{5,6},{6,5},{7,4},{8,11},{9,10},{10,... | collective-permute-start | bytes 36872 | tf_op jit(solution)/shard_map/ppermute | solution.py:163
  31.1 7.1 %collective-permute-start.3 = (bf16[48,128]{1,0:T(8,128)(2,1)S(1)}, bf16[48,128]{1,0:T(8,128)(2,1)S(1)}, u32[]{:S(2)}, u32[]{:S(2)}) collective-permute-start(bf16[48,128]{1,0:T(8,128)(2,1)S(1)} %get-tuple-element.29), channel_id=1, source_target_pairs={{0,4},{1,5},{2,6},{3,7},{4,0},{5,1},{6,2},{7,3},{8,12},{9,13},{10,... | collective-permute-start | bytes 36872 | tf_op jit(solution)/shard_map/ppermute | solution.py:163
  38.2 1.9 %collective-permute-start.4 = (bf16[48,128]{1,0:T(8,128)(2,1)S(1)}, bf16[48,128]{1,0:T(8,128)(2,1)S(1)}, u32[]{:S(2)}, u32[]{:S(2)}) collective-permute-start(bf16[48,128]{1,0:T(8,128)(2,1)S(1)} %get-tuple-element.28), channel_id=1, source_target_pairs={{0,5},{1,4},{2,7},{3,6},{4,1},{5,0},{6,3},{7,2},{8,13},{9,12},{10,... | collective-permute-start | bytes 36872 | tf_op jit(solution)/shard_map/ppermute | solution.py:163
  40.1 16.3 %all-to-all-start.1 = ((bf16[64,8,256]{2,1,0:T(8,128)(2,1)}), bf16[64,8,256]{2,1,0:T(8,128)(2,1)S(1)}, u32[]{:S(2)}, u32[]{:S(2)}) async-start(bf16[64,8,256]{2,1,0:T(8,128)(2,1)} %bitcast.34), calls=%async_computation.1 | async-start | bytes 524288 | tf_op jit(solution)/shard_map/all_to_all | solution.py:157
  56.4 4.9 %collective-permute-start.5 = (bf16[48,128]{1,0:T(8,128)(2,1)S(1)}, bf16[48,128]{1,0:T(8,128)(2,1)S(1)}, u32[]{:S(2)}, u32[]{:S(2)}) collective-permute-start(bf16[48,128]{1,0:T(8,128)(2,1)S(1)} %get-tuple-element.27), channel_id=1, source_target_pairs={{0,6},{1,7},{2,4},{3,5},{4,2},{5,3},{6,0},{7,1},{8,14},{9,15},{10,... | collective-permute-start | bytes 36872 | tf_op jit(solution)/shard_map/ppermute | solution.py:163
  61.4 2.0 %collective-permute-start.6 = (bf16[48,128]{1,0:T(8,128)(2,1)S(1)}, bf16[48,128]{1,0:T(8,128)(2,1)S(1)}, u32[]{:S(2)}, u32[]{:S(2)}) collective-permute-start(bf16[48,128]{1,0:T(8,128)(2,1)S(1)} %get-tuple-element.26), channel_id=1, source_target_pairs={{0,7},{1,6},{2,5},{3,4},{4,3},{5,2},{6,1},{7,0},{8,15},{9,14},{10,... | collective-permute-start | bytes 36872 | tf_op jit(solution)/shard_map/ppermute | solution.py:163
  63.5 3.8 %collective-permute-done.6 = bf16[48,128]{1,0:T(8,128)(2,1)S(1)} collective-permute-done((bf16[48,128]{1,0:T(8,128)(2,1)S(1)}, bf16[48,128]{1,0:T(8,128)(2,1)S(1)}, u32[]{:S(2)}, u32[]{:S(2)}) %collective-permute-start.6) | collective-permute-done | bytes 12320 | tf_op jit(solution)/shard_map/ppermute | solution.py:163
  67.3 2.6 %all-to-all-done.1 = bf16[64,8,256]{2,1,0:T(8,128)(2,1)S(1)} async-done(((bf16[64,8,256]{2,1,0:T(8,128)(2,1)}), bf16[64,8,256]{2,1,0:T(8,128)(2,1)S(1)}, u32[]{:S(2)}, u32[]{:S(2)}) %all-to-all-start.1) | async-done | bytes 262176 | tf_op jit(solution)/shard_map/all_to_all | solution.py:157
  73.2 6.2 %all-to-all-start.2 = ((bf16[8,512,256]{2,1,0:T(8,128)(2,1)}), bf16[8,512,256]{2,1,0:T(8,128)(2,1)S(1)}, u32[]{:S(2)}, u32[]{:S(2)}) async-start(bf16[8,512,256]{2,1,0:T(8,128)(2,1)} %broadcast_in_dim.2), calls=%async_computation.2 | async-start | bytes 4194304 | tf_op jit(solution)/shard_map/all_to_all | solution.py:29
  79.4 2.4 %collective-permute-start.7 = (bf16[48,1024]{1,0:T(8,128)(2,1)S(1)}, bf16[48,1024]{1,0:T(8,128)(2,1)S(1)}, u32[]{:S(2)}, u32[]{:S(2)}) collective-permute-start(bf16[48,1024]{1,0:T(8,128)(2,1)S(1)} %constant_dynamic-update-slice_fusion), channel_id=1, source_target_pairs={{0,32},{32,0},{64,96},{96,64},{1,33},{33,1},{65,97},{97,65},{2,34}... | collective-permute-start | bytes 294920 | tf_op jit(solution)/shard_map/ppermute | solution.py:167
  81.8 2.4 %collective-permute-start.8 = (bf16[48,1024]{1,0:T(8,128)(2,1)S(1)}, bf16[48,1024]{1,0:T(8,128)(2,1)S(1)}, u32[]{:S(2)}, u32[]{:S(2)}) collective-permute-start(bf16[48,1024]{1,0:T(8,128)(2,1)S(1)} %constant_dynamic-update-slice_fusion), channel_id=1, source_target_pairs={{0,64},{32,96},{64,0},{96,32},{1,65},{33,97},{65,1},{97,33},{2,66}... | collective-permute-start | bytes 294920 | tf_op jit(solution)/shard_map/ppermute | solution.py:167
  84.1 4.5 %collective-permute-start.9 = (bf16[48,1024]{1,0:T(8,128)(2,1)S(1)}, bf16[48,1024]{1,0:T(8,128)(2,1)S(1)}, u32[]{:S(2)}, u32[]{:S(2)}) collective-permute-start(bf16[48,1024]{1,0:T(8,128)(2,1)S(1)} %constant_dynamic-update-slice_fusion), channel_id=1, source_target_pairs={{0,96},{32,64},{64,32},{96,0},{1,97},{33,65},{65,33},{97,1},{2,98}... | collective-permute-start | bytes 294920 | tf_op jit(solution)/shard_map/ppermute | solution.py:167
  88.7 3.0 %collective-permute-done.8 = bf16[48,1024]{1,0:T(8,128)(2,1)S(1)} collective-permute-done((bf16[48,1024]{1,0:T(8,128)(2,1)S(1)}, bf16[48,1024]{1,0:T(8,128)(2,1)S(1)}, u32[]{:S(2)}, u32[]{:S(2)}) %collective-permute-start.8) | collective-permute-done | bytes 98336 | tf_op jit(solution)/shard_map/ppermute | solution.py:167
  91.7 2.9 %collective-permute-start.10 = (bf16[192,1024]{1,0:T(8,128)(2,1)S(1)}, bf16[192,1024]{1,0:T(8,128)(2,1)}, u32[]{:S(2)}, u32[]{:S(2)}) collective-permute-start(bf16[192,1024]{1,0:T(8,128)(2,1)S(1)} %constant_dynamic-update-slice_fusion.8.refs_0_), channel_id=1, source_target_pairs={{0,128},{128,256},{256,384},{384,512},{512,640},{640,768},{768,896... | collective-permute-start | bytes 1179656 | tf_op jit(solution)/shard_map/ppermute | solution.py:184
  94.6 3.6 %collective-permute-start.13 = (bf16[192,1024]{1,0:T(8,128)(2,1)S(1)}, bf16[192,1024]{1,0:T(8,128)(2,1)}, u32[]{:S(2)}, u32[]{:S(2)}) collective-permute-start(bf16[192,1024]{1,0:T(8,128)(2,1)S(1)} %constant_dynamic-update-slice_fusion.8.refs_0_), channel_id=1, source_target_pairs={{0,896},{128,0},{256,128},{384,256},{512,384},{640,512},{768,640},... | collective-permute-start | bytes 1179656 | tf_op jit(solution)/shard_map/ppermute | solution.py:185
  98.2 4.2 %collective-permute-done.10.refs_1_ = bf16[192,1024]{1,0:T(8,128)(2,1)} collective-permute-done((bf16[192,1024]{1,0:T(8,128)(2,1)S(1)}, bf16[192,1024]{1,0:T(8,128)(2,1)}, u32[]{:S(2)}, u32[]{:S(2)}) %collective-permute-start.10) | collective-permute-done | bytes 393248 | tf_op jit(solution)/shard_map/ppermute | solution.py:184
  102.4 2.2 %collective-permute-start.11 = (bf16[192,1024]{1,0:T(8,128)(2,1)}, bf16[192,1024]{1,0:T(8,128)(2,1)S(1)}, u32[]{:S(2)}, u32[]{:S(2)}) collective-permute-start(bf16[192,1024]{1,0:T(8,128)(2,1)} %collective-permute-done.10.refs_1_), channel_id=1, source_target_pairs={{0,128},{128,256},{256,384},{384,512},{512,640},{640,768},{768,896... | collective-permute-start | bytes 1179656 | tf_op jit(solution)/shard_map/ppermute | solution.py:184
  104.7 4.2 %collective-permute-start.14 = (bf16[192,1024]{1,0:T(8,128)(2,1)}, bf16[192,1024]{1,0:T(8,128)(2,1)S(1)}, u32[]{:S(2)}, u32[]{:S(2)}) collective-permute-start(bf16[192,1024]{1,0:T(8,128)(2,1)} %collective-permute-done.13.refs_2_), channel_id=1, source_target_pairs={{0,896},{128,0},{256,128},{384,256},{512,384},{640,512},{768,640},... | collective-permute-start | bytes 1179656 | tf_op jit(solution)/shard_map/ppermute | solution.py:185
  109.0 3.7 %collective-permute-done.11.refs_3_ = bf16[192,1024]{1,0:T(8,128)(2,1)S(1)} collective-permute-done((bf16[192,1024]{1,0:T(8,128)(2,1)}, bf16[192,1024]{1,0:T(8,128)(2,1)S(1)}, u32[]{:S(2)}, u32[]{:S(2)}) %collective-permute-start.11) | collective-permute-done | bytes 393248 | tf_op jit(solution)/shard_map/ppermute | solution.py:184
  112.7 1.9 %collective-permute-start.12 = (bf16[192,1024]{1,0:T(8,128)(2,1)S(1)}, bf16[192,1024]{1,0:T(8,128)(2,1)}, u32[]{:S(2)}, u32[]{:S(2)}) collective-permute-start(bf16[192,1024]{1,0:T(8,128)(2,1)S(1)} %collective-permute-done.11.refs_3_), channel_id=1, source_target_pairs={{0,128},{128,256},{256,384},{384,512},{512,640},{640,768},{768,896... | collective-permute-start | bytes 1179656 | tf_op jit(solution)/shard_map/ppermute | solution.py:184
  114.6 4.6 %collective-permute-start.15 = (bf16[192,1024]{1,0:T(8,128)(2,1)S(1)}, bf16[192,1024]{1,0:T(8,128)(2,1)}, u32[]{:S(2)}, u32[]{:S(2)}) collective-permute-start(bf16[192,1024]{1,0:T(8,128)(2,1)S(1)} %collective-permute-done.14.refs_4_), channel_id=1, source_target_pairs={{0,896},{128,0},{256,128},{384,256},{512,384},{640,512},{768,640},... | collective-permute-start | bytes 1179656 | tf_op jit(solution)/shard_map/ppermute | solution.py:185
  119.9 1.9 %collective-permute-start.16 = (bf16[96,1024]{1,0:T(8,128)(2,1)}, bf16[96,1024]{1,0:T(8,128)(2,1)S(1)}, u32[]{:S(2)}, u32[]{:S(2)}) collective-permute-start(bf16[96,1024]{1,0:T(8,128)(2,1)} %slice.8), channel_id=1, source_target_pairs={{0,256},{128,384},{256,512},{384,640},{512,768},{640,896},{768,0},... | collective-permute-start | bytes 589832 | tf_op jit(solution)/shard_map/ppermute | solution.py:181
  122.5 5.5 %collective-permute-start.17 = (bf16[96,1024]{1,0:T(8,128)(2,1)}, bf16[96,1024]{1,0:T(8,128)(2,1)}, u32[]{:S(2)}, u32[]{:S(2)}) collective-permute-start(bf16[96,1024]{1,0:T(8,128)(2,1)} %slice.9), channel_id=1, source_target_pairs={{0,768},{128,896},{256,0},{384,128},{512,256},{640,384},{768,512},... | collective-permute-start | bytes 589832 | tf_op jit(solution)/shard_map/ppermute | solution.py:182
  130.2 6.1 %collective-permute-done.17.refs_8_ = bf16[96,1024]{1,0:T(8,128)(2,1)} collective-permute-done((bf16[96,1024]{1,0:T(8,128)(2,1)}, bf16[96,1024]{1,0:T(8,128)(2,1)}, u32[]{:S(2)}, u32[]{:S(2)}) %collective-permute-start.17) | collective-permute-done | bytes 196640 | tf_op jit(solution)/shard_map/ppermute | solution.py:182
  136.3 5.7 %collective-permute-start.18 = (bf16[8,4,128,256]{3,2,1,0:T(8,128)(2,1)S(1)}, bf16[8,4,128,256]{3,2,1,0:T(8,128)(2,1)}, u32[]{:S(2)}, u32[]{:S(2)}) collective-permute-start(bf16[8,4,128,256]{3,2,1,0:T(8,128)(2,1)S(1)} %bitcast.30), channel_id=1, source_target_pairs={{0,16},{16,0},{1,17},{17,1},{2,18},{18,2},{3,19},{19,3},{4,20},{20... | collective-permute-start | bytes 6291464 | tf_op jit(solution)/shard_map/ppermute | solution.py:193
  142.0 5.4 %shard_map.68.refs_10_ = bf16[2,208,256]{2,1,0:T(8,128)(2,1)} custom-call(s32[19]{0:T(128)} %concatenate.10.index, bf16[192,1024]{1,0:T(8,128)(2,1)} %copy-done.4, bf16[192,1024]{1,0:T(8,128)(2,1)} %collective-permute-done.10.refs_1_, bf16[192,1024]{1,0:T(8,128)(2,1)} %collective-permute-done.13.refs_2_, bf16[192,1024]{1,0:T(8,128)(2,1)} %copy-done.2, ...), custom_call_target="tpu_custom_call" | custom-call | flops 805306368 | bytes 7340032 | tf_op jit(solution)/shard_map/pallas_call | solution.py:95
  147.4 5.3 %shard_map.69 = bf16[2,2,208,256]{3,2,1,0:T(8,128)(2,1)} custom-call(s32[19]{0:T(128)} %concatenate.10.index, bf16[192,1024]{1,0:T(8,128)(2,1)} %copy-done.4, bf16[192,1024]{1,0:T(8,128)(2,1)} %collective-permute-done.10.refs_1_, bf16[192,1024]{1,0:T(8,128)(2,1)} %collective-permute-done.13.refs_2_, bf16[192,1024]{1,0:T(8,128)(2,1)} %copy-done.2, ...), custom_call_target="tpu_custom_call" | custom-call | flops 805306368 | bytes 7340032 | tf_op jit(solution)/shard_map/pallas_call | solution.py:95
  152.8 20.6 %all_to_all.20.parts = bf16[4,208,256]{2,1,0:T(8,128)(2,1)S(1)} all-to-all(bf16[4,208,256]{2,1,0:T(8,128)(2,1)} %bitcast.32), channel_id=1, replica_groups=mesh['zh'=2,'zl'=4,'y1'=2,'y0'=2,'c'=2,'yh'=2,'x'=8] {'c','yh'}, dimensions={0} | all-to-all | bytes 851968 | tf_op jit(solution)/shard_map/all_to_all | solution.py:196
  (52 shorter events, 10.1 us)
Async XLA Ops:
  2.2 19.5 %all-to-all-start = ((bf16[8,48,128]{2,1,0:T(8,128)(2,1)}), bf16[8,48,128]{2,1,0:T(8,128)(2,1)S(1)}, u32[]{:S(2)}, u32[]{:S(2)}) async-start(bf16[8,48,128]{2,1,0:T(8,128)(2,1)} %bitcast.1), calls=%async_computation | async-start | bytes 196608 | tf_op jit(solution)/shard_map/all_to_all | solution.py:155
  21.8 34.6 %collective-permute-start = (bf16[48,128]{1,0:T(8,128)(2,1)S(1)}, bf16[48,128]{1,0:T(8,128)(2,1)S(1)}, u32[]{:S(2)}, u32[]{:S(2)}) collective-permute-start(bf16[48,128]{1,0:T(8,128)(2,1)S(1)} %get-tuple-element.32), channel_id=1, source_target_pairs={{0,1},{1,0},{2,3},{3,2},{4,5},{5,4},{6,7},{7,6},{8,9},{9,8},{10,11... | collective-permute-start | bytes 36872 | tf_op jit(solution)/shard_map/ppermute | solution.py:163
  24.9 36.5 %collective-permute-start.1 = (bf16[48,128]{1,0:T(8,128)(2,1)S(1)}, bf16[48,128]{1,0:T(8,128)(2,1)S(1)}, u32[]{:S(2)}, u32[]{:S(2)}) collective-permute-start(bf16[48,128]{1,0:T(8,128)(2,1)S(1)} %get-tuple-element.31), channel_id=1, source_target_pairs={{0,2},{1,3},{2,0},{3,1},{4,6},{5,7},{6,4},{7,5},{8,10},{9,11},{10,... | collective-permute-start | bytes 36872 | tf_op jit(solution)/shard_map/ppermute | solution.py:163
  29.0 34.4 %collective-permute-start.2 = (bf16[48,128]{1,0:T(8,128)(2,1)S(1)}, bf16[48,128]{1,0:T(8,128)(2,1)S(1)}, u32[]{:S(2)}, u32[]{:S(2)}) collective-permute-start(bf16[48,128]{1,0:T(8,128)(2,1)S(1)} %get-tuple-element.30), channel_id=1, source_target_pairs={{0,3},{1,2},{2,1},{3,0},{4,7},{5,6},{6,5},{7,4},{8,11},{9,10},{10,... | collective-permute-start | bytes 36872 | tf_op jit(solution)/shard_map/ppermute | solution.py:163
  31.1 32.4 %collective-permute-start.3 = (bf16[48,128]{1,0:T(8,128)(2,1)S(1)}, bf16[48,128]{1,0:T(8,128)(2,1)S(1)}, u32[]{:S(2)}, u32[]{:S(2)}) collective-permute-start(bf16[48,128]{1,0:T(8,128)(2,1)S(1)} %get-tuple-element.29), channel_id=1, source_target_pairs={{0,4},{1,5},{2,6},{3,7},{4,0},{5,1},{6,2},{7,3},{8,12},{9,13},{10,... | collective-permute-start | bytes 36872 | tf_op jit(solution)/shard_map/ppermute | solution.py:163
  38.2 25.3 %collective-permute-start.4 = (bf16[48,128]{1,0:T(8,128)(2,1)S(1)}, bf16[48,128]{1,0:T(8,128)(2,1)S(1)}, u32[]{:S(2)}, u32[]{:S(2)}) collective-permute-start(bf16[48,128]{1,0:T(8,128)(2,1)S(1)} %get-tuple-element.28), channel_id=1, source_target_pairs={{0,5},{1,4},{2,7},{3,6},{4,1},{5,0},{6,3},{7,2},{8,13},{9,12},{10,... | collective-permute-start | bytes 36872 | tf_op jit(solution)/shard_map/ppermute | solution.py:163
  40.1 29.8 %all-to-all-start.1 = ((bf16[64,8,256]{2,1,0:T(8,128)(2,1)}), bf16[64,8,256]{2,1,0:T(8,128)(2,1)S(1)}, u32[]{:S(2)}, u32[]{:S(2)}) async-start(bf16[64,8,256]{2,1,0:T(8,128)(2,1)} %bitcast.34), calls=%async_computation.1 | async-start | bytes 524288 | tf_op jit(solution)/shard_map/all_to_all | solution.py:157
  56.4 7.1 %collective-permute-start.5 = (bf16[48,128]{1,0:T(8,128)(2,1)S(1)}, bf16[48,128]{1,0:T(8,128)(2,1)S(1)}, u32[]{:S(2)}, u32[]{:S(2)}) collective-permute-start(bf16[48,128]{1,0:T(8,128)(2,1)S(1)} %get-tuple-element.27), channel_id=1, source_target_pairs={{0,6},{1,7},{2,4},{3,5},{4,2},{5,3},{6,0},{7,1},{8,14},{9,15},{10,... | collective-permute-start | bytes 36872 | tf_op jit(solution)/shard_map/ppermute | solution.py:163
  61.4 5.9 %collective-permute-start.6 = (bf16[48,128]{1,0:T(8,128)(2,1)S(1)}, bf16[48,128]{1,0:T(8,128)(2,1)S(1)}, u32[]{:S(2)}, u32[]{:S(2)}) collective-permute-start(bf16[48,128]{1,0:T(8,128)(2,1)S(1)} %get-tuple-element.26), channel_id=1, source_target_pairs={{0,7},{1,6},{2,5},{3,4},{4,3},{5,2},{6,1},{7,0},{8,15},{9,14},{10,... | collective-permute-start | bytes 36872 | tf_op jit(solution)/shard_map/ppermute | solution.py:163
  73.2 46.0 %copy-start.6 = (s32[8]{0:T(128)S(1)}, s32[8]{0:T(128)}, u32[]{:S(2)}) copy-start(s32[8]{0:T(128)} %constant.88.clone) | copy-start | bytes 100
  73.2 63.1 %all-to-all-start.2 = ((bf16[8,512,256]{2,1,0:T(8,128)(2,1)}), bf16[8,512,256]{2,1,0:T(8,128)(2,1)S(1)}, u32[]{:S(2)}, u32[]{:S(2)}) async-start(bf16[8,512,256]{2,1,0:T(8,128)(2,1)} %broadcast_in_dim.2), calls=%async_computation.2 | async-start | bytes 4194304 | tf_op jit(solution)/shard_map/all_to_all | solution.py:29
  79.4 9.3 %collective-permute-start.7 = (bf16[48,1024]{1,0:T(8,128)(2,1)S(1)}, bf16[48,1024]{1,0:T(8,128)(2,1)S(1)}, u32[]{:S(2)}, u32[]{:S(2)}) collective-permute-start(bf16[48,1024]{1,0:T(8,128)(2,1)S(1)} %constant_dynamic-update-slice_fusion), channel_id=1, source_target_pairs={{0,32},{32,0},{64,96},{96,64},{1,33},{33,1},{65,97},{97,65},{2,34}... | collective-permute-start | bytes 294920 | tf_op jit(solution)/shard_map/ppermute | solution.py:167
  81.8 9.9 %collective-permute-start.8 = (bf16[48,1024]{1,0:T(8,128)(2,1)S(1)}, bf16[48,1024]{1,0:T(8,128)(2,1)S(1)}, u32[]{:S(2)}, u32[]{:S(2)}) collective-permute-start(bf16[48,1024]{1,0:T(8,128)(2,1)S(1)} %constant_dynamic-update-slice_fusion), channel_id=1, source_target_pairs={{0,64},{32,96},{64,0},{96,32},{1,65},{33,97},{65,1},{97,33},{2,66}... | collective-permute-start | bytes 294920 | tf_op jit(solution)/shard_map/ppermute | solution.py:167
  84.1 7.6 %collective-permute-start.9 = (bf16[48,1024]{1,0:T(8,128)(2,1)S(1)}, bf16[48,1024]{1,0:T(8,128)(2,1)S(1)}, u32[]{:S(2)}, u32[]{:S(2)}) collective-permute-start(bf16[48,1024]{1,0:T(8,128)(2,1)S(1)} %constant_dynamic-update-slice_fusion), channel_id=1, source_target_pairs={{0,96},{32,64},{64,32},{96,0},{1,97},{33,65},{65,33},{97,1},{2,98}... | collective-permute-start | bytes 294920 | tf_op jit(solution)/shard_map/ppermute | solution.py:167
  91.7 50.3 %copy-start.4 = (bf16[192,1024]{1,0:T(8,128)(2,1)}, bf16[192,1024]{1,0:T(8,128)(2,1)S(1)}, u32[]{:S(2)}) copy-start(bf16[192,1024]{1,0:T(8,128)(2,1)S(1)} %constant_dynamic-update-slice_fusion.8.refs_0_) | copy-start | bytes 1179652
  91.7 10.7 %collective-permute-start.10 = (bf16[192,1024]{1,0:T(8,128)(2,1)S(1)}, bf16[192,1024]{1,0:T(8,128)(2,1)}, u32[]{:S(2)}, u32[]{:S(2)}) collective-permute-start(bf16[192,1024]{1,0:T(8,128)(2,1)S(1)} %constant_dynamic-update-slice_fusion.8.refs_0_), channel_id=1, source_target_pairs={{0,128},{128,256},{256,384},{384,512},{512,640},{640,768},{768,896... | collective-permute-start | bytes 1179656 | tf_op jit(solution)/shard_map/ppermute | solution.py:184
  94.6 10.1 %collective-permute-start.13 = (bf16[192,1024]{1,0:T(8,128)(2,1)S(1)}, bf16[192,1024]{1,0:T(8,128)(2,1)}, u32[]{:S(2)}, u32[]{:S(2)}) collective-permute-start(bf16[192,1024]{1,0:T(8,128)(2,1)S(1)} %constant_dynamic-update-slice_fusion.8.refs_0_), channel_id=1, source_target_pairs={{0,896},{128,0},{256,128},{384,256},{512,384},{640,512},{768,640},... | collective-permute-start | bytes 1179656 | tf_op jit(solution)/shard_map/ppermute | solution.py:185
  102.4 10.2 %collective-permute-start.11 = (bf16[192,1024]{1,0:T(8,128)(2,1)}, bf16[192,1024]{1,0:T(8,128)(2,1)S(1)}, u32[]{:S(2)}, u32[]{:S(2)}) collective-permute-start(bf16[192,1024]{1,0:T(8,128)(2,1)} %collective-permute-done.10.refs_1_), channel_id=1, source_target_pairs={{0,128},{128,256},{256,384},{384,512},{512,640},{640,768},{768,896... | collective-permute-start | bytes 1179656 | tf_op jit(solution)/shard_map/ppermute | solution.py:184
  104.7 9.9 %collective-permute-start.14 = (bf16[192,1024]{1,0:T(8,128)(2,1)}, bf16[192,1024]{1,0:T(8,128)(2,1)S(1)}, u32[]{:S(2)}, u32[]{:S(2)}) collective-permute-start(bf16[192,1024]{1,0:T(8,128)(2,1)} %collective-permute-done.13.refs_2_), channel_id=1, source_target_pairs={{0,896},{128,0},{256,128},{384,256},{512,384},{640,512},{768,640},... | collective-permute-start | bytes 1179656 | tf_op jit(solution)/shard_map/ppermute | solution.py:185
  112.7 29.3 %copy-start.2 = (bf16[192,1024]{1,0:T(8,128)(2,1)}, bf16[192,1024]{1,0:T(8,128)(2,1)S(1)}, u32[]{:S(2)}) copy-start(bf16[192,1024]{1,0:T(8,128)(2,1)S(1)} %collective-permute-done.11.refs_3_) | copy-start | bytes 1179652
  112.7 23.6 %collective-permute-start.12 = (bf16[192,1024]{1,0:T(8,128)(2,1)S(1)}, bf16[192,1024]{1,0:T(8,128)(2,1)}, u32[]{:S(2)}, u32[]{:S(2)}) collective-permute-start(bf16[192,1024]{1,0:T(8,128)(2,1)S(1)} %collective-permute-done.11.refs_3_), channel_id=1, source_target_pairs={{0,128},{128,256},{256,384},{384,512},{512,640},{640,768},{768,896... | collective-permute-start | bytes 1179656 | tf_op jit(solution)/shard_map/ppermute | solution.py:184
  114.6 27.4 %copy-start.3 = (bf16[192,1024]{1,0:T(8,128)(2,1)}, bf16[192,1024]{1,0:T(8,128)(2,1)S(1)}, u32[]{:S(2)}) copy-start(bf16[192,1024]{1,0:T(8,128)(2,1)S(1)} %collective-permute-done.14.refs_4_) | copy-start | bytes 1179652
  114.6 21.7 %collective-permute-start.15 = (bf16[192,1024]{1,0:T(8,128)(2,1)S(1)}, bf16[192,1024]{1,0:T(8,128)(2,1)}, u32[]{:S(2)}, u32[]{:S(2)}) collective-permute-start(bf16[192,1024]{1,0:T(8,128)(2,1)S(1)} %collective-permute-done.14.refs_4_), channel_id=1, source_target_pairs={{0,896},{128,0},{256,128},{384,256},{512,384},{640,512},{768,640},... | collective-permute-start | bytes 1179656 | tf_op jit(solution)/shard_map/ppermute | solution.py:185
  119.9 10.3 %collective-permute-start.16 = (bf16[96,1024]{1,0:T(8,128)(2,1)}, bf16[96,1024]{1,0:T(8,128)(2,1)S(1)}, u32[]{:S(2)}, u32[]{:S(2)}) collective-permute-start(bf16[96,1024]{1,0:T(8,128)(2,1)} %slice.8), channel_id=1, source_target_pairs={{0,256},{128,384},{256,512},{384,640},{512,768},{640,896},{768,0},... | collective-permute-start | bytes 589832 | tf_op jit(solution)/shard_map/ppermute | solution.py:181
  122.5 13.8 %collective-permute-start.17 = (bf16[96,1024]{1,0:T(8,128)(2,1)}, bf16[96,1024]{1,0:T(8,128)(2,1)}, u32[]{:S(2)}, u32[]{:S(2)}) collective-permute-start(bf16[96,1024]{1,0:T(8,128)(2,1)} %slice.9), channel_id=1, source_target_pairs={{0,768},{128,896},{256,0},{384,128},{512,256},{640,384},{768,512},... | collective-permute-start | bytes 589832 | tf_op jit(solution)/shard_map/ppermute | solution.py:182
  130.2 11.8 %copy-start.5 = (bf16[96,1024]{1,0:T(8,128)(2,1)}, bf16[96,1024]{1,0:T(8,128)(2,1)S(1)}, u32[]{:S(2)}) copy-start(bf16[96,1024]{1,0:T(8,128)(2,1)S(1)} %collective-permute-done.16.refs_7_) | copy-start | bytes 589828
  136.3 5.7 %copy-start.1 = (bf16[8,512,256]{2,1,0:T(8,128)(2,1)}, bf16[8,512,256]{2,1,0:T(8,128)(2,1)S(1)}, u32[]{:S(2)}) copy-start(bf16[8,512,256]{2,1,0:T(8,128)(2,1)S(1)} %all-to-all-done.2) | copy-start | bytes 6291460
  136.3 11.1 %collective-permute-start.18 = (bf16[8,4,128,256]{3,2,1,0:T(8,128)(2,1)S(1)}, bf16[8,4,128,256]{3,2,1,0:T(8,128)(2,1)}, u32[]{:S(2)}, u32[]{:S(2)}) collective-permute-start(bf16[8,4,128,256]{3,2,1,0:T(8,128)(2,1)S(1)} %bitcast.30), channel_id=1, source_target_pairs={{0,16},{16,0},{1,17},{17,1},{2,18},{18,2},{3,19},{19,3},{4,20},{20... | collective-permute-start | bytes 6291464 | tf_op jit(solution)/shard_map/ppermute | solution.py:193
  147.4 26.0 %copy-start = (s32[19]{0:T(128)S(1)}, s32[19]{0:T(128)}, u32[]{:S(2)}) copy-start(s32[19]{0:T(128)} %concatenate.10.index) | copy-start | bytes 232

commit v8 on v6

--- a/solution.py
+++ b/solution.py
@@ -38,7 +38,7 @@
     groups, _, rows, depth = a_buf.shape
     cols = b_buf.shape[-1]
     b_copies = [
-        pltpu.make_async_copy(weights.at[:, q], b_buf.at[q], b_sem.at[q]) for q in range(NZL)
+        pltpu.make_async_copy(weights.at[i], b_buf.at[:, i], b_sem.at[i]) for i in range(NX)
     ]
     places = [a_buf.at[index[s], index[NZ + s]] for s in range(NZ)]
     places[-1:] = [places[-1].at[: rows // 2], places[-1].at[rows // 2 :]]
@@ -49,10 +49,9 @@
         copy.start()
     if first:
         sums[...] = jnp.zeros_like(sums)
-    for copy in a_copies:
+    for copy in a_copies + b_copies:
         copy.wait()
     for q in range(NZL):
-        b_copies[q].wait()
         left = a_buf[:, q].reshape(groups * rows, depth)
         part = jnp.dot(left, b_buf[q].reshape(depth, cols), preferred_element_type=jnp.float32)
         part = part.reshape(groups, rows, cols)
@@ -104,7 +103,7 @@
             pltpu.VMEM((NZL, NX, LANES, cols), jnp.bfloat16),
         ]
         + (totals if first else totals[:1])
-        + [pltpu.SemaphoreType.DMA((len(blocks),)), pltpu.SemaphoreType.DMA((NZL,))],
+        + [pltpu.SemaphoreType.DMA((len(blocks),)), pltpu.SemaphoreType.DMA((NX,))],
         compiler_params=pltpu.CompilerParams(vmem_limit_bytes=60 * 2**20),
         cost_estimate=pl.CostEstimate(
             flops=2 * NZ * rows * depth * cols,
@@ -159,9 +158,8 @@
         policy.reshape(8, 64, 256).transpose(1, 0, 2), DP, 0, 0, tiled=True
     )
     own = pieces.transpose(1, 0, 2).reshape(toks, NX * LANES)
-    own = jnp.concatenate(
-        [own] + [lax.ppermute(own, YL, [(i, i ^ e) for i in range(NYL)]) for e in range(1, NYL)]
-    )
+    for e in (1, 2):
+        own = jnp.concatenate([own, lax.ppermute(own, YL, [(i, i ^ e) for i in range(NYL)])])
     rows = own.shape[0]
     own, arrived = lax.optimization_barrier((own, arrived))
     policy_slice = arrived.reshape(ref_weight.shape)

time: 163 us -> 165 us (1.012)
  waiting for transfers between devices: 28.9 us -> 34.1 us
  starting transfers between devices: 60.9 us -> 58.3 us
  Pallas kernels: 13.9 us -> 12.1 us
    ppermute x3 -> x2, waiting for transfers between devices: 7.63 us -> 12.7 us  [body(): lax.ppermute(own, YL, [(i, i ^ e) for i in range(NYL)])]
    pallas_call x2, Pallas kernels: 12.5 us -> 10.7 us  [gate_parts(): pl.pallas_call(functools.partial(gate_kernel, first), out_shape=jax.Shape...]
    ppermute x3 -> x2, starting transfers between devices: 9.27 us -> 7.53 us  [body(): lax.ppermute(own, YL, [(i, i ^ e) for i in range(NYL)])]
  transfers between devices with their start and end apart: 14 -> 13, of which waited for: 7 -> 6; matrix products, arithmetic and copies ran while one was open for 1% -> 1% of each run, Pallas kernels for 4% -> 3%
where the time goes in v8:
time: 165 us; the launch traced here: 162 us
  starting transfers between devices  58.3 us (35%)
  blocking collectives  51.8 us (31%)
  waiting for transfers between devices  34.1 us (21%)
  Pallas kernels  12.1 us (7%)
  local copies, waits for them, and re-layouts  3.8 us (2%)
    all_to_all x1, blocking collectives, body(): pieces = lax.all_to_all(pieces, ('zl', 'y1'), 0, 0, tiled=True)  19.5 us
    all_to_all x1, blocking collectives, body(): lax.all_to_all(parts.reshape(4, *parts.shape[2:]), ('c', 'yh'), 0, 0, til...  18.5 us
    all_to_all x1, starting transfers between devices, body(): lax.all_to_all(policy.reshape(8, 64, 256).transpose(1, 0, 2), DP, 0, 0, t...  15.7 us
    all_to_all x1, blocking collectives, body(): pieces = lax.all_to_all(pieces, 'x', 0, 0, tiled=True)  13.8 us
    ppermute x3, starting transfers between devices, body(): down = lax.ppermute(down, Z, shift(NZ, -1))  13.4 us
    ppermute x3, waiting for transfers between devices, body(): up = lax.ppermute(up, Z, shift(NZ, 1))  12.8 us
    ppermute x2, waiting for transfers between devices, body(): lax.ppermute(own, YL, [(i, i ^ e) for i in range(NYL)])  12.7 us
    pallas_call x2, Pallas kernels, gate_parts(): pl.pallas_call(functools.partial(gate_kernel, first), out_shape=jax.Shape...  10.7 us
  transfers between devices with their start and end apart: 13, of which 6 were waited for; matrix products, arithmetic and copies ran while one was open for 1% of the time, Pallas kernels for 3%

profile of v8, /device:TPU:1, one launch (start us, length us, event | category | flops | bytes accessed | tf_op | source)
XLA Modules:
  0.0 162.5 jit_solution(10547825561976018908)
XLA Ops:
  0.6 0.0 copy-start
  0.7 0.9 copy-done
  1.6 19.5 %all_to_all.25 = bf16[8,48,128]{2,1,0:T(8,128)(2,1)S(1)} all-to-all(bf16[8,48,128]{2,1,0:T(8,128)(2,1)S(1)} %bitcast.28), channel_id=1, replica_groups=mesh['zh'=2,'zl'=4,'y1'=2,'y0'=2,'c'=2,'yh'=2,'x'=8] {'zl','y1'}, dimensions={0} | all-to-all | bytes 196608 | tf_op jit(solution)/shard_map/all_to_all | solution.py:154
  21.0 13.8 %all_to_all.26 = bf16[8,48,128]{2,1,0:T(8,128)(2,1)S(1)} all-to-all(bf16[8,48,128]{2,1,0:T(8,128)(2,1)S(1)} %all_to_all.25), channel_id=1, replica_groups=mesh['zh'=2,'zl'=4,'y1'=2,'y0'=2,'c'=2,'yh'=2,'x'=8] {'x'}, dimensions={0} | all-to-all | bytes 196608 | tf_op jit(solution)/shard_map/all_to_all | solution.py:155
  34.9 3.3 %collective-permute-start = (bf16[48,1024]{1,0:T(8,128)(2,1)S(1)}, bf16[48,1024]{1,0:T(8,128)(2,1)S(1)}, u32[]{:S(2)}, u32[]{:S(2)}) collective-permute-start(bf16[48,1024]{1,0:T(8,128)(2,1)S(1)} %copy_bitcast_fusion), channel_id=1, source_target_pairs={{0,32},{32,0},{64,96},{96,64},{1,33},{33,1},{65,97},{97,65},{2,34}... | collective-permute-start | bytes 294920 | tf_op jit(solution)/shard_map/ppermute | solution.py:162
  38.2 15.7 %all-to-all-start.2 = ((bf16[64,8,256]{2,1,0:T(8,128)(2,1)}), bf16[64,8,256]{2,1,0:T(8,128)(2,1)S(1)}, u32[]{:S(2)}, u32[]{:S(2)}) async-start(bf16[64,8,256]{2,1,0:T(8,128)(2,1)} %bitcast.29), calls=%async_computation.2 | async-start | bytes 524288 | tf_op jit(solution)/shard_map/all_to_all | solution.py:157
  54.0 4.2 %collective-permute-start.1 = (bf16[96,1024]{1,0:T(8,128)(2,1)S(1)}, bf16[96,1024]{1,0:T(8,128)(2,1)S(1)}, u32[]{:S(2)}, u32[]{:S(2)}) collective-permute-start(bf16[96,1024]{1,0:T(8,128)(2,1)S(1)} %pad_maximum_fusion.1), channel_id=1, source_target_pairs={{0,64},{32,96},{64,0},{96,32},{1,65},{33,97},{65,1},{97,33},{2,66}... | collective-permute-start | bytes 589832 | tf_op jit(solution)/shard_map/ppermute | solution.py:162
  58.2 12.7 %collective-permute-done.1 = bf16[96,1024]{1,0:T(8,128)(2,1)S(1)} collective-permute-done((bf16[96,1024]{1,0:T(8,128)(2,1)S(1)}, bf16[96,1024]{1,0:T(8,128)(2,1)S(1)}, u32[]{:S(2)}, u32[]{:S(2)}) %collective-permute-start.1) | collective-permute-done | bytes 196640 | tf_op jit(solution)/shard_map/ppermute | solution.py:162
  70.9 0.8 all-to-all-done.2
  71.8 0.8 multiply_convert_fusion
  72.6 1.5 broadcast_in_dim.2
  74.1 3.7 %all-to-all-start.3 = ((bf16[8,512,256]{2,1,0:T(8,128)(2,1)}), bf16[8,512,256]{2,1,0:T(8,128)(2,1)S(1)}, u32[]{:S(2)}, u32[]{:S(2)}) async-start(bf16[8,512,256]{2,1,0:T(8,128)(2,1)} %broadcast_in_dim.2), calls=%async_computation.3 | async-start | bytes 4194304 | tf_op jit(solution)/shard_map/all_to_all | solution.py:29
  77.8 2.3 %collective-permute-start.2 = (bf16[192,1024]{1,0:T(8,128)(2,1)S(1)}, bf16[192,1024]{1,0:T(8,128)(2,1)S(1)}, u32[]{:S(2)}, u32[]{:S(2)}) collective-permute-start(bf16[192,1024]{1,0:T(8,128)(2,1)S(1)} %pad_maximum_fusion.refs_0_), channel_id=1, source_target_pairs={{0,128},{128,256},{256,384},{384,512},{512,640},{640,768},{768,896... | collective-permute-start | bytes 1179656 | tf_op jit(solution)/shard_map/ppermute | solution.py:179
  80.1 4.2 %collective-permute-start.5 = (bf16[192,1024]{1,0:T(8,128)(2,1)S(1)}, bf16[192,1024]{1,0:T(8,128)(2,1)}, u32[]{:S(2)}, u32[]{:S(2)}) collective-permute-start(bf16[192,1024]{1,0:T(8,128)(2,1)S(1)} %pad_maximum_fusion.refs_0_), channel_id=1, source_target_pairs={{0,896},{128,0},{256,128},{384,256},{512,384},{640,512},{768,640},... | collective-permute-start | bytes 1179656 | tf_op jit(solution)/shard_map/ppermute | solution.py:180
  84.3 6.9 %collective-permute-done.2.refs_1_ = bf16[192,1024]{1,0:T(8,128)(2,1)S(1)} collective-permute-done((bf16[192,1024]{1,0:T(8,128)(2,1)S(1)}, bf16[192,1024]{1,0:T(8,128)(2,1)S(1)}, u32[]{:S(2)}, u32[]{:S(2)}) %collective-permute-start.2) | collective-permute-done | bytes 393248 | tf_op jit(solution)/shard_map/ppermute | solution.py:179
  91.2 1.9 %collective-permute-start.3 = (bf16[192,1024]{1,0:T(8,128)(2,1)S(1)}, bf16[192,1024]{1,0:T(8,128)(2,1)S(1)}, u32[]{:S(2)}, u32[]{:S(2)}) collective-permute-start(bf16[192,1024]{1,0:T(8,128)(2,1)S(1)} %collective-permute-done.2.refs_1_), channel_id=1, source_target_pairs={{0,128},{128,256},{256,384},{384,512},{512,640},{640,768},{768,896... | collective-permute-start | bytes 1179656 | tf_op jit(solution)/shard_map/ppermute | solution.py:179
  93.1 4.6 %collective-permute-start.6 = (bf16[192,1024]{1,0:T(8,128)(2,1)}, bf16[192,1024]{1,0:T(8,128)(2,1)S(1)}, u32[]{:S(2)}, u32[]{:S(2)}) collective-permute-start(bf16[192,1024]{1,0:T(8,128)(2,1)} %collective-permute-done.5.refs_2_), channel_id=1, source_target_pairs={{0,896},{128,0},{256,128},{384,256},{512,384},{640,512},{768,640},... | collective-permute-start | bytes 1179656 | tf_op jit(solution)/shard_map/ppermute | solution.py:180
  97.7 6.0 %collective-permute-done.3.refs_3_ = bf16[192,1024]{1,0:T(8,128)(2,1)S(1)} collective-permute-done((bf16[192,1024]{1,0:T(8,128)(2,1)S(1)}, bf16[192,1024]{1,0:T(8,128)(2,1)S(1)}, u32[]{:S(2)}, u32[]{:S(2)}) %collective-permute-start.3) | collective-permute-done | bytes 393248 | tf_op jit(solution)/shard_map/ppermute | solution.py:179
  103.7 1.9 %collective-permute-start.4 = (bf16[192,1024]{1,0:T(8,128)(2,1)S(1)}, bf16[192,1024]{1,0:T(8,128)(2,1)}, u32[]{:S(2)}, u32[]{:S(2)}) collective-permute-start(bf16[192,1024]{1,0:T(8,128)(2,1)S(1)} %collective-permute-done.3.refs_3_), channel_id=1, source_target_pairs={{0,128},{128,256},{256,384},{384,512},{512,640},{640,768},{768,896... | collective-permute-start | bytes 1179656 | tf_op jit(solution)/shard_map/ppermute | solution.py:179
  105.6 4.6 %collective-permute-start.7 = (bf16[192,1024]{1,0:T(8,128)(2,1)S(1)}, bf16[192,1024]{1,0:T(8,128)(2,1)}, u32[]{:S(2)}, u32[]{:S(2)}) collective-permute-start(bf16[192,1024]{1,0:T(8,128)(2,1)S(1)} %collective-permute-done.6.refs_4_), channel_id=1, source_target_pairs={{0,896},{128,0},{256,128},{384,256},{512,384},{640,512},{768,640},... | collective-permute-start | bytes 1179656 | tf_op jit(solution)/shard_map/ppermute | solution.py:180
  110.2 0.7 slice.8
  110.9 1.9 %collective-permute-start.8 = (bf16[96,1024]{1,0:T(8,128)(2,1)}, bf16[96,1024]{1,0:T(8,128)(2,1)}, u32[]{:S(2)}, u32[]{:S(2)}) collective-permute-start(bf16[96,1024]{1,0:T(8,128)(2,1)} %slice.8), channel_id=1, source_target_pairs={{0,256},{128,384},{256,512},{384,640},{512,768},{640,896},{768,0},... | collective-permute-start | bytes 589832 | tf_op jit(solution)/shard_map/ppermute | solution.py:176
  112.8 0.7 slice.9
  113.5 5.5 %collective-permute-start.9 = (bf16[96,1024]{1,0:T(8,128)(2,1)}, bf16[96,1024]{1,0:T(8,128)(2,1)}, u32[]{:S(2)}, u32[]{:S(2)}) collective-permute-start(bf16[96,1024]{1,0:T(8,128)(2,1)} %slice.9), channel_id=1, source_target_pairs={{0,768},{128,896},{256,0},{384,128},{512,256},{640,384},{768,512},... | collective-permute-start | bytes 589832 | tf_op jit(solution)/shard_map/ppermute | solution.py:177
  119.0 0.6 pad_add_fusion.index
  119.6 4.0 %collective-permute-done.8.refs_7_ = bf16[96,1024]{1,0:T(8,128)(2,1)} collective-permute-done((bf16[96,1024]{1,0:T(8,128)(2,1)}, bf16[96,1024]{1,0:T(8,128)(2,1)}, u32[]{:S(2)}, u32[]{:S(2)}) %collective-permute-start.8) | collective-permute-done | bytes 196640 | tf_op jit(solution)/shard_map/ppermute | solution.py:176
  123.6 3.7 %collective-permute-done.9.refs_8_ = bf16[96,1024]{1,0:T(8,128)(2,1)} collective-permute-done((bf16[96,1024]{1,0:T(8,128)(2,1)}, bf16[96,1024]{1,0:T(8,128)(2,1)}, u32[]{:S(2)}, u32[]{:S(2)}) %collective-permute-start.9) | collective-permute-done | bytes 196640 | tf_op jit(solution)/shard_map/ppermute | solution.py:177
  127.3 4.5 %collective-permute-start.10 = (bf16[8,4,128,256]{3,2,1,0:T(8,128)(2,1)S(1)}, bf16[8,4,128,256]{3,2,1,0:T(8,128)(2,1)}, u32[]{:S(2)}, u32[]{:S(2)}) collective-permute-start(bf16[8,4,128,256]{3,2,1,0:T(8,128)(2,1)S(1)} %bitcast.25), channel_id=1, source_target_pairs={{0,16},{16,0},{1,17},{17,1},{2,18},{18,2},{3,19},{19,3},{4,20},{20... | collective-permute-start | bytes 6291464 | tf_op jit(solution)/shard_map/ppermute | solution.py:188
  131.9 5.4 %shard_map.68.refs_10_ = bf16[2,208,256]{2,1,0:T(8,128)(2,1)} custom-call(s32[18]{0:T(128)} %pad_add_fusion.index, bf16[192,1024]{1,0:T(8,128)(2,1)} %copy-done.3, bf16[192,1024]{1,0:T(8,128)(2,1)} %copy-done.6, bf16[192,1024]{1,0:T(8,128)(2,1)} %collective-permute-done.5.refs_2_, bf16[192,1024]{1,0:T(8,128)(2,1)} %copy-done.4, bf16[192,1024]{1,0:T(8,128)(2,1)} %copy-done.5, ...), custom_call_target="tpu_custom_call" | custom-call | flops 805306368 | bytes 7340032 | tf_op jit(solution)/shard_map/pallas_call | solution.py:94
  137.3 5.3 %shard_map.69 = bf16[2,2,208,256]{3,2,1,0:T(8,128)(2,1)} custom-call(s32[18]{0:T(128)} %pad_add_fusion.index, bf16[192,1024]{1,0:T(8,128)(2,1)} %copy-done.3, bf16[192,1024]{1,0:T(8,128)(2,1)} %copy-done.6, bf16[192,1024]{1,0:T(8,128)(2,1)} %collective-permute-done.5.refs_2_, bf16[192,1024]{1,0:T(8,128)(2,1)} %copy-done.4, bf16[192,1024]{1,0:T(8,128)(2,1)} %copy-done.5, ...), custom_call_target="tpu_custom_call" | custom-call | flops 805306368 | bytes 7340032 | tf_op jit(solution)/shard_map/pallas_call | solution.py:94
  142.6 18.5 %all_to_all.27.parts = bf16[4,208,256]{2,1,0:T(8,128)(2,1)S(1)} all-to-all(bf16[4,208,256]{2,1,0:T(8,128)(2,1)} %bitcast.27), channel_id=1, replica_groups=mesh['zh'=2,'zl'=4,'y1'=2,'y0'=2,'c'=2,'yh'=2,'x'=8] {'c','yh'}, dimensions={0} | all-to-all | bytes 851968 | tf_op jit(solution)/shard_map/all_to_all | solution.py:191
  161.0 1.4 shard_map.70
  (31 shorter events, 0.1 us)
Async XLA Ops:
  0.6 0.9 copy-start
  0.6 71.1 %copy-start.8 = (f32[512]{0:T(512)S(1)}, f32[512]{0:T(512)}, u32[]{:S(2)}) copy-start(f32[512]{0:T(512)} %param.8) | copy-start | bytes 6148
  1.5 70.2 %copy-start.7 = (bf16[512,256]{1,0:T(8,128)(2,1)S(1)}, bf16[512,256]{1,0:T(8,128)(2,1)}, u32[]{:S(2)}) copy-start(bf16[512,256]{1,0:T(8,128)(2,1)} %param.6) | copy-start | bytes 786436
  34.9 19.1 %collective-permute-start = (bf16[48,1024]{1,0:T(8,128)(2,1)S(1)}, bf16[48,1024]{1,0:T(8,128)(2,1)S(1)}, u32[]{:S(2)}, u32[]{:S(2)}) collective-permute-start(bf16[48,1024]{1,0:T(8,128)(2,1)S(1)} %copy_bitcast_fusion), channel_id=1, source_target_pairs={{0,32},{32,0},{64,96},{96,64},{1,33},{33,1},{65,97},{97,65},{2,34}... | collective-permute-start | bytes 294920 | tf_op jit(solution)/shard_map/ppermute | solution.py:162
  38.2 33.5 %all-to-all-start.2 = ((bf16[64,8,256]{2,1,0:T(8,128)(2,1)}), bf16[64,8,256]{2,1,0:T(8,128)(2,1)S(1)}, u32[]{:S(2)}, u32[]{:S(2)}) async-start(bf16[64,8,256]{2,1,0:T(8,128)(2,1)} %bitcast.29), calls=%async_computation.2 | async-start | bytes 524288 | tf_op jit(solution)/shard_map/all_to_all | solution.py:157
  54.0 16.9 %collective-permute-start.1 = (bf16[96,1024]{1,0:T(8,128)(2,1)S(1)}, bf16[96,1024]{1,0:T(8,128)(2,1)S(1)}, u32[]{:S(2)}, u32[]{:S(2)}) collective-permute-start(bf16[96,1024]{1,0:T(8,128)(2,1)S(1)} %pad_maximum_fusion.1), channel_id=1, source_target_pairs={{0,64},{32,96},{64,0},{96,32},{1,65},{33,97},{65,1},{97,33},{2,66}... | collective-permute-start | bytes 589832 | tf_op jit(solution)/shard_map/ppermute | solution.py:162
  70.9 9.2 %copy-start.3 = (bf16[192,1024]{1,0:T(8,128)(2,1)}, bf16[192,1024]{1,0:T(8,128)(2,1)S(1)}, u32[]{:S(2)}) copy-start(bf16[192,1024]{1,0:T(8,128)(2,1)S(1)} %pad_maximum_fusion.refs_0_) | copy-start | bytes 1179652
  74.1 36.1 %copy-start.9 = (s32[8]{0:T(128)S(1)}, s32[8]{0:T(128)}, u32[]{:S(2)}) copy-start(s32[8]{0:T(128)} %constant.59.clone) | copy-start | bytes 100
  74.1 53.3 %all-to-all-start.3 = ((bf16[8,512,256]{2,1,0:T(8,128)(2,1)}), bf16[8,512,256]{2,1,0:T(8,128)(2,1)S(1)}, u32[]{:S(2)}, u32[]{:S(2)}) async-start(bf16[8,512,256]{2,1,0:T(8,128)(2,1)} %broadcast_in_dim.2), calls=%async_computation.3 | async-start | bytes 4194304 | tf_op jit(solution)/shard_map/all_to_all | solution.py:29
  77.8 13.4 %collective-permute-start.2 = (bf16[192,1024]{1,0:T(8,128)(2,1)S(1)}, bf16[192,1024]{1,0:T(8,128)(2,1)S(1)}, u32[]{:S(2)}, u32[]{:S(2)}) collective-permute-start(bf16[192,1024]{1,0:T(8,128)(2,1)S(1)} %pad_maximum_fusion.refs_0_), channel_id=1, source_target_pairs={{0,128},{128,256},{256,384},{384,512},{512,640},{640,768},{768,896... | collective-permute-start | bytes 1179656 | tf_op jit(solution)/shard_map/ppermute | solution.py:179
  80.1 13.0 %collective-permute-start.5 = (bf16[192,1024]{1,0:T(8,128)(2,1)S(1)}, bf16[192,1024]{1,0:T(8,128)(2,1)}, u32[]{:S(2)}, u32[]{:S(2)}) collective-permute-start(bf16[192,1024]{1,0:T(8,128)(2,1)S(1)} %pad_maximum_fusion.refs_0_), channel_id=1, source_target_pairs={{0,896},{128,0},{256,128},{384,256},{512,384},{640,512},{768,640},... | collective-permute-start | bytes 1179656 | tf_op jit(solution)/shard_map/ppermute | solution.py:180
  91.2 40.6 %copy-start.6 = (bf16[192,1024]{1,0:T(8,128)(2,1)}, bf16[192,1024]{1,0:T(8,128)(2,1)S(1)}, u32[]{:S(2)}) copy-start(bf16[192,1024]{1,0:T(8,128)(2,1)S(1)} %collective-permute-done.2.refs_1_) | copy-start | bytes 1179652
  91.2 12.5 %collective-permute-start.3 = (bf16[192,1024]{1,0:T(8,128)(2,1)S(1)}, bf16[192,1024]{1,0:T(8,128)(2,1)S(1)}, u32[]{:S(2)}, u32[]{:S(2)}) collective-permute-start(bf16[192,1024]{1,0:T(8,128)(2,1)S(1)} %collective-permute-done.2.refs_1_), channel_id=1, source_target_pairs={{0,128},{128,256},{256,384},{384,512},{512,640},{640,768},{768,896... | collective-permute-start | bytes 1179656 | tf_op jit(solution)/shard_map/ppermute | solution.py:179
  93.1 12.5 %collective-permute-start.6 = (bf16[192,1024]{1,0:T(8,128)(2,1)}, bf16[192,1024]{1,0:T(8,128)(2,1)S(1)}, u32[]{:S(2)}, u32[]{:S(2)}) collective-permute-start(bf16[192,1024]{1,0:T(8,128)(2,1)} %collective-permute-done.5.refs_2_), channel_id=1, source_target_pairs={{0,896},{128,0},{256,128},{384,256},{512,384},{640,512},{768,640},... | collective-permute-start | bytes 1179656 | tf_op jit(solution)/shard_map/ppermute | solution.py:180
  103.7 28.2 %copy-start.4 = (bf16[192,1024]{1,0:T(8,128)(2,1)}, bf16[192,1024]{1,0:T(8,128)(2,1)S(1)}, u32[]{:S(2)}) copy-start(bf16[192,1024]{1,0:T(8,128)(2,1)S(1)} %collective-permute-done.3.refs_3_) | copy-start | bytes 1179652
  103.7 23.6 %collective-permute-start.4 = (bf16[192,1024]{1,0:T(8,128)(2,1)S(1)}, bf16[192,1024]{1,0:T(8,128)(2,1)}, u32[]{:S(2)}, u32[]{:S(2)}) collective-permute-start(bf16[192,1024]{1,0:T(8,128)(2,1)S(1)} %collective-permute-done.3.refs_3_), channel_id=1, source_target_pairs={{0,128},{128,256},{256,384},{384,512},{512,640},{640,768},{768,896... | collective-permute-start | bytes 1179656 | tf_op jit(solution)/shard_map/ppermute | solution.py:179
  105.6 26.2 %copy-start.5 = (bf16[192,1024]{1,0:T(8,128)(2,1)}, bf16[192,1024]{1,0:T(8,128)(2,1)S(1)}, u32[]{:S(2)}) copy-start(bf16[192,1024]{1,0:T(8,128)(2,1)S(1)} %collective-permute-done.6.refs_4_) | copy-start | bytes 1179652
  105.6 21.7 %collective-permute-start.7 = (bf16[192,1024]{1,0:T(8,128)(2,1)S(1)}, bf16[192,1024]{1,0:T(8,128)(2,1)}, u32[]{:S(2)}, u32[]{:S(2)}) collective-permute-start(bf16[192,1024]{1,0:T(8,128)(2,1)S(1)} %collective-permute-done.6.refs_4_), channel_id=1, source_target_pairs={{0,896},{128,0},{256,128},{384,256},{512,384},{640,512},{768,640},... | collective-permute-start | bytes 1179656 | tf_op jit(solution)/shard_map/ppermute | solution.py:180
  110.9 12.7 %collective-permute-start.8 = (bf16[96,1024]{1,0:T(8,128)(2,1)}, bf16[96,1024]{1,0:T(8,128)(2,1)}, u32[]{:S(2)}, u32[]{:S(2)}) collective-permute-start(bf16[96,1024]{1,0:T(8,128)(2,1)} %slice.8), channel_id=1, source_target_pairs={{0,256},{128,384},{256,512},{384,640},{512,768},{640,896},{768,0},... | collective-permute-start | bytes 589832 | tf_op jit(solution)/shard_map/ppermute | solution.py:176
  113.5 13.8 %collective-permute-start.9 = (bf16[96,1024]{1,0:T(8,128)(2,1)}, bf16[96,1024]{1,0:T(8,128)(2,1)}, u32[]{:S(2)}, u32[]{:S(2)}) collective-permute-start(bf16[96,1024]{1,0:T(8,128)(2,1)} %slice.9), channel_id=1, source_target_pairs={{0,768},{128,896},{256,0},{384,128},{512,256},{640,384},{768,512},... | collective-permute-start | bytes 589832 | tf_op jit(solution)/shard_map/ppermute | solution.py:177
  127.3 4.5 %copy-start.2 = (bf16[8,512,256]{2,1,0:T(8,128)(2,1)}, bf16[8,512,256]{2,1,0:T(8,128)(2,1)S(1)}, u32[]{:S(2)}) copy-start(bf16[8,512,256]{2,1,0:T(8,128)(2,1)S(1)} %all-to-all-done.3) | copy-start | bytes 6291460
  127.3 9.9 %collective-permute-start.10 = (bf16[8,4,128,256]{3,2,1,0:T(8,128)(2,1)S(1)}, bf16[8,4,128,256]{3,2,1,0:T(8,128)(2,1)}, u32[]{:S(2)}, u32[]{:S(2)}) collective-permute-start(bf16[8,4,128,256]{3,2,1,0:T(8,128)(2,1)S(1)} %bitcast.25), channel_id=1, source_target_pairs={{0,16},{16,0},{1,17},{17,1},{2,18},{18,2},{3,19},{19,3},{4,20},{20... | collective-permute-start | bytes 6291464 | tf_op jit(solution)/shard_map/ppermute | solution.py:188
  137.3 23.8 %copy-start.1 = (s32[18]{0:T(128)S(1)}, s32[18]{0:T(128)}, u32[]{:S(2)}) copy-start(s32[18]{0:T(128)} %pad_add_fusion.index) | copy-start | bytes 220

commit v9 on v8

--- a/solution.py
+++ b/solution.py
@@ -25,12 +25,18 @@
     return [(i, (i + by) % count) for i in range(count)]
 
 
+def apart():
+    return [
+        (z * 2 + c, (z + (2 if c == 0 else -2)) % NZ * 2 + c) for z in range(NZ) for c in range(2)
+    ]
+
+
 def spread(v, axes, count):
     return lax.all_to_all(jnp.broadcast_to(v[None], (count,) + v.shape), axes, 0, 0, tiled=True)
 
 
 def gate_kernel(first, index, *refs):
-    blocks, weights, refs = refs[: NZ + 1], refs[NZ + 1], refs[NZ + 2 :]
+    blocks, weights, refs = refs[:NZ], refs[NZ], refs[NZ + 1 :]
     if first:
         parts, a_buf, b_buf, acc, sums, a_sem, b_sem = refs
     else:
@@ -41,7 +47,6 @@
         pltpu.make_async_copy(weights.at[i], b_buf.at[:, i], b_sem.at[i]) for i in range(NX)
     ]
     places = [a_buf.at[index[s], index[NZ + s]] for s in range(NZ)]
-    places[-1:] = [places[-1].at[: rows // 2], places[-1].at[rows // 2 :]]
     a_copies = [
         pltpu.make_async_copy(h, to, a_sem.at[s]) for s, (h, to) in enumerate(zip(blocks, places))
     ]
@@ -158,8 +163,9 @@
         policy.reshape(8, 64, 256).transpose(1, 0, 2), DP, 0, 0, tiled=True
     )
     own = pieces.transpose(1, 0, 2).reshape(toks, NX * LANES)
-    for e in (1, 2):
-        own = jnp.concatenate([own, lax.ppermute(own, YL, [(i, i ^ e) for i in range(NYL)])])
+    own = jnp.concatenate(
+        [own] + [lax.ppermute(own, YL, [(i, i ^ e) for i in range(NYL)]) for e in range(1, NYL)]
+    )
     rows = own.shape[0]
     own, arrived = lax.optimization_barrier((own, arrived))
     policy_slice = arrived.reshape(ref_weight.shape)
@@ -172,19 +178,16 @@
     up = down = own
     for step in range(1, NZ // 2):
         if step == NZ // 2 - 1:
-            halves = (
-                lax.ppermute(up[: rows // 2], Z, shift(NZ, 2)),
-                lax.ppermute(down[rows // 2 :], Z, shift(NZ, -2)),
-            )
+            opposite = lax.ppermute(jnp.where(c == 0, up, down), Z + ("c",), apart())
         up = lax.ppermute(up, Z, shift(NZ, 1))
         down = lax.ppermute(down, Z, shift(NZ, -1))
         blocks += [up, down]
         offsets += [-step, step]
-    blocks += halves
+    blocks.append(opposite)
     offsets.append(NZ // 2)
     places = (z + jnp.array(offsets, jnp.int32)) & (NZ - 1)
     index = jnp.concatenate([places // NZL, places % NZL, jnp.stack([c, lax.axis_index(YL)])])
-    weights, index, *blocks[-4:] = lax.optimization_barrier((weights, index, *blocks[-4:]))
+    weights, index, *blocks[-3:] = lax.optimization_barrier((weights, index, *blocks[-3:]))
     others = lax.ppermute(weights, "c", shift(2, 1))
     parts = gate_parts(index, blocks, weights)
     parts = gate_parts(index, blocks, others, parts)

time: 165 us -> 164 us (level)
    ppermute x3, waiting for transfers between devices: 12.8 us -> 24.2 us  [body(): up = lax.ppermute(up, Z, shift(NZ, 1))]
    ppermute x2 -> x1, waiting for transfers between devices: 7.71 us -> 0.01 us  [body(): opposite = lax.ppermute(jnp.where(c == 0, up, down), Z + ('c',), apart())]
    ppermute x2 -> x3, waiting for transfers between devices: 12.7 us -> 7.63 us  [body(): lax.ppermute(own, YL, [(i, i ^ e) for i in range(NYL)])]
    ppermute x2 -> x1, starting transfers between devices: 7.37 us -> 4 us  [body(): opposite = lax.ppermute(jnp.where(c == 0, up, down), Z + ('c',), apart())]
    ppermute x3, starting transfers between devices: 6.1 us -> 8.49 us  [body(): up = lax.ppermute(up, Z, shift(NZ, 1))]
    ppermute x3, starting transfers between devices: 13.4 us -> 11 us  [body(): down = lax.ppermute(down, Z, shift(NZ, -1))]
    ppermute x2 -> x3, starting transfers between devices: 7.53 us -> 9.27 us  [body(): lax.ppermute(own, YL, [(i, i ^ e) for i in range(NYL)])]
  transfers between devices with their start and end apart: 13 -> 13, of which waited for: 6 -> 7; matrix products, arithmetic and copies ran while one was open for 1% -> 1% of each run, Pallas kernels for 3% -> 3%
where the time goes in v9:
time: 164 us; the launch traced here: 161 us
  starting transfers between devices  59.1 us (36%)
  blocking collectives  50.8 us (31%)
  waiting for transfers between devices  33.9 us (21%)
  Pallas kernels  12.1 us (7%)
  local copies, waits for them, and re-layouts  2.41 us (1%)
  other arithmetic  2.26 us (1%)
    ppermute x3, waiting for transfers between devices, body(): up = lax.ppermute(up, Z, shift(NZ, 1))  24.2 us
    all_to_all x1, blocking collectives, body(): pieces = lax.all_to_all(pieces, ('zl', 'y1'), 0, 0, tiled=True)  19.5 us
    all_to_all x1, blocking collectives, body(): lax.all_to_all(parts.reshape(4, *parts.shape[2:]), ('c', 'yh'), 0, 0, til...  17.5 us
    all_to_all x1, starting transfers between devices, body(): lax.all_to_all(policy.reshape(8, 64, 256).transpose(1, 0, 2), DP, 0, 0, t...  16.6 us
    all_to_all x1, blocking collectives, body(): pieces = lax.all_to_all(pieces, 'x', 0, 0, tiled=True)  13.8 us
    ppermute x3, starting transfers between devices, body(): down = lax.ppermute(down, Z, shift(NZ, -1))  11 us
    pallas_call x2, Pallas kernels, gate_parts(): pl.pallas_call(functools.partial(gate_kernel, first), out_shape=jax.Shape...  10.7 us
    ppermute x3, starting transfers between devices, body(): lax.ppermute(own, YL, [(i, i ^ e) for i in range(NYL)])  9.27 us
  transfers between devices with their start and end apart: 13, of which 7 were waited for; matrix products, arithmetic and copies ran while one was open for 1% of the time, Pallas kernels for 3%

profile of v9, /device:TPU:1, one launch (start us, length us, event | category | flops | bytes accessed | tf_op | source)
XLA Modules:
  0.0 161.5 jit_solution(885796473576955302)
XLA Ops:
  0.6 0.0 copy-start
  0.7 0.9 copy-done
  1.6 19.5 %all_to_all.25 = bf16[8,48,128]{2,1,0:T(8,128)(2,1)S(1)} all-to-all(bf16[8,48,128]{2,1,0:T(8,128)(2,1)S(1)} %bitcast.28), channel_id=1, replica_groups=mesh['zh'=2,'zl'=4,'y1'=2,'y0'=2,'c'=2,'yh'=2,'x'=8] {'zl','y1'}, dimensions={0} | all-to-all | bytes 196608 | tf_op jit(solution)/shard_map/all_to_all | solution.py:159
  21.0 13.8 %all_to_all.26 = bf16[8,48,128]{2,1,0:T(8,128)(2,1)S(1)} all-to-all(bf16[8,48,128]{2,1,0:T(8,128)(2,1)S(1)} %all_to_all.25), channel_id=1, replica_groups=mesh['zh'=2,'zl'=4,'y1'=2,'y0'=2,'c'=2,'yh'=2,'x'=8] {'x'}, dimensions={0} | all-to-all | bytes 196608 | tf_op jit(solution)/shard_map/all_to_all | solution.py:160
  34.9 16.6 %all-to-all-start.2 = ((bf16[64,8,256]{2,1,0:T(8,128)(2,1)}), bf16[64,8,256]{2,1,0:T(8,128)(2,1)S(1)}, u32[]{:S(2)}, u32[]{:S(2)}) async-start(bf16[64,8,256]{2,1,0:T(8,128)(2,1)} %bitcast.29), calls=%async_computation.2 | async-start | bytes 524288 | tf_op jit(solution)/shard_map/all_to_all | solution.py:162
  51.5 5.1 %collective-permute-start.2 = (bf16[48,1024]{1,0:T(8,128)(2,1)S(1)}, bf16[48,1024]{1,0:T(8,128)(2,1)S(1)}, u32[]{:S(2)}, u32[]{:S(2)}) collective-permute-start(bf16[48,1024]{1,0:T(8,128)(2,1)S(1)} %copy_bitcast_fusion), channel_id=1, source_target_pairs={{0,96},{32,64},{64,32},{96,0},{1,97},{33,65},{65,33},{97,1},{2,98}... | collective-permute-start | bytes 294920 | tf_op jit(solution)/shard_map/ppermute | solution.py:167
  56.6 1.9 %collective-permute-start.1 = (bf16[48,1024]{1,0:T(8,128)(2,1)S(1)}, bf16[48,1024]{1,0:T(8,128)(2,1)S(1)}, u32[]{:S(2)}, u32[]{:S(2)}) collective-permute-start(bf16[48,1024]{1,0:T(8,128)(2,1)S(1)} %copy_bitcast_fusion), channel_id=1, source_target_pairs={{0,64},{32,96},{64,0},{96,32},{1,65},{33,97},{65,1},{97,33},{2,66}... | collective-permute-start | bytes 294920 | tf_op jit(solution)/shard_map/ppermute | solution.py:167
  58.5 2.3 %collective-permute-start = (bf16[48,1024]{1,0:T(8,128)(2,1)S(1)}, bf16[48,1024]{1,0:T(8,128)(2,1)S(1)}, u32[]{:S(2)}, u32[]{:S(2)}) collective-permute-start(bf16[48,1024]{1,0:T(8,128)(2,1)S(1)} %copy_bitcast_fusion), channel_id=1, source_target_pairs={{0,32},{32,0},{64,96},{96,64},{1,33},{33,1},{65,97},{97,65},{2,34}... | collective-permute-start | bytes 294920 | tf_op jit(solution)/shard_map/ppermute | solution.py:167
  60.8 0.8 collective-permute-done.2
  61.6 6.8 %collective-permute-done.1 = bf16[48,1024]{1,0:T(8,128)(2,1)S(1)} collective-permute-done((bf16[48,1024]{1,0:T(8,128)(2,1)S(1)}, bf16[48,1024]{1,0:T(8,128)(2,1)S(1)}, u32[]{:S(2)}, u32[]{:S(2)}) %collective-permute-start.1) | collective-permute-done | bytes 98336 | tf_op jit(solution)/shard_map/ppermute | solution.py:167
  68.4 0.8 all-to-all-done.2
  69.3 0.8 multiply_convert_fusion
  70.1 1.5 broadcast_in_dim.2
  71.6 3.7 %all-to-all-start.3 = ((bf16[8,512,256]{2,1,0:T(8,128)(2,1)}), bf16[8,512,256]{2,1,0:T(8,128)(2,1)S(1)}, u32[]{:S(2)}, u32[]{:S(2)}) async-start(bf16[8,512,256]{2,1,0:T(8,128)(2,1)} %broadcast_in_dim.2), calls=%async_computation.3 | async-start | bytes 4194304 | tf_op jit(solution)/shard_map/all_to_all | solution.py:35
  75.3 2.3 %collective-permute-start.3 = (bf16[192,1024]{1,0:T(8,128)(2,1)S(1)}, bf16[192,1024]{1,0:T(8,128)(2,1)S(1)}, u32[]{:S(2)}, u32[]{:S(2)}) collective-permute-start(bf16[192,1024]{1,0:T(8,128)(2,1)S(1)} %pad_maximum_fusion.refs_0_), channel_id=1, source_target_pairs={{0,128},{128,256},{256,384},{384,512},{512,640},{640,768},{768,896... | collective-permute-start | bytes 1179656 | tf_op jit(solution)/shard_map/ppermute | solution.py:182
  77.6 4.2 %collective-permute-start.6 = (bf16[192,1024]{1,0:T(8,128)(2,1)S(1)}, bf16[192,1024]{1,0:T(8,128)(2,1)}, u32[]{:S(2)}, u32[]{:S(2)}) collective-permute-start(bf16[192,1024]{1,0:T(8,128)(2,1)S(1)} %pad_maximum_fusion.refs_0_), channel_id=1, source_target_pairs={{0,896},{128,0},{256,128},{384,256},{512,384},{640,512},{768,640},... | collective-permute-start | bytes 1179656 | tf_op jit(solution)/shard_map/ppermute | solution.py:183
  81.8 6.9 %collective-permute-done.3.refs_1_ = bf16[192,1024]{1,0:T(8,128)(2,1)S(1)} collective-permute-done((bf16[192,1024]{1,0:T(8,128)(2,1)S(1)}, bf16[192,1024]{1,0:T(8,128)(2,1)S(1)}, u32[]{:S(2)}, u32[]{:S(2)}) %collective-permute-start.3) | collective-permute-done | bytes 393248 | tf_op jit(solution)/shard_map/ppermute | solution.py:182
  88.7 1.9 %collective-permute-start.4 = (bf16[192,1024]{1,0:T(8,128)(2,1)S(1)}, bf16[192,1024]{1,0:T(8,128)(2,1)S(1)}, u32[]{:S(2)}, u32[]{:S(2)}) collective-permute-start(bf16[192,1024]{1,0:T(8,128)(2,1)S(1)} %collective-permute-done.3.refs_1_), channel_id=1, source_target_pairs={{0,128},{128,256},{256,384},{384,512},{512,640},{640,768},{768,896... | collective-permute-start | bytes 1179656 | tf_op jit(solution)/shard_map/ppermute | solution.py:182
  90.6 4.6 %collective-permute-start.7 = (bf16[192,1024]{1,0:T(8,128)(2,1)}, bf16[192,1024]{1,0:T(8,128)(2,1)S(1)}, u32[]{:S(2)}, u32[]{:S(2)}) collective-permute-start(bf16[192,1024]{1,0:T(8,128)(2,1)} %collective-permute-done.6.refs_2_), channel_id=1, source_target_pairs={{0,896},{128,0},{256,128},{384,256},{512,384},{640,512},{768,640},... | collective-permute-start | bytes 1179656 | tf_op jit(solution)/shard_map/ppermute | solution.py:183
  95.2 6.0 %collective-permute-done.4.refs_3_ = bf16[192,1024]{1,0:T(8,128)(2,1)S(1)} collective-permute-done((bf16[192,1024]{1,0:T(8,128)(2,1)S(1)}, bf16[192,1024]{1,0:T(8,128)(2,1)S(1)}, u32[]{:S(2)}, u32[]{:S(2)}) %collective-permute-start.4) | collective-permute-done | bytes 393248 | tf_op jit(solution)/shard_map/ppermute | solution.py:182
  101.2 1.2 collective-permute-done.7.refs_4_
  102.4 0.8 broadcast_select_fusion
  103.2 4.0 %collective-permute-start.9 = (bf16[192,1024]{1,0:T(8,128)(2,1)}, bf16[192,1024]{1,0:T(8,128)(2,1)}, u32[]{:S(2)}, u32[]{:S(2)}) collective-permute-start(bf16[192,1024]{1,0:T(8,128)(2,1)} %broadcast_select_fusion), channel_id=1, source_target_pairs={{0,256},{16,784},{128,384},{144,912},{256,512},{272,16},{384,640},... | collective-permute-start | bytes 1179656 | tf_op jit(solution)/shard_map/ppermute | solution.py:181
  107.3 4.3 %collective-permute-start.5 = (bf16[192,1024]{1,0:T(8,128)(2,1)S(1)}, bf16[192,1024]{1,0:T(8,128)(2,1)}, u32[]{:S(2)}, u32[]{:S(2)}) collective-permute-start(bf16[192,1024]{1,0:T(8,128)(2,1)S(1)} %collective-permute-done.4.refs_3_), channel_id=1, source_target_pairs={{0,128},{128,256},{256,384},{384,512},{512,640},{640,768},{768,896... | collective-permute-start | bytes 1179656 | tf_op jit(solution)/shard_map/ppermute | solution.py:182
  111.6 2.2 %collective-permute-start.8 = (bf16[192,1024]{1,0:T(8,128)(2,1)S(1)}, bf16[192,1024]{1,0:T(8,128)(2,1)}, u32[]{:S(2)}, u32[]{:S(2)}) collective-permute-start(bf16[192,1024]{1,0:T(8,128)(2,1)S(1)} %collective-permute-done.7.refs_4_), channel_id=1, source_target_pairs={{0,896},{128,0},{256,128},{384,256},{512,384},{640,512},{768,640},... | collective-permute-start | bytes 1179656 | tf_op jit(solution)/shard_map/ppermute | solution.py:183
  113.8 0.6 pad_add_fusion.index
  114.4 11.4 %collective-permute-done.5.refs_5_ = bf16[192,1024]{1,0:T(8,128)(2,1)} collective-permute-done((bf16[192,1024]{1,0:T(8,128)(2,1)S(1)}, bf16[192,1024]{1,0:T(8,128)(2,1)}, u32[]{:S(2)}, u32[]{:S(2)}) %collective-permute-start.5) | collective-permute-done | bytes 393248 | tf_op jit(solution)/shard_map/ppermute | solution.py:182
  125.8 6.0 %collective-permute-start.10 = (bf16[8,4,128,256]{3,2,1,0:T(8,128)(2,1)S(1)}, bf16[8,4,128,256]{3,2,1,0:T(8,128)(2,1)}, u32[]{:S(2)}, u32[]{:S(2)}) collective-permute-start(bf16[8,4,128,256]{3,2,1,0:T(8,128)(2,1)S(1)} %bitcast.25), channel_id=1, source_target_pairs={{0,16},{16,0},{1,17},{17,1},{2,18},{18,2},{3,19},{19,3},{4,20},{20... | collective-permute-start | bytes 6291464 | tf_op jit(solution)/shard_map/ppermute | solution.py:191
  131.8 5.4 %shard_map.68.refs_9_ = bf16[2,208,256]{2,1,0:T(8,128)(2,1)} custom-call(s32[18]{0:T(128)} %pad_add_fusion.index, bf16[192,1024]{1,0:T(8,128)(2,1)} %copy-done.3, bf16[192,1024]{1,0:T(8,128)(2,1)} %copy-done.6, bf16[192,1024]{1,0:T(8,128)(2,1)} %collective-permute-done.6.refs_2_, bf16[192,1024]{1,0:T(8,128)(2,1)} %copy-done.4, bf16[192,1024]{1,0:T(8,128)(2,1)} %copy-done.5, ...), custom_call_target="tpu_custom_call" | custom-call | flops 805306368 | bytes 7340032 | tf_op jit(solution)/shard_map/pallas_call | solution.py:99
  137.2 5.3 %shard_map.69 = bf16[2,2,208,256]{3,2,1,0:T(8,128)(2,1)} custom-call(s32[18]{0:T(128)} %pad_add_fusion.index, bf16[192,1024]{1,0:T(8,128)(2,1)} %copy-done.3, bf16[192,1024]{1,0:T(8,128)(2,1)} %copy-done.6, bf16[192,1024]{1,0:T(8,128)(2,1)} %collective-permute-done.6.refs_2_, bf16[192,1024]{1,0:T(8,128)(2,1)} %copy-done.4, bf16[192,1024]{1,0:T(8,128)(2,1)} %copy-done.5, ...), custom_call_target="tpu_custom_call" | custom-call | flops 805306368 | bytes 7340032 | tf_op jit(solution)/shard_map/pallas_call | solution.py:99
  142.5 17.5 %all_to_all.27.parts = bf16[4,208,256]{2,1,0:T(8,128)(2,1)S(1)} all-to-all(bf16[4,208,256]{2,1,0:T(8,128)(2,1)} %bitcast.27), channel_id=1, replica_groups=mesh['zh'=2,'zl'=4,'y1'=2,'y0'=2,'c'=2,'yh'=2,'x'=8] {'c','yh'}, dimensions={0} | all-to-all | bytes 851968 | tf_op jit(solution)/shard_map/all_to_all | solution.py:194
  160.1 1.4 shard_map.70
  (29 shorter events, 0.1 us)
Async XLA Ops:
  0.6 0.9 copy-start
  0.6 68.6 %copy-start.8 = (f32[512]{0:T(512)S(1)}, f32[512]{0:T(512)}, u32[]{:S(2)}) copy-start(f32[512]{0:T(512)} %param.8) | copy-start | bytes 6148
  1.5 67.7 %copy-start.7 = (bf16[512,256]{1,0:T(8,128)(2,1)S(1)}, bf16[512,256]{1,0:T(8,128)(2,1)}, u32[]{:S(2)}) copy-start(bf16[512,256]{1,0:T(8,128)(2,1)} %param.6) | copy-start | bytes 786436
  34.9 34.4 %all-to-all-start.2 = ((bf16[64,8,256]{2,1,0:T(8,128)(2,1)}), bf16[64,8,256]{2,1,0:T(8,128)(2,1)S(1)}, u32[]{:S(2)}, u32[]{:S(2)}) async-start(bf16[64,8,256]{2,1,0:T(8,128)(2,1)} %bitcast.29), calls=%async_computation.2 | async-start | bytes 524288 | tf_op jit(solution)/shard_map/all_to_all | solution.py:162
  51.5 10.1 %collective-permute-start.2 = (bf16[48,1024]{1,0:T(8,128)(2,1)S(1)}, bf16[48,1024]{1,0:T(8,128)(2,1)S(1)}, u32[]{:S(2)}, u32[]{:S(2)}) collective-permute-start(bf16[48,1024]{1,0:T(8,128)(2,1)S(1)} %copy_bitcast_fusion), channel_id=1, source_target_pairs={{0,96},{32,64},{64,32},{96,0},{1,97},{33,65},{65,33},{97,1},{2,98}... | collective-permute-start | bytes 294920 | tf_op jit(solution)/shard_map/ppermute | solution.py:167
  56.6 11.8 %collective-permute-start.1 = (bf16[48,1024]{1,0:T(8,128)(2,1)S(1)}, bf16[48,1024]{1,0:T(8,128)(2,1)S(1)}, u32[]{:S(2)}, u32[]{:S(2)}) collective-permute-start(bf16[48,1024]{1,0:T(8,128)(2,1)S(1)} %copy_bitcast_fusion), channel_id=1, source_target_pairs={{0,64},{32,96},{64,0},{96,32},{1,65},{33,97},{65,1},{97,33},{2,66}... | collective-permute-start | bytes 294920 | tf_op jit(solution)/shard_map/ppermute | solution.py:167
  58.5 9.9 %collective-permute-start = (bf16[48,1024]{1,0:T(8,128)(2,1)S(1)}, bf16[48,1024]{1,0:T(8,128)(2,1)S(1)}, u32[]{:S(2)}, u32[]{:S(2)}) collective-permute-start(bf16[48,1024]{1,0:T(8,128)(2,1)S(1)} %copy_bitcast_fusion), channel_id=1, source_target_pairs={{0,32},{32,0},{64,96},{96,64},{1,33},{33,1},{65,97},{97,65},{2,34}... | collective-permute-start | bytes 294920 | tf_op jit(solution)/shard_map/ppermute | solution.py:167
  68.4 9.2 %copy-start.3 = (bf16[192,1024]{1,0:T(8,128)(2,1)}, bf16[192,1024]{1,0:T(8,128)(2,1)S(1)}, u32[]{:S(2)}) copy-start(bf16[192,1024]{1,0:T(8,128)(2,1)S(1)} %pad_maximum_fusion.refs_0_) | copy-start | bytes 1179652
  71.5 42.2 %copy-start.9 = (s32[8]{0:T(128)S(1)}, s32[8]{0:T(128)}, u32[]{:S(2)}) copy-start(s32[8]{0:T(128)} %constant.60.clone) | copy-start | bytes 100
  71.6 54.2 %all-to-all-start.3 = ((bf16[8,512,256]{2,1,0:T(8,128)(2,1)}), bf16[8,512,256]{2,1,0:T(8,128)(2,1)S(1)}, u32[]{:S(2)}, u32[]{:S(2)}) async-start(bf16[8,512,256]{2,1,0:T(8,128)(2,1)} %broadcast_in_dim.2), calls=%async_computation.3 | async-start | bytes 4194304 | tf_op jit(solution)/shard_map/all_to_all | solution.py:35
  75.3 13.4 %collective-permute-start.3 = (bf16[192,1024]{1,0:T(8,128)(2,1)S(1)}, bf16[192,1024]{1,0:T(8,128)(2,1)S(1)}, u32[]{:S(2)}, u32[]{:S(2)}) collective-permute-start(bf16[192,1024]{1,0:T(8,128)(2,1)S(1)} %pad_maximum_fusion.refs_0_), channel_id=1, source_target_pairs={{0,128},{128,256},{256,384},{384,512},{512,640},{640,768},{768,896... | collective-permute-start | bytes 1179656 | tf_op jit(solution)/shard_map/ppermute | solution.py:182
  77.6 13.0 %collective-permute-start.6 = (bf16[192,1024]{1,0:T(8,128)(2,1)S(1)}, bf16[192,1024]{1,0:T(8,128)(2,1)}, u32[]{:S(2)}, u32[]{:S(2)}) collective-permute-start(bf16[192,1024]{1,0:T(8,128)(2,1)S(1)} %pad_maximum_fusion.refs_0_), channel_id=1, source_target_pairs={{0,896},{128,0},{256,128},{384,256},{512,384},{640,512},{768,640},... | collective-permute-start | bytes 1179656 | tf_op jit(solution)/shard_map/ppermute | solution.py:183
  88.7 43.1 %copy-start.6 = (bf16[192,1024]{1,0:T(8,128)(2,1)}, bf16[192,1024]{1,0:T(8,128)(2,1)S(1)}, u32[]{:S(2)}) copy-start(bf16[192,1024]{1,0:T(8,128)(2,1)S(1)} %collective-permute-done.3.refs_1_) | copy-start | bytes 1179652
  88.7 12.5 %collective-permute-start.4 = (bf16[192,1024]{1,0:T(8,128)(2,1)S(1)}, bf16[192,1024]{1,0:T(8,128)(2,1)S(1)}, u32[]{:S(2)}, u32[]{:S(2)}) collective-permute-start(bf16[192,1024]{1,0:T(8,128)(2,1)S(1)} %collective-permute-done.3.refs_1_), channel_id=1, source_target_pairs={{0,128},{128,256},{256,384},{384,512},{512,640},{640,768},{768,896... | collective-permute-start | bytes 1179656 | tf_op jit(solution)/shard_map/ppermute | solution.py:182
  90.6 11.8 %collective-permute-start.7 = (bf16[192,1024]{1,0:T(8,128)(2,1)}, bf16[192,1024]{1,0:T(8,128)(2,1)S(1)}, u32[]{:S(2)}, u32[]{:S(2)}) collective-permute-start(bf16[192,1024]{1,0:T(8,128)(2,1)} %collective-permute-done.6.refs_2_), channel_id=1, source_target_pairs={{0,896},{128,0},{256,128},{384,256},{512,384},{640,512},{768,640},... | collective-permute-start | bytes 1179656 | tf_op jit(solution)/shard_map/ppermute | solution.py:183
  101.2 30.6 %copy-start.4 = (bf16[192,1024]{1,0:T(8,128)(2,1)}, bf16[192,1024]{1,0:T(8,128)(2,1)S(1)}, u32[]{:S(2)}) copy-start(bf16[192,1024]{1,0:T(8,128)(2,1)S(1)} %collective-permute-done.4.refs_3_) | copy-start | bytes 1179652
  102.4 29.4 %copy-start.5 = (bf16[192,1024]{1,0:T(8,128)(2,1)}, bf16[192,1024]{1,0:T(8,128)(2,1)S(1)}, u32[]{:S(2)}) copy-start(bf16[192,1024]{1,0:T(8,128)(2,1)S(1)} %collective-permute-done.7.refs_4_) | copy-start | bytes 1179652
  103.2 22.5 %collective-permute-start.9 = (bf16[192,1024]{1,0:T(8,128)(2,1)}, bf16[192,1024]{1,0:T(8,128)(2,1)}, u32[]{:S(2)}, u32[]{:S(2)}) collective-permute-start(bf16[192,1024]{1,0:T(8,128)(2,1)} %broadcast_select_fusion), channel_id=1, source_target_pairs={{0,256},{16,784},{128,384},{144,912},{256,512},{272,16},{384,640},... | collective-permute-start | bytes 1179656 | tf_op jit(solution)/shard_map/ppermute | solution.py:181
  107.3 18.5 %collective-permute-start.5 = (bf16[192,1024]{1,0:T(8,128)(2,1)S(1)}, bf16[192,1024]{1,0:T(8,128)(2,1)}, u32[]{:S(2)}, u32[]{:S(2)}) collective-permute-start(bf16[192,1024]{1,0:T(8,128)(2,1)S(1)} %collective-permute-done.4.refs_3_), channel_id=1, source_target_pairs={{0,128},{128,256},{256,384},{384,512},{512,640},{640,768},{768,896... | collective-permute-start | bytes 1179656 | tf_op jit(solution)/shard_map/ppermute | solution.py:182
  111.6 14.2 %collective-permute-start.8 = (bf16[192,1024]{1,0:T(8,128)(2,1)S(1)}, bf16[192,1024]{1,0:T(8,128)(2,1)}, u32[]{:S(2)}, u32[]{:S(2)}) collective-permute-start(bf16[192,1024]{1,0:T(8,128)(2,1)S(1)} %collective-permute-done.7.refs_4_), channel_id=1, source_target_pairs={{0,896},{128,0},{256,128},{384,256},{512,384},{640,512},{768,640},... | collective-permute-start | bytes 1179656 | tf_op jit(solution)/shard_map/ppermute | solution.py:183
  125.7 6.1 %copy-start.2 = (bf16[8,512,256]{2,1,0:T(8,128)(2,1)}, bf16[8,512,256]{2,1,0:T(8,128)(2,1)S(1)}, u32[]{:S(2)}) copy-start(bf16[8,512,256]{2,1,0:T(8,128)(2,1)S(1)} %all-to-all-done.3) | copy-start | bytes 6291460
  125.8 11.5 %collective-permute-start.10 = (bf16[8,4,128,256]{3,2,1,0:T(8,128)(2,1)S(1)}, bf16[8,4,128,256]{3,2,1,0:T(8,128)(2,1)}, u32[]{:S(2)}, u32[]{:S(2)}) collective-permute-start(bf16[8,4,128,256]{3,2,1,0:T(8,128)(2,1)S(1)} %bitcast.25), channel_id=1, source_target_pairs={{0,16},{16,0},{1,17},{17,1},{2,18},{18,2},{3,19},{19,3},{4,20},{20... | collective-permute-start | bytes 6291464 | tf_op jit(solution)/shard_map/ppermute | solution.py:191
  137.2 22.8 %copy-start.1 = (s32[18]{0:T(128)S(1)}, s32[18]{0:T(128)}, u32[]{:S(2)}) copy-start(s32[18]{0:T(128)} %pad_add_fusion.index) | copy-start | bytes 220

commit v10 on v8

--- a/solution.py
+++ b/solution.py
@@ -158,8 +158,9 @@
         policy.reshape(8, 64, 256).transpose(1, 0, 2), DP, 0, 0, tiled=True
     )
     own = pieces.transpose(1, 0, 2).reshape(toks, NX * LANES)
-    for e in (1, 2):
-        own = jnp.concatenate([own, lax.ppermute(own, YL, [(i, i ^ e) for i in range(NYL)])])
+    own = jnp.concatenate(
+        [own] + [lax.ppermute(own, YL, [(i, i ^ e) for i in range(NYL)]) for e in range(1, NYL)]
+    )
     rows = own.shape[0]
     own, arrived = lax.optimization_barrier((own, arrived))
     policy_slice = arrived.reshape(ref_weight.shape)

time: 165 us -> 162 us (0.982)
  waiting for transfers between devices: 34.1 us -> 28.9 us
  starting transfers between devices: 58.3 us -> 60.9 us
    ppermute x2 -> x3, waiting for transfers between devices: 12.7 us -> 7.63 us  [body(): lax.ppermute(own, YL, [(i, i ^ e) for i in range(NYL)])]
    ppermute x2 -> x3, starting transfers between devices: 7.53 us -> 9.27 us  [body(): lax.ppermute(own, YL, [(i, i ^ e) for i in range(NYL)])]
  transfers between devices with their start and end apart: 13 -> 14, of which waited for: 6 -> 7; matrix products, arithmetic and copies ran while one was open for 1% -> 1% of each run, Pallas kernels for 3% -> 3%
where the time goes in v10:
time: 162 us; the launch traced here: 159 us
  starting transfers between devices  60.9 us (38%)
  blocking collectives  50.6 us (31%)
  waiting for transfers between devices  28.9 us (18%)
  Pallas kernels  12.1 us (7%)
  local copies, waits for them, and re-layouts  3.78 us (2%)
    all_to_all x1, blocking collectives, body(): pieces = lax.all_to_all(pieces, ('zl', 'y1'), 0, 0, tiled=True)  19.5 us
    all_to_all x1, blocking collectives, body(): lax.all_to_all(parts.reshape(4, *parts.shape[2:]), ('c', 'yh'), 0, 0, til...  17.3 us
    all_to_all x1, starting transfers between devices, body(): lax.all_to_all(policy.reshape(8, 64, 256).transpose(1, 0, 2), DP, 0, 0, t...  16.6 us
    all_to_all x1, blocking collectives, body(): pieces = lax.all_to_all(pieces, 'x', 0, 0, tiled=True)  13.8 us
    ppermute x3, starting transfers between devices, body(): down = lax.ppermute(down, Z, shift(NZ, -1))  13.4 us
    ppermute x3, waiting for transfers between devices, body(): up = lax.ppermute(up, Z, shift(NZ, 1))  12.8 us
    pallas_call x2, Pallas kernels, gate_parts(): pl.pallas_call(functools.partial(gate_kernel, first), out_shape=jax.Shape...  10.7 us
    ppermute x3, starting transfers between devices, body(): lax.ppermute(own, YL, [(i, i ^ e) for i in range(NYL)])  9.27 us
  transfers between devices with their start and end apart: 14, of which 7 were waited for; matrix products, arithmetic and copies ran while one was open for 1% of the time, Pallas kernels for 3%

profile of v10, /device:TPU:1, one launch (start us, length us, event | category | flops | bytes accessed | tf_op | source)
XLA Modules:
  0.0 158.8 jit_solution(13290432288342607805)
XLA Ops:
  0.7 0.9 copy-done
  1.6 19.5 %all_to_all.25 = bf16[8,48,128]{2,1,0:T(8,128)(2,1)S(1)} all-to-all(bf16[8,48,128]{2,1,0:T(8,128)(2,1)S(1)} %bitcast.28), channel_id=1, replica_groups=mesh['zh'=2,'zl'=4,'y1'=2,'y0'=2,'c'=2,'yh'=2,'x'=8] {'zl','y1'}, dimensions={0} | all-to-all | bytes 196608 | tf_op jit(solution)/shard_map/all_to_all | solution.py:154
  21.0 13.8 %all_to_all.26 = bf16[8,48,128]{2,1,0:T(8,128)(2,1)S(1)} all-to-all(bf16[8,48,128]{2,1,0:T(8,128)(2,1)S(1)} %all_to_all.25), channel_id=1, replica_groups=mesh['zh'=2,'zl'=4,'y1'=2,'y0'=2,'c'=2,'yh'=2,'x'=8] {'x'}, dimensions={0} | all-to-all | bytes 196608 | tf_op jit(solution)/shard_map/all_to_all | solution.py:155
  34.9 16.6 %all-to-all-start.2 = ((bf16[64,8,256]{2,1,0:T(8,128)(2,1)}), bf16[64,8,256]{2,1,0:T(8,128)(2,1)S(1)}, u32[]{:S(2)}, u32[]{:S(2)}) async-start(bf16[64,8,256]{2,1,0:T(8,128)(2,1)} %bitcast.29), calls=%async_computation.2 | async-start | bytes 524288 | tf_op jit(solution)/shard_map/all_to_all | solution.py:157
  51.5 5.1 %collective-permute-start.2 = (bf16[48,1024]{1,0:T(8,128)(2,1)S(1)}, bf16[48,1024]{1,0:T(8,128)(2,1)S(1)}, u32[]{:S(2)}, u32[]{:S(2)}) collective-permute-start(bf16[48,1024]{1,0:T(8,128)(2,1)S(1)} %copy_bitcast_fusion), channel_id=1, source_target_pairs={{0,96},{32,64},{64,32},{96,0},{1,97},{33,65},{65,33},{97,1},{2,98}... | collective-permute-start | bytes 294920 | tf_op jit(solution)/shard_map/ppermute | solution.py:162
  56.6 1.9 %collective-permute-start.1 = (bf16[48,1024]{1,0:T(8,128)(2,1)S(1)}, bf16[48,1024]{1,0:T(8,128)(2,1)S(1)}, u32[]{:S(2)}, u32[]{:S(2)}) collective-permute-start(bf16[48,1024]{1,0:T(8,128)(2,1)S(1)} %copy_bitcast_fusion), channel_id=1, source_target_pairs={{0,64},{32,96},{64,0},{96,32},{1,65},{33,97},{65,1},{97,33},{2,66}... | collective-permute-start | bytes 294920 | tf_op jit(solution)/shard_map/ppermute | solution.py:162
  58.5 2.3 %collective-permute-start = (bf16[48,1024]{1,0:T(8,128)(2,1)S(1)}, bf16[48,1024]{1,0:T(8,128)(2,1)S(1)}, u32[]{:S(2)}, u32[]{:S(2)}) collective-permute-start(bf16[48,1024]{1,0:T(8,128)(2,1)S(1)} %copy_bitcast_fusion), channel_id=1, source_target_pairs={{0,32},{32,0},{64,96},{96,64},{1,33},{33,1},{65,97},{97,65},{2,34}... | collective-permute-start | bytes 294920 | tf_op jit(solution)/shard_map/ppermute | solution.py:162
  60.8 0.8 collective-permute-done.2
  61.6 6.8 %collective-permute-done.1 = bf16[48,1024]{1,0:T(8,128)(2,1)S(1)} collective-permute-done((bf16[48,1024]{1,0:T(8,128)(2,1)S(1)}, bf16[48,1024]{1,0:T(8,128)(2,1)S(1)}, u32[]{:S(2)}, u32[]{:S(2)}) %collective-permute-start.1) | collective-permute-done | bytes 98336 | tf_op jit(solution)/shard_map/ppermute | solution.py:162
  68.4 0.8 all-to-all-done.2
  69.3 0.8 multiply_convert_fusion
  70.1 1.5 broadcast_in_dim.2
  71.6 3.7 %all-to-all-start.3 = ((bf16[8,512,256]{2,1,0:T(8,128)(2,1)}), bf16[8,512,256]{2,1,0:T(8,128)(2,1)S(1)}, u32[]{:S(2)}, u32[]{:S(2)}) async-start(bf16[8,512,256]{2,1,0:T(8,128)(2,1)} %broadcast_in_dim.2), calls=%async_computation.3 | async-start | bytes 4194304 | tf_op jit(solution)/shard_map/all_to_all | solution.py:29
  75.3 2.3 %collective-permute-start.3 = (bf16[192,1024]{1,0:T(8,128)(2,1)S(1)}, bf16[192,1024]{1,0:T(8,128)(2,1)S(1)}, u32[]{:S(2)}, u32[]{:S(2)}) collective-permute-start(bf16[192,1024]{1,0:T(8,128)(2,1)S(1)} %pad_maximum_fusion.refs_0_), channel_id=1, source_target_pairs={{0,128},{128,256},{256,384},{384,512},{512,640},{640,768},{768,896... | collective-permute-start | bytes 1179656 | tf_op jit(solution)/shard_map/ppermute | solution.py:180
  77.6 4.2 %collective-permute-start.6 = (bf16[192,1024]{1,0:T(8,128)(2,1)S(1)}, bf16[192,1024]{1,0:T(8,128)(2,1)}, u32[]{:S(2)}, u32[]{:S(2)}) collective-permute-start(bf16[192,1024]{1,0:T(8,128)(2,1)S(1)} %pad_maximum_fusion.refs_0_), channel_id=1, source_target_pairs={{0,896},{128,0},{256,128},{384,256},{512,384},{640,512},{768,640},... | collective-permute-start | bytes 1179656 | tf_op jit(solution)/shard_map/ppermute | solution.py:181
  81.8 6.9 %collective-permute-done.3.refs_1_ = bf16[192,1024]{1,0:T(8,128)(2,1)S(1)} collective-permute-done((bf16[192,1024]{1,0:T(8,128)(2,1)S(1)}, bf16[192,1024]{1,0:T(8,128)(2,1)S(1)}, u32[]{:S(2)}, u32[]{:S(2)}) %collective-permute-start.3) | collective-permute-done | bytes 393248 | tf_op jit(solution)/shard_map/ppermute | solution.py:180
  88.7 1.9 %collective-permute-start.4 = (bf16[192,1024]{1,0:T(8,128)(2,1)S(1)}, bf16[192,1024]{1,0:T(8,128)(2,1)S(1)}, u32[]{:S(2)}, u32[]{:S(2)}) collective-permute-start(bf16[192,1024]{1,0:T(8,128)(2,1)S(1)} %collective-permute-done.3.refs_1_), channel_id=1, source_target_pairs={{0,128},{128,256},{256,384},{384,512},{512,640},{640,768},{768,896... | collective-permute-start | bytes 1179656 | tf_op jit(solution)/shard_map/ppermute | solution.py:180
  90.6 4.6 %collective-permute-start.7 = (bf16[192,1024]{1,0:T(8,128)(2,1)}, bf16[192,1024]{1,0:T(8,128)(2,1)S(1)}, u32[]{:S(2)}, u32[]{:S(2)}) collective-permute-start(bf16[192,1024]{1,0:T(8,128)(2,1)} %collective-permute-done.6.refs_2_), channel_id=1, source_target_pairs={{0,896},{128,0},{256,128},{384,256},{512,384},{640,512},{768,640},... | collective-permute-start | bytes 1179656 | tf_op jit(solution)/shard_map/ppermute | solution.py:181
  95.2 6.0 %collective-permute-done.4.refs_3_ = bf16[192,1024]{1,0:T(8,128)(2,1)S(1)} collective-permute-done((bf16[192,1024]{1,0:T(8,128)(2,1)S(1)}, bf16[192,1024]{1,0:T(8,128)(2,1)S(1)}, u32[]{:S(2)}, u32[]{:S(2)}) %collective-permute-start.4) | collective-permute-done | bytes 393248 | tf_op jit(solution)/shard_map/ppermute | solution.py:180
  101.2 1.9 %collective-permute-start.5 = (bf16[192,1024]{1,0:T(8,128)(2,1)S(1)}, bf16[192,1024]{1,0:T(8,128)(2,1)}, u32[]{:S(2)}, u32[]{:S(2)}) collective-permute-start(bf16[192,1024]{1,0:T(8,128)(2,1)S(1)} %collective-permute-done.4.refs_3_), channel_id=1, source_target_pairs={{0,128},{128,256},{256,384},{384,512},{512,640},{640,768},{768,896... | collective-permute-start | bytes 1179656 | tf_op jit(solution)/shard_map/ppermute | solution.py:180
  103.1 4.6 %collective-permute-start.8 = (bf16[192,1024]{1,0:T(8,128)(2,1)S(1)}, bf16[192,1024]{1,0:T(8,128)(2,1)}, u32[]{:S(2)}, u32[]{:S(2)}) collective-permute-start(bf16[192,1024]{1,0:T(8,128)(2,1)S(1)} %collective-permute-done.7.refs_4_), channel_id=1, source_target_pairs={{0,896},{128,0},{256,128},{384,256},{512,384},{640,512},{768,640},... | collective-permute-start | bytes 1179656 | tf_op jit(solution)/shard_map/ppermute | solution.py:181
  107.7 0.7 slice.8
  108.4 1.9 %collective-permute-start.9 = (bf16[96,1024]{1,0:T(8,128)(2,1)}, bf16[96,1024]{1,0:T(8,128)(2,1)}, u32[]{:S(2)}, u32[]{:S(2)}) collective-permute-start(bf16[96,1024]{1,0:T(8,128)(2,1)} %slice.8), channel_id=1, source_target_pairs={{0,256},{128,384},{256,512},{384,640},{512,768},{640,896},{768,0},... | collective-permute-start | bytes 589832 | tf_op jit(solution)/shard_map/ppermute | solution.py:177
  110.3 0.7 slice.9
  111.0 5.5 %collective-permute-start.10 = (bf16[96,1024]{1,0:T(8,128)(2,1)}, bf16[96,1024]{1,0:T(8,128)(2,1)}, u32[]{:S(2)}, u32[]{:S(2)}) collective-permute-start(bf16[96,1024]{1,0:T(8,128)(2,1)} %slice.9), channel_id=1, source_target_pairs={{0,768},{128,896},{256,0},{384,128},{512,256},{640,384},{768,512},... | collective-permute-start | bytes 589832 | tf_op jit(solution)/shard_map/ppermute | solution.py:178
  117.2 3.9 %collective-permute-done.9.refs_7_ = bf16[96,1024]{1,0:T(8,128)(2,1)} collective-permute-done((bf16[96,1024]{1,0:T(8,128)(2,1)}, bf16[96,1024]{1,0:T(8,128)(2,1)}, u32[]{:S(2)}, u32[]{:S(2)}) %collective-permute-start.9) | collective-permute-done | bytes 196640 | tf_op jit(solution)/shard_map/ppermute | solution.py:177
  121.1 3.7 %collective-permute-done.10.refs_8_ = bf16[96,1024]{1,0:T(8,128)(2,1)} collective-permute-done((bf16[96,1024]{1,0:T(8,128)(2,1)}, bf16[96,1024]{1,0:T(8,128)(2,1)}, u32[]{:S(2)}, u32[]{:S(2)}) %collective-permute-start.10) | collective-permute-done | bytes 196640 | tf_op jit(solution)/shard_map/ppermute | solution.py:178
  124.8 4.5 %collective-permute-start.11 = (bf16[8,4,128,256]{3,2,1,0:T(8,128)(2,1)S(1)}, bf16[8,4,128,256]{3,2,1,0:T(8,128)(2,1)}, u32[]{:S(2)}, u32[]{:S(2)}) collective-permute-start(bf16[8,4,128,256]{3,2,1,0:T(8,128)(2,1)S(1)} %bitcast.25), channel_id=1, source_target_pairs={{0,16},{16,0},{1,17},{17,1},{2,18},{18,2},{3,19},{19,3},{4,20},{20... | collective-permute-start | bytes 6291464 | tf_op jit(solution)/shard_map/ppermute | solution.py:189
  129.4 5.4 %shard_map.68.refs_10_ = bf16[2,208,256]{2,1,0:T(8,128)(2,1)} custom-call(s32[18]{0:T(128)} %pad_add_fusion.index, bf16[192,1024]{1,0:T(8,128)(2,1)} %copy-done.3, bf16[192,1024]{1,0:T(8,128)(2,1)} %copy-done.6, bf16[192,1024]{1,0:T(8,128)(2,1)} %collective-permute-done.6.refs_2_, bf16[192,1024]{1,0:T(8,128)(2,1)} %copy-done.4, bf16[192,1024]{1,0:T(8,128)(2,1)} %copy-done.5, ...), custom_call_target="tpu_custom_call" | custom-call | flops 805306368 | bytes 7340032 | tf_op jit(solution)/shard_map/pallas_call | solution.py:94
  134.8 5.3 %shard_map.69 = bf16[2,2,208,256]{3,2,1,0:T(8,128)(2,1)} custom-call(s32[18]{0:T(128)} %pad_add_fusion.index, bf16[192,1024]{1,0:T(8,128)(2,1)} %copy-done.3, bf16[192,1024]{1,0:T(8,128)(2,1)} %copy-done.6, bf16[192,1024]{1,0:T(8,128)(2,1)} %collective-permute-done.6.refs_2_, bf16[192,1024]{1,0:T(8,128)(2,1)} %copy-done.4, bf16[192,1024]{1,0:T(8,128)(2,1)} %copy-done.5, ...), custom_call_target="tpu_custom_call" | custom-call | flops 805306368 | bytes 7340032 | tf_op jit(solution)/shard_map/pallas_call | solution.py:94
  140.1 17.3 %all_to_all.27.parts = bf16[4,208,256]{2,1,0:T(8,128)(2,1)S(1)} all-to-all(bf16[4,208,256]{2,1,0:T(8,128)(2,1)} %bitcast.27), channel_id=1, replica_groups=mesh['zh'=2,'zl'=4,'y1'=2,'y0'=2,'c'=2,'yh'=2,'x'=8] {'c','yh'}, dimensions={0} | all-to-all | bytes 851968 | tf_op jit(solution)/shard_map/all_to_all | solution.py:192
  157.4 1.4 shard_map.70
  (32 shorter events, 0.8 us)
Async XLA Ops:
  0.6 0.9 copy-start
  0.6 68.6 %copy-start.8 = (f32[512]{0:T(512)S(1)}, f32[512]{0:T(512)}, u32[]{:S(2)}) copy-start(f32[512]{0:T(512)} %param.8) | copy-start | bytes 6148
  1.5 67.7 %copy-start.7 = (bf16[512,256]{1,0:T(8,128)(2,1)S(1)}, bf16[512,256]{1,0:T(8,128)(2,1)}, u32[]{:S(2)}) copy-start(bf16[512,256]{1,0:T(8,128)(2,1)} %param.6) | copy-start | bytes 786436
  34.9 34.4 %all-to-all-start.2 = ((bf16[64,8,256]{2,1,0:T(8,128)(2,1)}), bf16[64,8,256]{2,1,0:T(8,128)(2,1)S(1)}, u32[]{:S(2)}, u32[]{:S(2)}) async-start(bf16[64,8,256]{2,1,0:T(8,128)(2,1)} %bitcast.29), calls=%async_computation.2 | async-start | bytes 524288 | tf_op jit(solution)/shard_map/all_to_all | solution.py:157
  51.5 10.1 %collective-permute-start.2 = (bf16[48,1024]{1,0:T(8,128)(2,1)S(1)}, bf16[48,1024]{1,0:T(8,128)(2,1)S(1)}, u32[]{:S(2)}, u32[]{:S(2)}) collective-permute-start(bf16[48,1024]{1,0:T(8,128)(2,1)S(1)} %copy_bitcast_fusion), channel_id=1, source_target_pairs={{0,96},{32,64},{64,32},{96,0},{1,97},{33,65},{65,33},{97,1},{2,98}... | collective-permute-start | bytes 294920 | tf_op jit(solution)/shard_map/ppermute | solution.py:162
  56.6 11.8 %collective-permute-start.1 = (bf16[48,1024]{1,0:T(8,128)(2,1)S(1)}, bf16[48,1024]{1,0:T(8,128)(2,1)S(1)}, u32[]{:S(2)}, u32[]{:S(2)}) collective-permute-start(bf16[48,1024]{1,0:T(8,128)(2,1)S(1)} %copy_bitcast_fusion), channel_id=1, source_target_pairs={{0,64},{32,96},{64,0},{96,32},{1,65},{33,97},{65,1},{97,33},{2,66}... | collective-permute-start | bytes 294920 | tf_op jit(solution)/shard_map/ppermute | solution.py:162
  58.5 9.9 %collective-permute-start = (bf16[48,1024]{1,0:T(8,128)(2,1)S(1)}, bf16[48,1024]{1,0:T(8,128)(2,1)S(1)}, u32[]{:S(2)}, u32[]{:S(2)}) collective-permute-start(bf16[48,1024]{1,0:T(8,128)(2,1)S(1)} %copy_bitcast_fusion), channel_id=1, source_target_pairs={{0,32},{32,0},{64,96},{96,64},{1,33},{33,1},{65,97},{97,65},{2,34}... | collective-permute-start | bytes 294920 | tf_op jit(solution)/shard_map/ppermute | solution.py:162
  68.4 9.2 %copy-start.3 = (bf16[192,1024]{1,0:T(8,128)(2,1)}, bf16[192,1024]{1,0:T(8,128)(2,1)S(1)}, u32[]{:S(2)}) copy-start(bf16[192,1024]{1,0:T(8,128)(2,1)S(1)} %pad_maximum_fusion.refs_0_) | copy-start | bytes 1179652
  71.6 36.1 %copy-start.9 = (s32[8]{0:T(128)S(1)}, s32[8]{0:T(128)}, u32[]{:S(2)}) copy-start(s32[8]{0:T(128)} %constant.59.clone) | copy-start | bytes 100
  71.6 53.2 %all-to-all-start.3 = ((bf16[8,512,256]{2,1,0:T(8,128)(2,1)}), bf16[8,512,256]{2,1,0:T(8,128)(2,1)S(1)}, u32[]{:S(2)}, u32[]{:S(2)}) async-start(bf16[8,512,256]{2,1,0:T(8,128)(2,1)} %broadcast_in_dim.2), calls=%async_computation.3 | async-start | bytes 4194304 | tf_op jit(solution)/shard_map/all_to_all | solution.py:29
  75.3 13.4 %collective-permute-start.3 = (bf16[192,1024]{1,0:T(8,128)(2,1)S(1)}, bf16[192,1024]{1,0:T(8,128)(2,1)S(1)}, u32[]{:S(2)}, u32[]{:S(2)}) collective-permute-start(bf16[192,1024]{1,0:T(8,128)(2,1)S(1)} %pad_maximum_fusion.refs_0_), channel_id=1, source_target_pairs={{0,128},{128,256},{256,384},{384,512},{512,640},{640,768},{768,896... | collective-permute-start | bytes 1179656 | tf_op jit(solution)/shard_map/ppermute | solution.py:180
  77.6 13.0 %collective-permute-start.6 = (bf16[192,1024]{1,0:T(8,128)(2,1)S(1)}, bf16[192,1024]{1,0:T(8,128)(2,1)}, u32[]{:S(2)}, u32[]{:S(2)}) collective-permute-start(bf16[192,1024]{1,0:T(8,128)(2,1)S(1)} %pad_maximum_fusion.refs_0_), channel_id=1, source_target_pairs={{0,896},{128,0},{256,128},{384,256},{512,384},{640,512},{768,640},... | collective-permute-start | bytes 1179656 | tf_op jit(solution)/shard_map/ppermute | solution.py:181
  88.7 40.6 %copy-start.6 = (bf16[192,1024]{1,0:T(8,128)(2,1)}, bf16[192,1024]{1,0:T(8,128)(2,1)S(1)}, u32[]{:S(2)}) copy-start(bf16[192,1024]{1,0:T(8,128)(2,1)S(1)} %collective-permute-done.3.refs_1_) | copy-start | bytes 1179652
  88.7 12.5 %collective-permute-start.4 = (bf16[192,1024]{1,0:T(8,128)(2,1)S(1)}, bf16[192,1024]{1,0:T(8,128)(2,1)S(1)}, u32[]{:S(2)}, u32[]{:S(2)}) collective-permute-start(bf16[192,1024]{1,0:T(8,128)(2,1)S(1)} %collective-permute-done.3.refs_1_), channel_id=1, source_target_pairs={{0,128},{128,256},{256,384},{384,512},{512,640},{640,768},{768,896... | collective-permute-start | bytes 1179656 | tf_op jit(solution)/shard_map/ppermute | solution.py:180
  90.6 12.5 %collective-permute-start.7 = (bf16[192,1024]{1,0:T(8,128)(2,1)}, bf16[192,1024]{1,0:T(8,128)(2,1)S(1)}, u32[]{:S(2)}, u32[]{:S(2)}) collective-permute-start(bf16[192,1024]{1,0:T(8,128)(2,1)} %collective-permute-done.6.refs_2_), channel_id=1, source_target_pairs={{0,896},{128,0},{256,128},{384,256},{512,384},{640,512},{768,640},... | collective-permute-start | bytes 1179656 | tf_op jit(solution)/shard_map/ppermute | solution.py:181
  101.2 28.2 %copy-start.4 = (bf16[192,1024]{1,0:T(8,128)(2,1)}, bf16[192,1024]{1,0:T(8,128)(2,1)S(1)}, u32[]{:S(2)}) copy-start(bf16[192,1024]{1,0:T(8,128)(2,1)S(1)} %collective-permute-done.4.refs_3_) | copy-start | bytes 1179652
  101.2 23.6 %collective-permute-start.5 = (bf16[192,1024]{1,0:T(8,128)(2,1)S(1)}, bf16[192,1024]{1,0:T(8,128)(2,1)}, u32[]{:S(2)}, u32[]{:S(2)}) collective-permute-start(bf16[192,1024]{1,0:T(8,128)(2,1)S(1)} %collective-permute-done.4.refs_3_), channel_id=1, source_target_pairs={{0,128},{128,256},{256,384},{384,512},{512,640},{640,768},{768,896... | collective-permute-start | bytes 1179656 | tf_op jit(solution)/shard_map/ppermute | solution.py:180
  103.1 26.2 %copy-start.5 = (bf16[192,1024]{1,0:T(8,128)(2,1)}, bf16[192,1024]{1,0:T(8,128)(2,1)S(1)}, u32[]{:S(2)}) copy-start(bf16[192,1024]{1,0:T(8,128)(2,1)S(1)} %collective-permute-done.7.refs_4_) | copy-start | bytes 1179652
  103.1 21.7 %collective-permute-start.8 = (bf16[192,1024]{1,0:T(8,128)(2,1)S(1)}, bf16[192,1024]{1,0:T(8,128)(2,1)}, u32[]{:S(2)}, u32[]{:S(2)}) collective-permute-start(bf16[192,1024]{1,0:T(8,128)(2,1)S(1)} %collective-permute-done.7.refs_4_), channel_id=1, source_target_pairs={{0,896},{128,0},{256,128},{384,256},{512,384},{640,512},{768,640},... | collective-permute-start | bytes 1179656 | tf_op jit(solution)/shard_map/ppermute | solution.py:181
  108.4 12.7 %collective-permute-start.9 = (bf16[96,1024]{1,0:T(8,128)(2,1)}, bf16[96,1024]{1,0:T(8,128)(2,1)}, u32[]{:S(2)}, u32[]{:S(2)}) collective-permute-start(bf16[96,1024]{1,0:T(8,128)(2,1)} %slice.8), channel_id=1, source_target_pairs={{0,256},{128,384},{256,512},{384,640},{512,768},{640,896},{768,0},... | collective-permute-start | bytes 589832 | tf_op jit(solution)/shard_map/ppermute | solution.py:177
  111.0 13.8 %collective-permute-start.10 = (bf16[96,1024]{1,0:T(8,128)(2,1)}, bf16[96,1024]{1,0:T(8,128)(2,1)}, u32[]{:S(2)}, u32[]{:S(2)}) collective-permute-start(bf16[96,1024]{1,0:T(8,128)(2,1)} %slice.9), channel_id=1, source_target_pairs={{0,768},{128,896},{256,0},{384,128},{512,256},{640,384},{768,512},... | collective-permute-start | bytes 589832 | tf_op jit(solution)/shard_map/ppermute | solution.py:178
  124.8 4.6 %copy-start.2 = (bf16[8,512,256]{2,1,0:T(8,128)(2,1)}, bf16[8,512,256]{2,1,0:T(8,128)(2,1)S(1)}, u32[]{:S(2)}) copy-start(bf16[8,512,256]{2,1,0:T(8,128)(2,1)S(1)} %all-to-all-done.3) | copy-start | bytes 6291460
  124.8 9.9 %collective-permute-start.11 = (bf16[8,4,128,256]{3,2,1,0:T(8,128)(2,1)S(1)}, bf16[8,4,128,256]{3,2,1,0:T(8,128)(2,1)}, u32[]{:S(2)}, u32[]{:S(2)}) collective-permute-start(bf16[8,4,128,256]{3,2,1,0:T(8,128)(2,1)S(1)} %bitcast.25), channel_id=1, source_target_pairs={{0,16},{16,0},{1,17},{17,1},{2,18},{18,2},{3,19},{19,3},{4,20},{20... | collective-permute-start | bytes 6291464 | tf_op jit(solution)/shard_map/ppermute | solution.py:189
  134.7 22.6 %copy-start.1 = (s32[18]{0:T(128)S(1)}, s32[18]{0:T(128)}, u32[]{:S(2)}) copy-start(s32[18]{0:T(128)} %pad_add_fusion.index) | copy-start | bytes 220

commit v11 on v10

--- a/solution.py
+++ b/solution.py
@@ -153,10 +153,16 @@
     pieces = pieces.reshape(NZL * micro, toks, LANES)
     pieces = lax.all_to_all(pieces, ("zl", "y1"), 0, 0, tiled=True)
     pieces = lax.all_to_all(pieces, "x", 0, 0, tiled=True)
+    first = c == 0
+    policy = policy.reshape(8, 64, 256).transpose(1, 0, 2).reshape(32, 2, 8, 256)
+    kept = lax.dynamic_index_in_dim(policy, c, 1, keepdims=False)
+    swapped = lax.dynamic_index_in_dim(policy, 1 - c, 1, keepdims=False)
+    swapped = lax.ppermute(swapped, "c", shift(2, 1))
+    policy = jnp.stack(
+        [jnp.where(first, kept, swapped), jnp.where(first, swapped, kept)], axis=1
+    ).reshape(32, 16, 256)
     pieces, policy = lax.optimization_barrier((pieces, policy))
-    arrived = lax.all_to_all(
-        policy.reshape(8, 64, 256).transpose(1, 0, 2), DP, 0, 0, tiled=True
-    )
+    arrived = lax.all_to_all(policy, Z + YL, 0, 0, tiled=True)
     own = pieces.transpose(1, 0, 2).reshape(toks, NX * LANES)
     own = jnp.concatenate(
         [own] + [lax.ppermute(own, YL, [(i, i ^ e) for i in range(NYL)]) for e in range(1, NYL)]

time: 162 us -> 156 us (0.963); the launches traced: 159 us -> 155 us
  blocking collectives: 50.6 us -> 18.4 us
  starting transfers between devices: 60.9 us -> 80.2 us
  waiting for transfers between devices: 28.9 us -> 34.9 us
    all_to_all x2 -> x0, blocking collectives: 33.3 us -> none  [the longest x1 19.5 us: body(): pieces = lax.all_to_all(pieces, ('zl', 'y1'), 0, 0, tiled=True)]
    all_to_all x1 -> x3, starting transfers between devices: 16.6 us -> 30.6 us  [the longest x1 12.8 us: body(): pieces = lax.all_to_all(pieces, ('zl', 'y1'), 0, 0, tiled=True)]
    all_to_all x1, waiting for transfers between devices: 0.01 us -> 7.44 us  [spread(): lax.all_to_all(jnp.broadcast_to(v[None], (count,) + v.shape), axes, 0, 0,...]
    ppermute x0 -> x1, starting transfers between devices: none -> 7.27 us  [body(): swapped = lax.ppermute(swapped, 'c', shift(2, 1))]
    all_to_all x1 -> x3, waiting for transfers between devices: 0.83 us -> 5.92 us  [the longest x1 5.91 us: body(): pieces = lax.all_to_all(pieces, 'x', 0, 0, tiled=True)]
    ppermute x3, waiting for transfers between devices: 12.8 us -> 7.78 us  [body(): up = lax.ppermute(up, Z, shift(NZ, 1))]
    ppermute x1, waiting for transfers between devices: 3.92 us -> 1.79 us  [body(): lax.ppermute(up[:rows // 2], Z, shift(NZ, 2))]
    ppermute x1, starting transfers between devices: 4.5 us -> 2.39 us  [body(): others = lax.ppermute(weights, 'c', shift(2, 1))]
  transfers between devices with their start and end apart: 14 -> 17, of which waited for: 7 -> 7; matrix products, arithmetic and copies ran while one was open for 1% -> 3% of each run, Pallas kernels for 3% -> 3%
where the time goes in v11:
time: 156 us; the launch traced here: 155 us
  starting transfers between devices  80.2 us (51%)
  waiting for transfers between devices  34.9 us (22%)
  blocking collectives  18.4 us (12%)
  Pallas kernels  12.1 us (8%)
  local copies, waits for them, and re-layouts  5.36 us (3%)
  other arithmetic  3.14 us (2%)
    all_to_all x1, blocking collectives, body(): lax.all_to_all(parts.reshape(4, *parts.shape[2:]), ('c', 'yh'), 0, 0, til...  18.4 us
    all_to_all x1, starting transfers between devices, body(): pieces = lax.all_to_all(pieces, ('zl', 'y1'), 0, 0, tiled=True)  12.8 us
    all_to_all x1, starting transfers between devices, body(): arrived = lax.all_to_all(policy, Z + YL, 0, 0, tiled=True)  12.7 us
    ppermute x3, starting transfers between devices, body(): down = lax.ppermute(down, Z, shift(NZ, -1))  12.6 us
    pallas_call x2, Pallas kernels, gate_parts(): pl.pallas_call(functools.partial(gate_kernel, first), out_shape=jax.Shape...  10.7 us
    ppermute x3, starting transfers between devices, body(): lax.ppermute(own, YL, [(i, i ^ e) for i in range(NYL)])  9.27 us
    ppermute x3, waiting for transfers between devices, body(): up = lax.ppermute(up, Z, shift(NZ, 1))  7.78 us
    all_to_all x1, waiting for transfers between devices, spread(): lax.all_to_all(jnp.broadcast_to(v[None], (count,) + v.shape), axes, 0, 0,...  7.44 us
  transfers between devices with their start and end apart: 17, of which 7 were waited for; matrix products, arithmetic and copies ran while one was open for 3% of the time, Pallas kernels for 3%

profile of v11, /device:TPU:1, one launch (start us, length us, event | category | flops | bytes accessed | tf_op | source)
XLA Modules:
  0.0 155.1 jit_solution(10305530477101583525)
XLA Ops:
  0.7 0.9 copy-done
  2.2 12.8 %all-to-all-start = ((bf16[8,48,128]{2,1,0:T(8,128)(2,1)}), bf16[8,48,128]{2,1,0:T(8,128)(2,1)}, u32[]{:S(2)}, u32[]{:S(2)}) async-start(bf16[8,48,128]{2,1,0:T(8,128)(2,1)} %bitcast.1), calls=%async_computation | async-start | bytes 196608 | tf_op jit(solution)/shard_map/all_to_all | solution.py:154
  15.0 0.9 dynamic-slice_bitcast_fusion
  15.9 7.3 %collective-permute-start = (bf16[32,8,256]{2,1,0:T(8,128)(2,1)S(1)}, bf16[32,8,256]{2,1,0:T(8,128)(2,1)S(1)}, u32[]{:S(2)}, u32[]{:S(2)}) collective-permute-start(bf16[32,8,256]{2,1,0:T(8,128)(2,1)S(1)} %dynamic-slice_bitcast_fusion), channel_id=1, source_target_pairs={{0,16},{16,0},{1,17},{17,1},{2,18},{18,2},{3,19},{19,3},{4,20},{20... | collective-permute-start | bytes 393224 | tf_op jit(solution)/shard_map/ppermute | solution.py:160
  23.2 5.1 %all-to-all-start.1 = ((bf16[8,48,128]{2,1,0:T(8,128)(2,1)}), bf16[8,48,128]{2,1,0:T(8,128)(2,1)S(1)}, u32[]{:S(2)}, u32[]{:S(2)}) async-start(bf16[8,48,128]{2,1,0:T(8,128)(2,1)} %all-to-all-done), calls=%async_computation.1 | async-start | bytes 196608 | tf_op jit(solution)/shard_map/all_to_all | solution.py:155
  28.3 0.9 fusion.2
  30.0 5.9 %all-to-all-done.1 = bf16[8,48,128]{2,1,0:T(8,128)(2,1)S(1)} async-done(((bf16[8,48,128]{2,1,0:T(8,128)(2,1)}), bf16[8,48,128]{2,1,0:T(8,128)(2,1)S(1)}, u32[]{:S(2)}, u32[]{:S(2)}) %all-to-all-start.1) | async-done | bytes 98336 | tf_op jit(solution)/shard_map/all_to_all | solution.py:155
  35.9 12.7 %all-to-all-start.2 = ((bf16[32,16,256]{2,1,0:T(8,128)(2,1)}), bf16[32,16,256]{2,1,0:T(8,128)(2,1)S(1)}, u32[]{:S(2)}, u32[]{:S(2)}) async-start(bf16[32,16,256]{2,1,0:T(8,128)(2,1)} %maximum_bitcast_fusion), calls=%async_computation.2 | async-start | bytes 524288 | tf_op jit(solution)/shard_map/all_to_all | solution.py:165
  48.6 4.9 %collective-permute-start.3 = (bf16[48,1024]{1,0:T(8,128)(2,1)S(1)}, bf16[48,1024]{1,0:T(8,128)(2,1)S(1)}, u32[]{:S(2)}, u32[]{:S(2)}) collective-permute-start(bf16[48,1024]{1,0:T(8,128)(2,1)S(1)} %copy_bitcast_fusion), channel_id=1, source_target_pairs={{0,96},{32,64},{64,32},{96,0},{1,97},{33,65},{65,33},{97,1},{2,98}... | collective-permute-start | bytes 294920 | tf_op jit(solution)/shard_map/ppermute | solution.py:168
  53.6 1.9 %collective-permute-start.2 = (bf16[48,1024]{1,0:T(8,128)(2,1)S(1)}, bf16[48,1024]{1,0:T(8,128)(2,1)S(1)}, u32[]{:S(2)}, u32[]{:S(2)}) collective-permute-start(bf16[48,1024]{1,0:T(8,128)(2,1)S(1)} %copy_bitcast_fusion), channel_id=1, source_target_pairs={{0,64},{32,96},{64,0},{96,32},{1,65},{33,97},{65,1},{97,33},{2,66}... | collective-permute-start | bytes 294920 | tf_op jit(solution)/shard_map/ppermute | solution.py:168
  55.5 2.4 %collective-permute-start.1 = (bf16[48,1024]{1,0:T(8,128)(2,1)S(1)}, bf16[48,1024]{1,0:T(8,128)(2,1)S(1)}, u32[]{:S(2)}, u32[]{:S(2)}) collective-permute-start(bf16[48,1024]{1,0:T(8,128)(2,1)S(1)} %copy_bitcast_fusion), channel_id=1, source_target_pairs={{0,32},{32,0},{64,96},{96,64},{1,33},{33,1},{65,97},{97,65},{2,34}... | collective-permute-start | bytes 294920 | tf_op jit(solution)/shard_map/ppermute | solution.py:168
  57.9 6.5 %collective-permute-done.2 = bf16[48,1024]{1,0:T(8,128)(2,1)S(1)} collective-permute-done((bf16[48,1024]{1,0:T(8,128)(2,1)S(1)}, bf16[48,1024]{1,0:T(8,128)(2,1)S(1)}, u32[]{:S(2)}, u32[]{:S(2)}) %collective-permute-start.2) | collective-permute-done | bytes 98336 | tf_op jit(solution)/shard_map/ppermute | solution.py:168
  65.3 1.5 broadcast_in_dim.2
  66.8 3.7 %all-to-all-start.3 = ((bf16[8,512,256]{2,1,0:T(8,128)(2,1)}), bf16[8,512,256]{2,1,0:T(8,128)(2,1)S(1)}, u32[]{:S(2)}, u32[]{:S(2)}) async-start(bf16[8,512,256]{2,1,0:T(8,128)(2,1)} %broadcast_in_dim.2), calls=%async_computation.3 | async-start | bytes 4194304 | tf_op jit(solution)/shard_map/all_to_all | solution.py:29
  70.5 3.1 %collective-permute-start.4 = (bf16[192,1024]{1,0:T(8,128)(2,1)S(1)}, bf16[192,1024]{1,0:T(8,128)(2,1)S(1)}, u32[]{:S(2)}, u32[]{:S(2)}) collective-permute-start(bf16[192,1024]{1,0:T(8,128)(2,1)S(1)} %pad_maximum_fusion.refs_0_), channel_id=1, source_target_pairs={{0,128},{128,256},{256,384},{384,512},{512,640},{640,768},{768,896... | collective-permute-start | bytes 1179656 | tf_op jit(solution)/shard_map/ppermute | solution.py:186
  73.7 3.4 %collective-permute-start.7 = (bf16[192,1024]{1,0:T(8,128)(2,1)S(1)}, bf16[192,1024]{1,0:T(8,128)(2,1)}, u32[]{:S(2)}, u32[]{:S(2)}) collective-permute-start(bf16[192,1024]{1,0:T(8,128)(2,1)S(1)} %pad_maximum_fusion.refs_0_), channel_id=1, source_target_pairs={{0,896},{128,0},{256,128},{384,256},{512,384},{640,512},{768,640},... | collective-permute-start | bytes 1179656 | tf_op jit(solution)/shard_map/ppermute | solution.py:187
  77.1 4.3 %collective-permute-done.4.refs_1_ = bf16[192,1024]{1,0:T(8,128)(2,1)S(1)} collective-permute-done((bf16[192,1024]{1,0:T(8,128)(2,1)S(1)}, bf16[192,1024]{1,0:T(8,128)(2,1)S(1)}, u32[]{:S(2)}, u32[]{:S(2)}) %collective-permute-start.4) | collective-permute-done | bytes 393248 | tf_op jit(solution)/shard_map/ppermute | solution.py:186
  81.3 1.9 %collective-permute-start.5 = (bf16[192,1024]{1,0:T(8,128)(2,1)S(1)}, bf16[192,1024]{1,0:T(8,128)(2,1)S(1)}, u32[]{:S(2)}, u32[]{:S(2)}) collective-permute-start(bf16[192,1024]{1,0:T(8,128)(2,1)S(1)} %collective-permute-done.4.refs_1_), channel_id=1, source_target_pairs={{0,128},{128,256},{256,384},{384,512},{512,640},{640,768},{768,896... | collective-permute-start | bytes 1179656 | tf_op jit(solution)/shard_map/ppermute | solution.py:186
  83.3 4.6 %collective-permute-start.8 = (bf16[192,1024]{1,0:T(8,128)(2,1)}, bf16[192,1024]{1,0:T(8,128)(2,1)S(1)}, u32[]{:S(2)}, u32[]{:S(2)}) collective-permute-start(bf16[192,1024]{1,0:T(8,128)(2,1)} %collective-permute-done.7.refs_2_), channel_id=1, source_target_pairs={{0,896},{128,0},{256,128},{384,256},{512,384},{640,512},{768,640},... | collective-permute-start | bytes 1179656 | tf_op jit(solution)/shard_map/ppermute | solution.py:187
  87.9 3.5 %collective-permute-done.5.refs_3_ = bf16[192,1024]{1,0:T(8,128)(2,1)S(1)} collective-permute-done((bf16[192,1024]{1,0:T(8,128)(2,1)S(1)}, bf16[192,1024]{1,0:T(8,128)(2,1)S(1)}, u32[]{:S(2)}, u32[]{:S(2)}) %collective-permute-start.5) | collective-permute-done | bytes 393248 | tf_op jit(solution)/shard_map/ppermute | solution.py:186
  91.4 1.9 %collective-permute-start.6 = (bf16[192,1024]{1,0:T(8,128)(2,1)S(1)}, bf16[192,1024]{1,0:T(8,128)(2,1)}, u32[]{:S(2)}, u32[]{:S(2)}) collective-permute-start(bf16[192,1024]{1,0:T(8,128)(2,1)S(1)} %collective-permute-done.5.refs_3_), channel_id=1, source_target_pairs={{0,128},{128,256},{256,384},{384,512},{512,640},{640,768},{768,896... | collective-permute-start | bytes 1179656 | tf_op jit(solution)/shard_map/ppermute | solution.py:186
  93.3 4.6 %collective-permute-start.9 = (bf16[192,1024]{1,0:T(8,128)(2,1)S(1)}, bf16[192,1024]{1,0:T(8,128)(2,1)}, u32[]{:S(2)}, u32[]{:S(2)}) collective-permute-start(bf16[192,1024]{1,0:T(8,128)(2,1)S(1)} %collective-permute-done.8.refs_4_), channel_id=1, source_target_pairs={{0,896},{128,0},{256,128},{384,256},{512,384},{640,512},{768,640},... | collective-permute-start | bytes 1179656 | tf_op jit(solution)/shard_map/ppermute | solution.py:187
  98.6 1.9 %collective-permute-start.10 = (bf16[96,1024]{1,0:T(8,128)(2,1)}, bf16[96,1024]{1,0:T(8,128)(2,1)}, u32[]{:S(2)}, u32[]{:S(2)}) collective-permute-start(bf16[96,1024]{1,0:T(8,128)(2,1)} %slice.8), channel_id=1, source_target_pairs={{0,256},{128,384},{256,512},{384,640},{512,768},{640,896},{768,0},... | collective-permute-start | bytes 589832 | tf_op jit(solution)/shard_map/ppermute | solution.py:183
  101.2 5.5 %collective-permute-start.11 = (bf16[96,1024]{1,0:T(8,128)(2,1)}, bf16[96,1024]{1,0:T(8,128)(2,1)}, u32[]{:S(2)}, u32[]{:S(2)}) collective-permute-start(bf16[96,1024]{1,0:T(8,128)(2,1)} %slice.9), channel_id=1, source_target_pairs={{0,768},{128,896},{256,0},{384,128},{512,256},{640,384},{768,512},... | collective-permute-start | bytes 589832 | tf_op jit(solution)/shard_map/ppermute | solution.py:184
  107.4 1.8 %collective-permute-done.10.refs_7_ = bf16[96,1024]{1,0:T(8,128)(2,1)} collective-permute-done((bf16[96,1024]{1,0:T(8,128)(2,1)}, bf16[96,1024]{1,0:T(8,128)(2,1)}, u32[]{:S(2)}, u32[]{:S(2)}) %collective-permute-start.10) | collective-permute-done | bytes 196640 | tf_op jit(solution)/shard_map/ppermute | solution.py:183
  109.1 5.5 %collective-permute-done.11.refs_8_ = bf16[96,1024]{1,0:T(8,128)(2,1)} collective-permute-done((bf16[96,1024]{1,0:T(8,128)(2,1)}, bf16[96,1024]{1,0:T(8,128)(2,1)}, u32[]{:S(2)}, u32[]{:S(2)}) %collective-permute-start.11) | collective-permute-done | bytes 196640 | tf_op jit(solution)/shard_map/ppermute | solution.py:184
  114.7 7.4 %all-to-all-done.3 = bf16[8,512,256]{2,1,0:T(8,128)(2,1)S(1)} async-done(((bf16[8,512,256]{2,1,0:T(8,128)(2,1)}), bf16[8,512,256]{2,1,0:T(8,128)(2,1)S(1)}, u32[]{:S(2)}, u32[]{:S(2)}) %all-to-all-start.3) | async-done | bytes 2097184 | tf_op jit(solution)/shard_map/all_to_all | solution.py:29
  122.1 2.4 %collective-permute-start.12 = (bf16[8,4,128,256]{3,2,1,0:T(8,128)(2,1)S(1)}, bf16[8,4,128,256]{3,2,1,0:T(8,128)(2,1)}, u32[]{:S(2)}, u32[]{:S(2)}) collective-permute-start(bf16[8,4,128,256]{3,2,1,0:T(8,128)(2,1)S(1)} %bitcast.44), channel_id=1, source_target_pairs={{0,16},{16,0},{1,17},{17,1},{2,18},{18,2},{3,19},{19,3},{4,20},{20... | collective-permute-start | bytes 6291464 | tf_op jit(solution)/shard_map/ppermute | solution.py:195
  124.6 5.4 %shard_map.68.refs_10_ = bf16[2,208,256]{2,1,0:T(8,128)(2,1)} custom-call(s32[18]{0:T(128)} %pad_add_fusion.index, bf16[192,1024]{1,0:T(8,128)(2,1)} %copy-done.3, bf16[192,1024]{1,0:T(8,128)(2,1)} %copy-done.6, bf16[192,1024]{1,0:T(8,128)(2,1)} %collective-permute-done.7.refs_2_, bf16[192,1024]{1,0:T(8,128)(2,1)} %copy-done.4, bf16[192,1024]{1,0:T(8,128)(2,1)} %copy-done.5, ...), custom_call_target="tpu_custom_call" | custom-call | flops 805306368 | bytes 7340032 | tf_op jit(solution)/shard_map/pallas_call | solution.py:94
  130.0 5.3 %shard_map.69 = bf16[2,2,208,256]{3,2,1,0:T(8,128)(2,1)} custom-call(s32[18]{0:T(128)} %pad_add_fusion.index, bf16[192,1024]{1,0:T(8,128)(2,1)} %copy-done.3, bf16[192,1024]{1,0:T(8,128)(2,1)} %copy-done.6, bf16[192,1024]{1,0:T(8,128)(2,1)} %collective-permute-done.7.refs_2_, bf16[192,1024]{1,0:T(8,128)(2,1)} %copy-done.4, bf16[192,1024]{1,0:T(8,128)(2,1)} %copy-done.5, ...), custom_call_target="tpu_custom_call" | custom-call | flops 805306368 | bytes 7340032 | tf_op jit(solution)/shard_map/pallas_call | solution.py:94
  135.3 18.4 %all_to_all.25.parts = bf16[4,208,256]{2,1,0:T(8,128)(2,1)S(1)} all-to-all(bf16[4,208,256]{2,1,0:T(8,128)(2,1)} %bitcast.46), channel_id=1, replica_groups=mesh['zh'=2,'zl'=4,'y1'=2,'y0'=2,'c'=2,'yh'=2,'x'=8] {'c','yh'}, dimensions={0} | all-to-all | bytes 851968 | tf_op jit(solution)/shard_map/all_to_all | solution.py:198
  153.7 1.4 shard_map.70
  (39 shorter events, 4.3 us)
Async XLA Ops:
  0.6 0.9 copy-start
  0.6 63.8 %copy-start.8 = (f32[512]{0:T(512)S(1)}, f32[512]{0:T(512)}, u32[]{:S(2)}) copy-start(f32[512]{0:T(512)} %param.8) | copy-start | bytes 6148
  1.5 62.9 %copy-start.7 = (bf16[512,256]{1,0:T(8,128)(2,1)S(1)}, bf16[512,256]{1,0:T(8,128)(2,1)}, u32[]{:S(2)}) copy-start(bf16[512,256]{1,0:T(8,128)(2,1)} %param.6) | copy-start | bytes 786436
  2.2 21.0 %all-to-all-start = ((bf16[8,48,128]{2,1,0:T(8,128)(2,1)}), bf16[8,48,128]{2,1,0:T(8,128)(2,1)}, u32[]{:S(2)}, u32[]{:S(2)}) async-start(bf16[8,48,128]{2,1,0:T(8,128)(2,1)} %bitcast.1), calls=%async_computation | async-start | bytes 196608 | tf_op jit(solution)/shard_map/all_to_all | solution.py:154
  15.9 12.4 %collective-permute-start = (bf16[32,8,256]{2,1,0:T(8,128)(2,1)S(1)}, bf16[32,8,256]{2,1,0:T(8,128)(2,1)S(1)}, u32[]{:S(2)}, u32[]{:S(2)}) collective-permute-start(bf16[32,8,256]{2,1,0:T(8,128)(2,1)S(1)} %dynamic-slice_bitcast_fusion), channel_id=1, source_target_pairs={{0,16},{16,0},{1,17},{17,1},{2,18},{18,2},{3,19},{19,3},{4,20},{20... | collective-permute-start | bytes 393224 | tf_op jit(solution)/shard_map/ppermute | solution.py:160
  23.2 12.7 %all-to-all-start.1 = ((bf16[8,48,128]{2,1,0:T(8,128)(2,1)}), bf16[8,48,128]{2,1,0:T(8,128)(2,1)S(1)}, u32[]{:S(2)}, u32[]{:S(2)}) async-start(bf16[8,48,128]{2,1,0:T(8,128)(2,1)} %all-to-all-done), calls=%async_computation.1 | async-start | bytes 196608 | tf_op jit(solution)/shard_map/all_to_all | solution.py:155
  35.9 28.6 %all-to-all-start.2 = ((bf16[32,16,256]{2,1,0:T(8,128)(2,1)}), bf16[32,16,256]{2,1,0:T(8,128)(2,1)S(1)}, u32[]{:S(2)}, u32[]{:S(2)}) async-start(bf16[32,16,256]{2,1,0:T(8,128)(2,1)} %maximum_bitcast_fusion), calls=%async_computation.2 | async-start | bytes 524288 | tf_op jit(solution)/shard_map/all_to_all | solution.py:165
  48.6 9.3 %collective-permute-start.3 = (bf16[48,1024]{1,0:T(8,128)(2,1)S(1)}, bf16[48,1024]{1,0:T(8,128)(2,1)S(1)}, u32[]{:S(2)}, u32[]{:S(2)}) collective-permute-start(bf16[48,1024]{1,0:T(8,128)(2,1)S(1)} %copy_bitcast_fusion), channel_id=1, source_target_pairs={{0,96},{32,64},{64,32},{96,0},{1,97},{33,65},{65,33},{97,1},{2,98}... | collective-permute-start | bytes 294920 | tf_op jit(solution)/shard_map/ppermute | solution.py:168
  53.6 10.8 %collective-permute-start.2 = (bf16[48,1024]{1,0:T(8,128)(2,1)S(1)}, bf16[48,1024]{1,0:T(8,128)(2,1)S(1)}, u32[]{:S(2)}, u32[]{:S(2)}) collective-permute-start(bf16[48,1024]{1,0:T(8,128)(2,1)S(1)} %copy_bitcast_fusion), channel_id=1, source_target_pairs={{0,64},{32,96},{64,0},{96,32},{1,65},{33,97},{65,1},{97,33},{2,66}... | collective-permute-start | bytes 294920 | tf_op jit(solution)/shard_map/ppermute | solution.py:168
  55.5 8.9 %collective-permute-start.1 = (bf16[48,1024]{1,0:T(8,128)(2,1)S(1)}, bf16[48,1024]{1,0:T(8,128)(2,1)S(1)}, u32[]{:S(2)}, u32[]{:S(2)}) collective-permute-start(bf16[48,1024]{1,0:T(8,128)(2,1)S(1)} %copy_bitcast_fusion), channel_id=1, source_target_pairs={{0,32},{32,0},{64,96},{96,64},{1,33},{33,1},{65,97},{97,65},{2,34}... | collective-permute-start | bytes 294920 | tf_op jit(solution)/shard_map/ppermute | solution.py:168
  64.4 9.2 %copy-start.3 = (bf16[192,1024]{1,0:T(8,128)(2,1)}, bf16[192,1024]{1,0:T(8,128)(2,1)S(1)}, u32[]{:S(2)}) copy-start(bf16[192,1024]{1,0:T(8,128)(2,1)S(1)} %pad_maximum_fusion.refs_0_) | copy-start | bytes 1179652
  66.8 31.1 %copy-start.9 = (s32[8]{0:T(128)S(1)}, s32[8]{0:T(128)}, u32[]{:S(2)}) copy-start(s32[8]{0:T(128)} %constant.68.clone) | copy-start | bytes 100
  66.8 55.3 %all-to-all-start.3 = ((bf16[8,512,256]{2,1,0:T(8,128)(2,1)}), bf16[8,512,256]{2,1,0:T(8,128)(2,1)S(1)}, u32[]{:S(2)}, u32[]{:S(2)}) async-start(bf16[8,512,256]{2,1,0:T(8,128)(2,1)} %broadcast_in_dim.2), calls=%async_computation.3 | async-start | bytes 4194304 | tf_op jit(solution)/shard_map/all_to_all | solution.py:29
  70.5 10.8 %collective-permute-start.4 = (bf16[192,1024]{1,0:T(8,128)(2,1)S(1)}, bf16[192,1024]{1,0:T(8,128)(2,1)S(1)}, u32[]{:S(2)}, u32[]{:S(2)}) collective-permute-start(bf16[192,1024]{1,0:T(8,128)(2,1)S(1)} %pad_maximum_fusion.refs_0_), channel_id=1, source_target_pairs={{0,128},{128,256},{256,384},{384,512},{512,640},{640,768},{768,896... | collective-permute-start | bytes 1179656 | tf_op jit(solution)/shard_map/ppermute | solution.py:186
  73.7 9.6 %collective-permute-start.7 = (bf16[192,1024]{1,0:T(8,128)(2,1)S(1)}, bf16[192,1024]{1,0:T(8,128)(2,1)}, u32[]{:S(2)}, u32[]{:S(2)}) collective-permute-start(bf16[192,1024]{1,0:T(8,128)(2,1)S(1)} %pad_maximum_fusion.refs_0_), channel_id=1, source_target_pairs={{0,896},{128,0},{256,128},{384,256},{512,384},{640,512},{768,640},... | collective-permute-start | bytes 1179656 | tf_op jit(solution)/shard_map/ppermute | solution.py:187
  81.3 43.2 %copy-start.6 = (bf16[192,1024]{1,0:T(8,128)(2,1)}, bf16[192,1024]{1,0:T(8,128)(2,1)S(1)}, u32[]{:S(2)}) copy-start(bf16[192,1024]{1,0:T(8,128)(2,1)S(1)} %collective-permute-done.4.refs_1_) | copy-start | bytes 1179652
  81.3 10.0 %collective-permute-start.5 = (bf16[192,1024]{1,0:T(8,128)(2,1)S(1)}, bf16[192,1024]{1,0:T(8,128)(2,1)S(1)}, u32[]{:S(2)}, u32[]{:S(2)}) collective-permute-start(bf16[192,1024]{1,0:T(8,128)(2,1)S(1)} %collective-permute-done.4.refs_1_), channel_id=1, source_target_pairs={{0,128},{128,256},{256,384},{384,512},{512,640},{640,768},{768,896... | collective-permute-start | bytes 1179656 | tf_op jit(solution)/shard_map/ppermute | solution.py:186
  83.3 10.0 %collective-permute-start.8 = (bf16[192,1024]{1,0:T(8,128)(2,1)}, bf16[192,1024]{1,0:T(8,128)(2,1)S(1)}, u32[]{:S(2)}, u32[]{:S(2)}) collective-permute-start(bf16[192,1024]{1,0:T(8,128)(2,1)} %collective-permute-done.7.refs_2_), channel_id=1, source_target_pairs={{0,896},{128,0},{256,128},{384,256},{512,384},{640,512},{768,640},... | collective-permute-start | bytes 1179656 | tf_op jit(solution)/shard_map/ppermute | solution.py:187
  91.4 33.2 %copy-start.4 = (bf16[192,1024]{1,0:T(8,128)(2,1)}, bf16[192,1024]{1,0:T(8,128)(2,1)S(1)}, u32[]{:S(2)}) copy-start(bf16[192,1024]{1,0:T(8,128)(2,1)S(1)} %collective-permute-done.5.refs_3_) | copy-start | bytes 1179652
  91.4 23.3 %collective-permute-start.6 = (bf16[192,1024]{1,0:T(8,128)(2,1)S(1)}, bf16[192,1024]{1,0:T(8,128)(2,1)}, u32[]{:S(2)}, u32[]{:S(2)}) collective-permute-start(bf16[192,1024]{1,0:T(8,128)(2,1)S(1)} %collective-permute-done.5.refs_3_), channel_id=1, source_target_pairs={{0,128},{128,256},{256,384},{384,512},{512,640},{640,768},{768,896... | collective-permute-start | bytes 1179656 | tf_op jit(solution)/shard_map/ppermute | solution.py:186
  93.3 31.2 %copy-start.5 = (bf16[192,1024]{1,0:T(8,128)(2,1)}, bf16[192,1024]{1,0:T(8,128)(2,1)S(1)}, u32[]{:S(2)}) copy-start(bf16[192,1024]{1,0:T(8,128)(2,1)S(1)} %collective-permute-done.8.refs_4_) | copy-start | bytes 1179652
  93.3 21.4 %collective-permute-start.9 = (bf16[192,1024]{1,0:T(8,128)(2,1)S(1)}, bf16[192,1024]{1,0:T(8,128)(2,1)}, u32[]{:S(2)}, u32[]{:S(2)}) collective-permute-start(bf16[192,1024]{1,0:T(8,128)(2,1)S(1)} %collective-permute-done.8.refs_4_), channel_id=1, source_target_pairs={{0,896},{128,0},{256,128},{384,256},{512,384},{640,512},{768,640},... | collective-permute-start | bytes 1179656 | tf_op jit(solution)/shard_map/ppermute | solution.py:187
  98.6 10.5 %collective-permute-start.10 = (bf16[96,1024]{1,0:T(8,128)(2,1)}, bf16[96,1024]{1,0:T(8,128)(2,1)}, u32[]{:S(2)}, u32[]{:S(2)}) collective-permute-start(bf16[96,1024]{1,0:T(8,128)(2,1)} %slice.8), channel_id=1, source_target_pairs={{0,256},{128,384},{256,512},{384,640},{512,768},{640,896},{768,0},... | collective-permute-start | bytes 589832 | tf_op jit(solution)/shard_map/ppermute | solution.py:183
  101.2 13.4 %collective-permute-start.11 = (bf16[96,1024]{1,0:T(8,128)(2,1)}, bf16[96,1024]{1,0:T(8,128)(2,1)}, u32[]{:S(2)}, u32[]{:S(2)}) collective-permute-start(bf16[96,1024]{1,0:T(8,128)(2,1)} %slice.9), channel_id=1, source_target_pairs={{0,768},{128,896},{256,0},{384,128},{512,256},{640,384},{768,512},... | collective-permute-start | bytes 589832 | tf_op jit(solution)/shard_map/ppermute | solution.py:184
  122.1 2.4 %copy-start.2 = (bf16[8,512,256]{2,1,0:T(8,128)(2,1)}, bf16[8,512,256]{2,1,0:T(8,128)(2,1)S(1)}, u32[]{:S(2)}) copy-start(bf16[8,512,256]{2,1,0:T(8,128)(2,1)S(1)} %all-to-all-done.3) | copy-start | bytes 6291460
  122.1 7.8 %collective-permute-start.12 = (bf16[8,4,128,256]{3,2,1,0:T(8,128)(2,1)S(1)}, bf16[8,4,128,256]{3,2,1,0:T(8,128)(2,1)}, u32[]{:S(2)}, u32[]{:S(2)}) collective-permute-start(bf16[8,4,128,256]{3,2,1,0:T(8,128)(2,1)S(1)} %bitcast.44), channel_id=1, source_target_pairs={{0,16},{16,0},{1,17},{17,1},{2,18},{18,2},{3,19},{19,3},{4,20},{20... | collective-permute-start | bytes 6291464 | tf_op jit(solution)/shard_map/ppermute | solution.py:195
  129.9 23.7 %copy-start.1 = (s32[18]{0:T(128)S(1)}, s32[18]{0:T(128)}, u32[]{:S(2)}) copy-start(s32[18]{0:T(128)} %pad_add_fusion.index) | copy-start | bytes 220

commit v12 on v11

--- a/solution.py
+++ b/solution.py
@@ -164,11 +164,10 @@
     pieces, policy = lax.optimization_barrier((pieces, policy))
     arrived = lax.all_to_all(policy, Z + YL, 0, 0, tiled=True)
     own = pieces.transpose(1, 0, 2).reshape(toks, NX * LANES)
-    own = jnp.concatenate(
-        [own] + [lax.ppermute(own, YL, [(i, i ^ e) for i in range(NYL)]) for e in range(1, NYL)]
-    )
+    others = [lax.ppermute(own, YL, [(i, i ^ e) for i in range(NYL)]) for e in range(1, NYL)]
+    *others[:2], arrived = lax.optimization_barrier((*others[:2], arrived))
+    own = jnp.concatenate([own] + others)
     rows = own.shape[0]
-    own, arrived = lax.optimization_barrier((own, arrived))
     policy_slice = arrived.reshape(ref_weight.shape)
     ref_f = ref_weight.astype(jnp.float32)
     blended = (ref_f + ema_rate * (policy_slice.astype(jnp.float32) - ref_f)).astype(jnp.bfloat16)

time: 156 us -> 160 us (1.026)
  starting transfers between devices: 80.2 us -> 88.2 us
  waiting for transfers between devices: 34.9 us -> 30 us
    all_to_all x1, waiting for transfers between devices: 7.44 us -> 0.01 us  [spread(): lax.all_to_all(jnp.broadcast_to(v[None], (count,) + v.shape), axes, 0, 0,...]
    ppermute x1, starting transfers between devices: 2.39 us -> 9.59 us  [body(): others = lax.ppermute(weights, 'c', shift(2, 1))]
    ppermute x3, waiting for transfers between devices: 6.47 us -> 9.54 us  [body(): lax.ppermute(own, YL, [(i, i ^ e) for i in range(NYL)])]
    ppermute x1, waiting for transfers between devices: 1.79 us -> 4.01 us  [body(): lax.ppermute(up[:rows // 2], Z, shift(NZ, 2))]
    ppermute x1, waiting for transfers between devices: 5.52 us -> 3.34 us  [body(): lax.ppermute(down[rows // 2:], Z, shift(NZ, -2))]
  transfers between devices with their start and end apart: 17 -> 17, of which waited for: 7 -> 8; matrix products, arithmetic and copies ran while one was open for 3% -> 3% of each run, Pallas kernels for 3% -> 3%
where the time goes in v12:
time: 160 us; the launch traced here: 158 us
  starting transfers between devices  88.2 us (55%)
  waiting for transfers between devices  30 us (19%)
  blocking collectives  17.8 us (11%)
  Pallas kernels  12.1 us (8%)
  local copies, waits for them, and re-layouts  5.41 us (3%)
  other arithmetic  3.09 us (2%)
    all_to_all x1, blocking collectives, body(): lax.all_to_all(parts.reshape(4, *parts.shape[2:]), ('c', 'yh'), 0, 0, til...  17.8 us
    all_to_all x1, starting transfers between devices, body(): pieces = lax.all_to_all(pieces, ('zl', 'y1'), 0, 0, tiled=True)  12.8 us
    all_to_all x1, starting transfers between devices, body(): arrived = lax.all_to_all(policy, Z + YL, 0, 0, tiled=True)  12.7 us
    ppermute x3, starting transfers between devices, body(): down = lax.ppermute(down, Z, shift(NZ, -1))  12.6 us
    pallas_call x2, Pallas kernels, gate_parts(): pl.pallas_call(functools.partial(gate_kernel, first), out_shape=jax.Shape...  10.7 us
    ppermute x3, starting transfers between devices, body(): lax.ppermute(own, YL, [(i, i ^ e) for i in range(NYL)])  10.1 us
    ppermute x1, starting transfers between devices, body(): others = lax.ppermute(weights, 'c', shift(2, 1))  9.59 us
    ppermute x3, waiting for transfers between devices, body(): lax.ppermute(own, YL, [(i, i ^ e) for i in range(NYL)])  9.54 us
  transfers between devices with their start and end apart: 17, of which 8 were waited for; matrix products, arithmetic and copies ran while one was open for 3% of the time, Pallas kernels for 3%

profile of v12, /device:TPU:1, one launch (start us, length us, event | category | flops | bytes accessed | tf_op | source)
XLA Modules:
  0.0 157.6 jit_solution(14057484467979604008)
XLA Ops:
  0.7 0.9 copy-done
  2.2 12.8 %all-to-all-start = ((bf16[8,48,128]{2,1,0:T(8,128)(2,1)}), bf16[8,48,128]{2,1,0:T(8,128)(2,1)}, u32[]{:S(2)}, u32[]{:S(2)}) async-start(bf16[8,48,128]{2,1,0:T(8,128)(2,1)} %bitcast.1), calls=%async_computation | async-start | bytes 196608 | tf_op jit(solution)/shard_map/all_to_all | solution.py:154
  15.0 0.9 dynamic-slice_bitcast_fusion
  15.9 7.3 %collective-permute-start = (bf16[32,8,256]{2,1,0:T(8,128)(2,1)S(1)}, bf16[32,8,256]{2,1,0:T(8,128)(2,1)S(1)}, u32[]{:S(2)}, u32[]{:S(2)}) collective-permute-start(bf16[32,8,256]{2,1,0:T(8,128)(2,1)S(1)} %dynamic-slice_bitcast_fusion), channel_id=1, source_target_pairs={{0,16},{16,0},{1,17},{17,1},{2,18},{18,2},{3,19},{19,3},{4,20},{20... | collective-permute-start | bytes 393224 | tf_op jit(solution)/shard_map/ppermute | solution.py:160
  23.2 5.1 %all-to-all-start.1 = ((bf16[8,48,128]{2,1,0:T(8,128)(2,1)}), bf16[8,48,128]{2,1,0:T(8,128)(2,1)S(1)}, u32[]{:S(2)}, u32[]{:S(2)}) async-start(bf16[8,48,128]{2,1,0:T(8,128)(2,1)} %all-to-all-done), calls=%async_computation.1 | async-start | bytes 196608 | tf_op jit(solution)/shard_map/all_to_all | solution.py:155
  28.3 0.9 fusion.2
  30.0 5.9 %all-to-all-done.1 = bf16[8,48,128]{2,1,0:T(8,128)(2,1)S(1)} async-done(((bf16[8,48,128]{2,1,0:T(8,128)(2,1)}), bf16[8,48,128]{2,1,0:T(8,128)(2,1)S(1)}, u32[]{:S(2)}, u32[]{:S(2)}) %all-to-all-start.1) | async-done | bytes 98336 | tf_op jit(solution)/shard_map/all_to_all | solution.py:155
  35.9 12.7 %all-to-all-start.2 = ((bf16[32,16,256]{2,1,0:T(8,128)(2,1)}), bf16[32,16,256]{2,1,0:T(8,128)(2,1)S(1)}, u32[]{:S(2)}, u32[]{:S(2)}) async-start(bf16[32,16,256]{2,1,0:T(8,128)(2,1)} %maximum_bitcast_fusion), calls=%async_computation.2 | async-start | bytes 524288 | tf_op jit(solution)/shard_map/all_to_all | solution.py:165
  48.6 3.1 %collective-permute-start.1 = (bf16[48,1024]{1,0:T(8,128)(2,1)S(1)}, bf16[48,1024]{1,0:T(8,128)(2,1)S(1)}, u32[]{:S(2)}, u32[]{:S(2)}) collective-permute-start(bf16[48,1024]{1,0:T(8,128)(2,1)S(1)} %copy_bitcast_fusion), channel_id=1, source_target_pairs={{0,32},{32,0},{64,96},{96,64},{1,33},{33,1},{65,97},{97,65},{2,34}... | collective-permute-start | bytes 294920 | tf_op jit(solution)/shard_map/ppermute | solution.py:167
  51.8 4.0 %collective-permute-start.2 = (bf16[48,1024]{1,0:T(8,128)(2,1)S(1)}, bf16[48,1024]{1,0:T(8,128)(2,1)S(1)}, u32[]{:S(2)}, u32[]{:S(2)}) collective-permute-start(bf16[48,1024]{1,0:T(8,128)(2,1)S(1)} %copy_bitcast_fusion), channel_id=1, source_target_pairs={{0,64},{32,96},{64,0},{96,32},{1,65},{33,97},{65,1},{97,33},{2,66}... | collective-permute-start | bytes 294920 | tf_op jit(solution)/shard_map/ppermute | solution.py:167
  55.8 5.4 %collective-permute-done.2 = bf16[48,1024]{1,0:T(8,128)(2,1)S(1)} collective-permute-done((bf16[48,1024]{1,0:T(8,128)(2,1)S(1)}, bf16[48,1024]{1,0:T(8,128)(2,1)S(1)}, u32[]{:S(2)}, u32[]{:S(2)}) %collective-permute-start.2) | collective-permute-done | bytes 98336 | tf_op jit(solution)/shard_map/ppermute | solution.py:167
  62.0 1.5 broadcast_in_dim.2
  63.5 3.7 %all-to-all-start.3 = ((bf16[8,512,256]{2,1,0:T(8,128)(2,1)}), bf16[8,512,256]{2,1,0:T(8,128)(2,1)S(1)}, u32[]{:S(2)}, u32[]{:S(2)}) async-start(bf16[8,512,256]{2,1,0:T(8,128)(2,1)} %broadcast_in_dim.2), calls=%async_computation.3 | async-start | bytes 4194304 | tf_op jit(solution)/shard_map/all_to_all | solution.py:29
  67.2 2.9 %collective-permute-start.3 = (bf16[48,1024]{1,0:T(8,128)(2,1)S(1)}, bf16[48,1024]{1,0:T(8,128)(2,1)S(1)}, u32[]{:S(2)}, u32[]{:S(2)}) collective-permute-start(bf16[48,1024]{1,0:T(8,128)(2,1)S(1)} %copy_bitcast_fusion), channel_id=1, source_target_pairs={{0,96},{32,64},{64,32},{96,0},{1,97},{33,65},{65,33},{97,1},{2,98}... | collective-permute-start | bytes 294920 | tf_op jit(solution)/shard_map/ppermute | solution.py:167
  70.2 4.2 %collective-permute-done.3 = bf16[48,1024]{1,0:T(8,128)(2,1)S(1)} collective-permute-done((bf16[48,1024]{1,0:T(8,128)(2,1)S(1)}, bf16[48,1024]{1,0:T(8,128)(2,1)S(1)}, u32[]{:S(2)}, u32[]{:S(2)}) %collective-permute-start.3) | collective-permute-done | bytes 98336 | tf_op jit(solution)/shard_map/ppermute | solution.py:167
  74.4 3.1 %collective-permute-start.4 = (bf16[192,1024]{1,0:T(8,128)(2,1)S(1)}, bf16[192,1024]{1,0:T(8,128)(2,1)}, u32[]{:S(2)}, u32[]{:S(2)}) collective-permute-start(bf16[192,1024]{1,0:T(8,128)(2,1)S(1)} %constant_dynamic-update-slice_fusion.refs_0_), channel_id=1, source_target_pairs={{0,128},{128,256},{256,384},{384,512},{512,640},{640,768},{768,896... | collective-permute-start | bytes 1179656 | tf_op jit(solution)/shard_map/ppermute | solution.py:185
  77.5 3.4 %collective-permute-start.7 = (bf16[192,1024]{1,0:T(8,128)(2,1)S(1)}, bf16[192,1024]{1,0:T(8,128)(2,1)}, u32[]{:S(2)}, u32[]{:S(2)}) collective-permute-start(bf16[192,1024]{1,0:T(8,128)(2,1)S(1)} %constant_dynamic-update-slice_fusion.refs_0_), channel_id=1, source_target_pairs={{0,896},{128,0},{256,128},{384,256},{512,384},{640,512},{768,640},... | collective-permute-start | bytes 1179656 | tf_op jit(solution)/shard_map/ppermute | solution.py:186
  80.9 3.5 %collective-permute-done.4.refs_1_ = bf16[192,1024]{1,0:T(8,128)(2,1)} collective-permute-done((bf16[192,1024]{1,0:T(8,128)(2,1)S(1)}, bf16[192,1024]{1,0:T(8,128)(2,1)}, u32[]{:S(2)}, u32[]{:S(2)}) %collective-permute-start.4) | collective-permute-done | bytes 393248 | tf_op jit(solution)/shard_map/ppermute | solution.py:185
  84.4 1.9 %collective-permute-start.5 = (bf16[192,1024]{1,0:T(8,128)(2,1)}, bf16[192,1024]{1,0:T(8,128)(2,1)S(1)}, u32[]{:S(2)}, u32[]{:S(2)}) collective-permute-start(bf16[192,1024]{1,0:T(8,128)(2,1)} %collective-permute-done.4.refs_1_), channel_id=1, source_target_pairs={{0,128},{128,256},{256,384},{384,512},{512,640},{640,768},{768,896... | collective-permute-start | bytes 1179656 | tf_op jit(solution)/shard_map/ppermute | solution.py:185
  86.4 4.5 %collective-permute-start.8 = (bf16[192,1024]{1,0:T(8,128)(2,1)}, bf16[192,1024]{1,0:T(8,128)(2,1)S(1)}, u32[]{:S(2)}, u32[]{:S(2)}) collective-permute-start(bf16[192,1024]{1,0:T(8,128)(2,1)} %collective-permute-done.7.refs_2_), channel_id=1, source_target_pairs={{0,896},{128,0},{256,128},{384,256},{512,384},{640,512},{768,640},... | collective-permute-start | bytes 1179656 | tf_op jit(solution)/shard_map/ppermute | solution.py:186
  91.0 3.6 %collective-permute-done.5.refs_3_ = bf16[192,1024]{1,0:T(8,128)(2,1)S(1)} collective-permute-done((bf16[192,1024]{1,0:T(8,128)(2,1)}, bf16[192,1024]{1,0:T(8,128)(2,1)S(1)}, u32[]{:S(2)}, u32[]{:S(2)}) %collective-permute-start.5) | collective-permute-done | bytes 393248 | tf_op jit(solution)/shard_map/ppermute | solution.py:185
  94.5 1.9 %collective-permute-start.6 = (bf16[192,1024]{1,0:T(8,128)(2,1)S(1)}, bf16[192,1024]{1,0:T(8,128)(2,1)}, u32[]{:S(2)}, u32[]{:S(2)}) collective-permute-start(bf16[192,1024]{1,0:T(8,128)(2,1)S(1)} %collective-permute-done.5.refs_3_), channel_id=1, source_target_pairs={{0,128},{128,256},{256,384},{384,512},{512,640},{640,768},{768,896... | collective-permute-start | bytes 1179656 | tf_op jit(solution)/shard_map/ppermute | solution.py:185
  96.4 4.7 %collective-permute-start.9 = (bf16[192,1024]{1,0:T(8,128)(2,1)S(1)}, bf16[192,1024]{1,0:T(8,128)(2,1)}, u32[]{:S(2)}, u32[]{:S(2)}) collective-permute-start(bf16[192,1024]{1,0:T(8,128)(2,1)S(1)} %collective-permute-done.8.refs_4_), channel_id=1, source_target_pairs={{0,896},{128,0},{256,128},{384,256},{512,384},{640,512},{768,640},... | collective-permute-start | bytes 1179656 | tf_op jit(solution)/shard_map/ppermute | solution.py:186
  101.9 1.9 %collective-permute-start.10 = (bf16[96,1024]{1,0:T(8,128)(2,1)}, bf16[96,1024]{1,0:T(8,128)(2,1)}, u32[]{:S(2)}, u32[]{:S(2)}) collective-permute-start(bf16[96,1024]{1,0:T(8,128)(2,1)} %slice.8), channel_id=1, source_target_pairs={{0,256},{128,384},{256,512},{384,640},{512,768},{640,896},{768,0},... | collective-permute-start | bytes 589832 | tf_op jit(solution)/shard_map/ppermute | solution.py:182
  104.5 5.4 %collective-permute-start.11 = (bf16[96,1024]{1,0:T(8,128)(2,1)}, bf16[96,1024]{1,0:T(8,128)(2,1)}, u32[]{:S(2)}, u32[]{:S(2)}) collective-permute-start(bf16[96,1024]{1,0:T(8,128)(2,1)} %slice.9), channel_id=1, source_target_pairs={{0,768},{128,896},{256,0},{384,128},{512,256},{640,384},{768,512},... | collective-permute-start | bytes 589832 | tf_op jit(solution)/shard_map/ppermute | solution.py:183
  110.6 4.0 %collective-permute-done.10.refs_7_ = bf16[96,1024]{1,0:T(8,128)(2,1)} collective-permute-done((bf16[96,1024]{1,0:T(8,128)(2,1)}, bf16[96,1024]{1,0:T(8,128)(2,1)}, u32[]{:S(2)}, u32[]{:S(2)}) %collective-permute-start.10) | collective-permute-done | bytes 196640 | tf_op jit(solution)/shard_map/ppermute | solution.py:182
  114.6 3.3 %collective-permute-done.11.refs_8_ = bf16[96,1024]{1,0:T(8,128)(2,1)} collective-permute-done((bf16[96,1024]{1,0:T(8,128)(2,1)}, bf16[96,1024]{1,0:T(8,128)(2,1)}, u32[]{:S(2)}, u32[]{:S(2)}) %collective-permute-start.11) | collective-permute-done | bytes 196640 | tf_op jit(solution)/shard_map/ppermute | solution.py:183
  118.0 9.6 %collective-permute-start.12 = (bf16[8,4,128,256]{3,2,1,0:T(8,128)(2,1)S(1)}, bf16[8,4,128,256]{3,2,1,0:T(8,128)(2,1)}, u32[]{:S(2)}, u32[]{:S(2)}) collective-permute-start(bf16[8,4,128,256]{3,2,1,0:T(8,128)(2,1)S(1)} %bitcast.48), channel_id=1, source_target_pairs={{0,16},{16,0},{1,17},{17,1},{2,18},{18,2},{3,19},{19,3},{4,20},{20... | collective-permute-start | bytes 6291464 | tf_op jit(solution)/shard_map/ppermute | solution.py:194
  127.6 5.4 %shard_map.68.refs_10_ = bf16[2,208,256]{2,1,0:T(8,128)(2,1)} custom-call(s32[18]{0:T(128)} %pad_add_fusion.index, bf16[192,1024]{1,0:T(8,128)(2,1)} %copy-done.5, bf16[192,1024]{1,0:T(8,128)(2,1)} %collective-permute-done.4.refs_1_, bf16[192,1024]{1,0:T(8,128)(2,1)} %collective-permute-done.7.refs_2_, bf16[192,1024]{1,0:T(8,128)(2,1)} %copy-done.3, ...), custom_call_target="tpu_custom_call" | custom-call | flops 805306368 | bytes 7340032 | tf_op jit(solution)/shard_map/pallas_call | solution.py:94
  133.0 5.3 %shard_map.69 = bf16[2,2,208,256]{3,2,1,0:T(8,128)(2,1)} custom-call(s32[18]{0:T(128)} %pad_add_fusion.index, bf16[192,1024]{1,0:T(8,128)(2,1)} %copy-done.5, bf16[192,1024]{1,0:T(8,128)(2,1)} %collective-permute-done.4.refs_1_, bf16[192,1024]{1,0:T(8,128)(2,1)} %collective-permute-done.7.refs_2_, bf16[192,1024]{1,0:T(8,128)(2,1)} %copy-done.3, ...), custom_call_target="tpu_custom_call" | custom-call | flops 805306368 | bytes 7340032 | tf_op jit(solution)/shard_map/pallas_call | solution.py:94
  138.3 17.8 %all_to_all.25.parts = bf16[4,208,256]{2,1,0:T(8,128)(2,1)S(1)} all-to-all(bf16[4,208,256]{2,1,0:T(8,128)(2,1)} %bitcast.50), channel_id=1, replica_groups=mesh['zh'=2,'zl'=4,'y1'=2,'y0'=2,'c'=2,'yh'=2,'x'=8] {'c','yh'}, dimensions={0} | all-to-all | bytes 851968 | tf_op jit(solution)/shard_map/all_to_all | solution.py:197
  156.2 1.4 shard_map.70
  (40 shorter events, 4.4 us)
Async XLA Ops:
  0.6 0.9 copy-start
  0.6 60.5 %copy-start.7 = (f32[512]{0:T(512)S(1)}, f32[512]{0:T(512)}, u32[]{:S(2)}) copy-start(f32[512]{0:T(512)} %param.8) | copy-start | bytes 6148
  1.5 59.6 %copy-start.6 = (bf16[512,256]{1,0:T(8,128)(2,1)S(1)}, bf16[512,256]{1,0:T(8,128)(2,1)}, u32[]{:S(2)}) copy-start(bf16[512,256]{1,0:T(8,128)(2,1)} %param.6) | copy-start | bytes 786436
  2.2 21.0 %all-to-all-start = ((bf16[8,48,128]{2,1,0:T(8,128)(2,1)}), bf16[8,48,128]{2,1,0:T(8,128)(2,1)}, u32[]{:S(2)}, u32[]{:S(2)}) async-start(bf16[8,48,128]{2,1,0:T(8,128)(2,1)} %bitcast.1), calls=%async_computation | async-start | bytes 196608 | tf_op jit(solution)/shard_map/all_to_all | solution.py:154
  15.9 12.4 %collective-permute-start = (bf16[32,8,256]{2,1,0:T(8,128)(2,1)S(1)}, bf16[32,8,256]{2,1,0:T(8,128)(2,1)S(1)}, u32[]{:S(2)}, u32[]{:S(2)}) collective-permute-start(bf16[32,8,256]{2,1,0:T(8,128)(2,1)S(1)} %dynamic-slice_bitcast_fusion), channel_id=1, source_target_pairs={{0,16},{16,0},{1,17},{17,1},{2,18},{18,2},{3,19},{19,3},{4,20},{20... | collective-permute-start | bytes 393224 | tf_op jit(solution)/shard_map/ppermute | solution.py:160
  23.2 12.7 %all-to-all-start.1 = ((bf16[8,48,128]{2,1,0:T(8,128)(2,1)}), bf16[8,48,128]{2,1,0:T(8,128)(2,1)S(1)}, u32[]{:S(2)}, u32[]{:S(2)}) async-start(bf16[8,48,128]{2,1,0:T(8,128)(2,1)} %all-to-all-done), calls=%async_computation.1 | async-start | bytes 196608 | tf_op jit(solution)/shard_map/all_to_all | solution.py:155
  35.9 25.3 %all-to-all-start.2 = ((bf16[32,16,256]{2,1,0:T(8,128)(2,1)}), bf16[32,16,256]{2,1,0:T(8,128)(2,1)S(1)}, u32[]{:S(2)}, u32[]{:S(2)}) async-start(bf16[32,16,256]{2,1,0:T(8,128)(2,1)} %maximum_bitcast_fusion), calls=%async_computation.2 | async-start | bytes 524288 | tf_op jit(solution)/shard_map/all_to_all | solution.py:165
  48.6 7.1 %collective-permute-start.1 = (bf16[48,1024]{1,0:T(8,128)(2,1)S(1)}, bf16[48,1024]{1,0:T(8,128)(2,1)S(1)}, u32[]{:S(2)}, u32[]{:S(2)}) collective-permute-start(bf16[48,1024]{1,0:T(8,128)(2,1)S(1)} %copy_bitcast_fusion), channel_id=1, source_target_pairs={{0,32},{32,0},{64,96},{96,64},{1,33},{33,1},{65,97},{97,65},{2,34}... | collective-permute-start | bytes 294920 | tf_op jit(solution)/shard_map/ppermute | solution.py:167
  51.8 9.4 %collective-permute-start.2 = (bf16[48,1024]{1,0:T(8,128)(2,1)S(1)}, bf16[48,1024]{1,0:T(8,128)(2,1)S(1)}, u32[]{:S(2)}, u32[]{:S(2)}) collective-permute-start(bf16[48,1024]{1,0:T(8,128)(2,1)S(1)} %copy_bitcast_fusion), channel_id=1, source_target_pairs={{0,64},{32,96},{64,0},{96,32},{1,65},{33,97},{65,1},{97,33},{2,66}... | collective-permute-start | bytes 294920 | tf_op jit(solution)/shard_map/ppermute | solution.py:167
  63.5 37.7 %copy-start.8 = (s32[8]{0:T(128)S(1)}, s32[8]{0:T(128)}, u32[]{:S(2)}) copy-start(s32[8]{0:T(128)} %constant.68.clone) | copy-start | bytes 100
  63.5 54.5 %all-to-all-start.3 = ((bf16[8,512,256]{2,1,0:T(8,128)(2,1)}), bf16[8,512,256]{2,1,0:T(8,128)(2,1)S(1)}, u32[]{:S(2)}, u32[]{:S(2)}) async-start(bf16[8,512,256]{2,1,0:T(8,128)(2,1)} %broadcast_in_dim.2), calls=%async_computation.3 | async-start | bytes 4194304 | tf_op jit(solution)/shard_map/all_to_all | solution.py:29
  67.2 7.2 %collective-permute-start.3 = (bf16[48,1024]{1,0:T(8,128)(2,1)S(1)}, bf16[48,1024]{1,0:T(8,128)(2,1)S(1)}, u32[]{:S(2)}, u32[]{:S(2)}) collective-permute-start(bf16[48,1024]{1,0:T(8,128)(2,1)S(1)} %copy_bitcast_fusion), channel_id=1, source_target_pairs={{0,96},{32,64},{64,32},{96,0},{1,97},{33,65},{65,33},{97,1},{2,98}... | collective-permute-start | bytes 294920 | tf_op jit(solution)/shard_map/ppermute | solution.py:167
  74.4 53.2 %copy-start.5 = (bf16[192,1024]{1,0:T(8,128)(2,1)}, bf16[192,1024]{1,0:T(8,128)(2,1)S(1)}, u32[]{:S(2)}) copy-start(bf16[192,1024]{1,0:T(8,128)(2,1)S(1)} %constant_dynamic-update-slice_fusion.refs_0_) | copy-start | bytes 1179652
  74.4 10.0 %collective-permute-start.4 = (bf16[192,1024]{1,0:T(8,128)(2,1)S(1)}, bf16[192,1024]{1,0:T(8,128)(2,1)}, u32[]{:S(2)}, u32[]{:S(2)}) collective-permute-start(bf16[192,1024]{1,0:T(8,128)(2,1)S(1)} %constant_dynamic-update-slice_fusion.refs_0_), channel_id=1, source_target_pairs={{0,128},{128,256},{256,384},{384,512},{512,640},{640,768},{768,896... | collective-permute-start | bytes 1179656 | tf_op jit(solution)/shard_map/ppermute | solution.py:185
  77.5 8.9 %collective-permute-start.7 = (bf16[192,1024]{1,0:T(8,128)(2,1)S(1)}, bf16[192,1024]{1,0:T(8,128)(2,1)}, u32[]{:S(2)}, u32[]{:S(2)}) collective-permute-start(bf16[192,1024]{1,0:T(8,128)(2,1)S(1)} %constant_dynamic-update-slice_fusion.refs_0_), channel_id=1, source_target_pairs={{0,896},{128,0},{256,128},{384,256},{512,384},{640,512},{768,640},... | collective-permute-start | bytes 1179656 | tf_op jit(solution)/shard_map/ppermute | solution.py:186
  84.4 10.1 %collective-permute-start.5 = (bf16[192,1024]{1,0:T(8,128)(2,1)}, bf16[192,1024]{1,0:T(8,128)(2,1)S(1)}, u32[]{:S(2)}, u32[]{:S(2)}) collective-permute-start(bf16[192,1024]{1,0:T(8,128)(2,1)} %collective-permute-done.4.refs_1_), channel_id=1, source_target_pairs={{0,128},{128,256},{256,384},{384,512},{512,640},{640,768},{768,896... | collective-permute-start | bytes 1179656 | tf_op jit(solution)/shard_map/ppermute | solution.py:185
  86.4 10.0 %collective-permute-start.8 = (bf16[192,1024]{1,0:T(8,128)(2,1)}, bf16[192,1024]{1,0:T(8,128)(2,1)S(1)}, u32[]{:S(2)}, u32[]{:S(2)}) collective-permute-start(bf16[192,1024]{1,0:T(8,128)(2,1)} %collective-permute-done.7.refs_2_), channel_id=1, source_target_pairs={{0,896},{128,0},{256,128},{384,256},{512,384},{640,512},{768,640},... | collective-permute-start | bytes 1179656 | tf_op jit(solution)/shard_map/ppermute | solution.py:186
  94.5 33.1 %copy-start.3 = (bf16[192,1024]{1,0:T(8,128)(2,1)}, bf16[192,1024]{1,0:T(8,128)(2,1)S(1)}, u32[]{:S(2)}) copy-start(bf16[192,1024]{1,0:T(8,128)(2,1)S(1)} %collective-permute-done.5.refs_3_) | copy-start | bytes 1179652
  94.5 23.5 %collective-permute-start.6 = (bf16[192,1024]{1,0:T(8,128)(2,1)S(1)}, bf16[192,1024]{1,0:T(8,128)(2,1)}, u32[]{:S(2)}, u32[]{:S(2)}) collective-permute-start(bf16[192,1024]{1,0:T(8,128)(2,1)S(1)} %collective-permute-done.5.refs_3_), channel_id=1, source_target_pairs={{0,128},{128,256},{256,384},{384,512},{512,640},{640,768},{768,896... | collective-permute-start | bytes 1179656 | tf_op jit(solution)/shard_map/ppermute | solution.py:185
  96.4 31.2 %copy-start.4 = (bf16[192,1024]{1,0:T(8,128)(2,1)}, bf16[192,1024]{1,0:T(8,128)(2,1)S(1)}, u32[]{:S(2)}) copy-start(bf16[192,1024]{1,0:T(8,128)(2,1)S(1)} %collective-permute-done.8.refs_4_) | copy-start | bytes 1179652
  96.4 21.5 %collective-permute-start.9 = (bf16[192,1024]{1,0:T(8,128)(2,1)S(1)}, bf16[192,1024]{1,0:T(8,128)(2,1)}, u32[]{:S(2)}, u32[]{:S(2)}) collective-permute-start(bf16[192,1024]{1,0:T(8,128)(2,1)S(1)} %collective-permute-done.8.refs_4_), channel_id=1, source_target_pairs={{0,896},{128,0},{256,128},{384,256},{512,384},{640,512},{768,640},... | collective-permute-start | bytes 1179656 | tf_op jit(solution)/shard_map/ppermute | solution.py:186
  101.9 12.7 %collective-permute-start.10 = (bf16[96,1024]{1,0:T(8,128)(2,1)}, bf16[96,1024]{1,0:T(8,128)(2,1)}, u32[]{:S(2)}, u32[]{:S(2)}) collective-permute-start(bf16[96,1024]{1,0:T(8,128)(2,1)} %slice.8), channel_id=1, source_target_pairs={{0,256},{128,384},{256,512},{384,640},{512,768},{640,896},{768,0},... | collective-permute-start | bytes 589832 | tf_op jit(solution)/shard_map/ppermute | solution.py:182
  104.5 13.4 %collective-permute-start.11 = (bf16[96,1024]{1,0:T(8,128)(2,1)}, bf16[96,1024]{1,0:T(8,128)(2,1)}, u32[]{:S(2)}, u32[]{:S(2)}) collective-permute-start(bf16[96,1024]{1,0:T(8,128)(2,1)} %slice.9), channel_id=1, source_target_pairs={{0,768},{128,896},{256,0},{384,128},{512,256},{640,384},{768,512},... | collective-permute-start | bytes 589832 | tf_op jit(solution)/shard_map/ppermute | solution.py:183
  118.0 9.6 %copy-start.2 = (bf16[8,512,256]{2,1,0:T(8,128)(2,1)}, bf16[8,512,256]{2,1,0:T(8,128)(2,1)S(1)}, u32[]{:S(2)}) copy-start(bf16[8,512,256]{2,1,0:T(8,128)(2,1)S(1)} %all-to-all-done.3) | copy-start | bytes 6291460
  118.0 15.0 %collective-permute-start.12 = (bf16[8,4,128,256]{3,2,1,0:T(8,128)(2,1)S(1)}, bf16[8,4,128,256]{3,2,1,0:T(8,128)(2,1)}, u32[]{:S(2)}, u32[]{:S(2)}) collective-permute-start(bf16[8,4,128,256]{3,2,1,0:T(8,128)(2,1)S(1)} %bitcast.48), channel_id=1, source_target_pairs={{0,16},{16,0},{1,17},{17,1},{2,18},{18,2},{3,19},{19,3},{4,20},{20... | collective-permute-start | bytes 6291464 | tf_op jit(solution)/shard_map/ppermute | solution.py:194
  133.0 23.2 %copy-start.1 = (s32[18]{0:T(128)S(1)}, s32[18]{0:T(128)}, u32[]{:S(2)}) copy-start(s32[18]{0:T(128)} %pad_add_fusion.index) | copy-start | bytes 220
